TPU v7x, 128 devices: a whole 4x4x4 slice. The times are simulated.
128 devices in a mesh: dp: 16 (over x, y), head: 8 (over z, core).
Axes of the slice: x: 4, y: 4, z: 4, core: 2. Of those that a mesh axis runs over, the one named last changes fastest.
Arguments:
- inputs: bfloat16 [4096, 3072], P('dp'), may hold values from -6 to 6
- grad_y: bfloat16 [4096, 3072], P('dp'), may hold values from -1.5 to 1.5
- q_pre: bfloat16 [4096, 3072], P('dp', 'head'), may hold values from -6 to 6
- f_pre: bfloat16 [4096, 3072], P('dp', 'head'), may hold values from -6 to 10
- v_pre: bfloat16 [4096, 3072], P('dp', 'head'), may hold values from -6 to 6
- w_out: bfloat16 [3072, 3072], P('head'), may hold values from -0.109375 to 0.109375
- err_in: bfloat16 [16, 3, 3072, 3072], P('dp', None, None, 'head'), may hold values from -3 to 3
- err_out: bfloat16 [16, 3072, 3072], P('dp', 'head'), may hold values from -3 to 3
- basis_in: float32 [3, 64, 3072], P(None, None, 'head'), may hold values from -6 to 6
- basis_out: float32 [64, 3072], replicated, may hold values from -6 to 6
Outputs:
- new_err_in: bfloat16 [16, 3, 3072, 3072], P('dp', None, None, 'head')
- new_err_out: bfloat16 [16, 3072, 3072], P('dp', 'head')
- factor_in: float32 [3, 64, 3072], P(None, None, 'head')
- factor_out: float32 [64, 3072], replicated
All inputs are finite; a program needn't handle non-finite values.
Results may differ from a plain program's by a relative error of at most 0.0072.
The roundings to bfloat16 on the way count: a program that leaves them out, or rounds other values in their place, can miss the bound.
Values sent between devices are 32-bit elements; how exact they have to be, the bound alone decides.
No kernel may reach another device: no remote copies, remote signals or barrier semaphores. Data moves between devices by JAX's collectives and lax.ppermute only.
A program may use at most 128 MiB of HBM per device.

v0:
```python
import jax
import jax.numpy as jnp
from jax import lax
from jax.sharding import PartitionSpec as P

DK = 128
SEQ = 256
BLOCK = 32


EXACT = lax.Precision.HIGHEST


def recurrence_out(q_rows, f_rows, v_rows):
    tokens_here, columns = q_rows.shape
    heads_here = columns // DK
    sequences = tokens_here // SEQ
    blocks = SEQ // BLOCK

    def shaped(array):
        return array.reshape(sequences, blocks, BLOCK, heads_here, DK)

    queries = shaped(jax.nn.silu(q_rows))
    log_decay = shaped(jax.nn.log_sigmoid(f_rows))
    gate_keys = shaped(jax.nn.sigmoid(-f_rows))
    values = shaped(v_rows)
    running = jnp.cumsum(log_decay, axis=2)
    closing = running[:, :, -1]
    spread = running[:, :, :, None] - running[:, :, None]
    causal = lax.broadcasted_iota(jnp.int32, (BLOCK, BLOCK, 1, 1), 0) >= lax.broadcasted_iota(
        jnp.int32, (BLOCK, BLOCK, 1, 1), 1
    )
    weights = jnp.exp(jnp.where(causal, spread, -jnp.inf))
    scores = jnp.einsum("sntha,snuha,sntuha->snhtu", queries, gate_keys, weights, precision=EXACT)
    inner_part = jnp.einsum("snhtu,snuhb->snthb", scores, values, precision=EXACT)
    decayed_query = queries * jnp.exp(running)
    decayed_key = gate_keys * jnp.exp(closing[:, :, None] - running)

    def advance(state, items):
        query_block, key_block, value_block, close_block = items
        output = jnp.einsum("stha,shab->sthb", query_block, state, precision=EXACT)
        state = jnp.exp(close_block)[..., None] * state + jnp.einsum(
            "stha,sthb->shab", key_block, value_block, precision=EXACT
        )
        return (state, output)

    def leading(array):
        return jnp.moveaxis(array, 1, 0)

    initial = jnp.zeros((sequences, heads_here, DK, DK), jnp.float32)
    _, cross_part = lax.scan(
        advance,
        initial,
        (leading(decayed_query), leading(decayed_key), leading(values), leading(closing)),
    )
    total = inner_part + jnp.moveaxis(cross_part, 0, 1)
    return total.reshape(tokens_here, columns)


def orthonormal(rows):
    gram = jnp.dot(rows, rows.T, precision=EXACT)
    return jax.scipy.linalg.solve_triangular(jnp.linalg.cholesky(gram), rows, lower=True)


def solve_rows(gram, rows):
    return jax.scipy.linalg.solve_triangular(jnp.linalg.cholesky(gram), rows, lower=True)


def shards(inputs, grad_y, q_pre, f_pre, v_pre, w_out, err_in, err_out, basis_in, basis_out):
    data_count = lax.axis_size("dp")
    grad_o = jnp.dot(grad_y, w_out.T, preferred_element_type=jnp.float32).astype(jnp.bfloat16)
    hidden, pullback = jax.vjp(
        recurrence_out,
        q_pre.astype(jnp.float32),
        f_pre.astype(jnp.float32),
        v_pre.astype(jnp.float32),
    )
    grad_q, grad_f, grad_v = pullback(grad_o.astype(jnp.float32))
    hidden = hidden.astype(jnp.bfloat16)
    grads_pre = jnp.stack([grad_q, grad_f, grad_v]).astype(jnp.bfloat16)
    moment_out = jnp.einsum(
        "tc,td->cd", hidden, grad_y, preferred_element_type=jnp.float32
    ) + err_out[0].astype(jnp.float32)
    left_out = lax.psum(jnp.einsum("rd,cd->rc", basis_out, moment_out, precision=EXACT), "dp")
    gram_out = lax.psum(jnp.dot(left_out, left_out.T, precision=EXACT), "head")
    ortho_out = solve_rows(gram_out, left_out)
    moment_in = jnp.einsum(
        "td,ptc->pdc", inputs, grads_pre, preferred_element_type=jnp.float32
    ) + err_in[0].astype(jnp.float32)
    left_in = jnp.einsum("prc,pdc->prd", basis_in, moment_in, precision=EXACT)
    right_out = jnp.einsum("rc,cd->rd", ortho_out, moment_out, precision=EXACT)
    summed_in = lax.psum(left_in, ("dp", "head"))
    ortho_in = jax.vmap(orthonormal)(summed_in)
    factor_out = lax.psum(right_out, ("dp", "head"))
    factor_out = factor_out / data_count
    right_in = jnp.einsum("prd,pdc->prc", ortho_in, moment_in, precision=EXACT)
    factor_in = lax.psum(right_in, "dp") / data_count
    rest_in = moment_in - jnp.einsum("prd,prc->pdc", ortho_in, factor_in, precision=EXACT)
    rest_out = moment_out - jnp.einsum("rc,rd->cd", ortho_out, factor_out, precision=EXACT)
    return (
        rest_in[None].astype(jnp.bfloat16),
        rest_out[None].astype(jnp.bfloat16),
        factor_in,
        factor_out,
    )


def solution(mesh):
    placed = (
        P("dp", None),
        P("dp", None),
        P("dp", "head"),
        P("dp", "head"),
        P("dp", "head"),
        P("head", None),
        P("dp", None, None, "head"),
        P("dp", "head", None),
        P(None, None, "head"),
        P(),
    )
    return jax.shard_map(
        shards,
        mesh=mesh,
        in_specs=placed,
        out_specs=(P("dp", None, None, "head"), P("dp", "head", None), P(None, None, "head"), P()),
        check_vma=False,
    )
```

profile of v0, /device:TPU:0, one launch (start us, length us, event | category | flops | bytes accessed | tf_op | source)
XLA Modules:
  0.0 651.5 jit_solution(4561076155546976701)
XLA Ops:
  30.7 44.8 %while.42 = (s32[]{:T(128)}, f32[1,3,128,128]{3,2,1,0:T(8,128)S(1)}, f32[8,1,32,3,128]{4,2,3,1,0:T(8,128)}, f32[8,1,3,128,128]{4,3,2,1,0:T(8,128)}, f32[8,1,3,12...) while((s32[]{:T(128)}, ...), condition=%wide.region_2.3_spmd.clone, body=%wide.region_1.2_spmd.clone.sunk | while | flops 37994496 | bytes 1196677 | solution.py:51
  78.4 4.8 fusion.47
  86.7 5.3 convolution_bitcast_fusion.7
  92.1 3.1 convolution_convert_fusion
  99.2 8.9 %fusion.49 = f32[8,3,128,32]{2,3,1,0:T(8,128)} fusion(f32[8,3,128,32]{2,3,1,0:T(8,128)} %copy-done.26, f32[8,32,3,128]{3,1,2,0:T(8,128)} %copy-done.30, f32[8,3,32,32]{3,2,1,0:T(8,128)S(1)} %fusion.108, pred[32,32]{1,0:T(8,128)(4,1)S(1)} %iota_compare_fusion.2), kind=kLoop, calls=%fused_computation.69 | loop fusion | flops 15630336 | bytes 1278976
  108.2 6.8 %fusion.48 = f32[8,3,128,32]{2,3,1,0:T(8,128)} fusion(f32[8,3,128,32]{2,3,1,0:T(8,128)S(1)} %copy-done.29, f32[8,32,3,128]{3,1,2,0:T(8,128)S(1)} %copy-done.31, f32[8,3,32,32]{3,2,1,0:T(8,128)S(1)} %fusion.108, pred[32,32]{1,0:T(8,128)(4,1)S(1)} %iota_compare_fusion.2), kind=kLoop, calls=%fused_computation.67 | loop fusion | flops 15630336 | bytes 1278976
  115.1 9.9 %fusion.51 = (f32[8,32,3,128]{3,1,2,0:T(8,128)}, f32[8,32,3,128]{3,1,2,0:T(8,128)}) fusion(f32[8,3,128,32]{2,3,1,0:T(8,128)S(1)} %copy-done.27, f32[8,32,3,128]{3,1,2,0:T(8,128)} %copy-done.30, f32[8,3,128,32]{2,3,1,0:T(8,128)S(1)} %copy-done.29, f32[8,3,32,32]{3,2,1,0:T(8,128)} %copy-done.32, pred[32,32]{1,0:T(8,128)(4,1)S(1)} %iota_compare_fusion.2), kind=kLoop, calls=%fused_computation.72 | loop fusion | flops 24969216 | bytes 2065408 | tf_op jit(solution)/shard_map/transpose(jvp())/reduce_sum | solution.py:29
  126.1 105.6 %while.43 = (s32[]{:T(128)}, f32[1,3,128,128]{2,3,1,0:T(8,128)S(1)}, f32[8,1,32,3,128]{4,0,2,3,1:T(8,128)S(1)}, f32[8,1,32,3,128]{4,0,2,3,1:T(8,128)S(1)}, f32[8...) while((s32[]{:T(128)}, ...), condition=%wide.region_5.6_spmd.clone, body=%wide.region_3.5_spmd.clone.sunk | while | flops 75890688 | bytes 2774216 | solution.py:51
  132.9 2.5 dynamic_update_slice.79
  146.1 2.5 dynamic_update_slice.79
  159.3 2.5 dynamic_update_slice.79
  172.5 2.5 dynamic_update_slice.79
  202.8 2.5 dynamic_update_slice.78
  231.8 2.6 bitcast_add_fusion
  241.5 10.6 %copy.165 = bf16[1,3,3072,384]{2,3,1,0:T(8,128)(2,1)} copy(bf16[1,3,3072,384]{3,2,1,0:T(8,128)(2,1)} %param.20) | data formatting | bytes 14155776 | tf_op args[6]
  252.8 5.1 convert_add_fusion
  257.9 5.0 copy-done.2
  262.9 10.4 %convolution_bitcast_fusion.4 = f32[3,64,3072]{2,1,0:T(8,128)} fusion(f32[3,3072,384]{1,2,0:T(8,128)S(1)} %convert_add_fusion, f32[3,64,384]{2,1,0:T(8,128)S(1)} %copy-done.25), kind=kOutput, calls=%fused_computation.78 | convolution fusion | flops 2717908992 | bytes 16809984 | tf_op jit(solution)/shard_map/prc,pdc->prd/dot_general | solution.py:90
  274.6 27.5 %psum.38 = f32[64,64]{0,1:T(8,128)S(1)} all-reduce(f32[64,64]{0,1:T(8,128)S(1)} %fusion.125), channel_id=1, replica_groups=mesh['dp'=16,'head'=8] {'head'}, use_global_device_ids=true, to_apply=%region_15.16 | all-reduce | flops 4096 | bytes 32768 | tf_op jit(solution)/shard_map/psum | solution.py:85
  302.2 5.8 cholesky.61
  309.4 4.9 custom-call.17
  315.5 6.1 fusion.126
  321.7 152.5 %all-reduce.10.cloned.1.call-done = (f32[3,64,3072]{2,1,0:T(8,128)}, f32[64,3072]{1,0:T(8,128)}) async-done(((f32[3,64,3072]{2,1,0:T(8,128)}, f32[64,3072]{1,0:T(8,128)}), (f32[3,64,3072]{2,1,0:T(8,128)}, f32[64,3072]{1,0:T(8,128)})) %all-reduce.10.cloned.1.call-update) | async-done | bytes 3145744 | tf_op jit(solution)/shard_map/psum | solution.py:92
  475.5 4.9 fusion.123
  480.5 17.8 %custom-call.15 = f32[3,64,64]{2,1,0:T(8,128)S(1)} custom-call(f32[3,64,64]{2,1,0:T(8,128)S(1)} %fusion.114), custom_call_target="Cholesky" | custom-call | tf_op jit(solution)/shard_map/vmap(jit(cholesky))/cholesky | solution.py:62
  498.5 14.7 %custom-call.16 = f32[3,1,64,64]{2,3,1,0:T(8,128)S(1)} custom-call(f32[3,1,64,64]{3,2,1,0:T(8,128)S(1)} %select_bitcast_fusion), custom_call_target="InvertDiagBlocksLowerTriangular" | custom-call | tf_op jit(solution)/shard_map/vmap(jit(_solve_triangular))/triangular_solve | solution.py:62
  513.2 3.8 fusion.112
  517.0 17.9 %fusion.124 = f32[3,64,384]{2,1,0:T(8,128)} fusion(f32[3,64,3072]{2,1,0:T(8,128)S(1)} %fusion.112, f32[3,3072,384]{1,2,0:T(8,128)} %copy-done.2), kind=kOutput, calls=%fused_computation.192 | convolution fusion | flops 2717908992 | bytes 16809984 | tf_op jit(solution)/shard_map/prd,pdc->prc/dot_general | solution.py:96
  535.0 6.9 %fusion.53 = bf16[1,384,3072]{2,1,0:T(8,128)(2,1)} fusion(f32[384,3072]{1,0:T(8,128)} %copy-done.3, f32[64,384]{1,0:T(8,128)S(1)} %fusion.116, f32[64,3072]{1,0:T(8,128)S(1)} %broadcast_multiply_fusion), kind=kOutput, calls=%fused_computation.77 | convolution fusion | flops 908328960 | bytes 7962624 | tf_op jit(solution)/shard_map/rc,rd->cd/dot_general | solution.py:99
  541.8 74.6 %all-reduce.6.cloned.1.call-done = f32[3,64,384]{2,1,0:T(8,128)} async-done(((f32[3,64,384]{2,1,0:T(8,128)}), f32[3,64,384]{2,1,0:T(8,128)}) %all-reduce.6.cloned.1.call-update) | async-done | bytes 294928 | tf_op jit(solution)/shard_map/psum | solution.py:97
  617.4 17.1 %fusion.52 = bf16[1,3,3072,384]{2,3,1,0:T(8,128)(2,1)} fusion(f32[3,3072,384]{1,2,0:T(8,128)} %copy-done.2, f32[3,64,3072]{2,1,0:T(8,128)} %copy-done.4, f32[3,64,384]{2,1,0:T(8,128)S(1)} %broadcast_multiply_fusion.1), kind=kOutput, calls=%fused_computation.74 | convolution fusion | flops 2724986880 | bytes 23887872 | tf_op jit(solution)/shard_map/prd,prc->pdc/dot_general | solution.py:98
  634.5 10.3 %copy.175 = bf16[1,3,3072,384]{3,2,1,0:T(8,128)(2,1)} copy(bf16[1,3,3072,384]{2,3,1,0:T(8,128)(2,1)} %fusion.52) | data formatting | bytes 14155776
  (294 shorter events, 186.2 us)
Async XLA Ops:
  7.2 84.9 %copy-start = (bf16[384,3072]{1,0:T(8,128)(2,1)S(1)}, bf16[384,3072]{1,0:T(8,128)(2,1)}, u32[]{:S(2)}) copy-start(bf16[384,3072]{1,0:T(8,128)(2,1)} %param.19) | copy-start | bytes 7077892
  7.2 266.2 %all-reduce.8.cloned.1.call-start = ((), (), s32[]{:S(2)}) async-start(), calls=%async_computation.1 | async-start | bytes 196608 | tf_op jit(solution)/shard_map/psum | solution.py:84
  9.7 12.3 %copy-start.5 = (f32[256,384]{1,0:T(8,128)}, f32[256,384]{1,0:T(8,128)S(1)}, u32[]{:S(2)}) copy-start(f32[256,384]{1,0:T(8,128)S(1)} %copy.121) | copy-start | bytes 1179652
  24.0 5.1 copy-start.9
  75.5 7.7 %copy-start.14 = (bf16[8,32,3,128]{3,2,1,0:T(4,128)(2,1)S(1)}, bf16[8,32,3,128]{3,2,1,0:T(4,128)(2,1)}, u32[]{:S(2)}) copy-start(bf16[8,32,3,128]{3,2,1,0:T(4,128)(2,1)} %reshape.534) | copy-start | bytes 589828
  75.5 7.7 %copy-start.18 = (f32[8,1,32,3,128]{4,2,3,1,0:T(8,128)S(1)}, f32[8,1,32,3,128]{4,2,3,1,0:T(8,128)}, u32[]{:S(2)}) copy-start(f32[8,1,32,3,128]{4,2,3,1,0:T(8,128)} %get-tuple-element.324) | copy-start | bytes 1179652
  75.6 8.1 %copy-start.30 = (f32[8,32,3,128]{3,1,2,0:T(8,128)}, f32[8,32,3,128]{3,1,2,0:T(8,128)S(1)}, u32[]{:S(2)}) copy-start(f32[8,32,3,128]{3,1,2,0:T(8,128)S(1)} %copy.138) | copy-start | bytes 1179652
  75.6 8.2 %copy-start.7 = (bf16[1,384,3072]{2,1,0:T(8,128)(2,1)S(1)}, bf16[1,384,3072]{2,1,0:T(8,128)(2,1)}, u32[]{:S(2)}) copy-start(bf16[1,384,3072]{2,1,0:T(8,128)(2,1)} %param.21) | copy-start | bytes 7077892
  75.6 8.2 %copy-start.23 = (bf16[256,3072]{1,0:T(8,128)(2,1)S(1)}, bf16[256,3072]{1,0:T(8,128)(2,1)}, u32[]{:S(2)}) copy-start(bf16[256,3072]{1,0:T(8,128)(2,1)} %param.15) | copy-start | bytes 4718596
  76.9 6.8 %copy-start.26 = (f32[8,3,128,32]{2,3,1,0:T(8,128)}, f32[8,3,128,32]{2,3,1,0:T(8,128)S(1)}, u32[]{:S(2)}) copy-start(f32[8,3,128,32]{2,3,1,0:T(8,128)S(1)} %copy.221) | copy-start | bytes 1179652
  78.4 5.3 copy-start.28
  83.8 3.0 copy-start.24
  92.1 382.2 %all-reduce.10.cloned.1.call-start = ((), (), s32[]{:S(2)}) async-start(), calls=%async_computation.2 | async-start | bytes 6291456 | tf_op jit(solution)/shard_map/psum | solution.py:92
  95.2 13.0 %copy-start.29 = (f32[8,3,128,32]{2,3,1,0:T(8,128)S(1)}, f32[8,3,128,32]{2,3,1,0:T(8,128)}, u32[]{:S(2)}) copy-start(f32[8,3,128,32]{2,3,1,0:T(8,128)} %copy-done.28) | copy-start | bytes 1179652
  95.2 13.0 %copy-start.31 = (f32[8,32,3,128]{3,1,2,0:T(8,128)S(1)}, f32[8,32,3,128]{3,1,2,0:T(8,128)}, u32[]{:S(2)}) copy-start(f32[8,32,3,128]{3,1,2,0:T(8,128)} %copy-done.30) | copy-start | bytes 1179652
  99.2 8.9 %copy-start.32 = (f32[8,3,32,32]{3,2,1,0:T(8,128)}, f32[8,3,32,32]{3,2,1,0:T(8,128)S(1)}, u32[]{:S(2)}) copy-start(f32[8,3,32,32]{3,2,1,0:T(8,128)S(1)} %fusion.108) | copy-start | bytes 294916
  99.2 15.7 %copy-start.6 = (f32[256,384]{1,0:T(8,128)S(1)}, f32[256,384]{1,0:T(8,128)}, u32[]{:S(2)}) copy-start(f32[256,384]{1,0:T(8,128)} %copy-done.5) | copy-start | bytes 1179652
  108.2 6.9 %copy-start.27 = (f32[8,3,128,32]{2,3,1,0:T(8,128)S(1)}, f32[8,3,128,32]{2,3,1,0:T(8,128)}, u32[]{:S(2)}) copy-start(f32[8,3,128,32]{2,3,1,0:T(8,128)} %copy-done.26) | copy-start | bytes 1179652
  236.5 4.0 copy-start.13
  236.5 4.0 copy-start.17
  236.5 4.0 copy-start.20
  241.5 10.7 %copy-start.11 = (bf16[256,384]{0,1:T(8,128)(2,1)S(1)}, bf16[256,384]{0,1:T(8,128)(2,1)}, u32[]{:S(2)}) copy-start(bf16[256,384]{0,1:T(8,128)(2,1)} %copy-done.10) | copy-start | bytes 589828
  241.5 10.7 %copy-start.21 = (f32[256,384]{0,1:T(8,128)S(1)}, f32[256,384]{0,1:T(8,128)}, u32[]{:S(2)}) copy-start(f32[256,384]{0,1:T(8,128)} %copy.142) | copy-start | bytes 1179652
  241.5 10.7 %copy-start.22 = (f32[256,384]{0,1:T(8,128)S(1)}, f32[256,384]{0,1:T(8,128)}, u32[]{:S(2)}) copy-start(f32[256,384]{0,1:T(8,128)} %copy.147) | copy-start | bytes 1179652
  241.5 11.3 %copy-start.16 = (bf16[256,3072]{1,0:T(8,128)(2,1)S(1)}, bf16[256,3072]{1,0:T(8,128)(2,1)}, u32[]{:S(2)}) copy-start(bf16[256,3072]{1,0:T(8,128)(2,1)} %param.14) | copy-start | bytes 4718596
  252.8 10.1 %copy-start.25 = (f32[3,64,384]{2,1,0:T(8,128)S(1)}, f32[3,64,384]{2,1,0:T(8,128)}, u32[]{:S(2)}) copy-start(f32[3,64,384]{2,1,0:T(8,128)} %param.22) | copy-start | bytes 884740
  257.9 5.1 copy-start.2
  321.6 294.8 %all-reduce.6.cloned.1.call-start = ((), (), s32[]{:S(2)}) async-start(), calls=%async_computation | async-start | bytes 589824 | tf_op jit(solution)/shard_map/psum | solution.py:97
  475.4 59.5 %copy-start.8 = (f32[64,3072]{1,0:T(8,128)}, f32[64,3072]{1,0:T(8,128)S(1)}, u32[]{:S(2)}) copy-start(f32[64,3072]{1,0:T(8,128)S(1)} %broadcast_multiply_fusion) | copy-start | bytes 2359300
  517.0 17.9 %copy-start.4 = (f32[3,64,3072]{2,1,0:T(8,128)}, f32[3,64,3072]{2,1,0:T(8,128)S(1)}, u32[]{:S(2)}) copy-start(f32[3,64,3072]{2,1,0:T(8,128)S(1)} %fusion.112) | copy-start | bytes 7077892
  617.4 17.1 %copy-start.15 = (f32[3,64,384]{2,1,0:T(8,128)}, f32[3,64,384]{2,1,0:T(8,128)S(1)}, u32[]{:S(2)}) copy-start(f32[3,64,384]{2,1,0:T(8,128)S(1)} %broadcast_multiply_fusion.1) | copy-start | bytes 884740
  617.4 27.4 %copy-start.1 = (bf16[384,3072]{1,0:T(8,128)(2,1)S(1)}, bf16[384,3072]{1,0:T(8,128)(2,1)}, u32[]{:S(2)}) copy-start(bf16[384,3072]{1,0:T(8,128)(2,1)} %param.19) | copy-start | bytes 7077892
  (4 other events, 5.3 us)
Sparse Core Ops, SparseCore 0:
  92.2 84.4 all-reduce.7
  321.8 152.4 all-reduce.9
  535.1 81.3 all-reduce.5
where the time goes:
time: 664 us; the launch traced here: 652 us
  waiting for transfers between devices  227 us (34%)
  matrix products  154 us (23%)
  local copies, waits for them, and re-layouts  128 us (19%)
  other arithmetic  98.7 us (15%)
  blocking collectives  27.5 us (4%)
  between operations  14.7 us (2%)
    psum x1, waiting for transfers between devices, shards(): summed_in = lax.psum(left_in, ('dp', 'head'))  153 us
    psum x1, waiting for transfers between devices, shards(): factor_in = lax.psum(right_in, 'dp') / data_count  74.6 us
    dynamic_update_slice x48, local copies, waits for them, and re-layouts, recurrence_out(): lax.scan(advance, initial, (leading(decayed_query), leading(decayed_key),...  50.2 us
    unnamed x79, local copies, waits for them, and re-layouts  36.5 us
    dot_general x24, matrix products, advance(): output = jnp.einsum('stha,shab->sthb', query_block, state, precision=EXACT)  34.8 us
    dot_general x24, matrix products, advance(): jnp.einsum('stha,sthb->shab', key_block, value_block, precision=EXACT)  34 us
    psum x1, blocking collectives, shards(): gram_out = lax.psum(jnp.dot(left_out, left_out.T, precision=EXACT), 'head')  27.5 us
    another operation x4, other arithmetic, orthonormal(): jnp.linalg.cholesky(gram)  17.9 us
  transfers between devices with their start and end apart: 3, of which 2 were waited for; matrix products, arithmetic and copies ran while one was open for 28% of the time, Pallas kernels for 0%

commit v1 on v0

v1 whole, which is shorter than its diff:
```python
import functools

import jax
import jax.numpy as jnp
from jax import lax
from jax.experimental import pallas as pl
from jax.experimental.pallas import tpu as pltpu
from jax.sharding import Mesh, PartitionSpec as P

TOK = 256
DK = 128
HEADS = 3
COLS = HEADS * DK
RANK = 64
D = 3072
HALF = D // 2
TILE = 512
STEPS = HALF // TILE
CT = TILE // 128
N_DP = 16
CHIPS = 64
L_ROWS = 12 * 3 * RANK
LO_ROWS = HEADS * RANK
ROWS1 = 2560
RI_ROWS = 9 * RANK
RO_ROWS = 12 * RANK
ROWS2 = 1536

f32 = jnp.float32
bf16 = jnp.bfloat16
EXACT = lax.Precision.HIGHEST
VMEM = 48 * 1024 * 1024
SHIFTS = ((0, 1), (0, 2), (0, 3))


def nn(a, b):
    return lax.dot_general(a, b, (((1,), (0,)), ((), ())), preferred_element_type=f32)


def nt(a, b):
    return lax.dot_general(a, b, (((1,), (1,)), ((), ())), preferred_element_type=f32)


def tn(a, b):
    return lax.dot_general(a, b, (((0,), (0,)), ((), ())), preferred_element_type=f32)


def exact_nn(a, b):
    return lax.dot_general(a, b, (((1,), (0,)), ((), ())), precision=EXACT, preferred_element_type=f32)


def exact_nt(a, b):
    return lax.dot_general(a, b, (((1,), (1,)), ((), ())), precision=EXACT, preferred_element_type=f32)


def split2(a):
    high = a.astype(bf16)
    return high, (a - high.astype(f32)).astype(bf16)


def split3(a):
    high = a.astype(bf16)
    rest = a - high.astype(f32)
    mid = rest.astype(bf16)
    return high, mid, (rest - mid.astype(f32)).astype(bf16)


def stacked(a):
    return jnp.concatenate(split2(a), axis=0)


def folded(a):
    half = a.shape[0] // 2
    return a[:half] + a[half:]


def recurrence_kernel(gy_ref, w_ref, q_ref, f_ref, v_ref, hid_ref, grad_ref):
    grad_o = nt(gy_ref[...], w_ref[...]).astype(bf16)
    q = q_ref[...].astype(f32)
    f = f_ref[...].astype(f32)
    v = v_ref[...]
    q_gate = 1.0 / (1.0 + jnp.exp(-q))
    query = q * q_gate
    small = jnp.exp(-jnp.abs(f))
    key = jnp.where(f >= 0, small, 1.0) / (1.0 + small)
    decay = jnp.where(f >= 0, 1.0, small) / (1.0 + small)
    log_decay = jnp.minimum(f, 0.0) - jnp.log1p(small)

    row = lax.broadcasted_iota(jnp.int32, (TOK, TOK), 0)
    col = lax.broadcasted_iota(jnp.int32, (TOK, TOK), 1)
    lower = jnp.where(row >= col, 1.0, 0.0).astype(bf16)
    upper = jnp.where(row <= col, 1.0, 0.0).astype(bf16)
    differ = row ^ col
    high, mid, low = split3(log_decay)
    running = nn(lower, high) + (nn(lower, mid) + nn(lower, low))

    scores = jnp.zeros((TOK, TOK), f32)
    grad_s = split2(nt(grad_o, v))
    grad_st = split2(nt(v, grad_o))
    grad_query = jnp.zeros((TOK, DK), f32)
    grad_key = jnp.zeros((TOK, DK), f32)
    for size in (128, 64, 32, 16, 8):
        blocks = running.reshape(TOK // (2 * size), 2 * size, DK)
        spread = (blocks - blocks[:, size - 1 : size, :]).reshape(TOK, DK)
        if size > 8:
            q_scale = jnp.exp(jnp.minimum(spread, 0.0))
            k_scale = jnp.exp(jnp.minimum(-spread, 0.0))
            within = (differ >= size) & (differ < 2 * size)
            mask = within & (row > col)
            mask_t = within & (row < col)
        else:
            q_scale = jnp.exp(spread)
            k_scale = jnp.exp(-spread)
            within = differ < 2 * size
            mask = within & (row >= col)
            mask_t = within & (row <= col)
        q_high, q_low = split2(query * q_scale)
        k_high, k_low = split2(key * k_scale)
        level = nt(
            jnp.concatenate([q_high, q_high, q_low], axis=1),
            jnp.concatenate([k_high, k_low, k_high], axis=1),
        )
        scores = jnp.where(mask, level, scores)
        keep = jnp.where(mask, 1.0, 0.0).astype(bf16)
        keep_t = jnp.where(mask_t, 1.0, 0.0).astype(bf16)
        both = nn(grad_s[0] * keep, jnp.concatenate([k_high, k_low], axis=1))
        grad_query += q_scale * (both[:, :DK] + both[:, DK:] + nn(grad_s[1] * keep, k_high))
        both = nn(grad_st[0] * keep_t, jnp.concatenate([q_high, q_low], axis=1))
        grad_key += k_scale * (both[:, :DK] + both[:, DK:] + nn(grad_st[1] * keep_t, q_high))
    s_high, s_low = split2(scores)
    hid_ref[...] = (nn(s_high, v) + nn(s_low, v)).astype(bf16)
    grad_v = tn(s_high, grad_o) + tn(s_low, grad_o)
    high, mid, low = split3(query * grad_query - key * grad_key)
    grad_decay = nn(upper, high) + (nn(upper, mid) + nn(upper, low))
    grad_ref[0] = (grad_query * (q_gate + query * (1.0 - q_gate))).astype(bf16)
    grad_ref[1] = (key * (grad_decay - grad_key * decay)).astype(bf16)
    grad_ref[2] = grad_v.astype(bf16)


def recurrence(grad_y, w_out, q_pre, f_pre, v_pre):
    per_head = pl.BlockSpec((TOK, DK), lambda h: (0, h))
    return pl.pallas_call(
        recurrence_kernel,
        grid=(HEADS,),
        in_specs=[
            pl.BlockSpec((TOK, D), lambda h: (0, 0)),
            pl.BlockSpec((DK, D), lambda h: (h, 0)),
            per_head,
            per_head,
            per_head,
        ],
        out_specs=[per_head, pl.BlockSpec((3, TOK, DK), lambda h: (0, 0, h))],
        out_shape=[
            jax.ShapeDtypeStruct((TOK, COLS), bf16),
            jax.ShapeDtypeStruct((3, TOK, COLS), bf16),
        ],
        compiler_params=pltpu.CompilerParams(vmem_limit_bytes=VMEM),
        name="recurrence",
    )(grad_y, w_out, q_pre, f_pre, v_pre)


def tiles_of(a):
    return [a[:, 128 * i : 128 * (i + 1)] for i in range(a.shape[1] // 128)]


def left_kernel(half_ref, x_ref, gy_ref, grads_ref, hid_ref, err_in_ref, err_out_ref, basis_in_ref,
                basis_out_ref, left_ref, left_out_ref, token_scr):
    step = pl.program_id(0)

    @pl.when(step == 0)
    def _():
        for p in range(3):
            token_scr[p] = stacked(folded(nt(stacked(basis_in_ref[p]), grads_ref[p])))
        left_out_ref[...] = jnp.zeros_like(left_out_ref)

    for p in range(3):
        part = nn(token_scr[p], x_ref[...]) + nt(stacked(basis_in_ref[p]), err_in_ref[p])
        for i, tile in enumerate(tiles_of(folded(part))):
            left_ref[i, RANK * p : RANK * (p + 1), :] = tile
    basis = stacked(basis_out_ref[...])
    tokens = stacked(folded(nt(basis, gy_ref[...])))
    part = folded(nt(basis, err_out_ref[...]) + nn(tokens, hid_ref[...]))
    for i, tile in enumerate(tiles_of(part)):
        left_out_ref[i] += tile


def left(half, inputs, grad_y, grads, hidden, err_in, err_out, basis_in, basis_out):
    return pl.pallas_call(
        left_kernel,
        grid_spec=pltpu.PrefetchScalarGridSpec(
            num_scalar_prefetch=1,
            grid=(STEPS,),
            in_specs=[
                pl.BlockSpec((TOK, TILE), lambda j, h: (0, h[0] * STEPS + j)),
                pl.BlockSpec((TOK, TILE), lambda j, h: (0, h[0] * STEPS + j)),
                pl.BlockSpec((3, TOK, COLS), lambda j, h: (0, 0, 0)),
                pl.BlockSpec((TOK, COLS), lambda j, h: (0, 0)),
                pl.BlockSpec((3, TILE, COLS), lambda j, h: (0, h[0] * STEPS + j, 0)),
                pl.BlockSpec((COLS, TILE), lambda j, h: (0, h[0] * STEPS + j)),
                pl.BlockSpec((3, RANK, COLS), lambda j, h: (0, 0, 0)),
                pl.BlockSpec((RANK, TILE), lambda j, h: (0, h[0] * STEPS + j)),
            ],
            out_specs=[
                pl.BlockSpec((CT, 3 * RANK, 128), lambda j, h: (j, 0, 0)),
                pl.BlockSpec((HEADS, RANK, 128), lambda j, h: (0, 0, 0)),
            ],
            scratch_shapes=[pltpu.VMEM((3, 2 * RANK, TOK), bf16)],
        ),
        out_shape=[
            jax.ShapeDtypeStruct((12, 3 * RANK, 128), f32),
            jax.ShapeDtypeStruct((HEADS, RANK, 128), f32),
        ],
        compiler_params=pltpu.CompilerParams(vmem_limit_bytes=VMEM),
        name="left",
    )(half, inputs, grad_y, grads, hidden, err_in, err_out, basis_in, basis_out)


def wide(block, rows):
    return jnp.concatenate([block[i * rows : (i + 1) * rows] for i in range(block.shape[0] // rows)], axis=1)


def right_kernel(halves_ref, left_ref, left_out_ref, x_ref, gy_ref, hid_ref, err_in_ref, err_out_ref,
                 right_ref, token_ref, right_out_ref, gram_ref, out_scr):
    step = pl.program_id(0)

    @pl.when(step == 0)
    def _():
        right_ref[...] = jnp.zeros_like(right_ref)
        token_ref[...] = jnp.zeros_like(token_ref)
        left_out = wide(left_out_ref[...], RANK)
        gram_ref[...] = jnp.concatenate([exact_nt(left_out, left_out), jnp.zeros((RANK, RANK), f32)], axis=1)
        factor = stacked(left_out)
        out_scr[:, :COLS] = factor
        out_scr[:, COLS:] = stacked(folded(nt(factor, hid_ref[...])))

    rows = wide(left_ref[...], 3 * RANK)
    for p in range(3):
        factor = stacked(rows[RANK * p : RANK * (p + 1)])
        right_ref[p] += folded(nn(factor, err_in_ref[p]))
        token_ref[p] += folded(nt(factor, x_ref[...]))
    part = folded(nn(out_scr[:, :COLS], err_out_ref[...]) + nn(out_scr[:, COLS:], gy_ref[...]))
    for i, tile in enumerate(tiles_of(part)):
        right_out_ref[i] = tile


def right(halves, gathered, own, inputs, grad_y, hidden, err_in, err_out):
    return pl.pallas_call(
        right_kernel,
        grid_spec=pltpu.PrefetchScalarGridSpec(
            num_scalar_prefetch=1,
            grid=(STEPS,),
            in_specs=[
                pl.BlockSpec((CT * 3 * RANK, 128), lambda j, h: (j, 0)),
                pl.BlockSpec((LO_ROWS, 128), lambda j, h: (L_ROWS // LO_ROWS, 0)),
                pl.BlockSpec((TOK, TILE), lambda j, h: (0, h[0] * STEPS + j)),
                pl.BlockSpec((TOK, TILE), lambda j, h: (0, h[1] * STEPS + j)),
                pl.BlockSpec((TOK, COLS), lambda j, h: (0, 0)),
                pl.BlockSpec((3, TILE, COLS), lambda j, h: (0, h[0] * STEPS + j, 0)),
                pl.BlockSpec((COLS, TILE), lambda j, h: (0, h[1] * STEPS + j)),
            ],
            out_specs=[
                pl.BlockSpec((3, RANK, COLS), lambda j, h: (0, 0, 0)),
                pl.BlockSpec((3, RANK, TOK), lambda j, h: (0, 0, 0)),
                pl.BlockSpec((CT, RANK, 128), lambda j, h: (j, 0, 0)),
                pl.BlockSpec((RANK, 128), lambda j, h: (0, 0)),
            ],
            scratch_shapes=[pltpu.VMEM((2 * RANK, COLS + TOK), bf16)],
        ),
        out_shape=[
            jax.ShapeDtypeStruct((3, RANK, COLS), f32),
            jax.ShapeDtypeStruct((3, RANK, TOK), f32),
            jax.ShapeDtypeStruct((12, RANK, 128), f32),
            jax.ShapeDtypeStruct((RANK, 128), f32),
        ],
        compiler_params=pltpu.CompilerParams(vmem_limit_bytes=VMEM),
        name="right",
    )(halves, gathered, own, inputs, grad_y, hidden, err_in, err_out)


def join_kernel(right_a_ref, right_b_ref, token_a_ref, token_b_ref, grads_ref, keep_ref, arrived_ref, out_ref):
    for p in range(3):
        tokens = stacked(token_a_ref[p] + token_b_ref[p])
        total = right_a_ref[p] + right_b_ref[p] + folded(nn(tokens, grads_ref[p]))
        for i, tile in enumerate(tiles_of(total)):
            out_ref[pl.ds((HEADS * p + i) * RANK, RANK), :] = tile
    out_ref[RI_ROWS : RI_ROWS + RO_ROWS, :] = keep_ref[...] + arrived_ref[...]
    out_ref[RI_ROWS + RO_ROWS :, :] = jnp.zeros((ROWS2 - RI_ROWS - RO_ROWS, 128), f32)


def join(*operands):
    return pl.pallas_call(
        join_kernel,
        out_shape=jax.ShapeDtypeStruct((ROWS2, 128), f32),
        compiler_params=pltpu.CompilerParams(vmem_limit_bytes=VMEM),
        name="join",
    )(*operands)


def ortho_kernel(own_half_ref, own_ref, other_ref, left_out_ref, gram_out_ref, x_ref, turned_ref, ortho_ref,
                 ortho_out_ref, inverse_ref, work_scr):
    step = pl.program_id(0)

    @pl.when(step == 0)
    def _():
        eye = jnp.where(
            lax.broadcasted_iota(jnp.int32, (RANK, RANK), 0) == lax.broadcasted_iota(jnp.int32, (RANK, RANK), 1),
            1.0,
            0.0,
        )
        for p in range(3):
            gram = jnp.zeros((RANK, RANK), f32)
            for ref in (own_ref, other_ref):
                for i in range(STEPS):
                    rows = jnp.concatenate(
                        [ref[pl.ds((CT * i + t) * 3 * RANK + RANK * p, RANK), :] for t in range(CT)], axis=1
                    )
                    gram += exact_nt(rows, rows)
            work_scr[p] = jnp.concatenate([gram, eye], axis=1)
        work_scr[3] = jnp.concatenate([gram_out_ref[:, :RANK], eye], axis=1)
        lane = lax.broadcasted_iota(jnp.int32, (4, RANK, 128), 2)
        sub = lax.broadcasted_iota(jnp.int32, (4, RANK, 128), 1)

        def eliminate(j, work):
            pivot_row = jnp.sum(jnp.where(sub == j, work, 0.0), axis=1, keepdims=True)
            pivot = jnp.sum(jnp.where(lane[:, :1] == j, pivot_row, 0.0), axis=2, keepdims=True)
            column = jnp.sum(jnp.where((lane == j) & (sub > j), work, 0.0), axis=2, keepdims=True)
            return work - column * (pivot_row / pivot)

        work = lax.fori_loop(0, RANK, eliminate, work_scr[...])
        diagonal = jnp.sum(jnp.where(lane == sub, work, 0.0), axis=2, keepdims=True)
        inverse_ref[...] = work * lax.rsqrt(diagonal)
        left_out = wide(left_out_ref[...], RANK)
        ortho_out_ref[...] = exact_nn(inverse_ref[3, :, RANK:], left_out)

    turned_ref[...] = x_ref[...].astype(f32).T.astype(bf16)
    first = step < STEPS
    block = pl.ds(pl.multiple_of(lax.rem(step, STEPS) * (CT * 3 * RANK), CT * 3 * RANK), CT * 3 * RANK)

    def turn(ref):
        rows = wide(ref[block, :], 3 * RANK)
        for p in range(3):
            high, low = split2(exact_nn(inverse_ref[p, :, RANK:], rows[RANK * p : RANK * (p + 1)]))
            both = jnp.concatenate([high.astype(f32), low.astype(f32)], axis=0)
            ortho_ref[p] = both.T.astype(bf16)

    @pl.when(first)
    def _():
        turn(own_ref)

    @pl.when(jnp.logical_not(first))
    def _():
        turn(other_ref)


def ortho(half, own, other, gram_out, inputs):
    def column(j, h):
        return lax.rem(j // STEPS + h[0], 2) * STEPS + lax.rem(j, STEPS)

    whole = pl.BlockSpec((L_ROWS, 128), lambda j, h: (0, 0))
    return pl.pallas_call(
        ortho_kernel,
        grid_spec=pltpu.PrefetchScalarGridSpec(
            num_scalar_prefetch=1,
            grid=(2 * STEPS,),
            in_specs=[
                whole,
                whole,
                pl.BlockSpec((LO_ROWS, 128), lambda j, h: (L_ROWS // LO_ROWS, 0)),
                pl.BlockSpec((RANK, 128), lambda j, h: (0, 0)),
                pl.BlockSpec((TOK, TILE), lambda j, h: (0, column(j, h))),
            ],
            out_specs=[
                pl.BlockSpec((TILE, TOK), lambda j, h: (column(j, h), 0)),
                pl.BlockSpec((3, TILE, 128), lambda j, h: (0, column(j, h), 0)),
                pl.BlockSpec((RANK, COLS), lambda j, h: (0, 0)),
                pl.BlockSpec((4, RANK, 128), lambda j, h: (0, 0, 0)),
            ],
            scratch_shapes=[pltpu.VMEM((4, RANK, 128), f32)],
        ),
        out_shape=[
            jax.ShapeDtypeStruct((D, TOK), bf16),
            jax.ShapeDtypeStruct((3, D, 128), bf16),
            jax.ShapeDtypeStruct((RANK, COLS), f32),
            jax.ShapeDtypeStruct((4, RANK, 128), f32),
        ],
        compiler_params=pltpu.CompilerParams(vmem_limit_bytes=VMEM),
        name="ortho",
    )(half, own, other, own, gram_out, inputs)


def rest_kernel(half_ref, summed_in_ref, own_ref, other_ref, inverse_ref, turned_ref, ortho_ref, ortho_out_ref,
                grads_ref, hid_ref, gy_ref, err_in_ref, err_out_ref, rest_in_ref, rest_out_ref, factor_in_ref,
                factor_out_ref, in_scr, out_scr):
    step = pl.program_id(0)

    @pl.when(step == 0)
    def _():
        for p in range(3):
            right = wide(summed_in_ref[pl.ds(HEADS * RANK * p, HEADS * RANK), :], RANK) * (1.0 / N_DP)
            factor = exact_nn(inverse_ref[p, :, RANK:], right)
            factor_in_ref[p] = factor
            high, low = split2(-factor)
            in_scr[p] = jnp.concatenate([high, high, low, jnp.zeros_like(low)], axis=0)
        high, low = split2(ortho_out_ref[...])
        out_scr[...] = jnp.concatenate([high, high, low, jnp.zeros_like(low)], axis=0)

    def output_factor(ref):
        right = wide(ref[...], RANK) * (1.0 / N_DP)
        factor_out_ref[...] = exact_nn(inverse_ref[3, :, RANK:], right)

    @pl.when(step < STEPS)
    def _():
        output_factor(own_ref)

    @pl.when(step >= STEPS)
    def _():
        output_factor(other_ref)

    high, low = split2(-factor_out_ref[...])
    weights = jnp.concatenate([high, low, high, jnp.zeros_like(low)], axis=0)
    rest_out = tn(hid_ref[...], gy_ref[...]) + tn(out_scr[...], weights) + err_out_ref[...].astype(f32)
    rest_out_ref[...] = rest_out.astype(bf16)
    for p in range(3):
        both = jnp.concatenate([turned_ref[...], ortho_ref[p], ortho_ref[p]], axis=1)
        weights = jnp.concatenate([grads_ref[p], in_scr[p]], axis=0)
        rest_in_ref[p] = (nn(both, weights) + err_in_ref[p].astype(f32)).astype(bf16)


def rest(half, summed, other, inverse, turned, ortho_in, ortho_out, grads, hidden, grad_y, err_in, err_out):
    def column(j, h):
        return lax.rem(j // STEPS + h[0], 2) * STEPS + lax.rem(j, STEPS)

    return pl.pallas_call(
        rest_kernel,
        grid_spec=pltpu.PrefetchScalarGridSpec(
            num_scalar_prefetch=1,
            grid=(2 * STEPS,),
            in_specs=[
                pl.BlockSpec((RI_ROWS, 128), lambda j, h: (0, 0)),
                pl.BlockSpec((CT * RANK, 128), lambda j, h: (jnp.minimum(j, STEPS - 1), 0)),
                pl.BlockSpec((CT * RANK, 128), lambda j, h: (jnp.maximum(j - STEPS, 0), 0)),
                pl.BlockSpec((4, RANK, 128), lambda j, h: (0, 0, 0)),
                pl.BlockSpec((TILE, TOK), lambda j, h: (column(j, h), 0)),
                pl.BlockSpec((3, TILE, 128), lambda j, h: (0, column(j, h), 0)),
                pl.BlockSpec((RANK, COLS), lambda j, h: (0, 0)),
                pl.BlockSpec((3, TOK, COLS), lambda j, h: (0, 0, 0)),
                pl.BlockSpec((TOK, COLS), lambda j, h: (0, 0)),
                pl.BlockSpec((TOK, TILE), lambda j, h: (0, column(j, h))),
                pl.BlockSpec((3, TILE, COLS), lambda j, h: (0, column(j, h), 0)),
                pl.BlockSpec((COLS, TILE), lambda j, h: (0, column(j, h))),
            ],
            out_specs=[
                pl.BlockSpec((3, TILE, COLS), lambda j, h: (0, column(j, h), 0)),
                pl.BlockSpec((COLS, TILE), lambda j, h: (0, column(j, h))),
                pl.BlockSpec((3, RANK, COLS), lambda j, h: (0, 0, 0)),
                pl.BlockSpec((RANK, TILE), lambda j, h: (0, column(j, h))),
            ],
            scratch_shapes=[pltpu.VMEM((3, 4 * RANK, COLS), bf16), pltpu.VMEM((4 * RANK, COLS), bf16)],
        ),
        out_shape=[
            jax.ShapeDtypeStruct((3, D, COLS), bf16),
            jax.ShapeDtypeStruct((COLS, D), bf16),
            jax.ShapeDtypeStruct((3, RANK, COLS), f32),
            jax.ShapeDtypeStruct((RANK, D), f32),
        ],
        compiler_params=pltpu.CompilerParams(vmem_limit_bytes=VMEM),
        name="rest",
    )(half, summed, summed[RI_ROWS : RI_ROWS + RO_ROWS], other, inverse, turned, ortho_in, ortho_out, grads, hidden, grad_y, err_in, err_out)


CHIP = ("x", "y", "z")
SWAP = [(0, 1), (1, 0)]


def all_summed(rows, total_rows, per_z):
    each = total_rows // CHIPS
    received = lax.all_to_all(rows.reshape(CHIPS, each, 128), CHIP, 0, 0)
    over_xy = jnp.sum(received.reshape(N_DP, 4, each, 128), axis=0)
    total = jnp.sum(over_xy, axis=0)
    me = (lax.axis_index("x") * 4 + lax.axis_index("y")) * 4 + lax.axis_index("z")
    row = me * each + lax.broadcasted_iota(jnp.int32, (1, each, 1), 1)
    answer = jnp.where(per_z(row), over_xy, total[None])
    answer = jnp.broadcast_to(answer[None], (N_DP, 4, each, 128)).reshape(CHIPS, each, 128)
    return lax.all_to_all(answer, CHIP, 0, 0).reshape(total_rows, 128)


def shards(inputs, grad_y, q_pre, f_pre, v_pre, w_out, err_in, err_out, basis_in, basis_out):
    err_in = err_in[0]
    err_out = err_out[0]
    core = lax.axis_index("c").astype(jnp.int32)
    mine = core[None]
    theirs = 1 - mine
    hidden, grads = recurrence(grad_y, w_out, q_pre, f_pre, v_pre)
    local = (inputs, grad_y, grads, hidden, err_in, err_out, basis_in, basis_out)
    send, left_out_a = left(theirs, *local)
    arrived = lax.ppermute(send, "c", SWAP)
    keep, left_out_b = left(mine, *local)
    rows = jnp.concatenate(
        [
            (keep + arrived).reshape(L_ROWS, 128),
            (left_out_a + left_out_b).reshape(LO_ROWS, 128),
            jnp.zeros((ROWS1 - L_ROWS - LO_ROWS, 128), f32),
        ]
    )
    own = all_summed(rows, ROWS1, lambda row: row >= L_ROWS)
    other = lax.ppermute(own, "c", SWAP)
    right_a, token_a, send, gram_part = right(
        jnp.concatenate([mine, theirs]), own, own, inputs, grad_y, hidden, err_in, err_out
    )
    arrived = lax.ppermute(send, "c", SWAP)
    gram_out = gram_part + lax.ppermute(gram_part, "c", SWAP)
    gram_out = gram_out + sum(
        lax.ppermute(gram_out, "z", [(a, (a + shift) % 4) for a in range(4)]) for shift in (1, 2, 3)
    )
    right_b, token_b, keep, _ = right(
        jnp.concatenate([theirs, mine]), other, own, inputs, grad_y, hidden, err_in, err_out
    )
    rows = join(right_a, right_b, token_a, token_b, grads, keep.reshape(RO_ROWS, 128), arrived.reshape(RO_ROWS, 128))
    summed = all_summed(rows, ROWS2, lambda row: row < RI_ROWS)
    turned, ortho_in, ortho_out, inverse = ortho(mine, own, other, gram_out, inputs)
    other_right = lax.ppermute(summed[RI_ROWS : RI_ROWS + RO_ROWS], "c", SWAP)
    rest_in, rest_out, factor_in, factor_out = rest(
        mine, summed, other_right, inverse, turned, ortho_in, ortho_out, grads, hidden, grad_y, err_in, err_out
    )
    return rest_in[None], rest_out[None], factor_in, factor_out


def solution(mesh):
    fine = Mesh(mesh.devices.reshape(4, 4, 4, 2), ("x", "y", "z", "c"))
    dp, head = ("x", "y"), ("z", "c")
    placed = (
        P(dp, None),
        P(dp, None),
        P(dp, head),
        P(dp, head),
        P(dp, head),
        P(head, None),
        P(dp, None, None, head),
        P(dp, head, None),
        P(None, None, head),
        P(),
    )
    return jax.shard_map(
        shards,
        mesh=fine,
        in_specs=placed,
        out_specs=(P(dp, None, None, head), P(dp, head, None), P(None, None, head), P()),
        check_vma=False,
    )
```

time: 664 us -> 182 us (0.27); the launches traced: 652 us -> 181 us
  waiting for transfers between devices: 227 us -> 44.4 us
  matrix products: 154 us -> 0 us
  local copies, waits for them, and re-layouts: 128 us -> 6.2 us
  other arithmetic: 98.7 us -> 2.24 us
  Pallas kernels: 0 us -> 61.7 us
  starting transfers between devices: 0.12 us -> 20.4 us
  blocking collectives: 27.5 us -> 45.2 us
  between operations: 14.7 us -> 0.91 us
    psum x3 -> x0, waiting for transfers between devices: 227 us -> none  [the longest x1 153 us: shards(): summed_in = lax.psum(left_in, ('dp', 'head'))]
    dot_general x62 -> x0, matrix products: 149 us -> none  [the longest x24 34.8 us: advance(): output = jnp.einsum('stha,shab->sthb', query_block, state, precision=EXACT)]
    pallas_call x0 -> x8, Pallas kernels: none -> 61.7 us  [the longest x1 16.3 us: ortho(): pl.pallas_call(ortho_kernel, grid_spec=pltpu.PrefetchScalarGridSpec(num_s...]
    dynamic_update_slice x48 -> x0, local copies, waits for them, and re-layouts: 50.2 us -> none  [recurrence_out(): lax.scan(advance, initial, (leading(decayed_query), leading(decayed_key),...]
    another operation x16 -> x0, other arithmetic: 48.7 us -> none  [the longest x4 17.9 us: orthonormal(): jnp.linalg.cholesky(gram)]
    all_to_all x0 -> x2, blocking collectives: none -> 45.2 us  [all_summed(): return lax.all_to_all(answer, CHIP, 0, 0).reshape(total_rows, 128)]
    all_to_all x0 -> x2, waiting for transfers between devices: none -> 38.2 us  [all_summed(): received = lax.all_to_all(rows.reshape(CHIPS, each, 128), CHIP, 0, 0)]
    unnamed x79 -> x34, local copies, waits for them, and re-layouts: 36.5 us -> 5.91 us
  transfers between devices with their start and end apart: 3 -> 10, of which waited for: 2 -> 6; matrix products, arithmetic and copies ran while one was open for 28% -> 0% of each run, Pallas kernels for 0% -> 18%
where the time goes in v1:
time: 182 us; the launch traced here: 181 us
  Pallas kernels  61.7 us (34%)
  blocking collectives  45.2 us (25%)
  waiting for transfers between devices  44.4 us (24%)
  starting transfers between devices  20.4 us (11%)
  local copies, waits for them, and re-layouts  6.2 us (3%)
  other arithmetic  2.24 us (1%)
    all_to_all x2, blocking collectives, all_summed(): return lax.all_to_all(answer, CHIP, 0, 0).reshape(total_rows, 128)  45.2 us
    all_to_all x2, waiting for transfers between devices, all_summed(): received = lax.all_to_all(rows.reshape(CHIPS, each, 128), CHIP, 0, 0)  38.2 us
    all_to_all x2, starting transfers between devices, all_summed(): received = lax.all_to_all(rows.reshape(CHIPS, each, 128), CHIP, 0, 0)  16.3 us
    pallas_call x1, Pallas kernels, ortho(): pl.pallas_call(ortho_kernel, grid_spec=pltpu.PrefetchScalarGridSpec(num_s...  16.3 us
    pallas_call x1, Pallas kernels, rest(): pl.pallas_call(rest_kernel, grid_spec=pltpu.PrefetchScalarGridSpec(num_sc...  14 us
    pallas_call x2, Pallas kernels, right(): pl.pallas_call(right_kernel, grid_spec=pltpu.PrefetchScalarGridSpec(num_s...  10.9 us
    pallas_call x2, Pallas kernels, left(): pl.pallas_call(left_kernel, grid_spec=pltpu.PrefetchScalarGridSpec(num_sc...  10.8 us
    pallas_call x1, Pallas kernels, recurrence(): pl.pallas_call(recurrence_kernel, grid=(HEADS,), in_specs=[pl.BlockSpec((...  8.63 us
  transfers between devices with their start and end apart: 10, of which 6 were waited for; matrix products, arithmetic and copies ran while one was open for 0% of the time, Pallas kernels for 18%

profile of v1, /device:TPU:0, one launch (start us, length us, event | category | flops | bytes accessed | tf_op | source)
XLA Modules:
  0.0 181.1 jit_solution(14963316590299742127)
XLA Ops:
  0.7 1.4 copy-done
  2.1 1.7 copy-done.12
  3.7 0.9 copy-done.14
  4.6 0.9 copy-done.15
  5.6 0.9 copy-done.16
  6.5 8.6 %recurrence.1 = (bf16[256,384]{1,0:T(8,128)(2,1)S(1)}, bf16[3,256,384]{2,1,0:T(8,128)(2,1)S(1)}) custom-call(bf16[256,3072]{1,0:T(8,128)(2,1)S(1)} %copy-done, bf16[384,3072]{1,0:T(8,128)(2,1)S(1)} %copy-done.12, bf16[256,384]{1,0:T(8,128)(2,1)S(1)} %copy-done.14, bf16[256,384]{1,0:T(8,128)(2,1)S(1)} %copy-done.15, bf16[256,384]{1,0:T(8,128)(2,1)S(1)} %copy-done.16), custom_call_target="tpu_custom_call" | custom-call | tf_op jit(solution)/shard_map/recurrence/pallas_call | solution.py:142
  15.2 5.4 %left.3 = (f32[12,192,128]{2,1,0:T(8,128)S(1)}, f32[3,64,128]{2,1,0:T(8,128)S(1)}) custom-call(s32[1]{0:T(128)S(6)} %sub.3.half_ref, bf16[256,3072]{1,0:T(8,128)(2,1)S(1)} %copy-done.3, bf16[256,3072]{1,0:T(8,128)(2,1)} %gy_ref.11, bf16[3,256,384]{2,1,0:T(8,128)(2,1)S(1)} %get-tuple-element.25.grads_ref, bf16[256,384]{1,0:T(8,128)(2,1)S(1)} %get-tuple-element.26.hid_ref, ...), custom_call_target="tpu_custom_call" | custom-call | tf_op jit(solution)/shard_map/left/pallas_call | solution.py:188
  20.7 5.4 %left.2 = (f32[12,192,128]{2,1,0:T(8,128)S(1)}, f32[3,64,128]{2,1,0:T(8,128)S(1)}) custom-call(s32[1]{0:T(128)} %bitcast.half_ref.own_half_ref, bf16[256,3072]{1,0:T(8,128)(2,1)S(1)} %copy-done.3, bf16[256,3072]{1,0:T(8,128)(2,1)} %gy_ref.11, bf16[3,256,384]{2,1,0:T(8,128)(2,1)S(1)} %get-tuple-element.25.grads_ref, ...), custom_call_target="tpu_custom_call" | custom-call | tf_op jit(solution)/shard_map/left/pallas_call | solution.py:188
  26.2 0.1 add.54
  26.4 1.5 maximum_maximum_fusion
  27.8 11.5 %all-to-all-start = ((f32[64,40,128]{2,1,0:T(8,128)}), f32[64,40,128]{2,1,0:T(8,128)S(1)}, u32[]{:S(2)}, u32[]{:S(2)}) async-start(f32[64,40,128]{2,1,0:T(8,128)} %bitcast.5), calls=%async_computation | async-start | bytes 2621440 | tf_op jit(solution)/shard_map/all_to_all | solution.py:477
  39.4 22.1 %all-to-all-done = f32[64,40,128]{2,1,0:T(8,128)S(1)} async-done(((f32[64,40,128]{2,1,0:T(8,128)}), f32[64,40,128]{2,1,0:T(8,128)S(1)}, u32[]{:S(2)}, u32[]{:S(2)}) %all-to-all-start) | async-done | bytes 1310752 | tf_op jit(solution)/shard_map/all_to_all | solution.py:477
  61.5 0.1 reduce_sum.37
  61.7 0.1 broadcast_in_dim.63
  61.8 25.7 %all_to_all.20 = f32[64,40,128]{2,1,0:T(8,128)S(1)} all-to-all(f32[64,40,128]{2,1,0:T(8,128)S(1)} %bitcast.41), channel_id=1, replica_groups=mesh['x'=4,'y'=4,'z'=4,'c'=2] {'x','y','z'}, dimensions={0} | all-to-all | bytes 2621440 | tf_op jit(solution)/shard_map/all_to_all | solution.py:484
  87.6 5.2 %right.2 = (f32[3,64,384]{2,1,0:T(8,128)S(1)}, f32[3,64,256]{2,1,0:T(8,128)S(1)}, f32[12,64,128]{2,1,0:T(8,128)S(1)}, f32[64,128]{1,0:T(8,128)S(1)}) custom-call(s32[2]{0:T(128)S(1)} %pad_add_fusion.halves_ref, f32[2560,128]{1,0:T(8,128)S(1)} %bitcast.19, f32[2560,128]{1,0:T(8,128)S(1)} %bitcast.20, bf16[256,3072]{1,0:T(8,128)(2,1)S(1)} %copy-done.4, ...), custom_call_target="tpu_custom_call" | custom-call | tf_op jit(solution)/shard_map/right/pallas_call | solution.py:247
  92.8 0.6 collective-permute-start.2
  93.5 5.7 %right.3 = (f32[3,64,384]{2,1,0:T(8,128)S(1)}, f32[3,64,256]{2,1,0:T(8,128)S(1)}, f32[12,64,128]{2,1,0:T(8,128)S(1)}, f32[64,128]{1,0:T(8,128)}) custom-call(s32[2]{0:T(128)S(1)} %pad_add_fusion.1.halves_ref, f32[2560,128]{1,0:T(8,128)S(1)} %collective-permute-done.1.left_ref.other_ref, f32[2560,128]{1,0:T(8,128)S(1)} %bitcast.21, ...), custom_call_target="tpu_custom_call" | custom-call | tf_op jit(solution)/shard_map/right/pallas_call | solution.py:247
  99.2 1.1 join.1
  100.3 4.8 %all-to-all-start.2 = ((f32[64,24,128]{2,1,0:T(8,128)}), f32[64,24,128]{2,1,0:T(8,128)S(1)}, u32[]{:S(2)}, u32[]{:S(2)}) async-start(f32[64,24,128]{2,1,0:T(8,128)} %bitcast.11), calls=%async_computation.2 | async-start | bytes 1572864 | tf_op jit(solution)/shard_map/all_to_all | solution.py:477
  105.2 16.1 %all-to-all-done.2 = f32[64,24,128]{2,1,0:T(8,128)S(1)} async-done(((f32[64,24,128]{2,1,0:T(8,128)}), f32[64,24,128]{2,1,0:T(8,128)S(1)}, u32[]{:S(2)}, u32[]{:S(2)}) %all-to-all-start.2) | async-done | bytes 786464 | tf_op jit(solution)/shard_map/all_to_all | solution.py:477
  121.6 19.6 %all_to_all.21 = f32[64,24,128]{2,1,0:T(8,128)S(1)} all-to-all(f32[64,24,128]{2,1,0:T(8,128)S(1)} %bitcast.43), channel_id=1, replica_groups=mesh['x'=4,'y'=4,'z'=4,'c'=2] {'x','y','z'}, dimensions={0} | all-to-all | bytes 1572864 | tf_op jit(solution)/shard_map/all_to_all | solution.py:484
  141.3 0.5 collective-permute-start.4
  141.8 1.3 collective-permute-done.4
  143.0 0.9 collective-permute-start.7
  143.9 1.7 collective-permute-start.6
  145.7 0.1 collective-permute-start.5
  145.8 1.1 collective-permute-done.7
  147.0 2.4 %collective-permute-done.6 = f32[64,128]{1,0:T(8,128)S(1)} collective-permute-done((f32[64,128]{1,0:T(8,128)S(1)}, f32[64,128]{1,0:T(8,128)S(1)}, u32[]{:S(2)}, u32[]{:S(2)}) %collective-permute-start.6) | collective-permute-done | bytes 32800 | tf_op jit(solution)/shard_map/ppermute | solution.py:513
  149.4 1.4 collective-permute-done.5
  150.9 16.3 %ortho.1 = (bf16[3072,256]{1,0:T(8,128)(2,1)S(1)}, bf16[3,3072,128]{2,1,0:T(8,128)(2,1)}, f32[64,384]{1,0:T(8,128)S(1)}, f32[4,64,128]{2,1,0:T(8,128)S(1)}) custom-call(s32[1]{0:T(128)} %bitcast.half_ref.own_half_ref, f32[2560,128]{1,0:T(8,128)S(1)} %bitcast.22, f32[2560,128]{1,0:T(8,128)S(1)} %copy-done.7, f32[2560,128]{1,0:T(8,128)S(1)} %bitcast.23, ...), custom_call_target="tpu_custom_call" | custom-call | tf_op jit(solution)/shard_map/ortho/pallas_call | solution.py:360
  167.2 14.0 %rest.1 = (bf16[3,3072,384]{2,1,0:T(8,128)(2,1)}, bf16[384,3072]{1,0:T(8,128)(2,1)}, f32[3,64,384]{2,1,0:T(8,128)}, f32[64,3072]{1,0:T(8,128)}) custom-call(s32[1]{0:T(128)} %bitcast.half_ref.own_half_ref, f32[1536,128]{1,0:T(8,128)S(1)} %bitcast.24, f32[768,128]{1,0:T(8,128)S(1)} %bitcast.26, f32[768,128]{1,0:T(8,128)S(1)} %collective-permute-done.3.other_ref, ...), custom_call_target="tpu_custom_call" | custom-call | tf_op jit(solution)/shard_map/rest/pallas_call | solution.py:433
  (52 shorter events, 1.0 us)
Async XLA Ops:
  0.6 1.4 copy-start
  2.1 1.7 copy-start.12
  3.7 0.9 copy-start.14
  4.6 0.9 copy-start.15
  5.6 0.9 copy-start.16
  6.5 8.7 %copy-start.3 = (bf16[256,3072]{1,0:T(8,128)(2,1)S(1)}, bf16[256,3072]{1,0:T(8,128)(2,1)}, u32[]{:S(2)}) copy-start(bf16[256,3072]{1,0:T(8,128)(2,1)} %x_ref.9) | copy-start | bytes 4718596
  6.5 8.7 %copy-start.11 = (f32[64,3072]{1,0:T(8,128)S(1)}, f32[64,3072]{1,0:T(8,128)}, u32[]{:S(2)}) copy-start(f32[64,3072]{1,0:T(8,128)} %basis_out_ref.3) | copy-start | bytes 2359300
  6.5 8.7 %copy-start.13 = (f32[3,64,384]{2,1,0:T(8,128)S(1)}, f32[3,64,384]{2,1,0:T(8,128)}, u32[]{:S(2)}) copy-start(f32[3,64,384]{2,1,0:T(8,128)} %basis_in_ref.3) | copy-start | bytes 884740
  15.1 5.6 %copy-start.8 = (bf16[256,384]{1,0:T(8,128)(2,1)}, bf16[256,384]{1,0:T(8,128)(2,1)S(1)}, u32[]{:S(2)}) copy-start(bf16[256,384]{1,0:T(8,128)(2,1)S(1)} %get-tuple-element.26.hid_ref) | copy-start | bytes 589828
  20.6 5.6 %collective-permute-start = (f32[12,192,128]{2,1,0:T(8,128)S(1)}, f32[12,192,128]{2,1,0:T(8,128)S(1)}, u32[]{:S(2)}, u32[]{:S(2)}) collective-permute-start(f32[12,192,128]{2,1,0:T(8,128)S(1)} %get-tuple-element.28), channel_id=1, source_target_pairs={{0,1},{1,0},{2,3},{3,2},{4,5},{5,4},{6,7},{7,6},{8,9},{9,8},{10,11... | collective-permute-start | bytes 3538952 | tf_op jit(solution)/shard_map/ppermute | solution.py:496
  27.8 33.6 %all-to-all-start = ((f32[64,40,128]{2,1,0:T(8,128)}), f32[64,40,128]{2,1,0:T(8,128)S(1)}, u32[]{:S(2)}, u32[]{:S(2)}) async-start(f32[64,40,128]{2,1,0:T(8,128)} %bitcast.5), calls=%async_computation | async-start | bytes 2621440 | tf_op jit(solution)/shard_map/all_to_all | solution.py:477
  61.7 25.9 %copy-start.4 = (bf16[256,3072]{1,0:T(8,128)(2,1)S(1)}, bf16[256,3072]{1,0:T(8,128)(2,1)}, u32[]{:S(2)}) copy-start(bf16[256,3072]{1,0:T(8,128)(2,1)} %x_ref.9) | copy-start | bytes 4718596
  61.8 25.8 %copy-start.1 = (bf16[256,3072]{1,0:T(8,128)(2,1)S(1)}, bf16[256,3072]{1,0:T(8,128)(2,1)}, u32[]{:S(2)}) copy-start(bf16[256,3072]{1,0:T(8,128)(2,1)} %gy_ref.11) | copy-start | bytes 4718596
  61.8 25.8 %copy-start.9 = (bf16[256,384]{1,0:T(8,128)(2,1)S(1)}, bf16[256,384]{1,0:T(8,128)(2,1)}, u32[]{:S(2)}) copy-start(bf16[256,384]{1,0:T(8,128)(2,1)} %copy-done.8) | copy-start | bytes 589828
  87.5 5.9 %collective-permute-start.1 = (f32[2560,128]{1,0:T(8,128)S(1)}, f32[2560,128]{1,0:T(8,128)S(1)}, u32[]{:S(2)}, u32[]{:S(2)}) collective-permute-start(f32[2560,128]{1,0:T(8,128)S(1)} %bitcast.18), channel_id=1, source_target_pairs={{0,1},{1,0},{2,3},{3,2},{4,5},{5,4},{6,7},{7,6},{8,9},{9,8},{10,11... | collective-permute-start | bytes 3932168 | tf_op jit(solution)/shard_map/ppermute | solution.py:506
  92.8 6.4 %collective-permute-start.2 = (f32[12,64,128]{2,1,0:T(8,128)S(1)}, f32[12,64,128]{2,1,0:T(8,128)S(1)}, u32[]{:S(2)}, u32[]{:S(2)}) collective-permute-start(f32[12,64,128]{2,1,0:T(8,128)S(1)} %get-tuple-element.36), channel_id=1, source_target_pairs={{0,1},{1,0},{2,3},{3,2},{4,5},{5,4},{6,7},{7,6},{8,9},{9,8},{10,11... | collective-permute-start | bytes 1179656 | tf_op jit(solution)/shard_map/ppermute | solution.py:510
  93.5 5.7 %copy-start.6 = (f32[2560,128]{1,0:T(8,128)}, f32[2560,128]{1,0:T(8,128)S(1)}, u32[]{:S(2)}) copy-start(f32[2560,128]{1,0:T(8,128)S(1)} %collective-permute-done.1.left_ref.other_ref) | copy-start | bytes 3932164
  100.3 21.0 %all-to-all-start.2 = ((f32[64,24,128]{2,1,0:T(8,128)}), f32[64,24,128]{2,1,0:T(8,128)S(1)}, u32[]{:S(2)}, u32[]{:S(2)}) async-start(f32[64,24,128]{2,1,0:T(8,128)} %bitcast.11), calls=%async_computation.2 | async-start | bytes 1572864 | tf_op jit(solution)/shard_map/all_to_all | solution.py:477
  121.5 29.3 %copy-start.7 = (f32[2560,128]{1,0:T(8,128)S(1)}, f32[2560,128]{1,0:T(8,128)}, u32[]{:S(2)}) copy-start(f32[2560,128]{1,0:T(8,128)} %copy-done.6) | copy-start | bytes 3932164
  121.6 29.2 %copy-start.5 = (bf16[256,3072]{1,0:T(8,128)(2,1)S(1)}, bf16[256,3072]{1,0:T(8,128)(2,1)}, u32[]{:S(2)}) copy-start(bf16[256,3072]{1,0:T(8,128)(2,1)} %x_ref.9) | copy-start | bytes 4718596
  141.2 26.0 %collective-permute-start.3 = (f32[768,128]{1,0:T(8,128)S(1)}, f32[768,128]{1,0:T(8,128)S(1)}, u32[]{:S(2)}, u32[]{:S(2)}) collective-permute-start(f32[768,128]{1,0:T(8,128)S(1)} %bitcast.25), channel_id=1, source_target_pairs={{0,1},{1,0},{2,3},{3,2},{4,5},{5,4},{6,7},{7,6},{8,9},{9,8},{10,11... | collective-permute-start | bytes 1179656 | tf_op jit(solution)/shard_map/ppermute | solution.py:521
  141.3 1.8 collective-permute-start.4
  143.0 3.9 %collective-permute-start.7 = (f32[64,128]{1,0:T(8,128)S(1)}, f32[64,128]{1,0:T(8,128)S(1)}, u32[]{:S(2)}, u32[]{:S(2)}) collective-permute-start(f32[64,128]{1,0:T(8,128)S(1)} %add.56), channel_id=1, source_target_pairs={{0,6},{2,0},{4,2},{6,4},{1,7},{3,1},{5,3},{7,5},{8,14},{10,8},{12,... | collective-permute-start | bytes 98312 | tf_op jit(solution)/shard_map/ppermute | solution.py:513
  143.9 5.4 %collective-permute-start.6 = (f32[64,128]{1,0:T(8,128)S(1)}, f32[64,128]{1,0:T(8,128)S(1)}, u32[]{:S(2)}, u32[]{:S(2)}) collective-permute-start(f32[64,128]{1,0:T(8,128)S(1)} %add.56), channel_id=1, source_target_pairs={{0,4},{2,6},{4,0},{6,2},{1,5},{3,7},{5,1},{7,3},{8,12},{10,14},{12... | collective-permute-start | bytes 98312 | tf_op jit(solution)/shard_map/ppermute | solution.py:513
  145.7 5.1 %collective-permute-start.5 = (f32[64,128]{1,0:T(8,128)S(1)}, f32[64,128]{1,0:T(8,128)S(1)}, u32[]{:S(2)}, u32[]{:S(2)}) collective-permute-start(f32[64,128]{1,0:T(8,128)S(1)} %add.56), channel_id=1, source_target_pairs={{0,2},{2,4},{4,6},{6,0},{1,3},{3,5},{5,7},{7,1},{8,10},{10,12},{12... | collective-permute-start | bytes 98312 | tf_op jit(solution)/shard_map/ppermute | solution.py:513
  150.8 16.3 %copy-start.2 = (bf16[256,3072]{1,0:T(8,128)(2,1)S(1)}, bf16[256,3072]{1,0:T(8,128)(2,1)}, u32[]{:S(2)}) copy-start(bf16[256,3072]{1,0:T(8,128)(2,1)} %gy_ref.11) | copy-start | bytes 4718596
  150.8 16.3 %copy-start.10 = (bf16[256,384]{1,0:T(8,128)(2,1)S(1)}, bf16[256,384]{1,0:T(8,128)(2,1)}, u32[]{:S(2)}) copy-start(bf16[256,384]{1,0:T(8,128)(2,1)} %copy-done.8) | copy-start | bytes 589828

commit v2 on v1

v2 whole, which is shorter than its diff:
```python
import functools

import jax
import jax.numpy as jnp
from jax import lax
from jax.experimental import pallas as pl
from jax.experimental.pallas import tpu as pltpu
from jax.sharding import Mesh, PartitionSpec as P

TOK = 256
DK = 128
HEADS = 3
COLS = HEADS * DK
RANK = 64
D = 3072
HALF = D // 2
TILE = 512
STEPS = HALF // TILE
CT = TILE // 128
N_DP = 16
CHIPS = 64
L_ROWS = 12 * 3 * RANK
LO_ROWS = HEADS * RANK
ROWS1 = 2560
EACH1 = 40
L_STEP = CT * 3 * RANK
RI_ROWS = 9 * RANK
RO_ROWS = 12 * RANK
ROWS2 = 768
EACH2 = 48
PIECE = HEADS * RANK

f32 = jnp.float32
bf16 = jnp.bfloat16
EXACT = lax.Precision.HIGHEST
VMEM = 24 * 1024 * 1024


def cost(us):
    return pl.CostEstimate(flops=int(us * 1e9), bytes_accessed=int(us * 3e6), transcendentals=0)


def nn(a, b):
    return lax.dot_general(a, b, (((1,), (0,)), ((), ())), preferred_element_type=f32)


def nt(a, b):
    return lax.dot_general(a, b, (((1,), (1,)), ((), ())), preferred_element_type=f32)


def tn(a, b):
    return lax.dot_general(a, b, (((0,), (0,)), ((), ())), preferred_element_type=f32)


def exact_nn(a, b):
    return lax.dot_general(a, b, (((1,), (0,)), ((), ())), precision=EXACT, preferred_element_type=f32)


def exact_nt(a, b):
    return lax.dot_general(a, b, (((1,), (1,)), ((), ())), precision=EXACT, preferred_element_type=f32)


def split2(a):
    high = a.astype(bf16)
    return high, (a - high.astype(f32)).astype(bf16)


def split3(a):
    high = a.astype(bf16)
    rest = a - high.astype(f32)
    mid = rest.astype(bf16)
    return high, mid, (rest - mid.astype(f32)).astype(bf16)


def stacked(a):
    return jnp.concatenate(split2(a), axis=0)


def folded(a):
    half = a.shape[0] // 2
    return a[:half] + a[half:]


def recurrence_kernel(gy_ref, w_ref, q_ref, f_ref, v_ref, *refs):
    sources, (hid_ref, grad_ref), kept, sem = refs[:4], refs[4:6], refs[6:10], refs[10]
    copies = [pltpu.make_async_copy(a, b, sem.at[i]) for i, (a, b) in enumerate(zip(sources, kept))]

    @pl.when(pl.program_id(0) == 0)
    def _():
        for copy in copies:
            copy.start()

    grad_o = nt(gy_ref[...], w_ref[...]).astype(bf16)
    q = q_ref[...].astype(f32)
    f = f_ref[...].astype(f32)
    v = v_ref[...]
    q_gate = 1.0 / (1.0 + jnp.exp(-q))
    query = q * q_gate
    small = jnp.exp(-jnp.abs(f))
    key = jnp.where(f >= 0, small, 1.0) / (1.0 + small)
    decay = jnp.where(f >= 0, 1.0, small) / (1.0 + small)
    log_decay = jnp.minimum(f, 0.0) - jnp.log1p(small)

    row = lax.broadcasted_iota(jnp.int32, (TOK, TOK), 0)
    col = lax.broadcasted_iota(jnp.int32, (TOK, TOK), 1)
    lower = jnp.where(row >= col, 1.0, 0.0).astype(bf16)
    upper = jnp.where(row <= col, 1.0, 0.0).astype(bf16)
    differ = row ^ col
    high, mid, low = split3(log_decay)
    running = nn(lower, high) + (nn(lower, mid) + nn(lower, low))

    scores = jnp.zeros((TOK, TOK), f32)
    grad_s = split2(nt(grad_o, v))
    grad_st = split2(nt(v, grad_o))
    grad_query = jnp.zeros((TOK, DK), f32)
    grad_key = jnp.zeros((TOK, DK), f32)
    for size in (128, 64, 32, 16, 8):
        blocks = running.reshape(TOK // (2 * size), 2 * size, DK)
        spread = (blocks - blocks[:, size - 1 : size, :]).reshape(TOK, DK)
        if size > 8:
            q_scale = jnp.exp(jnp.minimum(spread, 0.0))
            k_scale = jnp.exp(jnp.minimum(-spread, 0.0))
            within = (differ >= size) & (differ < 2 * size)
            mask = within & (row > col)
            mask_t = within & (row < col)
        else:
            q_scale = jnp.exp(spread)
            k_scale = jnp.exp(-spread)
            within = differ < 2 * size
            mask = within & (row >= col)
            mask_t = within & (row <= col)
        q_high, q_low = split2(query * q_scale)
        k_high, k_low = split2(key * k_scale)
        level = nt(
            jnp.concatenate([q_high, q_high, q_low], axis=1),
            jnp.concatenate([k_high, k_low, k_high], axis=1),
        )
        scores = jnp.where(mask, level, scores)
        keep = jnp.where(mask, 1.0, 0.0).astype(bf16)
        keep_t = jnp.where(mask_t, 1.0, 0.0).astype(bf16)
        both = nn(grad_s[0] * keep, jnp.concatenate([k_high, k_low], axis=1))
        grad_query += q_scale * (both[:, :DK] + both[:, DK:] + nn(grad_s[1] * keep, k_high))
        both = nn(grad_st[0] * keep_t, jnp.concatenate([q_high, q_low], axis=1))
        grad_key += k_scale * (both[:, :DK] + both[:, DK:] + nn(grad_st[1] * keep_t, q_high))
    s_high, s_low = split2(scores)
    hid_ref[...] = (nn(s_high, v) + nn(s_low, v)).astype(bf16)
    grad_v = tn(s_high, grad_o) + tn(s_low, grad_o)
    high, mid, low = split3(query * grad_query - key * grad_key)
    grad_decay = nn(upper, high) + (nn(upper, mid) + nn(upper, low))
    grad_ref[0] = (grad_query * (q_gate + query * (1.0 - q_gate))).astype(bf16)
    grad_ref[1] = (key * (grad_decay - grad_key * decay)).astype(bf16)
    grad_ref[2] = grad_v.astype(bf16)

    @pl.when(pl.program_id(0) == HEADS - 1)
    def _():
        for copy in copies:
            copy.wait()


def held(*arrays):
    return [pltpu.with_memory_space_constraint(a, pltpu.VMEM) for a in arrays]


def streamed(*arrays):
    return [pltpu.with_memory_space_constraint(a, pltpu.HBM) for a in arrays]


ANY = pl.BlockSpec(memory_space=pl.ANY)


def fetched(step, steps, column, width, sources, slots, sem):
    def copies(j):
        at = pl.ds(pl.multiple_of(column(j) * width, width), width)
        for i, (axis, source) in enumerate(sources):
            index = [slice(None)] * len(source.shape)
            index[axis] = at
            yield pltpu.make_async_copy(source.at[tuple(index)], slots[i].at[j], sem.at[i, j])

    @pl.when(step == 0)
    def _():
        for j in range(steps):
            for copy in copies(j):
                copy.start()

    for copy in copies(step):
        copy.wait()
    return [slot.at[step] for slot in slots]


def recurrence(grad_y, w_out, q_pre, f_pre, v_pre, keep):
    per_head = pl.BlockSpec((TOK, DK), lambda h: (0, h))
    anywhere = pl.BlockSpec(memory_space=pl.ANY)
    operands = (grad_y, w_out, q_pre, f_pre, v_pre) + keep
    return pl.pallas_call(
        recurrence_kernel,
        grid=(HEADS,),
        in_specs=[
            pl.BlockSpec((TOK, D), lambda h: (0, 0)),
            pl.BlockSpec((DK, D), lambda h: (h, 0)),
            per_head,
            per_head,
            per_head,
        ]
        + [anywhere] * len(keep),
        out_specs=[per_head, pl.BlockSpec((3, TOK, DK), lambda h: (0, 0, h))] + [anywhere] * len(keep),
        out_shape=[
            jax.ShapeDtypeStruct((TOK, COLS), bf16),
            jax.ShapeDtypeStruct((3, TOK, COLS), bf16),
        ]
        + [pltpu.VMEM(a.shape, a.dtype) for a in keep],
        scratch_shapes=[pltpu.SemaphoreType.DMA((len(keep),))],
        cost_estimate=cost(8),
        compiler_params=pltpu.CompilerParams(vmem_limit_bytes=VMEM),
        name="recurrence",
    )(*streamed(*operands))


def tiles_of(a):
    return [a[:, 128 * i : 128 * (i + 1)] for i in range(a.shape[1] // 128)]


def left_tokens(grads_ref, basis_in_ref, token_scr):
    for p in range(3):
        token_scr[p] = stacked(folded(nt(stacked(basis_in_ref[p]), grads_ref[p])))


def left_tile(p, x_ref, err_in_ref, basis_in_ref, token_scr):
    part = nn(token_scr[p], x_ref[...]) + nt(stacked(basis_in_ref[p]), err_in_ref[p])
    return tiles_of(folded(part))


def left_send_kernel(half_ref, x_ref, grads_ref, err_in_ref, basis_in_ref, left_ref, token_scr):
    @pl.when(pl.program_id(0) == 0)
    def _():
        left_tokens(grads_ref, basis_in_ref, token_scr)

    for p in range(3):
        for i, tile in enumerate(left_tile(p, x_ref, err_in_ref, basis_in_ref, token_scr)):
            at = (3 * i + p) * RANK
            left_ref[at : at + RANK, :] = tile


def left_keep_kernel(half_ref, x_ref, grads_ref, err_in_ref, basis_in_ref, arrived_ref, left_out_ref, rows_ref, token_scr):
    step = pl.program_id(0)

    @pl.when(step == 0)
    def _():
        left_tokens(grads_ref, basis_in_ref, token_scr)
        rows_ref[L_ROWS : L_ROWS + LO_ROWS, :] = left_out_ref[...]
        rows_ref[L_ROWS + LO_ROWS :, :] = jnp.zeros((ROWS1 - L_ROWS - LO_ROWS, 128), f32)

    for p in range(3):
        for i, tile in enumerate(left_tile(p, x_ref, err_in_ref, basis_in_ref, token_scr)):
            at = (3 * i + p) * RANK
            rows_ref[pl.ds(pl.multiple_of(step * L_STEP + at, RANK), RANK), :] = tile + arrived_ref[at : at + RANK, :]


def left(half, inputs, grads, err_in, basis_in, arrived=None, left_out_part=None):
    keep = arrived is not None
    specs = [
        pl.BlockSpec((TOK, TILE), lambda j, h: (0, h[0] * STEPS + j)),
        pl.BlockSpec((3, TOK, COLS), lambda j, h: (0, 0, 0)),
        pl.BlockSpec((3, TILE, COLS), lambda j, h: (0, h[0] * STEPS + j, 0)),
        pl.BlockSpec((3, RANK, COLS), lambda j, h: (0, 0, 0)),
    ]
    by_step = pl.BlockSpec((L_STEP, 128), lambda j, h: (j, 0))
    if keep:
        specs += [by_step, pl.BlockSpec((LO_ROWS, 128), lambda j, h: (0, 0))]
    return pl.pallas_call(
        left_keep_kernel if keep else left_send_kernel,
        grid_spec=pltpu.PrefetchScalarGridSpec(
            num_scalar_prefetch=1,
            grid=(STEPS,),
            in_specs=specs,
            out_specs=pl.BlockSpec((ROWS1, 128), lambda j, h: (0, 0)) if keep else by_step,
            scratch_shapes=[pltpu.VMEM((3, 2 * RANK, TOK), bf16)],
        ),
        out_shape=jax.ShapeDtypeStruct((ROWS1 if keep else L_ROWS, 128), f32),
        cost_estimate=cost(3),
        compiler_params=pltpu.CompilerParams(vmem_limit_bytes=VMEM),
        name="left_keep" if keep else "left_send",
    )(half, *held(inputs), grads, *held(err_in), basis_in, *((arrived, left_out_part) if keep else ()))


def left_out_kernel(gy_ref, hid_ref, err_out_ref, basis_out_ref, left_out_ref):
    @pl.when(pl.program_id(0) == 0)
    def _():
        left_out_ref[...] = jnp.zeros_like(left_out_ref)

    basis = stacked(basis_out_ref[...])
    tokens = stacked(folded(nt(basis, gy_ref[...])))
    part = folded(nt(basis, err_out_ref[...]) + nn(tokens, hid_ref[...]))
    for i, tile in enumerate(tiles_of(part)):
        left_out_ref[RANK * i : RANK * (i + 1), :] += tile


def left_out(grad_y, hidden, err_out, basis_out):
    return pl.pallas_call(
        left_out_kernel,
        grid=(D // 1024,),
        in_specs=[
            pl.BlockSpec((TOK, 1024), lambda j: (0, j)),
            pl.BlockSpec((TOK, COLS), lambda j: (0, 0)),
            pl.BlockSpec((COLS, 1024), lambda j: (0, j)),
            pl.BlockSpec((RANK, 1024), lambda j: (0, j)),
        ],
        out_specs=pl.BlockSpec((LO_ROWS, 128), lambda j: (0, 0)),
        out_shape=jax.ShapeDtypeStruct((LO_ROWS, 128), f32),
        cost_estimate=cost(4),
        compiler_params=pltpu.CompilerParams(vmem_limit_bytes=VMEM),
        name="left_out",
    )(*held(grad_y), hidden, *held(err_out), basis_out)


def turned_kernel(x_ref, turned_ref):
    turned_ref[...] = x_ref[...].astype(f32).T.astype(bf16)


def turned(inputs):
    return pl.pallas_call(
        turned_kernel,
        grid=(D // TILE,),
        in_specs=[pl.BlockSpec((TOK, TILE), lambda j: (0, j))],
        out_specs=pl.BlockSpec((TILE, TOK), lambda j: (j, 0)),
        out_shape=pltpu.HBM((D, TOK), bf16),
        cost_estimate=cost(3),
        compiler_params=pltpu.CompilerParams(vmem_limit_bytes=VMEM),
        name="turned",
    )(*streamed(inputs))


def wide(block, rows):
    return jnp.concatenate([block[i * rows : (i + 1) * rows] for i in range(block.shape[0] // rows)], axis=1)


def answer_left_kernel(me_ref, received_ref, answer_ref):
    over_xy = []
    for z in range(4):
        total = received_ref[z]
        for i in range(1, N_DP):
            total += received_ref[4 * i + z]
        over_xy.append(total)
    total = (over_xy[0] + over_xy[1]) + (over_xy[2] + over_xy[3])
    row = me_ref[0] * EACH1 + lax.broadcasted_iota(jnp.int32, (EACH1, 128), 0)
    for z in range(4):
        answer = jnp.where(row >= L_ROWS, over_xy[z], total)
        for i in range(N_DP):
            answer_ref[4 * i + z] = answer


def answer_left(me, received):
    whole = pl.BlockSpec((CHIPS, EACH1, 128), lambda j, m: (0, 0, 0))
    return pl.pallas_call(
        answer_left_kernel,
        grid_spec=pltpu.PrefetchScalarGridSpec(num_scalar_prefetch=1, grid=(1,), in_specs=[whole], out_specs=whole),
        out_shape=jax.ShapeDtypeStruct((CHIPS, EACH1, 128), f32),
        cost_estimate=cost(2),
        compiler_params=pltpu.CompilerParams(vmem_limit_bytes=VMEM),
        name="answer_left",
    )(me, received)


def answer_right_kernel(received_ref, answer_ref):
    total = received_ref[0]
    for i in range(1, N_DP):
        total += received_ref[i]
    for i in range(N_DP):
        answer_ref[i] = total


def answer_right(received):
    return pl.pallas_call(
        answer_right_kernel,
        out_shape=jax.ShapeDtypeStruct((N_DP, EACH2, 128), f32),
        cost_estimate=cost(1),
        compiler_params=pltpu.CompilerParams(vmem_limit_bytes=VMEM),
        name="answer_right",
    )(received)


def right_out_kernel(place_ref, left_out_ref, hid_ref, gy_hbm, err_out_hbm, right_out_ref, gram_ref, out_scr,
                     gy_scr, err_out_scr, sem):
    step = pl.program_id(0)

    def column(j):
        return lax.rem(place_ref[0] + 1 + j // 4, 2) * 4 + lax.rem(place_ref[1] + lax.rem(j, 4), 4)

    gy_ref, err_out_ref = fetched(step, 8, column, COLS, [(1, gy_hbm), (1, err_out_hbm)], [gy_scr, err_out_scr], sem)

    @pl.when(step == 0)
    def _():
        left_out = wide(left_out_ref[...], RANK)
        gram_ref[...] = jnp.concatenate([exact_nt(left_out, left_out), jnp.zeros((RANK, RANK), f32)], axis=1)
        factor = stacked(left_out)
        out_scr[:, :COLS] = factor
        out_scr[:, COLS:] = stacked(folded(nt(factor, hid_ref[...])))

    part = folded(nn(out_scr[:, :COLS], err_out_ref[...]) + nn(out_scr[:, COLS:], gy_ref[...]))
    for i, tile in enumerate(tiles_of(part)):
        right_out_ref[i] = tile


def right_out(place, left_out_sum, grad_y, hidden, err_out):
    return pl.pallas_call(
        right_out_kernel,
        grid_spec=pltpu.PrefetchScalarGridSpec(
            num_scalar_prefetch=1,
            grid=(8,),
            in_specs=[
                pl.BlockSpec((LO_ROWS, 128), lambda j, h: (0, 0)),
                pl.BlockSpec((TOK, COLS), lambda j, h: (0, 0)),
                ANY,
                ANY,
            ],
            out_specs=[
                pl.BlockSpec((3, RANK, 128), lambda j, h: (j, 0, 0)),
                pl.BlockSpec((RANK, 128), lambda j, h: (0, 0)),
            ],
            scratch_shapes=[
                pltpu.VMEM((2 * RANK, COLS + TOK), bf16),
                pltpu.VMEM((8, TOK, COLS), bf16),
                pltpu.VMEM((8, COLS, COLS), bf16),
                pltpu.SemaphoreType.DMA((2, 8)),
            ],
        ),
        out_shape=[
            jax.ShapeDtypeStruct((24, RANK, 128), f32),
            jax.ShapeDtypeStruct((RANK, 128), f32),
        ],
        cost_estimate=cost(3),
        compiler_params=pltpu.CompilerParams(vmem_limit_bytes=VMEM),
        name="right_out",
    )(place, left_out_sum, hidden, *streamed(grad_y, err_out))


def right_kernel(half_ref, own_ref, other_ref, x_hbm, err_in_hbm, right_ref, token_ref, x_scr, err_in_scr, sem):
    step = pl.program_id(0)

    def column(j):
        return lax.rem(j // STEPS + half_ref[0], 2) * STEPS + lax.rem(j, STEPS)

    x_ref, err_in_ref = fetched(step, 2 * STEPS, column, TILE, [(1, x_hbm), (1, err_in_hbm)], [x_scr, err_in_scr], sem)

    @pl.when(step == 0)
    def _():
        right_ref[...] = jnp.zeros_like(right_ref)
        token_ref[...] = jnp.zeros_like(token_ref)

    def add(ref):
        rows = wide(ref[...], 3 * RANK)
        for p in range(3):
            factor = stacked(rows[RANK * p : RANK * (p + 1)])
            right_ref[p] += folded(nn(factor, err_in_ref[p]))
            token_ref[p] += folded(nt(factor, x_ref[...]))

    @pl.when(step < STEPS)
    def _():
        add(own_ref)

    @pl.when(step >= STEPS)
    def _():
        add(other_ref)


def right(half, own, other, inputs, err_in):
    return pl.pallas_call(
        right_kernel,
        grid_spec=pltpu.PrefetchScalarGridSpec(
            num_scalar_prefetch=1,
            grid=(2 * STEPS,),
            in_specs=[
                pl.BlockSpec((L_STEP, 128), lambda j, h: (jnp.minimum(j, STEPS - 1), 0)),
                pl.BlockSpec((L_STEP, 128), lambda j, h: (jnp.maximum(j - STEPS, 0), 0)),
                ANY,
                ANY,
            ],
            out_specs=[
                pl.BlockSpec((3, RANK, COLS), lambda j, h: (0, 0, 0)),
                pl.BlockSpec((3, RANK, TOK), lambda j, h: (0, 0, 0)),
            ],
            scratch_shapes=[
                pltpu.VMEM((2 * STEPS, TOK, TILE), bf16),
                pltpu.VMEM((2 * STEPS, 3, TILE, COLS), bf16),
                pltpu.SemaphoreType.DMA((2, 2 * STEPS)),
            ],
        ),
        out_shape=[
            jax.ShapeDtypeStruct((3, RANK, COLS), f32),
            jax.ShapeDtypeStruct((3, RANK, TOK), f32),
        ],
        cost_estimate=cost(6),
        compiler_params=pltpu.CompilerParams(vmem_limit_bytes=VMEM),
        name="right",
    )(half, own, other, *streamed(inputs, err_in))


def join_kernel(right_ref, token_ref, grads_ref, own_ref, first_ref, second_ref, third_ref, rows_ref, gram_ref):
    for p in range(3):
        total = right_ref[p] + folded(nn(stacked(token_ref[p]), grads_ref[p]))
        for i, tile in enumerate(tiles_of(total)):
            rows_ref[pl.ds((HEADS * p + i) * RANK, RANK), :] = tile
    piece = (own_ref[...] + first_ref[...]) + (second_ref[...] + third_ref[...])
    rows_ref[RI_ROWS:, :] = piece[:PIECE]
    gram_ref[...] = piece[PIECE:]


def join(*operands):
    return pl.pallas_call(
        join_kernel,
        out_shape=[jax.ShapeDtypeStruct((ROWS2, 128), f32), jax.ShapeDtypeStruct((RANK, 128), f32)],
        cost_estimate=cost(1),
        compiler_params=pltpu.CompilerParams(vmem_limit_bytes=VMEM),
        name="join",
    )(*operands)


def invert_kernel(own_ref, other_ref, left_out_ref, gram_out_ref, inverse_ref, ortho_out_ref):
    eye = jnp.where(
        lax.broadcasted_iota(jnp.int32, (RANK, RANK), 0) == lax.broadcasted_iota(jnp.int32, (RANK, RANK), 1),
        1.0,
        0.0,
    )
    for p in range(3):
        gram = jnp.zeros((RANK, RANK), f32)
        for ref in (own_ref, other_ref):
            for i in range(STEPS):
                rows = jnp.concatenate(
                    [ref[pl.ds((CT * i + t) * 3 * RANK + RANK * p, RANK), :] for t in range(CT)], axis=1
                )
                gram += exact_nt(rows, rows)
        inverse_ref[p] = jnp.concatenate([gram, eye], axis=1)
    inverse_ref[3] = jnp.concatenate([gram_out_ref[:, :RANK], eye], axis=1)
    lane = lax.broadcasted_iota(jnp.int32, (4, RANK, 128), 2)
    sub = lax.broadcasted_iota(jnp.int32, (4, RANK, 128), 1)

    def eliminate(j, work):
        pivot_row = jnp.sum(jnp.where(sub == j, work, 0.0), axis=1, keepdims=True)
        pivot = jnp.sum(jnp.where(lane[:, :1] == j, pivot_row, 0.0), axis=2, keepdims=True)
        column = jnp.sum(jnp.where((lane == j) & (sub > j), work, 0.0), axis=2, keepdims=True)
        return work - column * (pivot_row / pivot)

    work = lax.fori_loop(0, RANK, eliminate, inverse_ref[...])
    diagonal = jnp.sum(jnp.where(lane == sub, work, 0.0), axis=2, keepdims=True)
    inverse = work * lax.rsqrt(diagonal)
    inverse_ref[...] = inverse
    ortho_out_ref[...] = exact_nn(inverse[3, :, RANK:], wide(left_out_ref[...], RANK))


def invert(own, other, left_out_sum, gram_out):
    return pl.pallas_call(
        invert_kernel,
        out_shape=[
            jax.ShapeDtypeStruct((4, RANK, 128), f32),
            jax.ShapeDtypeStruct((RANK, COLS), f32),
        ],
        cost_estimate=cost(10),
        compiler_params=pltpu.CompilerParams(vmem_limit_bytes=VMEM),
        name="invert",
    )(own, other, left_out_sum, gram_out)


def turn_kernel(half_ref, own_ref, other_ref, inverse_ref, ortho_ref):
    step = pl.program_id(0)

    def turn(ref):
        rows = wide(ref[...], 3 * RANK)
        for p in range(3):
            high, low = split2(exact_nn(inverse_ref[p, :, RANK:], rows[RANK * p : RANK * (p + 1)]))
            both = jnp.concatenate([high.astype(f32), low.astype(f32)], axis=0)
            ortho_ref[p] = both.T.astype(bf16)

    @pl.when(step < STEPS)
    def _():
        turn(own_ref)

    @pl.when(step >= STEPS)
    def _():
        turn(other_ref)


def turn(half, own, other, inverse):
    def column(j, h):
        return lax.rem(j // STEPS + h[0], 2) * STEPS + lax.rem(j, STEPS)

    return pl.pallas_call(
        turn_kernel,
        grid_spec=pltpu.PrefetchScalarGridSpec(
            num_scalar_prefetch=1,
            grid=(2 * STEPS,),
            in_specs=[
                pl.BlockSpec((CT * 3 * RANK, 128), lambda j, h: (jnp.minimum(j, STEPS - 1), 0)),
                pl.BlockSpec((CT * 3 * RANK, 128), lambda j, h: (jnp.maximum(j - STEPS, 0), 0)),
                pl.BlockSpec((4, RANK, 128), lambda j, h: (0, 0, 0)),
            ],
            out_specs=pl.BlockSpec((3, TILE, 128), lambda j, h: (0, column(j, h), 0)),
        ),
        out_shape=pltpu.HBM((3, D, 128), bf16),
        cost_estimate=cost(6),
        compiler_params=pltpu.CompilerParams(vmem_limit_bytes=VMEM),
        name="turn",
    )(half, own, other, inverse)


def rest_in_kernel(summed_in_ref, inverse_ref, grads_ref, turned_hbm, ortho_hbm, err_in_hbm, rest_in_ref,
                   factor_in_ref, in_scr, turned_scr, ortho_scr, err_in_scr, sem):
    step = pl.program_id(0)
    turned_ref, ortho_ref, err_in_ref = fetched(
        step,
        D // TILE,
        lambda j: j,
        TILE,
        [(0, turned_hbm), (1, ortho_hbm), (1, err_in_hbm)],
        [turned_scr, ortho_scr, err_in_scr],
        sem,
    )

    @pl.when(step == 0)
    def _():
        for p in range(3):
            right = wide(summed_in_ref[pl.ds(HEADS * RANK * p, HEADS * RANK), :], RANK) * (1.0 / N_DP)
            factor = exact_nn(inverse_ref[p, :, RANK:], right)
            factor_in_ref[p] = factor
            high, low = split2(-factor)
            in_scr[p] = jnp.concatenate([high, high, low, jnp.zeros_like(low)], axis=0)

    for p in range(3):
        both = jnp.concatenate([turned_ref[...], ortho_ref[p], ortho_ref[p]], axis=1)
        weights = jnp.concatenate([grads_ref[p], in_scr[p]], axis=0)
        rest_in_ref[p] = (nn(both, weights) + err_in_ref[p].astype(f32)).astype(bf16)


def rest_in(summed, inverse, turned, ortho_in, grads, err_in):
    return pl.pallas_call(
        rest_in_kernel,
        grid=(D // TILE,),
        in_specs=[
            pl.BlockSpec((RI_ROWS, 128), lambda j: (0, 0)),
            pl.BlockSpec((4, RANK, 128), lambda j: (0, 0, 0)),
            pl.BlockSpec((3, TOK, COLS), lambda j: (0, 0, 0)),
            ANY,
            ANY,
            ANY,
        ],
        out_specs=[
            pl.BlockSpec((3, TILE, COLS), lambda j: (0, j, 0)),
            pl.BlockSpec((3, RANK, COLS), lambda j: (0, 0, 0)),
        ],
        scratch_shapes=[
            pltpu.VMEM((3, 4 * RANK, COLS), bf16),
            pltpu.VMEM((D // TILE, TILE, TOK), bf16),
            pltpu.VMEM((D // TILE, 3, TILE, 128), bf16),
            pltpu.VMEM((D // TILE, 3, TILE, COLS), bf16),
            pltpu.SemaphoreType.DMA((3, D // TILE)),
        ],
        out_shape=[
            jax.ShapeDtypeStruct((3, D, COLS), bf16),
            jax.ShapeDtypeStruct((3, RANK, COLS), f32),
        ],
        cost_estimate=cost(10),
        compiler_params=pltpu.CompilerParams(vmem_limit_bytes=VMEM),
        name="rest_in",
    )(summed, inverse, grads, *streamed(turned, ortho_in, err_in))


def rest_out_kernel(place_ref, right_ref, inverse_ref, ortho_out_ref, hid_ref, gy_hbm, err_out_hbm, *refs):
    rest_out_ref, factor_out_ref, turned_scr, gy_scr, err_out_scr, sem = refs[-6:]
    step = pl.program_id(0)

    def column(j):
        return place_ref[0] * 4 + lax.rem(place_ref[1] + 4 - j, 4)

    gy_ref, err_out_ref = fetched(step, 4, column, COLS, [(1, gy_hbm), (1, err_out_hbm)], [gy_scr, err_out_scr], sem)

    @pl.when(step == 0)
    def _():
        high, low = split2(ortho_out_ref[...])
        stack = jnp.concatenate([high, high, low, jnp.zeros_like(low)], axis=0)
        turned_scr[:, :TOK] = hid_ref[...].astype(f32).T.astype(bf16)
        turned_scr[:, TOK:] = stack.astype(f32).T.astype(bf16)

    factor = exact_nn(inverse_ref[3, :, RANK:], wide(right_ref[...], RANK) * (1.0 / N_DP))
    factor_out_ref[...] = factor
    high, low = split2(-factor)
    weights = jnp.concatenate([gy_ref[...], high, low, high, jnp.zeros_like(low)], axis=0)
    rest_out_ref[...] = (nn(turned_scr[...], weights) + err_out_ref[...].astype(f32)).astype(bf16)


def rest_out(place, right_half, inverse, ortho_out, hidden, grad_y, err_out, before=()):
    def column(j, h):
        return h[0] * 4 + lax.rem(h[1] + 4 - j, 4)

    return pl.pallas_call(
        rest_out_kernel,
        grid_spec=pltpu.PrefetchScalarGridSpec(
            num_scalar_prefetch=1,
            grid=(4,),
            in_specs=[
                pl.BlockSpec((PIECE, 128), lambda j, h: (j, 0)),
                pl.BlockSpec((4, RANK, 128), lambda j, h: (0, 0, 0)),
                pl.BlockSpec((RANK, COLS), lambda j, h: (0, 0)),
                pl.BlockSpec((TOK, COLS), lambda j, h: (0, 0)),
            ]
            + [ANY] * (2 + len(before)),
            out_specs=[
                pl.BlockSpec((COLS, COLS), lambda j, h: (0, column(j, h))),
                pl.BlockSpec((RANK, COLS), lambda j, h: (0, column(j, h))),
            ],
            scratch_shapes=[
                pltpu.VMEM((COLS, 2 * TOK), bf16),
                pltpu.VMEM((4, TOK, COLS), bf16),
                pltpu.VMEM((4, COLS, COLS), bf16),
                pltpu.SemaphoreType.DMA((2, 4)),
            ],
        ),
        out_shape=[
            jax.ShapeDtypeStruct((COLS, D), bf16),
            jax.ShapeDtypeStruct((RANK, D), f32),
        ],
        input_output_aliases={7: 0, 8: 1} if before else {},
        cost_estimate=cost(3),
        compiler_params=pltpu.CompilerParams(vmem_limit_bytes=VMEM),
        name="rest_out",
    )(place, right_half, inverse, ortho_out, hidden, *streamed(grad_y, err_out), *before)


CHIP = ("x", "y", "z")
SWAP = [(0, 1), (1, 0)]
OTHERS = (2, 1, 3)


def ring(shift):
    return [(a, (a + shift) % 4) for a in range(4)]


def shards(inputs, grad_y, q_pre, f_pre, v_pre, w_out, err_in, err_out, basis_in, basis_out):
    keep = (err_in[0], err_out[0], inputs, grad_y)
    core = lax.axis_index("c").astype(jnp.int32)
    z = lax.axis_index("z").astype(jnp.int32)
    me = (lax.axis_index("x") * 4 + lax.axis_index("y")).astype(jnp.int32) * 4 + z
    mine = core[None]
    theirs = 1 - mine
    place = jnp.stack([core, z])
    their_place = jnp.stack([1 - core, z])
    hidden, grads, near_err_in, near_err_out, near_inputs, near_grad_y = recurrence(
        grad_y, w_out, q_pre, f_pre, v_pre, keep
    )
    err_in, err_out = keep[:2]
    send = left(theirs, near_inputs, grads, near_err_in, basis_in)
    arrived = lax.ppermute(send, "c", SWAP)
    left_out_part = left_out(near_grad_y, hidden, near_err_out, basis_out)
    rows = left(mine, near_inputs, grads, near_err_in, basis_in, arrived, left_out_part)

    rows, later_inputs = lax.optimization_barrier((rows, inputs))
    received = lax.all_to_all(rows.reshape(CHIPS, EACH1, 128), CHIP, 0, 0)
    inputs_turned = turned(later_inputs)
    received, inputs_turned = lax.optimization_barrier((received, inputs_turned))
    own = lax.all_to_all(answer_left(me[None], received), CHIP, 0, 0).reshape(ROWS1, 128)
    other = lax.ppermute(own, "c", SWAP)
    left_out_sum = own[L_ROWS : L_ROWS + LO_ROWS]

    partial_out, gram_out = right_out(place, left_out_sum, grad_y, hidden, err_out)
    quarters = partial_out.reshape(2, 4, PIECE, 128)
    send = jnp.concatenate([quarters[0].reshape(RO_ROWS, 128), gram_out])
    arrived = lax.ppermute(send, "c", SWAP)
    gram_out = gram_out + arrived[RO_ROWS:]
    quarters = quarters[1] + arrived[:RO_ROWS].reshape(4, PIECE, 128)
    pieces = [jnp.concatenate([quarters[shift], gram_out]) for shift in range(4)]
    pieces = [pieces[0]] + [lax.ppermute(pieces[shift], "z", ring(shift)) for shift in OTHERS]
    rows, gram_out = join(*right(mine, own, other, inputs, err_in), grads, *pieces)

    received = lax.all_to_all(rows.reshape(N_DP, EACH2, 128), ("x", "y"), 0, 0)
    inverse, ortho_out = invert(own, other, left_out_sum, gram_out)
    received, inverse, ortho_out = lax.optimization_barrier((received, inverse, ortho_out))
    everywhere = answer_right(received)
    everywhere, inverse = lax.optimization_barrier((everywhere, inverse))
    summed = lax.all_to_all(everywhere, ("x", "y"), 0, 0).reshape(ROWS2, 128)
    ortho_in = turn(mine, own, other, inverse)
    summed, ortho_in = lax.optimization_barrier((summed, ortho_in))

    pieces = [summed[RI_ROWS:]]
    pieces += [lax.ppermute(pieces[0], "z", ring(shift)) for shift in (1, 2, 3)]
    new_in, factor_in = rest_in(summed, inverse, inputs_turned, ortho_in, grads, err_in)
    pieces, factor_in = lax.optimization_barrier((pieces, factor_in))
    own_right = jnp.concatenate(pieces)
    other_right = lax.ppermute(own_right, "c", SWAP)
    halfway = rest_out(place, own_right, inverse, ortho_out, hidden, grad_y, err_out)
    new_out, factor_out = rest_out(
        their_place, other_right, inverse, ortho_out, hidden, grad_y, err_out, tuple(halfway)
    )
    return new_in[None], new_out[None], factor_in, factor_out


def solution(mesh):
    fine = Mesh(mesh.devices.reshape(4, 4, 4, 2), ("x", "y", "z", "c"))
    dp, head = ("x", "y"), ("z", "c")
    placed = (
        P(dp, None),
        P(dp, None),
        P(dp, head),
        P(dp, head),
        P(dp, head),
        P(head, None),
        P(dp, None, None, head),
        P(dp, head, None),
        P(None, None, head),
        P(),
    )
    return jax.shard_map(
        shards,
        mesh=fine,
        in_specs=placed,
        out_specs=(P(dp, None, None, head), P(dp, head, None), P(None, None, head), P()),
        check_vma=False,
    )
```

time: 182 us -> 159 us (0.87)
  blocking collectives: 45.2 us -> 0 us
  Pallas kernels: 61.7 us -> 76.6 us
  starting transfers between devices: 20.4 us -> 33.8 us
  local copies, waits for them, and re-layouts: 6.2 us -> 0.17 us
    all_to_all x2 -> x0, blocking collectives: 45.2 us -> none  [all_summed(): return lax.all_to_all(answer, CHIP, 0, 0).reshape(total_rows, 128)]
    pallas_call x5 -> x13, Pallas kernels: 42.2 us -> 59.5 us  [the longest x1 11.7 us: invert(): pl.pallas_call(invert_kernel, out_shape=[jax.ShapeDtypeStruct((4, RANK, 1...]
    all_to_all x2 -> x4, starting transfers between devices: 16.3 us -> 26.9 us  [the longest x1 11.5 us: shards(): received = lax.all_to_all(rows.reshape(CHIPS, EACH1, 128), CHIP, 0, 0)]
    unnamed x34 -> x7, local copies, waits for them, and re-layouts: 5.91 us -> 0.04 us
    ppermute x5 -> x7, waiting for transfers between devices: 6.24 us -> 1.2 us  [the longest x3 1.19 us: shards(): lax.ppermute(pieces[shift], 'z', ring(shift))]
    pallas_call x2 -> x1, Pallas kernels: 10.9 us -> 6.71 us  [right(): pl.pallas_call(right_kernel, grid_spec=pltpu.PrefetchScalarGridSpec(num_s...]
    all_to_all x2 -> x4, waiting for transfers between devices: 38.2 us -> 41.5 us  [the longest x1 20.9 us: shards(): lax.all_to_all(answer_left(me[None], received), CHIP, 0, 0)]
    ppermute x5 -> x7, starting transfers between devices: 3.36 us -> 6.28 us  [the longest x3 3.37 us: shards(): pieces += [lax.ppermute(pieces[0], 'z', ring(shift)) for shift in (1, 2, 3)]]
  transfers between devices with their start and end apart: 10 -> 14, of which waited for: 6 -> 5; matrix products, arithmetic and copies ran while one was open for 0% -> 1% of each run, Pallas kernels for 18% -> 33%
where the time goes in v2:
time: 159 us; the launch traced here: 157 us
  Pallas kernels  76.6 us (48%)
  waiting for transfers between devices  44.3 us (28%)
  starting transfers between devices  33.8 us (21%)
    all_to_all x1, waiting for transfers between devices, shards(): lax.all_to_all(answer_left(me[None], received), CHIP, 0, 0)  20.9 us
    all_to_all x1, waiting for transfers between devices, shards(): received = lax.all_to_all(rows.reshape(CHIPS, EACH1, 128), CHIP, 0, 0)  17.2 us
    pallas_call x1, Pallas kernels, invert(): pl.pallas_call(invert_kernel, out_shape=[jax.ShapeDtypeStruct((4, RANK, 1...  11.7 us
    all_to_all x1, starting transfers between devices, shards(): received = lax.all_to_all(rows.reshape(CHIPS, EACH1, 128), CHIP, 0, 0)  11.5 us
    pallas_call x1, Pallas kernels, recurrence(): pl.pallas_call(recurrence_kernel, grid=(HEADS,), in_specs=[pl.BlockSpec((...  10.4 us
    pallas_call x2, Pallas kernels, rest_out(): pl.pallas_call(rest_out_kernel, grid_spec=pltpu.PrefetchScalarGridSpec(nu...  10.2 us
    pallas_call x1, Pallas kernels, rest_in(): pl.pallas_call(rest_in_kernel, grid=(D // TILE,), in_specs=[pl.BlockSpec(...  9.41 us
    all_to_all x1, starting transfers between devices, shards(): summed = lax.all_to_all(everywhere, ('x', 'y'), 0, 0).reshape(ROWS2, 128)  6.97 us
  transfers between devices with their start and end apart: 14, of which 5 were waited for; matrix products, arithmetic and copies ran while one was open for 1% of the time, Pallas kernels for 33%

profile of v2, /device:TPU:0, one launch (start us, length us, event | category | flops | bytes accessed | tf_op | source)
XLA Modules:
  0.0 157.0 jit_solution(893825849487537334)
XLA Ops:
  0.6 10.4 %recurrence.1 = (bf16[256,384]{1,0:T(8,128)(2,1)S(1)}, bf16[3,256,384]{2,1,0:T(8,128)(2,1)S(1)}, bf16[3,3072,384]{2,1,0:T(8,128)(2,1)S(1)}, bf16[384,3072]{1,0:T...) custom-call(bf16[256,3072]{1,0:T(8,128)(2,1)} %gy_hbm.5, bf16[384,3072]{1,0:T(8,128)(2,1)} %w_ref.1, ...), custom_call_target="tpu_custom_call" | custom-call | flops 8000000000 | bytes 24000000 | tf_op jit(solution)/shard_map/recurrence/pallas_call | solution.py:194
  11.1 2.7 %left_send.1 = f32[2304,128]{1,0:T(8,128)S(1)} custom-call(s32[1]{0:T(128)S(6)} %sub.6.half_ref, bf16[256,3072]{1,0:T(8,128)(2,1)S(1)} %get-tuple-element.40.x_ref, bf16[3,256,384]{2,1,0:T(8,128)(2,1)S(1)} %get-tuple-element.41.grads_ref, bf16[3,3072,384]{2,1,0:T(8,128)(2,1)S(1)} %get-tuple-element.42.err_in_ref, f32[3,64,384]{2,1,0:T(8,128)S(1)} %copy-done), custom_call_target="tpu_custom_call" | custom-call | flops 3000000000 | bytes 9000000 | tf_op jit(solution)/shard_map/left_send/pallas_call | solution.py:269
  14.0 3.1 %left_out.1.left_out_ref = f32[192,128]{1,0:T(8,128)S(1)} custom-call(bf16[256,3072]{1,0:T(8,128)(2,1)S(1)} %get-tuple-element.43.gy_ref, bf16[256,384]{1,0:T(8,128)(2,1)S(1)} %get-tuple-element.44.hid_ref, bf16[384,3072]{1,0:T(8,128)(2,1)S(1)} %get-tuple-element.45.err_out_ref, f32[64,3072]{1,0:T(8,128)S(1)} %copy-done.1), custom_call_target="tpu_custom_call" | custom-call | flops 4000000000 | bytes 12000000 | tf_op jit(solution)/shard_map/left_out/pallas_call | solution.py:298
  17.1 3.8 %left_keep.1 = f32[2560,128]{1,0:T(8,128)} custom-call(s32[1]{0:T(128)} %bitcast.half_ref, bf16[256,3072]{1,0:T(8,128)(2,1)S(1)} %get-tuple-element.40.x_ref, bf16[3,256,384]{2,1,0:T(8,128)(2,1)S(1)} %get-tuple-element.41.grads_ref, bf16[3,3072,384]{2,1,0:T(8,128)(2,1)S(1)} %get-tuple-element.42.err_in_ref, f32[3,64,384]{2,1,0:T(8,128)S(1)} %copy-done, ...), custom_call_target="tpu_custom_call" | custom-call | flops 3000000000 | bytes 9000000 | tf_op jit(solution)/shard_map/left_keep/pallas_call | solution.py:269
  20.9 11.5 %all-to-all-start = ((f32[64,40,128]{2,1,0:T(8,128)}), f32[64,40,128]{2,1,0:T(8,128)S(1)}, u32[]{:S(2)}, u32[]{:S(2)}) async-start(f32[64,40,128]{2,1,0:T(8,128)} %bitcast.4), calls=%async_computation | async-start | bytes 2621440 | tf_op jit(solution)/shard_map/all_to_all | solution.py:754
  32.4 4.9 %turned.1.turned_hbm = bf16[3072,256]{1,0:T(8,128)(2,1)} custom-call(bf16[256,3072]{1,0:T(8,128)(2,1)} %x_hbm.1), custom_call_target="tpu_custom_call" | custom-call | flops 3000000000 | bytes 9000000 | tf_op jit(solution)/shard_map/turned/pallas_call | solution.py:320
  37.3 17.2 %all-to-all-done.received_ref = f32[64,40,128]{2,1,0:T(8,128)S(1)} async-done(((f32[64,40,128]{2,1,0:T(8,128)}), f32[64,40,128]{2,1,0:T(8,128)S(1)}, u32[]{:S(2)}, u32[]{:S(2)}) %all-to-all-start) | async-done | bytes 1310752 | tf_op jit(solution)/shard_map/all_to_all | solution.py:754
  54.5 1.2 answer_left.1
  55.8 4.7 %all-to-all-start.1 = ((f32[64,40,128]{2,1,0:T(8,128)}), f32[64,40,128]{2,1,0:T(8,128)S(1)}, u32[]{:S(2)}, u32[]{:S(2)}) async-start(f32[64,40,128]{2,1,0:T(8,128)} %answer_left.1), calls=%async_computation.1 | async-start | bytes 2621440 | tf_op jit(solution)/shard_map/all_to_all | solution.py:757
  60.5 20.9 %all-to-all-done.1 = f32[64,40,128]{2,1,0:T(8,128)S(1)} async-done(((f32[64,40,128]{2,1,0:T(8,128)}), f32[64,40,128]{2,1,0:T(8,128)S(1)}, u32[]{:S(2)}, u32[]{:S(2)}) %all-to-all-start.1) | async-done | bytes 1310752 | tf_op jit(solution)/shard_map/all_to_all | solution.py:757
  81.5 4.2 %right_out.1 = (f32[24,64,128]{2,1,0:T(8,128)S(1)}, f32[64,128]{1,0:T(8,128)S(1)}) custom-call(s32[2]{0:T(128)S(1)} %pad_add_fusion.place_ref, f32[192,128]{1,0:T(8,128)S(1)} %slice.42.left_out_ref, bf16[256,384]{1,0:T(8,128)(2,1)S(1)} %get-tuple-element.44.hid_ref, bf16[256,3072]{1,0:T(8,128)(2,1)} %gy_hbm.5, bf16[384,3072]{1,0:T(8,128)(2,1)} %bitcast.39), custom_call_target="tpu_custom_call" | custom-call | flops 3000000000 | bytes 9000000 | tf_op jit(solution)/shard_map/right_out/pallas_call | solution.py:404
  85.8 0.8 pad_maximum_fusion
  86.6 0.5 collective-permute-start.2
  87.1 1.6 %collective-permute-done.2 = f32[832,128]{1,0:T(8,128)S(1)} collective-permute-done((f32[832,128]{1,0:T(8,128)}, f32[832,128]{1,0:T(8,128)S(1)}, u32[]{:S(2)}, u32[]{:S(2)}) %collective-permute-start.2) | collective-permute-done | bytes 426016 | tf_op jit(solution)/shard_map/ppermute | solution.py:764
  88.9 0.9 collective-permute-start.5
  89.8 1.8 %collective-permute-start.3 = (f32[256,128]{1,0:T(8,128)S(1)}, f32[256,128]{1,0:T(8,128)S(1)}, u32[]{:S(2)}, u32[]{:S(2)}) collective-permute-start(f32[256,128]{1,0:T(8,128)S(1)} %get-tuple-element.83), channel_id=1, source_target_pairs={{0,4},{2,6},{4,0},{6,2},{1,5},{3,7},{5,1},{7,3},{8,12},{10,14},{12... | collective-permute-start | bytes 393224 | tf_op jit(solution)/shard_map/ppermute | solution.py:768
  91.6 0.1 collective-permute-start.4
  91.7 6.7 %right.1 = (f32[3,64,384]{2,1,0:T(8,128)S(1)}, f32[3,64,256]{2,1,0:T(8,128)S(1)}) custom-call(s32[1]{0:T(128)} %bitcast.half_ref, f32[2560,128]{1,0:T(8,128)S(1)} %bitcast.27, f32[2560,128]{1,0:T(8,128)} %collective-permute-done.1.other_ref, bf16[256,3072]{1,0:T(8,128)(2,1)} %x_hbm.1, bf16[3,3072,384]{2,1,0:T(8,128)(2,1)} %bitcast.36), custom_call_target="tpu_custom_call" | custom-call | flops 6000000000 | bytes 18000000 | tf_op jit(solution)/shard_map/right/pallas_call | solution.py:466
  98.4 1.2 collective-permute-done.4.second_ref
  99.6 1.0 join.1
  100.6 3.7 %all-to-all-start.2 = ((f32[16,48,128]{2,1,0:T(8,128)}), f32[16,48,128]{2,1,0:T(8,128)S(1)}, u32[]{:S(2)}, u32[]{:S(2)}) async-start(f32[16,48,128]{2,1,0:T(8,128)} %bitcast.14), calls=%async_computation.2 | async-start | bytes 786432 | tf_op jit(solution)/shard_map/all_to_all | solution.py:771
  104.4 11.7 %invert.1 = (f32[4,64,128]{2,1,0:T(8,128)S(1)}, f32[64,384]{1,0:T(8,128)S(1)}) custom-call(f32[2560,128]{1,0:T(8,128)S(1)} %bitcast.28, f32[2560,128]{1,0:T(8,128)} %collective-permute-done.1.other_ref, f32[192,128]{1,0:T(8,128)S(1)} %slice.42.left_out_ref, f32[64,128]{1,0:T(8,128)S(1)} %get-tuple-element.54.gram_out_ref), custom_call_target="tpu_custom_call" | custom-call | flops 10000000000 | bytes 30000000 | tf_op jit(solution)/shard_map/invert/pallas_call | solution.py:550
  116.1 0.8 answer_right.1
  116.9 7.0 %all-to-all-start.3 = ((f32[16,48,128]{2,1,0:T(8,128)}), f32[16,48,128]{2,1,0:T(8,128)S(1)}, u32[]{:S(2)}, u32[]{:S(2)}) async-start(f32[16,48,128]{2,1,0:T(8,128)} %answer_right.1), calls=%async_computation.3 | async-start | bytes 786432 | tf_op jit(solution)/shard_map/all_to_all | solution.py:776
  123.9 6.3 %turn.1.ortho_hbm = bf16[3,3072,128]{2,1,0:T(8,128)(2,1)} custom-call(s32[1]{0:T(128)} %bitcast.half_ref, f32[2560,128]{1,0:T(8,128)S(1)} %bitcast.29, f32[2560,128]{1,0:T(8,128)} %collective-permute-done.1.other_ref, f32[4,64,128]{2,1,0:T(8,128)S(1)} %get-tuple-element.60.inverse_ref), custom_call_target="tpu_custom_call" | custom-call | flops 6000000000 | bytes 18000000 | tf_op jit(solution)/shard_map/turn/pallas_call | solution.py:585
  130.1 3.3 %all-to-all-done.3 = f32[16,48,128]{2,1,0:T(8,128)S(1)} async-done(((f32[16,48,128]{2,1,0:T(8,128)}), f32[16,48,128]{2,1,0:T(8,128)S(1)}, u32[]{:S(2)}, u32[]{:S(2)}) %all-to-all-start.3) | async-done | bytes 393248 | tf_op jit(solution)/shard_map/all_to_all | solution.py:776
  133.5 1.7 %collective-permute-start.8 = (f32[192,128]{1,0:T(8,128)S(1)}, f32[192,128]{1,0:T(8,128)S(1)}, u32[]{:S(2)}, u32[]{:S(2)}) collective-permute-start(f32[192,128]{1,0:T(8,128)S(1)} %slice.41), channel_id=1, source_target_pairs={{0,6},{2,0},{4,2},{6,4},{1,7},{3,1},{5,3},{7,5},{8,14},{10,8},{12,... | collective-permute-start | bytes 294920 | tf_op jit(solution)/shard_map/ppermute | solution.py:781
  135.2 0.6 collective-permute-start.7
  135.7 1.2 collective-permute-start.6
  136.9 9.4 %rest_in.1 = (bf16[3,3072,384]{2,1,0:T(8,128)(2,1)}, f32[3,64,384]{2,1,0:T(8,128)}) custom-call(f32[768,128]{1,0:T(8,128)S(1)} %bitcast.31, f32[4,64,128]{2,1,0:T(8,128)S(1)} %get-tuple-element.60.inverse_ref, bf16[3,256,384]{2,1,0:T(8,128)(2,1)S(1)} %get-tuple-element.41.grads_ref, bf16[3072,256]{1,0:T(8,128)(2,1)} %turned.1.turned_hbm, ...), custom_call_target="tpu_custom_call" | custom-call | flops 10000000000 | bytes 30000000 | tf_op jit(solution)/shard_map/rest_in/pallas_call | solution.py:633
  146.6 5.1 %rest_out.2 = (bf16[384,3072]{1,0:T(8,128)(2,1)}, f32[64,3072]{1,0:T(8,128)}) custom-call(s32[2]{0:T(128)S(1)} %pad_add_fusion.place_ref, f32[768,128]{1,0:T(8,128)S(1)} %constant_dynamic-update-slice_fusion.right_ref, f32[4,64,128]{2,1,0:T(8,128)S(1)} %get-tuple-element.60.inverse_ref, f32[64,384]{1,0:T(8,128)S(1)} %get-tuple-element.70.ortho_out_ref, ...), custom_call_target="tpu_custom_call" | custom-call | flops 3000000000 | bytes 9000000 | tf_op jit(solution)/shard_map/rest_out/pallas_call | solution.py:692
  151.7 5.1 %rest_out.3 = (bf16[384,3072]{1,0:T(8,128)(2,1)}, f32[64,3072]{1,0:T(8,128)}) custom-call(s32[2]{0:T(128)S(1)} %pad_add_fusion.1.place_ref, f32[768,128]{1,0:T(8,128)S(1)} %collective-permute-done.9.right_ref, f32[4,64,128]{2,1,0:T(8,128)S(1)} %get-tuple-element.60.inverse_ref, ...), custom_call_target="tpu_custom_call", output_to_operand_aliasing={{0}: (7, {}), {1}: (8, {})} | custom-call | flops 3000000000 | bytes 9000000 | tf_op jit(solution)/shard_map/rest_out/pallas_call | solution.py:692
  (30 shorter events, 0.7 us)
Async XLA Ops:
  0.6 10.5 %copy-start = (f32[3,64,384]{2,1,0:T(8,128)S(1)}, f32[3,64,384]{2,1,0:T(8,128)}, u32[]{:S(2)}) copy-start(f32[3,64,384]{2,1,0:T(8,128)} %basis_in_ref.3) | copy-start | bytes 884740
  11.1 2.9 %copy-start.1 = (f32[64,3072]{1,0:T(8,128)S(1)}, f32[64,3072]{1,0:T(8,128)}, u32[]{:S(2)}) copy-start(f32[64,3072]{1,0:T(8,128)} %basis_out_ref.1) | copy-start | bytes 2359300
  13.9 3.2 %collective-permute-start = (f32[2304,128]{1,0:T(8,128)S(1)}, f32[2304,128]{1,0:T(8,128)S(1)}, u32[]{:S(2)}, u32[]{:S(2)}) collective-permute-start(f32[2304,128]{1,0:T(8,128)S(1)} %left_send.1), channel_id=1, source_target_pairs={{0,1},{1,0},{2,3},{3,2},{4,5},{5,4},{6,7},{7,6},{8,9},{9,8},{10,11... | collective-permute-start | bytes 3538952 | tf_op jit(solution)/shard_map/ppermute | solution.py:749
  20.9 33.6 %all-to-all-start = ((f32[64,40,128]{2,1,0:T(8,128)}), f32[64,40,128]{2,1,0:T(8,128)S(1)}, u32[]{:S(2)}, u32[]{:S(2)}) async-start(f32[64,40,128]{2,1,0:T(8,128)} %bitcast.4), calls=%async_computation | async-start | bytes 2621440 | tf_op jit(solution)/shard_map/all_to_all | solution.py:754
  55.8 25.6 %all-to-all-start.1 = ((f32[64,40,128]{2,1,0:T(8,128)}), f32[64,40,128]{2,1,0:T(8,128)S(1)}, u32[]{:S(2)}, u32[]{:S(2)}) async-start(f32[64,40,128]{2,1,0:T(8,128)} %answer_left.1), calls=%async_computation.1 | async-start | bytes 2621440 | tf_op jit(solution)/shard_map/all_to_all | solution.py:757
  81.4 10.3 %collective-permute-start.1 = (f32[2560,128]{1,0:T(8,128)S(1)}, f32[2560,128]{1,0:T(8,128)}, u32[]{:S(2)}, u32[]{:S(2)}) collective-permute-start(f32[2560,128]{1,0:T(8,128)S(1)} %bitcast.26), channel_id=1, source_target_pairs={{0,1},{1,0},{2,3},{3,2},{4,5},{5,4},{6,7},{7,6},{8,9},{9,8},{10,11... | collective-permute-start | bytes 3932168 | tf_op jit(solution)/shard_map/ppermute | solution.py:758
  86.6 2.1 %collective-permute-start.2 = (f32[832,128]{1,0:T(8,128)}, f32[832,128]{1,0:T(8,128)S(1)}, u32[]{:S(2)}, u32[]{:S(2)}) collective-permute-start(f32[832,128]{1,0:T(8,128)} %pad_maximum_fusion), channel_id=1, source_target_pairs={{0,1},{1,0},{2,3},{3,2},{4,5},{5,4},{6,7},{7,6},{8,9},{9,8},{10,11... | collective-permute-start | bytes 1277960 | tf_op jit(solution)/shard_map/ppermute | solution.py:764
  88.9 9.5 %collective-permute-start.5 = (f32[256,128]{1,0:T(8,128)S(1)}, f32[256,128]{1,0:T(8,128)S(1)}, u32[]{:S(2)}, u32[]{:S(2)}) collective-permute-start(f32[256,128]{1,0:T(8,128)S(1)} %get-tuple-element.82), channel_id=1, source_target_pairs={{0,6},{2,0},{4,2},{6,4},{1,7},{3,1},{5,3},{7,5},{8,14},{10,8},{12,... | collective-permute-start | bytes 393224 | tf_op jit(solution)/shard_map/ppermute | solution.py:768
  89.8 8.6 %collective-permute-start.3 = (f32[256,128]{1,0:T(8,128)S(1)}, f32[256,128]{1,0:T(8,128)S(1)}, u32[]{:S(2)}, u32[]{:S(2)}) collective-permute-start(f32[256,128]{1,0:T(8,128)S(1)} %get-tuple-element.83), channel_id=1, source_target_pairs={{0,4},{2,6},{4,0},{6,2},{1,5},{3,7},{5,1},{7,3},{8,12},{10,14},{12... | collective-permute-start | bytes 393224 | tf_op jit(solution)/shard_map/ppermute | solution.py:768
  91.6 8.0 %collective-permute-start.4 = (f32[256,128]{1,0:T(8,128)S(1)}, f32[256,128]{1,0:T(8,128)S(1)}, u32[]{:S(2)}, u32[]{:S(2)}) collective-permute-start(f32[256,128]{1,0:T(8,128)S(1)} %get-tuple-element.84), channel_id=1, source_target_pairs={{0,2},{2,4},{4,6},{6,0},{1,3},{3,5},{5,7},{7,1},{8,10},{10,12},{12... | collective-permute-start | bytes 393224 | tf_op jit(solution)/shard_map/ppermute | solution.py:768
  100.6 15.5 %all-to-all-start.2 = ((f32[16,48,128]{2,1,0:T(8,128)}), f32[16,48,128]{2,1,0:T(8,128)S(1)}, u32[]{:S(2)}, u32[]{:S(2)}) async-start(f32[16,48,128]{2,1,0:T(8,128)} %bitcast.14), calls=%async_computation.2 | async-start | bytes 786432 | tf_op jit(solution)/shard_map/all_to_all | solution.py:771
  116.9 16.6 %all-to-all-start.3 = ((f32[16,48,128]{2,1,0:T(8,128)}), f32[16,48,128]{2,1,0:T(8,128)S(1)}, u32[]{:S(2)}, u32[]{:S(2)}) async-start(f32[16,48,128]{2,1,0:T(8,128)} %answer_right.1), calls=%async_computation.3 | async-start | bytes 786432 | tf_op jit(solution)/shard_map/all_to_all | solution.py:776
  133.5 12.8 %collective-permute-start.8 = (f32[192,128]{1,0:T(8,128)S(1)}, f32[192,128]{1,0:T(8,128)S(1)}, u32[]{:S(2)}, u32[]{:S(2)}) collective-permute-start(f32[192,128]{1,0:T(8,128)S(1)} %slice.41), channel_id=1, source_target_pairs={{0,6},{2,0},{4,2},{6,4},{1,7},{3,1},{5,3},{7,5},{8,14},{10,8},{12,... | collective-permute-start | bytes 294920 | tf_op jit(solution)/shard_map/ppermute | solution.py:781
  135.2 11.1 %collective-permute-start.7 = (f32[192,128]{1,0:T(8,128)S(1)}, f32[192,128]{1,0:T(8,128)S(1)}, u32[]{:S(2)}, u32[]{:S(2)}) collective-permute-start(f32[192,128]{1,0:T(8,128)S(1)} %slice.41), channel_id=1, source_target_pairs={{0,4},{2,6},{4,0},{6,2},{1,5},{3,7},{5,1},{7,3},{8,12},{10,14},{12... | collective-permute-start | bytes 294920 | tf_op jit(solution)/shard_map/ppermute | solution.py:781
  135.7 10.6 %collective-permute-start.6 = (f32[192,128]{1,0:T(8,128)S(1)}, f32[192,128]{1,0:T(8,128)S(1)}, u32[]{:S(2)}, u32[]{:S(2)}) collective-permute-start(f32[192,128]{1,0:T(8,128)S(1)} %slice.41), channel_id=1, source_target_pairs={{0,2},{2,4},{4,6},{6,0},{1,3},{3,5},{5,7},{7,1},{8,10},{10,12},{12... | collective-permute-start | bytes 294920 | tf_op jit(solution)/shard_map/ppermute | solution.py:781
  146.4 5.3 %collective-permute-start.9 = (f32[768,128]{1,0:T(8,128)S(1)}, f32[768,128]{1,0:T(8,128)S(1)}, u32[]{:S(2)}, u32[]{:S(2)}) collective-permute-start(f32[768,128]{1,0:T(8,128)S(1)} %constant_dynamic-update-slice_fusion.right_ref), channel_id=1, source_target_pairs={{0,1},{1,0},{2,3},{3,2},{4,5},{5,4},{6,7},{7,6},{8,9},{9,8},{10,11... | collective-permute-start | bytes 1179656 | tf_op jit(solution)/shard_map/ppermute | solution.py:785

commit v3 on v2

--- a/solution.py
+++ b/solution.py
@@ -72,6 +72,12 @@
     return high, mid, (rest - mid.astype(f32)).astype(bf16)
 
 
+def summed3(ones, a):
+    parts = nn(ones, jnp.concatenate(split3(a), axis=1))
+    width = a.shape[1]
+    return parts[:, :width] + (parts[:, width : 2 * width] + parts[:, 2 * width :])
+
+
 def stacked(a):
     return jnp.concatenate(split2(a), axis=0)
 
@@ -106,8 +112,7 @@
     lower = jnp.where(row >= col, 1.0, 0.0).astype(bf16)
     upper = jnp.where(row <= col, 1.0, 0.0).astype(bf16)
     differ = row ^ col
-    high, mid, low = split3(log_decay)
-    running = nn(lower, high) + (nn(lower, mid) + nn(lower, low))
+    running = summed3(lower, log_decay)
 
     scores = jnp.zeros((TOK, TOK), f32)
     grad_s = split2(nt(grad_o, v))
@@ -145,8 +150,7 @@
     s_high, s_low = split2(scores)
     hid_ref[...] = (nn(s_high, v) + nn(s_low, v)).astype(bf16)
     grad_v = tn(s_high, grad_o) + tn(s_low, grad_o)
-    high, mid, low = split3(query * grad_query - key * grad_key)
-    grad_decay = nn(upper, high) + (nn(upper, mid) + nn(upper, low))
+    grad_decay = summed3(upper, query * grad_query - key * grad_key)
     grad_ref[0] = (grad_query * (q_gate + query * (1.0 - q_gate))).astype(bf16)
     grad_ref[1] = (key * (grad_decay - grad_key * decay)).astype(bf16)
     grad_ref[2] = grad_v.astype(bf16)
@@ -219,92 +223,52 @@
     return [a[:, 128 * i : 128 * (i + 1)] for i in range(a.shape[1] // 128)]
 
 
-def left_tokens(grads_ref, basis_in_ref, token_scr):
-    for p in range(3):
-        token_scr[p] = stacked(folded(nt(stacked(basis_in_ref[p]), grads_ref[p])))
-
-
-def left_tile(p, x_ref, err_in_ref, basis_in_ref, token_scr):
-    part = nn(token_scr[p], x_ref[...]) + nt(stacked(basis_in_ref[p]), err_in_ref[p])
-    return tiles_of(folded(part))
-
-
-def left_send_kernel(half_ref, x_ref, grads_ref, err_in_ref, basis_in_ref, left_ref, token_scr):
-    @pl.when(pl.program_id(0) == 0)
-    def _():
-        left_tokens(grads_ref, basis_in_ref, token_scr)
-
-    for p in range(3):
-        for i, tile in enumerate(left_tile(p, x_ref, err_in_ref, basis_in_ref, token_scr)):
-            at = (3 * i + p) * RANK
-            left_ref[at : at + RANK, :] = tile
-
-
-def left_keep_kernel(half_ref, x_ref, grads_ref, err_in_ref, basis_in_ref, arrived_ref, left_out_ref, rows_ref, token_scr):
-    step = pl.program_id(0)
-
-    @pl.when(step == 0)
-    def _():
-        left_tokens(grads_ref, basis_in_ref, token_scr)
-        rows_ref[L_ROWS : L_ROWS + LO_ROWS, :] = left_out_ref[...]
-        rows_ref[L_ROWS + LO_ROWS :, :] = jnp.zeros((ROWS1 - L_ROWS - LO_ROWS, 128), f32)
-
-    for p in range(3):
-        for i, tile in enumerate(left_tile(p, x_ref, err_in_ref, basis_in_ref, token_scr)):
-            at = (3 * i + p) * RANK
-            rows_ref[pl.ds(pl.multiple_of(step * L_STEP + at, RANK), RANK), :] = tile + arrived_ref[at : at + RANK, :]
-
-
-def left(half, inputs, grads, err_in, basis_in, arrived=None, left_out_part=None):
-    keep = arrived is not None
-    specs = [
-        pl.BlockSpec((TOK, TILE), lambda j, h: (0, h[0] * STEPS + j)),
-        pl.BlockSpec((3, TOK, COLS), lambda j, h: (0, 0, 0)),
-        pl.BlockSpec((3, TILE, COLS), lambda j, h: (0, h[0] * STEPS + j, 0)),
-        pl.BlockSpec((3, RANK, COLS), lambda j, h: (0, 0, 0)),
-    ]
-    by_step = pl.BlockSpec((L_STEP, 128), lambda j, h: (j, 0))
-    if keep:
-        specs += [by_step, pl.BlockSpec((LO_ROWS, 128), lambda j, h: (0, 0))]
-    return pl.pallas_call(
-        left_keep_kernel if keep else left_send_kernel,
-        grid_spec=pltpu.PrefetchScalarGridSpec(
-            num_scalar_prefetch=1,
-            grid=(STEPS,),
-            in_specs=specs,
-            out_specs=pl.BlockSpec((ROWS1, 128), lambda j, h: (0, 0)) if keep else by_step,
-            scratch_shapes=[pltpu.VMEM((3, 2 * RANK, TOK), bf16)],
-        ),
-        out_shape=jax.ShapeDtypeStruct((ROWS1 if keep else L_ROWS, 128), f32),
+def left_tiles(half_ref, x_ref, grads_ref, err_in_ref, basis_in_ref):
+    bases = [stacked(basis_in_ref[p]) for p in range(3)]
+    tokens = jnp.concatenate([stacked(folded(nt(bases[p], grads_ref[p]))) for p in range(3)], axis=0)
+    for step in range(STEPS):
+        at = pl.ds(pl.multiple_of(half_ref[0] * HALF + step * TILE, TILE), TILE)
+        from_tokens = nn(tokens, x_ref[:, at])
+        for p in range(3):
+            part = from_tokens[2 * RANK * p : 2 * RANK * (p + 1)] + nt(bases[p], err_in_ref[p, at, :])
+            for i, tile in enumerate(tiles_of(folded(part))):
+                yield step * L_STEP + (3 * i + p) * RANK, tile
+
+
+def left_send_kernel(half_ref, x_ref, grads_ref, err_in_ref, basis_in_ref, left_ref):
+    for at, tile in left_tiles(half_ref, x_ref, grads_ref, err_in_ref, basis_in_ref):
+        left_ref[at : at + RANK, :] = tile
+
+
+def left_keep_kernel(half_ref, x_ref, grads_ref, err_in_ref, basis_in_ref, arrived_ref, left_out_ref, rows_ref):
+    rows_ref[L_ROWS : L_ROWS + LO_ROWS, :] = left_out_ref[...]
+    rows_ref[L_ROWS + LO_ROWS :, :] = jnp.zeros((ROWS1 - L_ROWS - LO_ROWS, 128), f32)
+    for at, tile in left_tiles(half_ref, x_ref, grads_ref, err_in_ref, basis_in_ref):
+        rows_ref[at : at + RANK, :] = tile + arrived_ref[at : at + RANK, :]
+
+
+def left(half, inputs, grads, err_in, basis_in, *arrived):
+    return pl.pallas_call(
+        left_keep_kernel if arrived else left_send_kernel,
+        in_specs=[pl.BlockSpec(memory_space=pltpu.SMEM)] + [pl.BlockSpec(memory_space=pltpu.VMEM)] * (4 + len(arrived)),
+        out_shape=jax.ShapeDtypeStruct((ROWS1 if arrived else L_ROWS, 128), f32),
         cost_estimate=cost(3),
         compiler_params=pltpu.CompilerParams(vmem_limit_bytes=VMEM),
-        name="left_keep" if keep else "left_send",
-    )(half, *held(inputs), grads, *held(err_in), basis_in, *((arrived, left_out_part) if keep else ()))
+        name="left_keep" if arrived else "left_send",
+    )(half, *held(inputs), grads, *held(err_in), basis_in, *arrived)
 
 
 def left_out_kernel(gy_ref, hid_ref, err_out_ref, basis_out_ref, left_out_ref):
-    @pl.when(pl.program_id(0) == 0)
-    def _():
-        left_out_ref[...] = jnp.zeros_like(left_out_ref)
-
     basis = stacked(basis_out_ref[...])
     tokens = stacked(folded(nt(basis, gy_ref[...])))
     part = folded(nt(basis, err_out_ref[...]) + nn(tokens, hid_ref[...]))
     for i, tile in enumerate(tiles_of(part)):
-        left_out_ref[RANK * i : RANK * (i + 1), :] += tile
+        left_out_ref[RANK * i : RANK * (i + 1), :] = tile
 
 
 def left_out(grad_y, hidden, err_out, basis_out):
     return pl.pallas_call(
         left_out_kernel,
-        grid=(D // 1024,),
-        in_specs=[
-            pl.BlockSpec((TOK, 1024), lambda j: (0, j)),
-            pl.BlockSpec((TOK, COLS), lambda j: (0, 0)),
-            pl.BlockSpec((COLS, 1024), lambda j: (0, j)),
-            pl.BlockSpec((RANK, 1024), lambda j: (0, j)),
-        ],
-        out_specs=pl.BlockSpec((LO_ROWS, 128), lambda j: (0, 0)),
         out_shape=jax.ShapeDtypeStruct((LO_ROWS, 128), f32),
         cost_estimate=cost(4),
         compiler_params=pltpu.CompilerParams(vmem_limit_bytes=VMEM),
@@ -447,11 +411,11 @@
         token_ref[...] = jnp.zeros_like(token_ref)
 
     def add(ref):
-        rows = wide(ref[...], 3 * RANK)
+        high, low = split2(wide(ref[...], 3 * RANK))
+        token_ref[...] += folded(nt(jnp.concatenate([high, low], axis=0), x_ref[...]))
         for p in range(3):
-            factor = stacked(rows[RANK * p : RANK * (p + 1)])
-            right_ref[p] += folded(nn(factor, err_in_ref[p]))
-            token_ref[p] += folded(nt(factor, x_ref[...]))
+            mine = slice(RANK * p, RANK * (p + 1))
+            right_ref[p] += folded(nn(jnp.concatenate([high[mine], low[mine]], axis=0), err_in_ref[p]))
 
     @pl.when(step < STEPS)
     def _():
@@ -476,7 +440,7 @@
             ],
             out_specs=[
                 pl.BlockSpec((3, RANK, COLS), lambda j, h: (0, 0, 0)),
-                pl.BlockSpec((3, RANK, TOK), lambda j, h: (0, 0, 0)),
+                pl.BlockSpec((3 * RANK, TOK), lambda j, h: (0, 0)),
             ],
             scratch_shapes=[
                 pltpu.VMEM((2 * STEPS, TOK, TILE), bf16),
@@ -486,7 +450,7 @@
         ),
         out_shape=[
             jax.ShapeDtypeStruct((3, RANK, COLS), f32),
-            jax.ShapeDtypeStruct((3, RANK, TOK), f32),
+            jax.ShapeDtypeStruct((3 * RANK, TOK), f32),
         ],
         cost_estimate=cost(6),
         compiler_params=pltpu.CompilerParams(vmem_limit_bytes=VMEM),
@@ -496,7 +460,7 @@
 
 def join_kernel(right_ref, token_ref, grads_ref, own_ref, first_ref, second_ref, third_ref, rows_ref, gram_ref):
     for p in range(3):
-        total = right_ref[p] + folded(nn(stacked(token_ref[p]), grads_ref[p]))
+        total = right_ref[p] + folded(nn(stacked(token_ref[RANK * p : RANK * (p + 1), :]), grads_ref[p]))
         for i, tile in enumerate(tiles_of(total)):
             rows_ref[pl.ds((HEADS * p + i) * RANK, RANK), :] = tile
     piece = (own_ref[...] + first_ref[...]) + (second_ref[...] + third_ref[...])
@@ -530,16 +494,20 @@
                 gram += exact_nt(rows, rows)
         inverse_ref[p] = jnp.concatenate([gram, eye], axis=1)
     inverse_ref[3] = jnp.concatenate([gram_out_ref[:, :RANK], eye], axis=1)
+    rows8 = lax.broadcasted_iota(jnp.int32, (1, 8, 1), 1)
+    tiles = [inverse_ref[:, 8 * t : 8 * t + 8, :] for t in range(RANK // 8)]
+    for j in range(RANK):
+        top, at = divmod(j, 8)
+        pivot_row = tiles[top][:, at : at + 1, :]
+        scaled = pivot_row * (1.0 / pivot_row[:, :, j : j + 1])
+        for t in range(top, RANK // 8):
+            column = tiles[t][:, :, j : j + 1]
+            if t == top:
+                column = jnp.where(rows8 > at, column, 0.0)
+            tiles[t] = tiles[t] - column * scaled
+    work = jnp.concatenate(tiles, axis=1)
     lane = lax.broadcasted_iota(jnp.int32, (4, RANK, 128), 2)
     sub = lax.broadcasted_iota(jnp.int32, (4, RANK, 128), 1)
-
-    def eliminate(j, work):
-        pivot_row = jnp.sum(jnp.where(sub == j, work, 0.0), axis=1, keepdims=True)
-        pivot = jnp.sum(jnp.where(lane[:, :1] == j, pivot_row, 0.0), axis=2, keepdims=True)
-        column = jnp.sum(jnp.where((lane == j) & (sub > j), work, 0.0), axis=2, keepdims=True)
-        return work - column * (pivot_row / pivot)
-
-    work = lax.fori_loop(0, RANK, eliminate, inverse_ref[...])
     diagonal = jnp.sum(jnp.where(lane == sub, work, 0.0), axis=2, keepdims=True)
     inverse = work * lax.rsqrt(diagonal)
     inverse_ref[...] = inverse
@@ -623,10 +591,11 @@
             high, low = split2(-factor)
             in_scr[p] = jnp.concatenate([high, high, low, jnp.zeros_like(low)], axis=0)
 
+    moments = nn(turned_ref[...], jnp.concatenate([grads_ref[p] for p in range(3)], axis=1))
     for p in range(3):
-        both = jnp.concatenate([turned_ref[...], ortho_ref[p], ortho_ref[p]], axis=1)
-        weights = jnp.concatenate([grads_ref[p], in_scr[p]], axis=0)
-        rest_in_ref[p] = (nn(both, weights) + err_in_ref[p].astype(f32)).astype(bf16)
+        moment = moments[:, COLS * p : COLS * (p + 1)] + err_in_ref[p].astype(f32)
+        both = jnp.concatenate([ortho_ref[p], ortho_ref[p]], axis=1)
+        rest_in_ref[p] = (moment + nn(both, in_scr[p])).astype(bf16)
 
 
 def rest_in(summed, inverse, turned, ortho_in, grads, err_in):
@@ -663,59 +632,65 @@
 
 
 def rest_out_kernel(place_ref, right_ref, inverse_ref, ortho_out_ref, hid_ref, gy_hbm, err_out_hbm, *refs):
-    rest_out_ref, factor_out_ref, turned_scr, gy_scr, err_out_scr, sem = refs[-6:]
-    step = pl.program_id(0)
+    rest_hbm, factor_hbm, gy_scr, err_out_scr, rest_scr, factor_scr, in_sem, out_sem = refs[-8:]
 
     def column(j):
-        return place_ref[0] * 4 + lax.rem(place_ref[1] + 4 - j, 4)
-
-    gy_ref, err_out_ref = fetched(step, 4, column, COLS, [(1, gy_hbm), (1, err_out_hbm)], [gy_scr, err_out_scr], sem)
-
-    @pl.when(step == 0)
-    def _():
-        high, low = split2(ortho_out_ref[...])
-        stack = jnp.concatenate([high, high, low, jnp.zeros_like(low)], axis=0)
-        turned_scr[:, :TOK] = hid_ref[...].astype(f32).T.astype(bf16)
-        turned_scr[:, TOK:] = stack.astype(f32).T.astype(bf16)
-
-    factor = exact_nn(inverse_ref[3, :, RANK:], wide(right_ref[...], RANK) * (1.0 / N_DP))
-    factor_out_ref[...] = factor
+        at = place_ref[0] * 4 + lax.rem(place_ref[1] + 4 - j, 4)
+        return pl.ds(pl.multiple_of(at * COLS, COLS), COLS)
+
+    into = [
+        (
+            pltpu.make_async_copy(gy_hbm.at[:, column(j)], gy_scr.at[j], in_sem.at[0, j]),
+            pltpu.make_async_copy(err_out_hbm.at[:, column(j)], err_out_scr.at[j], in_sem.at[1, j]),
+        )
+        for j in range(4)
+    ]
+    out = [
+        (
+            pltpu.make_async_copy(rest_scr.at[j], rest_hbm.at[:, column(j)], out_sem.at[0, j]),
+            pltpu.make_async_copy(factor_scr.at[j], factor_hbm.at[:, column(j)], out_sem.at[1, j]),
+        )
+        for j in range(4)
+    ]
+    for pair in into:
+        for copy in pair:
+            copy.start()
+    high, low = split2(ortho_out_ref[...])
+    stack = jnp.concatenate([high, high, low, jnp.zeros_like(low)], axis=0)
+    both = jnp.concatenate([hid_ref[...], stack], axis=0).astype(f32).T.astype(bf16)
+    right = jnp.concatenate([wide(right_ref[PIECE * j : PIECE * (j + 1), :], RANK) for j in range(4)], axis=1)
+    factor = exact_nn(inverse_ref[3, :, RANK:], right * (1.0 / N_DP))
     high, low = split2(-factor)
-    weights = jnp.concatenate([gy_ref[...], high, low, high, jnp.zeros_like(low)], axis=0)
-    rest_out_ref[...] = (nn(turned_scr[...], weights) + err_out_ref[...].astype(f32)).astype(bf16)
+    weights = jnp.concatenate([high, low, high, jnp.zeros_like(low)], axis=0)
+    for j in range(4):
+        mine = slice(COLS * j, COLS * (j + 1))
+        factor_scr[j] = factor[:, mine]
+        for copy in into[j]:
+            copy.wait()
+        total = nn(both, jnp.concatenate([gy_scr[j], weights[:, mine]], axis=0)) + err_out_scr[j].astype(f32)
+        rest_scr[j] = total.astype(bf16)
+        for copy in out[j]:
+            copy.start()
+    for pair in out:
+        for copy in pair:
+            copy.wait()
 
 
 def rest_out(place, right_half, inverse, ortho_out, hidden, grad_y, err_out, before=()):
-    def column(j, h):
-        return h[0] * 4 + lax.rem(h[1] + 4 - j, 4)
-
+    whole = pl.BlockSpec(memory_space=pltpu.VMEM)
     return pl.pallas_call(
         rest_out_kernel,
-        grid_spec=pltpu.PrefetchScalarGridSpec(
-            num_scalar_prefetch=1,
-            grid=(4,),
-            in_specs=[
-                pl.BlockSpec((PIECE, 128), lambda j, h: (j, 0)),
-                pl.BlockSpec((4, RANK, 128), lambda j, h: (0, 0, 0)),
-                pl.BlockSpec((RANK, COLS), lambda j, h: (0, 0)),
-                pl.BlockSpec((TOK, COLS), lambda j, h: (0, 0)),
-            ]
-            + [ANY] * (2 + len(before)),
-            out_specs=[
-                pl.BlockSpec((COLS, COLS), lambda j, h: (0, column(j, h))),
-                pl.BlockSpec((RANK, COLS), lambda j, h: (0, column(j, h))),
-            ],
-            scratch_shapes=[
-                pltpu.VMEM((COLS, 2 * TOK), bf16),
-                pltpu.VMEM((4, TOK, COLS), bf16),
-                pltpu.VMEM((4, COLS, COLS), bf16),
-                pltpu.SemaphoreType.DMA((2, 4)),
-            ],
-        ),
-        out_shape=[
-            jax.ShapeDtypeStruct((COLS, D), bf16),
-            jax.ShapeDtypeStruct((RANK, D), f32),
+        in_specs=[pl.BlockSpec(memory_space=pltpu.SMEM)] + [whole] * 4 + [ANY] * (2 + len(before)),
+        out_specs=[ANY, ANY],
+        scratch_shapes=[
+            pltpu.VMEM((4, TOK, COLS), bf16),
+            pltpu.VMEM((4, COLS, COLS), bf16),
+            pltpu.VMEM((4, COLS, COLS), bf16),
+            pltpu.VMEM((4, RANK, COLS), f32),
+            pltpu.SemaphoreType.DMA((2, 4)),
+            pltpu.SemaphoreType.DMA((2, 4)),
         ],
+        out_shape=[pltpu.HBM((COLS, D), bf16), pltpu.HBM((RANK, D), f32)],
         input_output_aliases={7: 0, 8: 1} if before else {},
         cost_estimate=cost(3),
         compiler_params=pltpu.CompilerParams(vmem_limit_bytes=VMEM),

time: 159 us -> 151 us (0.950)
  Pallas kernels: 76.6 us -> 67.9 us
  waiting for transfers between devices: 44.3 us -> 46 us
    pallas_call x5, Pallas kernels: 19.9 us -> 15 us  [the longest x2 8.76 us: rest_out(): pl.pallas_call(rest_out_kernel, in_specs=[pl.BlockSpec(memory_space=pltpu...]
    pallas_call x1, Pallas kernels: 11.7 us -> 8.96 us  [invert(): pl.pallas_call(invert_kernel, out_shape=[jax.ShapeDtypeStruct((4, RANK, 1...]
  transfers between devices with their start and end apart: 14 -> 14, of which waited for: 5 -> 7; matrix products, arithmetic and copies ran while one was open for 1% -> 1% of each run, Pallas kernels for 33% -> 31%
where the time goes in v3:
time: 151 us; the launch traced here: 149 us
  Pallas kernels  67.9 us (45%)
  waiting for transfers between devices  46 us (30%)
  starting transfers between devices  32.8 us (22%)
    all_to_all x1, waiting for transfers between devices, shards(): lax.all_to_all(answer_left(me[None], received), CHIP, 0, 0)  20.5 us
    all_to_all x1, waiting for transfers between devices, shards(): received = lax.all_to_all(rows.reshape(CHIPS, EACH1, 128), CHIP, 0, 0)  16.9 us
    all_to_all x1, starting transfers between devices, shards(): received = lax.all_to_all(rows.reshape(CHIPS, EACH1, 128), CHIP, 0, 0)  11.5 us
    pallas_call x1, Pallas kernels, recurrence(): pl.pallas_call(recurrence_kernel, grid=(HEADS,), in_specs=[pl.BlockSpec((...  10.3 us
    pallas_call x1, Pallas kernels, rest_in(): pl.pallas_call(rest_in_kernel, grid=(D // TILE,), in_specs=[pl.BlockSpec(...  8.98 us
    pallas_call x1, Pallas kernels, invert(): pl.pallas_call(invert_kernel, out_shape=[jax.ShapeDtypeStruct((4, RANK, 1...  8.96 us
    pallas_call x2, Pallas kernels, rest_out(): pl.pallas_call(rest_out_kernel, in_specs=[pl.BlockSpec(memory_space=pltpu...  8.76 us
    pallas_call x1, Pallas kernels, turn(): pl.pallas_call(turn_kernel, grid_spec=pltpu.PrefetchScalarGridSpec(num_sc...  6.25 us
  transfers between devices with their start and end apart: 14, of which 7 were waited for; matrix products, arithmetic and copies ran while one was open for 1% of the time, Pallas kernels for 31%

profile of v3, /device:TPU:0, one launch (start us, length us, event | category | flops | bytes accessed | tf_op | source)
XLA Modules:
  0.0 149.0 jit_solution(2299766551601105903)
XLA Ops:
  0.6 10.3 %recurrence.1 = (bf16[256,384]{1,0:T(8,128)(2,1)S(1)}, bf16[3,256,384]{2,1,0:T(8,128)(2,1)S(1)}, bf16[3,3072,384]{2,1,0:T(8,128)(2,1)S(1)}, bf16[384,3072]{1,0:T...) custom-call(bf16[256,3072]{1,0:T(8,128)(2,1)} %gy_hbm.5, bf16[384,3072]{1,0:T(8,128)(2,1)} %w_ref.1, ...), custom_call_target="tpu_custom_call" | custom-call | flops 8000000000 | bytes 24000000 | tf_op jit(solution)/shard_map/recurrence/pallas_call | solution.py:198
  11.0 1.6 %left_send.1 = f32[2304,128]{1,0:T(8,128)S(1)} custom-call(s32[1]{0:T(128)S(6)} %sub.6.half_ref, bf16[256,3072]{1,0:T(8,128)(2,1)S(1)} %get-tuple-element.40.x_ref, bf16[3,256,384]{2,1,0:T(8,128)(2,1)S(1)} %get-tuple-element.41.grads_ref, bf16[3,3072,384]{2,1,0:T(8,128)(2,1)S(1)} %get-tuple-element.42.err_in_ref, f32[3,64,384]{2,1,0:T(8,128)S(1)} %copy-done), custom_call_target="tpu_custom_call" | custom-call | flops 3000000000 | bytes 9000000 | tf_op jit(solution)/shard_map/left_send/pallas_call | solution.py:251
  12.7 1.9 %left_out.1.left_out_ref = f32[192,128]{1,0:T(8,128)S(1)} custom-call(bf16[256,3072]{1,0:T(8,128)(2,1)S(1)} %get-tuple-element.43.gy_ref, bf16[256,384]{1,0:T(8,128)(2,1)S(1)} %get-tuple-element.44.hid_ref, bf16[384,3072]{1,0:T(8,128)(2,1)S(1)} %get-tuple-element.45.err_out_ref, f32[64,3072]{1,0:T(8,128)S(1)} %copy-done.1), custom_call_target="tpu_custom_call" | custom-call | flops 4000000000 | bytes 12000000 | tf_op jit(solution)/shard_map/left_out/pallas_call | solution.py:270
  14.6 0.9 collective-permute-done.arrived_ref
  15.5 2.7 %left_keep.1 = f32[2560,128]{1,0:T(8,128)} custom-call(s32[1]{0:T(128)} %bitcast.half_ref, bf16[256,3072]{1,0:T(8,128)(2,1)S(1)} %get-tuple-element.40.x_ref, bf16[3,256,384]{2,1,0:T(8,128)(2,1)S(1)} %get-tuple-element.41.grads_ref, bf16[3,3072,384]{2,1,0:T(8,128)(2,1)S(1)} %get-tuple-element.42.err_in_ref, f32[3,64,384]{2,1,0:T(8,128)S(1)} %copy-done, ...), custom_call_target="tpu_custom_call" | custom-call | flops 3000000000 | bytes 9000000 | tf_op jit(solution)/shard_map/left_keep/pallas_call | solution.py:251
  18.3 11.5 %all-to-all-start = ((f32[64,40,128]{2,1,0:T(8,128)}), f32[64,40,128]{2,1,0:T(8,128)S(1)}, u32[]{:S(2)}, u32[]{:S(2)}) async-start(f32[64,40,128]{2,1,0:T(8,128)} %bitcast.4), calls=%async_computation | async-start | bytes 2621440 | tf_op jit(solution)/shard_map/all_to_all | solution.py:729
  29.8 4.9 %turned.1.turned_hbm = bf16[3072,256]{1,0:T(8,128)(2,1)} custom-call(bf16[256,3072]{1,0:T(8,128)(2,1)} %x_hbm.1), custom_call_target="tpu_custom_call" | custom-call | flops 3000000000 | bytes 9000000 | tf_op jit(solution)/shard_map/turned/pallas_call | solution.py:284
  34.7 16.9 %all-to-all-done.received_ref = f32[64,40,128]{2,1,0:T(8,128)S(1)} async-done(((f32[64,40,128]{2,1,0:T(8,128)}), f32[64,40,128]{2,1,0:T(8,128)S(1)}, u32[]{:S(2)}, u32[]{:S(2)}) %all-to-all-start) | async-done | bytes 1310752 | tf_op jit(solution)/shard_map/all_to_all | solution.py:729
  51.5 1.2 answer_left.1
  52.8 4.7 %all-to-all-start.1 = ((f32[64,40,128]{2,1,0:T(8,128)}), f32[64,40,128]{2,1,0:T(8,128)S(1)}, u32[]{:S(2)}, u32[]{:S(2)}) async-start(f32[64,40,128]{2,1,0:T(8,128)} %answer_left.1), calls=%async_computation.1 | async-start | bytes 2621440 | tf_op jit(solution)/shard_map/all_to_all | solution.py:732
  57.5 20.5 %all-to-all-done.1 = f32[64,40,128]{2,1,0:T(8,128)S(1)} async-done(((f32[64,40,128]{2,1,0:T(8,128)}), f32[64,40,128]{2,1,0:T(8,128)S(1)}, u32[]{:S(2)}, u32[]{:S(2)}) %all-to-all-start.1) | async-done | bytes 1310752 | tf_op jit(solution)/shard_map/all_to_all | solution.py:732
  78.1 4.2 %right_out.1 = (f32[24,64,128]{2,1,0:T(8,128)S(1)}, f32[64,128]{1,0:T(8,128)S(1)}) custom-call(s32[2]{0:T(128)S(1)} %pad_add_fusion.place_ref, f32[192,128]{1,0:T(8,128)S(1)} %slice.42.left_out_ref, bf16[256,384]{1,0:T(8,128)(2,1)S(1)} %get-tuple-element.44.hid_ref, bf16[256,3072]{1,0:T(8,128)(2,1)} %gy_hbm.5, bf16[384,3072]{1,0:T(8,128)(2,1)} %bitcast.39), custom_call_target="tpu_custom_call" | custom-call | flops 3000000000 | bytes 9000000 | tf_op jit(solution)/shard_map/right_out/pallas_call | solution.py:368
  82.4 0.8 pad_maximum_fusion
  83.7 1.6 %collective-permute-done.2 = f32[832,128]{1,0:T(8,128)S(1)} collective-permute-done((f32[832,128]{1,0:T(8,128)}, f32[832,128]{1,0:T(8,128)S(1)}, u32[]{:S(2)}, u32[]{:S(2)}) %collective-permute-start.2) | collective-permute-done | bytes 426016 | tf_op jit(solution)/shard_map/ppermute | solution.py:739
  85.5 1.0 collective-permute-start.5
  86.4 1.8 %collective-permute-start.3 = (f32[256,128]{1,0:T(8,128)S(1)}, f32[256,128]{1,0:T(8,128)S(1)}, u32[]{:S(2)}, u32[]{:S(2)}) collective-permute-start(f32[256,128]{1,0:T(8,128)S(1)} %get-tuple-element.83), channel_id=1, source_target_pairs={{0,4},{2,6},{4,0},{6,2},{1,5},{3,7},{5,1},{7,3},{8,12},{10,14},{12... | collective-permute-start | bytes 393224 | tf_op jit(solution)/shard_map/ppermute | solution.py:743
  88.3 6.2 %right.1 = (f32[3,64,384]{2,1,0:T(8,128)S(1)}, f32[192,256]{1,0:T(8,128)S(1)}) custom-call(s32[1]{0:T(128)} %bitcast.half_ref, f32[2560,128]{1,0:T(8,128)S(1)} %bitcast.27, f32[2560,128]{1,0:T(8,128)} %collective-permute-done.1.other_ref, bf16[256,3072]{1,0:T(8,128)(2,1)} %x_hbm.1, bf16[3,3072,384]{2,1,0:T(8,128)(2,1)} %bitcast.36), custom_call_target="tpu_custom_call" | custom-call | flops 6000000000 | bytes 18000000 | tf_op jit(solution)/shard_map/right/pallas_call | solution.py:430
  94.6 1.6 %collective-permute-done.4.second_ref = f32[256,128]{1,0:T(8,128)S(1)} collective-permute-done((f32[256,128]{1,0:T(8,128)S(1)}, f32[256,128]{1,0:T(8,128)S(1)}, u32[]{:S(2)}, u32[]{:S(2)}) %collective-permute-start.4) | collective-permute-done | bytes 131104 | tf_op jit(solution)/shard_map/ppermute | solution.py:743
  96.2 1.0 join.1
  97.2 3.7 %all-to-all-start.2 = ((f32[16,48,128]{2,1,0:T(8,128)}), f32[16,48,128]{2,1,0:T(8,128)S(1)}, u32[]{:S(2)}, u32[]{:S(2)}) async-start(f32[16,48,128]{2,1,0:T(8,128)} %bitcast.14), calls=%async_computation.2 | async-start | bytes 786432 | tf_op jit(solution)/shard_map/all_to_all | solution.py:746
  101.0 9.0 %invert.1 = (f32[4,64,128]{2,1,0:T(8,128)S(1)}, f32[64,384]{1,0:T(8,128)S(1)}) custom-call(f32[2560,128]{1,0:T(8,128)S(1)} %bitcast.28, f32[2560,128]{1,0:T(8,128)} %collective-permute-done.1.other_ref, f32[192,128]{1,0:T(8,128)S(1)} %slice.42.left_out_ref, f32[64,128]{1,0:T(8,128)S(1)} %get-tuple-element.54.gram_out_ref), custom_call_target="tpu_custom_call" | custom-call | flops 10000000000 | bytes 30000000 | tf_op jit(solution)/shard_map/invert/pallas_call | solution.py:518
  109.9 1.1 all-to-all-done.2.received_ref
  111.1 0.8 answer_right.1
  111.9 6.0 %all-to-all-start.3 = ((f32[16,48,128]{2,1,0:T(8,128)}), f32[16,48,128]{2,1,0:T(8,128)S(1)}, u32[]{:S(2)}, u32[]{:S(2)}) async-start(f32[16,48,128]{2,1,0:T(8,128)} %answer_right.1), calls=%async_computation.3 | async-start | bytes 786432 | tf_op jit(solution)/shard_map/all_to_all | solution.py:751
  117.9 6.3 %turn.1.ortho_hbm = bf16[3,3072,128]{2,1,0:T(8,128)(2,1)} custom-call(s32[1]{0:T(128)} %bitcast.half_ref, f32[2560,128]{1,0:T(8,128)S(1)} %bitcast.29, f32[2560,128]{1,0:T(8,128)} %collective-permute-done.1.other_ref, f32[4,64,128]{2,1,0:T(8,128)S(1)} %get-tuple-element.60.inverse_ref), custom_call_target="tpu_custom_call" | custom-call | flops 6000000000 | bytes 18000000 | tf_op jit(solution)/shard_map/turn/pallas_call | solution.py:553
  124.1 3.4 %all-to-all-done.3 = f32[16,48,128]{2,1,0:T(8,128)S(1)} async-done(((f32[16,48,128]{2,1,0:T(8,128)}), f32[16,48,128]{2,1,0:T(8,128)S(1)}, u32[]{:S(2)}, u32[]{:S(2)}) %all-to-all-start.3) | async-done | bytes 393248 | tf_op jit(solution)/shard_map/all_to_all | solution.py:751
  127.5 1.2 collective-permute-start.8
  128.7 0.8 collective-permute-start.7
  129.5 1.3 collective-permute-start.6
  130.8 9.0 %rest_in.1 = (bf16[3,3072,384]{2,1,0:T(8,128)(2,1)}, f32[3,64,384]{2,1,0:T(8,128)}) custom-call(f32[768,128]{1,0:T(8,128)S(1)} %bitcast.31, f32[4,64,128]{2,1,0:T(8,128)S(1)} %get-tuple-element.60.inverse_ref, bf16[3,256,384]{2,1,0:T(8,128)(2,1)S(1)} %get-tuple-element.41.grads_ref, bf16[3072,256]{1,0:T(8,128)(2,1)} %turned.1.turned_hbm, ...), custom_call_target="tpu_custom_call" | custom-call | flops 10000000000 | bytes 30000000 | tf_op jit(solution)/shard_map/rest_in/pallas_call | solution.py:602
  140.1 4.4 %rest_out.2 = (bf16[384,3072]{1,0:T(8,128)(2,1)}, f32[64,3072]{1,0:T(8,128)}) custom-call(s32[2]{0:T(128)S(1)} %pad_add_fusion.place_ref, f32[768,128]{1,0:T(8,128)S(1)} %constant_dynamic-update-slice_fusion.right_ref, f32[4,64,128]{2,1,0:T(8,128)S(1)} %get-tuple-element.60.inverse_ref, f32[64,384]{1,0:T(8,128)S(1)} %get-tuple-element.70.ortho_out_ref, ...), custom_call_target="tpu_custom_call" | custom-call | flops 3000000000 | bytes 9000000 | tf_op jit(solution)/shard_map/rest_out/pallas_call | solution.py:681
  144.5 4.4 %rest_out.3 = (bf16[384,3072]{1,0:T(8,128)(2,1)}, f32[64,3072]{1,0:T(8,128)}) custom-call(s32[2]{0:T(128)S(1)} %pad_add_fusion.1.place_ref, f32[768,128]{1,0:T(8,128)S(1)} %collective-permute-done.9.right_ref, f32[4,64,128]{2,1,0:T(8,128)S(1)} %get-tuple-element.60.inverse_ref, ...), custom_call_target="tpu_custom_call", output_to_operand_aliasing={{0}: (7, {}), {1}: (8, {})} | custom-call | flops 3000000000 | bytes 9000000 | tf_op jit(solution)/shard_map/rest_out/pallas_call | solution.py:681
  (30 shorter events, 1.3 us)
Async XLA Ops:
  0.6 10.3 %copy-start = (f32[3,64,384]{2,1,0:T(8,128)S(1)}, f32[3,64,384]{2,1,0:T(8,128)}, u32[]{:S(2)}) copy-start(f32[3,64,384]{2,1,0:T(8,128)} %basis_in_ref.3) | copy-start | bytes 884740
  11.0 1.8 %copy-start.1 = (f32[64,3072]{1,0:T(8,128)S(1)}, f32[64,3072]{1,0:T(8,128)}, u32[]{:S(2)}) copy-start(f32[64,3072]{1,0:T(8,128)} %basis_out_ref.1) | copy-start | bytes 2359300
  12.6 2.9 %collective-permute-start = (f32[2304,128]{1,0:T(8,128)S(1)}, f32[2304,128]{1,0:T(8,128)S(1)}, u32[]{:S(2)}, u32[]{:S(2)}) collective-permute-start(f32[2304,128]{1,0:T(8,128)S(1)} %left_send.1), channel_id=1, source_target_pairs={{0,1},{1,0},{2,3},{3,2},{4,5},{5,4},{6,7},{7,6},{8,9},{9,8},{10,11... | collective-permute-start | bytes 3538952 | tf_op jit(solution)/shard_map/ppermute | solution.py:724
  18.3 33.3 %all-to-all-start = ((f32[64,40,128]{2,1,0:T(8,128)}), f32[64,40,128]{2,1,0:T(8,128)S(1)}, u32[]{:S(2)}, u32[]{:S(2)}) async-start(f32[64,40,128]{2,1,0:T(8,128)} %bitcast.4), calls=%async_computation | async-start | bytes 2621440 | tf_op jit(solution)/shard_map/all_to_all | solution.py:729
  52.8 25.2 %all-to-all-start.1 = ((f32[64,40,128]{2,1,0:T(8,128)}), f32[64,40,128]{2,1,0:T(8,128)S(1)}, u32[]{:S(2)}, u32[]{:S(2)}) async-start(f32[64,40,128]{2,1,0:T(8,128)} %answer_left.1), calls=%async_computation.1 | async-start | bytes 2621440 | tf_op jit(solution)/shard_map/all_to_all | solution.py:732
  78.0 10.3 %collective-permute-start.1 = (f32[2560,128]{1,0:T(8,128)S(1)}, f32[2560,128]{1,0:T(8,128)}, u32[]{:S(2)}, u32[]{:S(2)}) collective-permute-start(f32[2560,128]{1,0:T(8,128)S(1)} %bitcast.26), channel_id=1, source_target_pairs={{0,1},{1,0},{2,3},{3,2},{4,5},{5,4},{6,7},{7,6},{8,9},{9,8},{10,11... | collective-permute-start | bytes 3932168 | tf_op jit(solution)/shard_map/ppermute | solution.py:733
  83.2 2.1 %collective-permute-start.2 = (f32[832,128]{1,0:T(8,128)}, f32[832,128]{1,0:T(8,128)S(1)}, u32[]{:S(2)}, u32[]{:S(2)}) collective-permute-start(f32[832,128]{1,0:T(8,128)} %pad_maximum_fusion), channel_id=1, source_target_pairs={{0,1},{1,0},{2,3},{3,2},{4,5},{5,4},{6,7},{7,6},{8,9},{9,8},{10,11... | collective-permute-start | bytes 1277960 | tf_op jit(solution)/shard_map/ppermute | solution.py:739
  85.5 9.1 %collective-permute-start.5 = (f32[256,128]{1,0:T(8,128)S(1)}, f32[256,128]{1,0:T(8,128)S(1)}, u32[]{:S(2)}, u32[]{:S(2)}) collective-permute-start(f32[256,128]{1,0:T(8,128)S(1)} %get-tuple-element.82), channel_id=1, source_target_pairs={{0,6},{2,0},{4,2},{6,4},{1,7},{3,1},{5,3},{7,5},{8,14},{10,8},{12,... | collective-permute-start | bytes 393224 | tf_op jit(solution)/shard_map/ppermute | solution.py:743
  86.4 8.2 %collective-permute-start.3 = (f32[256,128]{1,0:T(8,128)S(1)}, f32[256,128]{1,0:T(8,128)S(1)}, u32[]{:S(2)}, u32[]{:S(2)}) collective-permute-start(f32[256,128]{1,0:T(8,128)S(1)} %get-tuple-element.83), channel_id=1, source_target_pairs={{0,4},{2,6},{4,0},{6,2},{1,5},{3,7},{5,1},{7,3},{8,12},{10,14},{12... | collective-permute-start | bytes 393224 | tf_op jit(solution)/shard_map/ppermute | solution.py:743
  88.2 8.0 %collective-permute-start.4 = (f32[256,128]{1,0:T(8,128)S(1)}, f32[256,128]{1,0:T(8,128)S(1)}, u32[]{:S(2)}, u32[]{:S(2)}) collective-permute-start(f32[256,128]{1,0:T(8,128)S(1)} %get-tuple-element.84), channel_id=1, source_target_pairs={{0,2},{2,4},{4,6},{6,0},{1,3},{3,5},{5,7},{7,1},{8,10},{10,12},{12... | collective-permute-start | bytes 393224 | tf_op jit(solution)/shard_map/ppermute | solution.py:743
  97.2 13.9 %all-to-all-start.2 = ((f32[16,48,128]{2,1,0:T(8,128)}), f32[16,48,128]{2,1,0:T(8,128)S(1)}, u32[]{:S(2)}, u32[]{:S(2)}) async-start(f32[16,48,128]{2,1,0:T(8,128)} %bitcast.14), calls=%async_computation.2 | async-start | bytes 786432 | tf_op jit(solution)/shard_map/all_to_all | solution.py:746
  111.9 15.6 %all-to-all-start.3 = ((f32[16,48,128]{2,1,0:T(8,128)}), f32[16,48,128]{2,1,0:T(8,128)S(1)}, u32[]{:S(2)}, u32[]{:S(2)}) async-start(f32[16,48,128]{2,1,0:T(8,128)} %answer_right.1), calls=%async_computation.3 | async-start | bytes 786432 | tf_op jit(solution)/shard_map/all_to_all | solution.py:751
  127.5 12.3 %collective-permute-start.8 = (f32[192,128]{1,0:T(8,128)S(1)}, f32[192,128]{1,0:T(8,128)S(1)}, u32[]{:S(2)}, u32[]{:S(2)}) collective-permute-start(f32[192,128]{1,0:T(8,128)S(1)} %slice.41), channel_id=1, source_target_pairs={{0,6},{2,0},{4,2},{6,4},{1,7},{3,1},{5,3},{7,5},{8,14},{10,8},{12,... | collective-permute-start | bytes 294920 | tf_op jit(solution)/shard_map/ppermute | solution.py:756
  128.7 11.1 %collective-permute-start.7 = (f32[192,128]{1,0:T(8,128)S(1)}, f32[192,128]{1,0:T(8,128)S(1)}, u32[]{:S(2)}, u32[]{:S(2)}) collective-permute-start(f32[192,128]{1,0:T(8,128)S(1)} %slice.41), channel_id=1, source_target_pairs={{0,4},{2,6},{4,0},{6,2},{1,5},{3,7},{5,1},{7,3},{8,12},{10,14},{12... | collective-permute-start | bytes 294920 | tf_op jit(solution)/shard_map/ppermute | solution.py:756
  129.5 10.3 %collective-permute-start.6 = (f32[192,128]{1,0:T(8,128)S(1)}, f32[192,128]{1,0:T(8,128)S(1)}, u32[]{:S(2)}, u32[]{:S(2)}) collective-permute-start(f32[192,128]{1,0:T(8,128)S(1)} %slice.41), channel_id=1, source_target_pairs={{0,2},{2,4},{4,6},{6,0},{1,3},{3,5},{5,7},{7,1},{8,10},{10,12},{12... | collective-permute-start | bytes 294920 | tf_op jit(solution)/shard_map/ppermute | solution.py:756
  139.9 4.6 %collective-permute-start.9 = (f32[768,128]{1,0:T(8,128)S(1)}, f32[768,128]{1,0:T(8,128)S(1)}, u32[]{:S(2)}, u32[]{:S(2)}) collective-permute-start(f32[768,128]{1,0:T(8,128)S(1)} %constant_dynamic-update-slice_fusion.right_ref), channel_id=1, source_target_pairs={{0,1},{1,0},{2,3},{3,2},{4,5},{5,4},{6,7},{7,6},{8,9},{9,8},{10,11... | collective-permute-start | bytes 1179656 | tf_op jit(solution)/shard_map/ppermute | solution.py:760

commit v4 on v3

--- a/solution.py
+++ b/solution.py
@@ -87,53 +87,30 @@
     return a[:half] + a[half:]
 
 
-def recurrence_kernel(gy_ref, w_ref, q_ref, f_ref, v_ref, *refs):
-    sources, (hid_ref, grad_ref), kept, sem = refs[:4], refs[4:6], refs[6:10], refs[10]
-    copies = [pltpu.make_async_copy(a, b, sem.at[i]) for i, (a, b) in enumerate(zip(sources, kept))]
-
-    @pl.when(pl.program_id(0) == 0)
-    def _():
-        for copy in copies:
-            copy.start()
-
-    grad_o = nt(gy_ref[...], w_ref[...]).astype(bf16)
-    q = q_ref[...].astype(f32)
-    f = f_ref[...].astype(f32)
-    v = v_ref[...]
+def head_forward(q, f):
     q_gate = 1.0 / (1.0 + jnp.exp(-q))
     query = q * q_gate
     small = jnp.exp(-jnp.abs(f))
     key = jnp.where(f >= 0, small, 1.0) / (1.0 + small)
     decay = jnp.where(f >= 0, 1.0, small) / (1.0 + small)
     log_decay = jnp.minimum(f, 0.0) - jnp.log1p(small)
-
     row = lax.broadcasted_iota(jnp.int32, (TOK, TOK), 0)
     col = lax.broadcasted_iota(jnp.int32, (TOK, TOK), 1)
-    lower = jnp.where(row >= col, 1.0, 0.0).astype(bf16)
-    upper = jnp.where(row <= col, 1.0, 0.0).astype(bf16)
+    running = summed3(jnp.where(row >= col, 1.0, 0.0).astype(bf16), log_decay)
     differ = row ^ col
-    running = summed3(lower, log_decay)
-
     scores = jnp.zeros((TOK, TOK), f32)
-    grad_s = split2(nt(grad_o, v))
-    grad_st = split2(nt(v, grad_o))
-    grad_query = jnp.zeros((TOK, DK), f32)
-    grad_key = jnp.zeros((TOK, DK), f32)
+    levels = []
     for size in (128, 64, 32, 16, 8):
         blocks = running.reshape(TOK // (2 * size), 2 * size, DK)
         spread = (blocks - blocks[:, size - 1 : size, :]).reshape(TOK, DK)
         if size > 8:
             q_scale = jnp.exp(jnp.minimum(spread, 0.0))
             k_scale = jnp.exp(jnp.minimum(-spread, 0.0))
-            within = (differ >= size) & (differ < 2 * size)
-            mask = within & (row > col)
-            mask_t = within & (row < col)
+            mask = (differ >= size) & (differ < 2 * size) & (row > col)
         else:
             q_scale = jnp.exp(spread)
             k_scale = jnp.exp(-spread)
-            within = differ < 2 * size
-            mask = within & (row >= col)
-            mask_t = within & (row <= col)
+            mask = (differ < 2 * size) & (row >= col)
         q_high, q_low = split2(query * q_scale)
         k_high, k_low = split2(key * k_scale)
         level = nt(
@@ -141,24 +118,65 @@
             jnp.concatenate([k_high, k_low, k_high], axis=1),
         )
         scores = jnp.where(mask, level, scores)
+        levels.append((q_scale, k_scale, q_high, q_low, k_high, k_low))
+    return (query, key, decay, q_gate), levels, split2(scores)
+
+
+def head_backward(gates, levels, scores, v, grad_o):
+    query, key, decay, q_gate = gates
+    row = lax.broadcasted_iota(jnp.int32, (TOK, TOK), 0)
+    col = lax.broadcasted_iota(jnp.int32, (TOK, TOK), 1)
+    differ = row ^ col
+    grad_s = split2(nt(grad_o, v))
+    grad_st = split2(nt(v, grad_o))
+    grad_query = jnp.zeros((TOK, DK), f32)
+    grad_key = jnp.zeros((TOK, DK), f32)
+    for size, (q_scale, k_scale, q_high, q_low, k_high, k_low) in zip((128, 64, 32, 16, 8), levels):
+        if size > 8:
+            within = (differ >= size) & (differ < 2 * size)
+            mask, mask_t = within & (row > col), within & (row < col)
+        else:
+            within = differ < 2 * size
+            mask, mask_t = within & (row >= col), within & (row <= col)
         keep = jnp.where(mask, 1.0, 0.0).astype(bf16)
         keep_t = jnp.where(mask_t, 1.0, 0.0).astype(bf16)
         both = nn(grad_s[0] * keep, jnp.concatenate([k_high, k_low], axis=1))
         grad_query += q_scale * (both[:, :DK] + both[:, DK:] + nn(grad_s[1] * keep, k_high))
         both = nn(grad_st[0] * keep_t, jnp.concatenate([q_high, q_low], axis=1))
         grad_key += k_scale * (both[:, :DK] + both[:, DK:] + nn(grad_st[1] * keep_t, q_high))
-    s_high, s_low = split2(scores)
-    hid_ref[...] = (nn(s_high, v) + nn(s_low, v)).astype(bf16)
-    grad_v = tn(s_high, grad_o) + tn(s_low, grad_o)
+    grad_v = tn(scores[0], grad_o) + tn(scores[1], grad_o)
+    upper = jnp.where(row <= col, 1.0, 0.0).astype(bf16)
     grad_decay = summed3(upper, query * grad_query - key * grad_key)
-    grad_ref[0] = (grad_query * (q_gate + query * (1.0 - q_gate))).astype(bf16)
-    grad_ref[1] = (key * (grad_decay - grad_key * decay)).astype(bf16)
-    grad_ref[2] = grad_v.astype(bf16)
-
-    @pl.when(pl.program_id(0) == HEADS - 1)
-    def _():
-        for copy in copies:
-            copy.wait()
+    grad_q = grad_query * (q_gate + query * (1.0 - q_gate))
+    return grad_q, key * (grad_decay - grad_key * decay), grad_v
+
+
+def recurrence_kernel(q_hbm, f_hbm, v_hbm, gy_hbm, w_hbm, *refs):
+    sources, (hid_ref, grad_ref), kept, (q_scr, f_scr, v_scr, gy_scr, w_scr, sem) = (
+        refs[:4],
+        refs[4:6],
+        refs[6:10],
+        refs[10:],
+    )
+    pairs = list(zip((q_hbm, f_hbm, v_hbm, gy_hbm, w_hbm), (q_scr, f_scr, v_scr, gy_scr, w_scr)))
+    copies = [pltpu.make_async_copy(a, b, sem.at[i]) for i, (a, b) in enumerate(pairs + list(zip(sources, kept)))]
+    for copy in copies:
+        copy.start()
+    for copy in copies[:3]:
+        copy.wait()
+    for h in range(HEADS):
+        mine = slice(DK * h, DK * (h + 1))
+        gates, levels, scores = head_forward(q_scr[:, mine].astype(f32), f_scr[:, mine].astype(f32))
+        v = v_scr[:, mine]
+        hid_ref[:, mine] = (nn(scores[0], v) + nn(scores[1], v)).astype(bf16)
+        if h == 0:
+            for copy in copies[3:5]:
+                copy.wait()
+            grad_o = nt(gy_scr[...], w_scr[...]).astype(bf16)
+        for p, grad in enumerate(head_backward(gates, levels, scores, v, grad_o[:, mine])):
+            grad_ref[p, :, mine] = grad.astype(bf16)
+    for copy in copies[5:]:
+        copy.wait()
 
 
 def held(*arrays):
@@ -192,27 +210,19 @@
 
 
 def recurrence(grad_y, w_out, q_pre, f_pre, v_pre, keep):
-    per_head = pl.BlockSpec((TOK, DK), lambda h: (0, h))
-    anywhere = pl.BlockSpec(memory_space=pl.ANY)
-    operands = (grad_y, w_out, q_pre, f_pre, v_pre) + keep
+    operands = (q_pre, f_pre, v_pre, grad_y, w_out) + keep
+    whole = pl.BlockSpec(memory_space=pltpu.VMEM)
     return pl.pallas_call(
         recurrence_kernel,
-        grid=(HEADS,),
-        in_specs=[
-            pl.BlockSpec((TOK, D), lambda h: (0, 0)),
-            pl.BlockSpec((DK, D), lambda h: (h, 0)),
-            per_head,
-            per_head,
-            per_head,
-        ]
-        + [anywhere] * len(keep),
-        out_specs=[per_head, pl.BlockSpec((3, TOK, DK), lambda h: (0, 0, h))] + [anywhere] * len(keep),
+        in_specs=[ANY] * len(operands),
+        out_specs=[whole] * 2 + [ANY] * len(keep),
         out_shape=[
             jax.ShapeDtypeStruct((TOK, COLS), bf16),
             jax.ShapeDtypeStruct((3, TOK, COLS), bf16),
         ]
         + [pltpu.VMEM(a.shape, a.dtype) for a in keep],
-        scratch_shapes=[pltpu.SemaphoreType.DMA((len(keep),))],
+        scratch_shapes=[pltpu.VMEM(a.shape, a.dtype) for a in operands[:5]]
+        + [pltpu.SemaphoreType.DMA((len(operands),))],
         cost_estimate=cost(8),
         compiler_params=pltpu.CompilerParams(vmem_limit_bytes=VMEM),
         name="recurrence",
@@ -342,54 +352,48 @@
     )(received)
 
 
-def right_out_kernel(place_ref, left_out_ref, hid_ref, gy_hbm, err_out_hbm, right_out_ref, gram_ref, out_scr,
-                     gy_scr, err_out_scr, sem):
-    step = pl.program_id(0)
-
+def right_out_kernel(place_ref, left_out_ref, hid_ref, gy_hbm, err_out_hbm, send_ref, keep_ref, gy_scr, err_out_scr, sem):
     def column(j):
-        return lax.rem(place_ref[0] + 1 + j // 4, 2) * 4 + lax.rem(place_ref[1] + lax.rem(j, 4), 4)
-
-    gy_ref, err_out_ref = fetched(step, 8, column, COLS, [(1, gy_hbm), (1, err_out_hbm)], [gy_scr, err_out_scr], sem)
-
-    @pl.when(step == 0)
-    def _():
-        left_out = wide(left_out_ref[...], RANK)
-        gram_ref[...] = jnp.concatenate([exact_nt(left_out, left_out), jnp.zeros((RANK, RANK), f32)], axis=1)
-        factor = stacked(left_out)
-        out_scr[:, :COLS] = factor
-        out_scr[:, COLS:] = stacked(folded(nt(factor, hid_ref[...])))
-
-    part = folded(nn(out_scr[:, :COLS], err_out_ref[...]) + nn(out_scr[:, COLS:], gy_ref[...]))
-    for i, tile in enumerate(tiles_of(part)):
-        right_out_ref[i] = tile
+        at = lax.rem(place_ref[0] + 1 + j // 4, 2) * 4 + lax.rem(place_ref[1] + j % 4, 4)
+        return pl.ds(pl.multiple_of(at * COLS, COLS), COLS)
+
+    copies = [
+        (
+            pltpu.make_async_copy(gy_hbm.at[:, column(j)], gy_scr.at[j], sem.at[0, j]),
+            pltpu.make_async_copy(err_out_hbm.at[:, column(j)], err_out_scr.at[j], sem.at[1, j]),
+        )
+        for j in range(8)
+    ]
+    for pair in copies:
+        for copy in pair:
+            copy.start()
+    left_out = wide(left_out_ref[...], RANK)
+    factor = stacked(left_out)
+    both = jnp.concatenate([factor, stacked(folded(nt(factor, hid_ref[...])))], axis=1)
+    send_ref[RO_ROWS:, :] = jnp.concatenate([exact_nt(left_out, left_out), jnp.zeros((RANK, RANK), f32)], axis=1)
+    for j in range(8):
+        for copy in copies[j]:
+            copy.wait()
+        part = folded(nn(both, jnp.concatenate([err_out_scr[j], gy_scr[j]], axis=0)))
+        ref = send_ref if j < 4 else keep_ref
+        for i, tile in enumerate(tiles_of(part)):
+            at = (j % 4) * PIECE + i * RANK
+            ref[at : at + RANK, :] = tile
 
 
 def right_out(place, left_out_sum, grad_y, hidden, err_out):
+    whole = pl.BlockSpec(memory_space=pltpu.VMEM)
     return pl.pallas_call(
         right_out_kernel,
-        grid_spec=pltpu.PrefetchScalarGridSpec(
-            num_scalar_prefetch=1,
-            grid=(8,),
-            in_specs=[
-                pl.BlockSpec((LO_ROWS, 128), lambda j, h: (0, 0)),
-                pl.BlockSpec((TOK, COLS), lambda j, h: (0, 0)),
-                ANY,
-                ANY,
-            ],
-            out_specs=[
-                pl.BlockSpec((3, RANK, 128), lambda j, h: (j, 0, 0)),
-                pl.BlockSpec((RANK, 128), lambda j, h: (0, 0)),
-            ],
-            scratch_shapes=[
-                pltpu.VMEM((2 * RANK, COLS + TOK), bf16),
-                pltpu.VMEM((8, TOK, COLS), bf16),
-                pltpu.VMEM((8, COLS, COLS), bf16),
-                pltpu.SemaphoreType.DMA((2, 8)),
-            ],
-        ),
+        in_specs=[pl.BlockSpec(memory_space=pltpu.SMEM), whole, whole, ANY, ANY],
         out_shape=[
-            jax.ShapeDtypeStruct((24, RANK, 128), f32),
-            jax.ShapeDtypeStruct((RANK, 128), f32),
+            jax.ShapeDtypeStruct((RO_ROWS + RANK, 128), f32),
+            jax.ShapeDtypeStruct((RO_ROWS, 128), f32),
+        ],
+        scratch_shapes=[
+            pltpu.VMEM((8, TOK, COLS), bf16),
+            pltpu.VMEM((8, COLS, COLS), bf16),
+            pltpu.SemaphoreType.DMA((2, 8)),
         ],
         cost_estimate=cost(3),
         compiler_params=pltpu.CompilerParams(vmem_limit_bytes=VMEM),
@@ -397,73 +401,99 @@
     )(place, left_out_sum, hidden, *streamed(grad_y, err_out))
 
 
-def right_kernel(half_ref, own_ref, other_ref, x_hbm, err_in_hbm, right_ref, token_ref, x_scr, err_in_scr, sem):
-    step = pl.program_id(0)
-
-    def column(j):
-        return lax.rem(j // STEPS + half_ref[0], 2) * STEPS + lax.rem(j, STEPS)
-
-    x_ref, err_in_ref = fetched(step, 2 * STEPS, column, TILE, [(1, x_hbm), (1, err_in_hbm)], [x_scr, err_in_scr], sem)
-
-    @pl.when(step == 0)
-    def _():
-        right_ref[...] = jnp.zeros_like(right_ref)
-        token_ref[...] = jnp.zeros_like(token_ref)
-
-    def add(ref):
-        high, low = split2(wide(ref[...], 3 * RANK))
-        token_ref[...] += folded(nt(jnp.concatenate([high, low], axis=0), x_ref[...]))
-        for p in range(3):
-            mine = slice(RANK * p, RANK * (p + 1))
-            right_ref[p] += folded(nn(jnp.concatenate([high[mine], low[mine]], axis=0), err_in_ref[p]))
-
-    @pl.when(step < STEPS)
-    def _():
-        add(own_ref)
-
-    @pl.when(step >= STEPS)
-    def _():
-        add(other_ref)
-
-
-def right(half, own, other, inputs, err_in):
-    return pl.pallas_call(
-        right_kernel,
-        grid_spec=pltpu.PrefetchScalarGridSpec(
-            num_scalar_prefetch=1,
-            grid=(2 * STEPS,),
-            in_specs=[
-                pl.BlockSpec((L_STEP, 128), lambda j, h: (jnp.minimum(j, STEPS - 1), 0)),
-                pl.BlockSpec((L_STEP, 128), lambda j, h: (jnp.maximum(j - STEPS, 0), 0)),
-                ANY,
-                ANY,
-            ],
-            out_specs=[
-                pl.BlockSpec((3, RANK, COLS), lambda j, h: (0, 0, 0)),
-                pl.BlockSpec((3 * RANK, TOK), lambda j, h: (0, 0)),
-            ],
-            scratch_shapes=[
-                pltpu.VMEM((2 * STEPS, TOK, TILE), bf16),
-                pltpu.VMEM((2 * STEPS, 3, TILE, COLS), bf16),
-                pltpu.SemaphoreType.DMA((2, 2 * STEPS)),
-            ],
-        ),
+def right_tile(rows, x, err_in, rights):
+    high, low = split2(rows)
+    for p in range(3):
+        mine = slice(RANK * p, RANK * (p + 1))
+        rights[p] += folded(nn(jnp.concatenate([high[mine], low[mine]], axis=0), err_in[p]))
+    return folded(nt(jnp.concatenate([high, low], axis=0), x))
+
+
+def right_own_kernel(halves_ref, own_ref, x_hbm, err_in_hbm, right_ref, token_ref, x_out, err_in_out, x_scr, err_in_scr, sem):
+    def near(j):
+        at = pl.ds(pl.multiple_of(halves_ref[0] * HALF + j * TILE, TILE), TILE)
+        return (
+            pltpu.make_async_copy(x_hbm.at[:, at], x_scr.at[j], sem.at[0, j]),
+            pltpu.make_async_copy(err_in_hbm.at[:, at], err_in_scr.at[j], sem.at[1, j]),
+        )
+
+    def far(j):
+        at = pl.ds(pl.multiple_of(halves_ref[1] * HALF + j * TILE, TILE), TILE)
+        to = slice(j * TILE, (j + 1) * TILE)
+        return (
+            pltpu.make_async_copy(x_hbm.at[:, at], x_out.at[:, to], sem.at[2, j]),
+            pltpu.make_async_copy(err_in_hbm.at[:, at], err_in_out.at[:, to], sem.at[3, j]),
+        )
+
+    copies = [near(j) for j in range(STEPS)] + [far(j) for j in range(STEPS)]
+    for pair in copies:
+        for copy in pair:
+            copy.start()
+    rights = [jnp.zeros((RANK, COLS), f32)] * 3
+    tokens = jnp.zeros((3 * RANK, TOK), f32)
+    for j in range(STEPS):
+        for copy in copies[j]:
+            copy.wait()
+        rows = wide(own_ref[L_STEP * j : L_STEP * (j + 1), :], 3 * RANK)
+        tokens += right_tile(rows, x_scr[j], err_in_scr.at[j], rights)
+    token_ref[...] = tokens
+    for p in range(3):
+        right_ref[p] = rights[p]
+    for pair in copies[STEPS:]:
+        for copy in pair:
+            copy.wait()
+
+
+def right_own(halves, own, inputs, err_in):
+    whole = pl.BlockSpec(memory_space=pltpu.VMEM)
+    return pl.pallas_call(
+        right_own_kernel,
+        in_specs=[pl.BlockSpec(memory_space=pltpu.SMEM), whole, ANY, ANY],
+        out_specs=[whole, whole, ANY, ANY],
         out_shape=[
             jax.ShapeDtypeStruct((3, RANK, COLS), f32),
             jax.ShapeDtypeStruct((3 * RANK, TOK), f32),
-        ],
-        cost_estimate=cost(6),
-        compiler_params=pltpu.CompilerParams(vmem_limit_bytes=VMEM),
-        name="right",
-    )(half, own, other, *streamed(inputs, err_in))
-
-
-def join_kernel(right_ref, token_ref, grads_ref, own_ref, first_ref, second_ref, third_ref, rows_ref, gram_ref):
+            pltpu.VMEM((TOK, HALF), bf16),
+            pltpu.VMEM((3, HALF, COLS), bf16),
+        ],
+        scratch_shapes=[
+            pltpu.VMEM((STEPS, TOK, TILE), bf16),
+            pltpu.VMEM((STEPS, 3, TILE, COLS), bf16),
+            pltpu.SemaphoreType.DMA((4, STEPS)),
+        ],
+        cost_estimate=cost(4),
+        compiler_params=pltpu.CompilerParams(vmem_limit_bytes=VMEM),
+        name="right_own",
+    )(halves, own, *streamed(inputs, err_in))
+
+
+def right_other_kernel(other_ref, right_ref, token_ref, x_ref, err_in_ref, grads_ref, rows_ref):
+    rights = [right_ref[p] for p in range(3)]
+    tokens = token_ref[...]
+    for j in range(STEPS):
+        mine = slice(j * TILE, (j + 1) * TILE)
+        rows = wide(other_ref[L_STEP * j : L_STEP * (j + 1), :], 3 * RANK)
+        tokens += right_tile(rows, x_ref[:, mine], err_in_ref.at[:, mine], rights)
     for p in range(3):
-        total = right_ref[p] + folded(nn(stacked(token_ref[RANK * p : RANK * (p + 1), :]), grads_ref[p]))
+        total = rights[p] + folded(nn(stacked(tokens[RANK * p : RANK * (p + 1)]), grads_ref[p]))
         for i, tile in enumerate(tiles_of(total)):
-            rows_ref[pl.ds((HEADS * p + i) * RANK, RANK), :] = tile
+            at = (HEADS * p + i) * RANK
+            rows_ref[at : at + RANK, :] = tile
+
+
+def right_other(other, right_part, token_part, inputs, err_in, grads):
+    return pl.pallas_call(
+        right_other_kernel,
+        out_shape=jax.ShapeDtypeStruct((RI_ROWS, 128), f32),
+        cost_estimate=cost(4),
+        compiler_params=pltpu.CompilerParams(vmem_limit_bytes=VMEM),
+        name="right_other",
+    )(other, right_part, token_part, *held(inputs, err_in), grads)
+
+
+def join_kernel(right_ref, own_ref, first_ref, second_ref, third_ref, rows_ref, gram_ref):
     piece = (own_ref[...] + first_ref[...]) + (second_ref[...] + third_ref[...])
+    rows_ref[:RI_ROWS, :] = right_ref[...]
     rows_ref[RI_ROWS:, :] = piece[:PIECE]
     gram_ref[...] = piece[PIECE:]
 
@@ -484,27 +514,32 @@
         1.0,
         0.0,
     )
+    gram = jnp.zeros((3 * RANK, 3 * RANK), f32)
+    for ref in (own_ref, other_ref):
+        for i in range(STEPS):
+            rows = wide(ref[L_STEP * i : L_STEP * (i + 1), :], 3 * RANK)
+            gram += exact_nt(rows, rows)
     for p in range(3):
-        gram = jnp.zeros((RANK, RANK), f32)
-        for ref in (own_ref, other_ref):
-            for i in range(STEPS):
-                rows = jnp.concatenate(
-                    [ref[pl.ds((CT * i + t) * 3 * RANK + RANK * p, RANK), :] for t in range(CT)], axis=1
-                )
-                gram += exact_nt(rows, rows)
-        inverse_ref[p] = jnp.concatenate([gram, eye], axis=1)
+        mine = slice(RANK * p, RANK * (p + 1))
+        inverse_ref[p] = jnp.concatenate([gram[mine, mine], eye], axis=1)
     inverse_ref[3] = jnp.concatenate([gram_out_ref[:, :RANK], eye], axis=1)
     rows8 = lax.broadcasted_iota(jnp.int32, (1, 8, 1), 1)
     tiles = [inverse_ref[:, 8 * t : 8 * t + 8, :] for t in range(RANK // 8)]
-    for j in range(RANK):
+    for j in range(0, RANK, 2):
         top, at = divmod(j, 8)
-        pivot_row = tiles[top][:, at : at + 1, :]
-        scaled = pivot_row * (1.0 / pivot_row[:, :, j : j + 1])
+        first = tiles[top][:, at : at + 1, :]
+        second = tiles[top][:, at + 1 : at + 2, :]
+        first_scaled = first * (1.0 / first[:, :, j : j + 1])
+        ratio = first_scaled[:, :, j + 1 : j + 2]
+        second = second - second[:, :, j : j + 1] * first_scaled
+        second_scaled = second * (1.0 / second[:, :, j + 1 : j + 2])
         for t in range(top, RANK // 8):
             column = tiles[t][:, :, j : j + 1]
+            other = tiles[t][:, :, j + 1 : j + 2] - column * ratio
             if t == top:
                 column = jnp.where(rows8 > at, column, 0.0)
-            tiles[t] = tiles[t] - column * scaled
+                other = jnp.where(rows8 > at + 1, other, 0.0)
+            tiles[t] = tiles[t] - column * first_scaled - other * second_scaled
     work = jnp.concatenate(tiles, axis=1)
     lane = lax.broadcasted_iota(jnp.int32, (4, RANK, 128), 2)
     sub = lax.broadcasted_iota(jnp.int32, (4, RANK, 128), 1)
@@ -631,11 +666,10 @@
     )(summed, inverse, grads, *streamed(turned, ortho_in, err_in))
 
 
-def rest_out_kernel(place_ref, right_ref, inverse_ref, ortho_out_ref, hid_ref, gy_hbm, err_out_hbm, *refs):
-    rest_hbm, factor_hbm, gy_scr, err_out_scr, rest_scr, factor_scr, in_sem, out_sem = refs[-8:]
-
+def rest_out_kernel(place_ref, own_ref, other_ref, inverse_ref, ortho_out_ref, hid_ref, gy_hbm, err_out_hbm,
+                    rest_hbm, factor_hbm, gy_scr, err_out_scr, rest_scr, factor_scr, in_sem, out_sem):
     def column(j):
-        at = place_ref[0] * 4 + lax.rem(place_ref[1] + 4 - j, 4)
+        at = lax.rem(place_ref[0] + j // 4, 2) * 4 + lax.rem(place_ref[1] + 4 - j % 4, 4)
         return pl.ds(pl.multiple_of(at * COLS, COLS), COLS)
 
     into = [
@@ -643,14 +677,14 @@
             pltpu.make_async_copy(gy_hbm.at[:, column(j)], gy_scr.at[j], in_sem.at[0, j]),
             pltpu.make_async_copy(err_out_hbm.at[:, column(j)], err_out_scr.at[j], in_sem.at[1, j]),
         )
-        for j in range(4)
+        for j in range(8)
     ]
     out = [
         (
             pltpu.make_async_copy(rest_scr.at[j], rest_hbm.at[:, column(j)], out_sem.at[0, j]),
             pltpu.make_async_copy(factor_scr.at[j], factor_hbm.at[:, column(j)], out_sem.at[1, j]),
         )
-        for j in range(4)
+        for j in range(8)
     ]
     for pair in into:
         for copy in pair:
@@ -658,44 +692,47 @@
     high, low = split2(ortho_out_ref[...])
     stack = jnp.concatenate([high, high, low, jnp.zeros_like(low)], axis=0)
     both = jnp.concatenate([hid_ref[...], stack], axis=0).astype(f32).T.astype(bf16)
-    right = jnp.concatenate([wide(right_ref[PIECE * j : PIECE * (j + 1), :], RANK) for j in range(4)], axis=1)
-    factor = exact_nn(inverse_ref[3, :, RANK:], right * (1.0 / N_DP))
-    high, low = split2(-factor)
-    weights = jnp.concatenate([high, low, high, jnp.zeros_like(low)], axis=0)
-    for j in range(4):
-        mine = slice(COLS * j, COLS * (j + 1))
-        factor_scr[j] = factor[:, mine]
-        for copy in into[j]:
-            copy.wait()
-        total = nn(both, jnp.concatenate([gy_scr[j], weights[:, mine]], axis=0)) + err_out_scr[j].astype(f32)
-        rest_scr[j] = total.astype(bf16)
-        for copy in out[j]:
-            copy.start()
+    inverse = inverse_ref[3, :, RANK:]
+    for j in range(0, 8, 2):
+        ref = own_ref if j < 4 else other_ref
+        right = jnp.concatenate([wide(ref[PIECE * (k % 4) : PIECE * (k % 4 + 1), :], RANK) for k in (j, j + 1)], axis=1)
+        factor = exact_nn(inverse, right * (1.0 / N_DP))
+        high, low = split2(-factor)
+        for k in (j, j + 1):
+            for copy in into[k]:
+                copy.wait()
+        gy = jnp.concatenate([gy_scr[j], gy_scr[j + 1]], axis=1)
+        total = nn(both, jnp.concatenate([gy, high, low, high, jnp.zeros_like(low)], axis=0))
+        for i, k in enumerate((j, j + 1)):
+            mine = slice(COLS * i, COLS * (i + 1))
+            factor_scr[k] = factor[:, mine]
+            rest_scr[k] = (total[:, mine] + err_out_scr[k].astype(f32)).astype(bf16)
+            for copy in out[k]:
+                copy.start()
     for pair in out:
         for copy in pair:
             copy.wait()
 
 
-def rest_out(place, right_half, inverse, ortho_out, hidden, grad_y, err_out, before=()):
+def rest_out(place, own, other, inverse, ortho_out, hidden, grad_y, err_out):
     whole = pl.BlockSpec(memory_space=pltpu.VMEM)
     return pl.pallas_call(
         rest_out_kernel,
-        in_specs=[pl.BlockSpec(memory_space=pltpu.SMEM)] + [whole] * 4 + [ANY] * (2 + len(before)),
+        in_specs=[pl.BlockSpec(memory_space=pltpu.SMEM)] + [whole] * 5 + [ANY] * 2,
         out_specs=[ANY, ANY],
         scratch_shapes=[
-            pltpu.VMEM((4, TOK, COLS), bf16),
-            pltpu.VMEM((4, COLS, COLS), bf16),
-            pltpu.VMEM((4, COLS, COLS), bf16),
-            pltpu.VMEM((4, RANK, COLS), f32),
-            pltpu.SemaphoreType.DMA((2, 4)),
-            pltpu.SemaphoreType.DMA((2, 4)),
+            pltpu.VMEM((8, TOK, COLS), bf16),
+            pltpu.VMEM((8, COLS, COLS), bf16),
+            pltpu.VMEM((8, COLS, COLS), bf16),
+            pltpu.VMEM((8, RANK, COLS), f32),
+            pltpu.SemaphoreType.DMA((2, 8)),
+            pltpu.SemaphoreType.DMA((2, 8)),
         ],
         out_shape=[pltpu.HBM((COLS, D), bf16), pltpu.HBM((RANK, D), f32)],
-        input_output_aliases={7: 0, 8: 1} if before else {},
-        cost_estimate=cost(3),
+        cost_estimate=cost(6),
         compiler_params=pltpu.CompilerParams(vmem_limit_bytes=VMEM),
         name="rest_out",
-    )(place, right_half, inverse, ortho_out, hidden, *streamed(grad_y, err_out), *before)
+    )(place, own, other, inverse, ortho_out, hidden, *streamed(grad_y, err_out))
 
 
 CHIP = ("x", "y", "z")
@@ -715,7 +752,6 @@
     mine = core[None]
     theirs = 1 - mine
     place = jnp.stack([core, z])
-    their_place = jnp.stack([1 - core, z])
     hidden, grads, near_err_in, near_err_out, near_inputs, near_grad_y = recurrence(
         grad_y, w_out, q_pre, f_pre, v_pre, keep
     )
@@ -733,15 +769,15 @@
     other = lax.ppermute(own, "c", SWAP)
     left_out_sum = own[L_ROWS : L_ROWS + LO_ROWS]
 
-    partial_out, gram_out = right_out(place, left_out_sum, grad_y, hidden, err_out)
-    quarters = partial_out.reshape(2, 4, PIECE, 128)
-    send = jnp.concatenate([quarters[0].reshape(RO_ROWS, 128), gram_out])
+    send, keep_out = right_out(place, left_out_sum, grad_y, hidden, err_out)
     arrived = lax.ppermute(send, "c", SWAP)
-    gram_out = gram_out + arrived[RO_ROWS:]
-    quarters = quarters[1] + arrived[:RO_ROWS].reshape(4, PIECE, 128)
+    right_part = right_own(jnp.concatenate([mine, theirs]), own, inputs, err_in)
+    arrived, right_part = lax.optimization_barrier((arrived, right_part))
+    gram_out = send[RO_ROWS:] + arrived[RO_ROWS:]
+    quarters = (keep_out + arrived[:RO_ROWS]).reshape(4, PIECE, 128)
     pieces = [jnp.concatenate([quarters[shift], gram_out]) for shift in range(4)]
     pieces = [pieces[0]] + [lax.ppermute(pieces[shift], "z", ring(shift)) for shift in OTHERS]
-    rows, gram_out = join(*right(mine, own, other, inputs, err_in), grads, *pieces)
+    rows, gram_out = join(right_other(other, *right_part, grads), *pieces)
 
     received = lax.all_to_all(rows.reshape(N_DP, EACH2, 128), ("x", "y"), 0, 0)
     inverse, ortho_out = invert(own, other, left_out_sum, gram_out)
@@ -758,10 +794,7 @@
     pieces, factor_in = lax.optimization_barrier((pieces, factor_in))
     own_right = jnp.concatenate(pieces)
     other_right = lax.ppermute(own_right, "c", SWAP)
-    halfway = rest_out(place, own_right, inverse, ortho_out, hidden, grad_y, err_out)
-    new_out, factor_out = rest_out(
-        their_place, other_right, inverse, ortho_out, hidden, grad_y, err_out, tuple(halfway)
-    )
+    new_out, factor_out = rest_out(place, own_right, other_right, inverse, ortho_out, hidden, grad_y, err_out)
     return new_in[None], new_out[None], factor_in, factor_out
 
 

time: 151 us -> 153 us (1.013)
  Pallas kernels: 67.9 us -> 63.2 us
  waiting for transfers between devices: 46 us -> 49.2 us
  local copies, waits for them, and re-layouts: 0.17 us -> 2.72 us
  starting transfers between devices: 32.8 us -> 34.5 us
    ppermute x3, waiting for transfers between devices: 1.64 us -> 6.1 us  [shards(): lax.ppermute(pieces[shift], 'z', ring(shift))]
    pallas_call x2 -> x1, Pallas kernels: 8.76 us -> 5.82 us  [rest_out(): pl.pallas_call(rest_out_kernel, in_specs=[pl.BlockSpec(memory_space=pltpu...]
    unnamed x7 -> x13, local copies, waits for them, and re-layouts: 0.04 us -> 2.66 us
    pallas_call x1, Pallas kernels: 8.96 us -> 11.5 us  [invert(): pl.pallas_call(invert_kernel, out_shape=[jax.ShapeDtypeStruct((4, RANK, 1...]
    pallas_call x3 -> x4, Pallas kernels: 20.8 us -> 18.2 us  [the longest x1 8.59 us: recurrence(): pl.pallas_call(recurrence_kernel, in_specs=[ANY] * len(operands), out_spe...]
    ppermute x1, waiting for transfers between devices: 0.01 us -> 1.71 us  [shards(): other_right = lax.ppermute(own_right, 'c', SWAP)]
    ppermute x2, waiting for transfers between devices: 2.52 us -> 0.91 us  [shards(): arrived = lax.ppermute(send, 'c', SWAP)]
  transfers between devices with their start and end apart: 14 -> 14, of which waited for: 7 -> 8; matrix products, arithmetic and copies ran while one was open for 1% -> 0% of each run, Pallas kernels for 31% -> 28%
where the time goes in v4:
time: 153 us; the launch traced here: 151 us
  Pallas kernels  63.2 us (41%)
  waiting for transfers between devices  49.2 us (32%)
  starting transfers between devices  34.5 us (23%)
  local copies, waits for them, and re-layouts  2.72 us (2%)
    all_to_all x1, waiting for transfers between devices, shards(): lax.all_to_all(answer_left(me[None], received), CHIP, 0, 0)  20.3 us
    all_to_all x1, waiting for transfers between devices, shards(): received = lax.all_to_all(rows.reshape(CHIPS, EACH1, 128), CHIP, 0, 0)  16.9 us
    pallas_call x1, Pallas kernels, invert(): pl.pallas_call(invert_kernel, out_shape=[jax.ShapeDtypeStruct((4, RANK, 1...  11.5 us
    all_to_all x1, starting transfers between devices, shards(): received = lax.all_to_all(rows.reshape(CHIPS, EACH1, 128), CHIP, 0, 0)  11.5 us
    pallas_call x1, Pallas kernels, rest_in(): pl.pallas_call(rest_in_kernel, grid=(D // TILE,), in_specs=[pl.BlockSpec(...  8.98 us
    pallas_call x1, Pallas kernels, recurrence(): pl.pallas_call(recurrence_kernel, in_specs=[ANY] * len(operands), out_spe...  8.59 us
    all_to_all x1, starting transfers between devices, shards(): summed = lax.all_to_all(everywhere, ('x', 'y'), 0, 0).reshape(ROWS2, 128)  7.15 us
    ppermute x3, waiting for transfers between devices, shards(): lax.ppermute(pieces[shift], 'z', ring(shift))  6.1 us
  transfers between devices with their start and end apart: 14, of which 8 were waited for; matrix products, arithmetic and copies ran while one was open for 0% of the time, Pallas kernels for 28%

profile of v4, /device:TPU:0, one launch (start us, length us, event | category | flops | bytes accessed | tf_op | source)
XLA Modules:
  0.0 151.0 jit_solution(10950646546513275964)
XLA Ops:
  0.6 8.6 %recurrence.1 = (bf16[256,384]{1,0:T(8,128)(2,1)S(1)}, bf16[3,256,384]{2,1,0:T(8,128)(2,1)S(1)}, bf16[3,3072,384]{2,1,0:T(8,128)(2,1)S(1)}, bf16[384,3072]{1,0:T...) custom-call(bf16[256,384]{1,0:T(8,128)(2,1)} %q_hbm.1, bf16[256,384]{1,0:T(8,128)(2,1)} %f_hbm.1, ...), custom_call_target="tpu_custom_call" | custom-call | flops 8000000000 | bytes 24000000 | tf_op jit(solution)/shard_map/recurrence/pallas_call | solution.py:215
  9.3 1.6 %left_send.1 = f32[2304,128]{1,0:T(8,128)S(1)} custom-call(s32[1]{0:T(128)S(6)} %sub.3.half_ref, bf16[256,3072]{1,0:T(8,128)(2,1)S(1)} %get-tuple-element.45.x_ref, bf16[3,256,384]{2,1,0:T(8,128)(2,1)S(1)} %get-tuple-element.46.grads_ref, bf16[3,3072,384]{2,1,0:T(8,128)(2,1)S(1)} %get-tuple-element.47.err_in_ref, f32[3,64,384]{2,1,0:T(8,128)S(1)} %copy-done), custom_call_target="tpu_custom_call" | custom-call | flops 3000000000 | bytes 9000000 | tf_op jit(solution)/shard_map/left_send/pallas_call | solution.py:261
  11.0 1.9 %left_out.1.left_out_ref = f32[192,128]{1,0:T(8,128)S(1)} custom-call(bf16[256,3072]{1,0:T(8,128)(2,1)S(1)} %get-tuple-element.48.gy_ref, bf16[256,384]{1,0:T(8,128)(2,1)S(1)} %get-tuple-element.49.hid_ref, bf16[384,3072]{1,0:T(8,128)(2,1)S(1)} %get-tuple-element.50.err_out_ref, f32[64,3072]{1,0:T(8,128)S(1)} %copy-done.4), custom_call_target="tpu_custom_call" | custom-call | flops 4000000000 | bytes 12000000 | tf_op jit(solution)/shard_map/left_out/pallas_call | solution.py:280
  12.9 0.9 collective-permute-done.arrived_ref
  13.8 2.7 %left_keep.1 = f32[2560,128]{1,0:T(8,128)} custom-call(s32[1]{0:T(128)} %bitcast.1.half_ref, bf16[256,3072]{1,0:T(8,128)(2,1)S(1)} %get-tuple-element.45.x_ref, bf16[3,256,384]{2,1,0:T(8,128)(2,1)S(1)} %get-tuple-element.46.grads_ref, bf16[3,3072,384]{2,1,0:T(8,128)(2,1)S(1)} %get-tuple-element.47.err_in_ref, f32[3,64,384]{2,1,0:T(8,128)S(1)} %copy-done, ...), custom_call_target="tpu_custom_call" | custom-call | flops 3000000000 | bytes 9000000 | tf_op jit(solution)/shard_map/left_keep/pallas_call | solution.py:261
  16.6 11.5 %all-to-all-start = ((f32[64,40,128]{2,1,0:T(8,128)}), f32[64,40,128]{2,1,0:T(8,128)S(1)}, u32[]{:S(2)}, u32[]{:S(2)}) async-start(f32[64,40,128]{2,1,0:T(8,128)} %bitcast.4), calls=%async_computation | async-start | bytes 2621440 | tf_op jit(solution)/shard_map/all_to_all | solution.py:765
  28.1 4.9 %turned.1.turned_hbm = bf16[3072,256]{1,0:T(8,128)(2,1)} custom-call(bf16[256,3072]{1,0:T(8,128)(2,1)} %x_hbm.1), custom_call_target="tpu_custom_call" | custom-call | flops 3000000000 | bytes 9000000 | tf_op jit(solution)/shard_map/turned/pallas_call | solution.py:294
  33.0 16.9 %all-to-all-done.received_ref = f32[64,40,128]{2,1,0:T(8,128)S(1)} async-done(((f32[64,40,128]{2,1,0:T(8,128)}), f32[64,40,128]{2,1,0:T(8,128)S(1)}, u32[]{:S(2)}, u32[]{:S(2)}) %all-to-all-start) | async-done | bytes 1310752 | tf_op jit(solution)/shard_map/all_to_all | solution.py:765
  49.8 1.2 answer_left.1
  51.1 4.8 %all-to-all-start.1 = ((f32[64,40,128]{2,1,0:T(8,128)}), f32[64,40,128]{2,1,0:T(8,128)S(1)}, u32[]{:S(2)}, u32[]{:S(2)}) async-start(f32[64,40,128]{2,1,0:T(8,128)} %answer_left.1), calls=%async_computation.1 | async-start | bytes 2621440 | tf_op jit(solution)/shard_map/all_to_all | solution.py:768
  56.0 20.3 %all-to-all-done.1 = f32[64,40,128]{2,1,0:T(8,128)S(1)} async-done(((f32[64,40,128]{2,1,0:T(8,128)}), f32[64,40,128]{2,1,0:T(8,128)S(1)}, u32[]{:S(2)}, u32[]{:S(2)}) %all-to-all-start.1) | async-done | bytes 1310752 | tf_op jit(solution)/shard_map/all_to_all | solution.py:768
  76.4 4.0 %right_out.1 = (f32[832,128]{1,0:T(8,128)S(1)}, f32[768,128]{1,0:T(8,128)S(1)}) custom-call(s32[2]{0:T(128)S(1)} %pad_add_fusion.place_ref, f32[192,128]{1,0:T(8,128)S(1)} %slice.40.left_out_ref, bf16[256,384]{1,0:T(8,128)(2,1)S(1)} %get-tuple-element.49.hid_ref, bf16[256,3072]{1,0:T(8,128)(2,1)} %gy_hbm.5, bf16[384,3072]{1,0:T(8,128)(2,1)} %bitcast.22), custom_call_target="tpu_custom_call" | custom-call | flops 3000000000 | bytes 9000000 | tf_op jit(solution)/shard_map/right_out/pallas_call | solution.py:386
  81.1 4.2 %right_own.1 = (f32[3,64,384]{2,1,0:T(8,128)S(1)}, f32[192,256]{1,0:T(8,128)S(1)}, bf16[256,1536]{1,0:T(8,128)(2,1)S(1)}, bf16[3,1536,384]{2,1,0:T(8,128)(2,1)S(1)}) custom-call(s32[2]{0:T(128)S(1)} %pad_add_fusion.1.halves_ref, f32[2560,128]{1,0:T(8,128)S(1)} %bitcast.13, bf16[256,3072]{1,0:T(8,128)(2,1)} %x_hbm.1, bf16[3,3072,384]{2,1,0:T(8,128)(2,1)} %bitcast.19), custom_call_target="tpu_custom_call" | custom-call | flops 4000000000 | bytes 12000000 | tf_op jit(solution)/shard_map/right_own/pallas_call | solution.py:449
  85.4 0.9 collective-permute-start.5
  86.3 1.8 %collective-permute-start.3 = (f32[256,128]{1,0:T(8,128)S(1)}, f32[256,128]{1,0:T(8,128)S(1)}, u32[]{:S(2)}, u32[]{:S(2)}) collective-permute-start(f32[256,128]{1,0:T(8,128)S(1)} %get-tuple-element.91), channel_id=1, source_target_pairs={{0,4},{2,6},{4,0},{6,2},{1,5},{3,7},{5,1},{7,3},{8,12},{10,14},{12... | collective-permute-start | bytes 393224 | tf_op jit(solution)/shard_map/ppermute | solution.py:779
  88.2 1.5 right_other.1.right_ref
  89.7 2.1 %collective-permute-done.5.third_ref = f32[256,128]{1,0:T(8,128)S(1)} collective-permute-done((f32[256,128]{1,0:T(8,128)S(1)}, f32[256,128]{1,0:T(8,128)S(1)}, u32[]{:S(2)}, u32[]{:S(2)}) %collective-permute-start.5) | collective-permute-done | bytes 131104 | tf_op jit(solution)/shard_map/ppermute | solution.py:779
  91.8 2.4 %collective-permute-done.3.first_ref = f32[256,128]{1,0:T(8,128)S(1)} collective-permute-done((f32[256,128]{1,0:T(8,128)S(1)}, f32[256,128]{1,0:T(8,128)S(1)}, u32[]{:S(2)}, u32[]{:S(2)}) %collective-permute-start.3) | collective-permute-done | bytes 131104 | tf_op jit(solution)/shard_map/ppermute | solution.py:779
  94.2 1.6 %collective-permute-done.4.second_ref = f32[256,128]{1,0:T(8,128)S(1)} collective-permute-done((f32[256,128]{1,0:T(8,128)S(1)}, f32[256,128]{1,0:T(8,128)S(1)}, u32[]{:S(2)}, u32[]{:S(2)}) %collective-permute-start.4) | collective-permute-done | bytes 131104 | tf_op jit(solution)/shard_map/ppermute | solution.py:779
  96.6 3.6 %all-to-all-start.2 = ((f32[16,48,128]{2,1,0:T(8,128)}), f32[16,48,128]{2,1,0:T(8,128)S(1)}, u32[]{:S(2)}, u32[]{:S(2)}) async-start(f32[16,48,128]{2,1,0:T(8,128)} %bitcast.7), calls=%async_computation.2 | async-start | bytes 786432 | tf_op jit(solution)/shard_map/all_to_all | solution.py:782
  100.1 1.3 copy-done.2
  101.5 11.5 %invert.1 = (f32[4,64,128]{2,1,0:T(8,128)S(1)}, f32[64,384]{1,0:T(8,128)S(1)}) custom-call(f32[2560,128]{1,0:T(8,128)S(1)} %bitcast.14, f32[2560,128]{1,0:T(8,128)S(1)} %copy-done.2, f32[192,128]{1,0:T(8,128)S(1)} %slice.40.left_out_ref, f32[64,128]{1,0:T(8,128)S(1)} %get-tuple-element.66.gram_out_ref), custom_call_target="tpu_custom_call" | custom-call | flops 10000000000 | bytes 30000000 | tf_op jit(solution)/shard_map/invert/pallas_call | solution.py:553
  113.0 0.8 answer_right.1
  113.8 7.2 %all-to-all-start.3 = ((f32[16,48,128]{2,1,0:T(8,128)}), f32[16,48,128]{2,1,0:T(8,128)S(1)}, u32[]{:S(2)}, u32[]{:S(2)}) async-start(f32[16,48,128]{2,1,0:T(8,128)} %answer_right.1), calls=%async_computation.3 | async-start | bytes 786432 | tf_op jit(solution)/shard_map/all_to_all | solution.py:787
  121.0 1.3 copy-done.3
  122.3 4.8 %turn.1.ortho_hbm = bf16[3,3072,128]{2,1,0:T(8,128)(2,1)} custom-call(s32[1]{0:T(128)} %bitcast.1.half_ref, f32[2560,128]{1,0:T(8,128)S(1)} %bitcast.15, f32[2560,128]{1,0:T(8,128)S(1)} %copy-done.3, f32[4,64,128]{2,1,0:T(8,128)S(1)} %get-tuple-element.72.inverse_ref), custom_call_target="tpu_custom_call" | custom-call | flops 6000000000 | bytes 18000000 | tf_op jit(solution)/shard_map/turn/pallas_call | solution.py:588
  127.0 3.3 %all-to-all-done.3 = f32[16,48,128]{2,1,0:T(8,128)S(1)} async-done(((f32[16,48,128]{2,1,0:T(8,128)}), f32[16,48,128]{2,1,0:T(8,128)S(1)}, u32[]{:S(2)}, u32[]{:S(2)}) %all-to-all-start.3) | async-done | bytes 393248 | tf_op jit(solution)/shard_map/all_to_all | solution.py:787
  130.8 1.8 %collective-permute-start.7 = (f32[192,128]{1,0:T(8,128)S(1)}, f32[192,128]{1,0:T(8,128)S(1)}, u32[]{:S(2)}, u32[]{:S(2)}) collective-permute-start(f32[192,128]{1,0:T(8,128)S(1)} %slice.39), channel_id=1, source_target_pairs={{0,4},{2,6},{4,0},{6,2},{1,5},{3,7},{5,1},{7,3},{8,12},{10,14},{12... | collective-permute-start | bytes 294920 | tf_op jit(solution)/shard_map/ppermute | solution.py:792
  132.6 1.3 collective-permute-start.6
  133.9 9.0 %rest_in.1 = (bf16[3,3072,384]{2,1,0:T(8,128)(2,1)}, f32[3,64,384]{2,1,0:T(8,128)}) custom-call(f32[768,128]{1,0:T(8,128)S(1)} %bitcast.17, f32[4,64,128]{2,1,0:T(8,128)S(1)} %get-tuple-element.72.inverse_ref, bf16[3,256,384]{2,1,0:T(8,128)(2,1)S(1)} %get-tuple-element.46.grads_ref, bf16[3072,256]{1,0:T(8,128)(2,1)} %turned.1.turned_hbm, ...), custom_call_target="tpu_custom_call" | custom-call | flops 10000000000 | bytes 30000000 | tf_op jit(solution)/shard_map/rest_in/pallas_call | solution.py:637
  143.3 1.7 %collective-permute-done.9.other_ref = f32[768,128]{1,0:T(8,128)S(1)} collective-permute-done((f32[768,128]{1,0:T(8,128)S(1)}, f32[768,128]{1,0:T(8,128)S(1)}, u32[]{:S(2)}, u32[]{:S(2)}) %collective-permute-start.9) | collective-permute-done | bytes 393248 | tf_op jit(solution)/shard_map/ppermute | solution.py:796
  145.0 5.8 %rest_out.1 = (bf16[384,3072]{1,0:T(8,128)(2,1)}, f32[64,3072]{1,0:T(8,128)}) custom-call(s32[2]{0:T(128)S(1)} %pad_add_fusion.place_ref, f32[768,128]{1,0:T(8,128)S(1)} %constant_dynamic-update-slice_fusion.own_ref, f32[768,128]{1,0:T(8,128)S(1)} %collective-permute-done.9.other_ref, f32[4,64,128]{2,1,0:T(8,128)S(1)} %get-tuple-element.72.inverse_ref, ...), custom_call_target="tpu_custom_call" | custom-call | flops 6000000000 | bytes 18000000 | tf_op jit(solution)/shard_map/rest_out/pallas_call | solution.py:719
  (33 shorter events, 2.7 us)
Async XLA Ops:
  0.6 8.6 %copy-start = (f32[3,64,384]{2,1,0:T(8,128)S(1)}, f32[3,64,384]{2,1,0:T(8,128)}, u32[]{:S(2)}) copy-start(f32[3,64,384]{2,1,0:T(8,128)} %basis_in_ref.3) | copy-start | bytes 884740
  9.3 1.8 %copy-start.4 = (f32[64,3072]{1,0:T(8,128)S(1)}, f32[64,3072]{1,0:T(8,128)}, u32[]{:S(2)}) copy-start(f32[64,3072]{1,0:T(8,128)} %basis_out_ref.1) | copy-start | bytes 2359300
  10.9 2.9 %collective-permute-start = (f32[2304,128]{1,0:T(8,128)S(1)}, f32[2304,128]{1,0:T(8,128)S(1)}, u32[]{:S(2)}, u32[]{:S(2)}) collective-permute-start(f32[2304,128]{1,0:T(8,128)S(1)} %left_send.1), channel_id=1, source_target_pairs={{0,1},{1,0},{2,3},{3,2},{4,5},{5,4},{6,7},{7,6},{8,9},{9,8},{10,11... | collective-permute-start | bytes 3538952 | tf_op jit(solution)/shard_map/ppermute | solution.py:760
  16.6 33.3 %all-to-all-start = ((f32[64,40,128]{2,1,0:T(8,128)}), f32[64,40,128]{2,1,0:T(8,128)S(1)}, u32[]{:S(2)}, u32[]{:S(2)}) async-start(f32[64,40,128]{2,1,0:T(8,128)} %bitcast.4), calls=%async_computation | async-start | bytes 2621440 | tf_op jit(solution)/shard_map/all_to_all | solution.py:765
  51.1 25.2 %all-to-all-start.1 = ((f32[64,40,128]{2,1,0:T(8,128)}), f32[64,40,128]{2,1,0:T(8,128)S(1)}, u32[]{:S(2)}, u32[]{:S(2)}) async-start(f32[64,40,128]{2,1,0:T(8,128)} %answer_left.1), calls=%async_computation.1 | async-start | bytes 2621440 | tf_op jit(solution)/shard_map/all_to_all | solution.py:768
  76.3 11.9 %collective-permute-start.1 = (f32[2560,128]{1,0:T(8,128)S(1)}, f32[2560,128]{1,0:T(8,128)S(1)}, u32[]{:S(2)}, u32[]{:S(2)}) collective-permute-start(f32[2560,128]{1,0:T(8,128)S(1)} %bitcast.12), channel_id=1, source_target_pairs={{0,1},{1,0},{2,3},{3,2},{4,5},{5,4},{6,7},{7,6},{8,9},{9,8},{10,11... | collective-permute-start | bytes 3932168 | tf_op jit(solution)/shard_map/ppermute | solution.py:769
  80.4 4.8 %collective-permute-start.2 = (f32[832,128]{1,0:T(8,128)S(1)}, f32[832,128]{1,0:T(8,128)S(1)}, u32[]{:S(2)}, u32[]{:S(2)}) collective-permute-start(f32[832,128]{1,0:T(8,128)S(1)} %get-tuple-element.54), channel_id=1, source_target_pairs={{0,1},{1,0},{2,3},{3,2},{4,5},{5,4},{6,7},{7,6},{8,9},{9,8},{10,11... | collective-permute-start | bytes 1277960 | tf_op jit(solution)/shard_map/ppermute | solution.py:773
  85.4 6.4 %collective-permute-start.5 = (f32[256,128]{1,0:T(8,128)S(1)}, f32[256,128]{1,0:T(8,128)S(1)}, u32[]{:S(2)}, u32[]{:S(2)}) collective-permute-start(f32[256,128]{1,0:T(8,128)S(1)} %get-tuple-element.90), channel_id=1, source_target_pairs={{0,6},{2,0},{4,2},{6,4},{1,7},{3,1},{5,3},{7,5},{8,14},{10,8},{12,... | collective-permute-start | bytes 393224 | tf_op jit(solution)/shard_map/ppermute | solution.py:779
  86.3 7.9 %collective-permute-start.3 = (f32[256,128]{1,0:T(8,128)S(1)}, f32[256,128]{1,0:T(8,128)S(1)}, u32[]{:S(2)}, u32[]{:S(2)}) collective-permute-start(f32[256,128]{1,0:T(8,128)S(1)} %get-tuple-element.91), channel_id=1, source_target_pairs={{0,4},{2,6},{4,0},{6,2},{1,5},{3,7},{5,1},{7,3},{8,12},{10,14},{12... | collective-permute-start | bytes 393224 | tf_op jit(solution)/shard_map/ppermute | solution.py:779
  88.1 7.7 %collective-permute-start.4 = (f32[256,128]{1,0:T(8,128)S(1)}, f32[256,128]{1,0:T(8,128)S(1)}, u32[]{:S(2)}, u32[]{:S(2)}) collective-permute-start(f32[256,128]{1,0:T(8,128)S(1)} %get-tuple-element.92), channel_id=1, source_target_pairs={{0,2},{2,4},{4,6},{6,0},{1,3},{3,5},{5,7},{7,1},{8,10},{10,12},{12... | collective-permute-start | bytes 393224 | tf_op jit(solution)/shard_map/ppermute | solution.py:779
  88.2 1.5 copy-start.1
  96.6 16.4 %all-to-all-start.2 = ((f32[16,48,128]{2,1,0:T(8,128)}), f32[16,48,128]{2,1,0:T(8,128)S(1)}, u32[]{:S(2)}, u32[]{:S(2)}) async-start(f32[16,48,128]{2,1,0:T(8,128)} %bitcast.7), calls=%async_computation.2 | async-start | bytes 786432 | tf_op jit(solution)/shard_map/all_to_all | solution.py:782
  100.1 1.3 copy-start.2
  113.8 16.5 %all-to-all-start.3 = ((f32[16,48,128]{2,1,0:T(8,128)}), f32[16,48,128]{2,1,0:T(8,128)S(1)}, u32[]{:S(2)}, u32[]{:S(2)}) async-start(f32[16,48,128]{2,1,0:T(8,128)} %answer_right.1), calls=%async_computation.3 | async-start | bytes 786432 | tf_op jit(solution)/shard_map/all_to_all | solution.py:787
  120.9 1.3 copy-start.3
  130.3 12.6 %collective-permute-start.8 = (f32[192,128]{1,0:T(8,128)S(1)}, f32[192,128]{1,0:T(8,128)S(1)}, u32[]{:S(2)}, u32[]{:S(2)}) collective-permute-start(f32[192,128]{1,0:T(8,128)S(1)} %slice.39), channel_id=1, source_target_pairs={{0,6},{2,0},{4,2},{6,4},{1,7},{3,1},{5,3},{7,5},{8,14},{10,8},{12,... | collective-permute-start | bytes 294920 | tf_op jit(solution)/shard_map/ppermute | solution.py:792
  130.8 12.1 %collective-permute-start.7 = (f32[192,128]{1,0:T(8,128)S(1)}, f32[192,128]{1,0:T(8,128)S(1)}, u32[]{:S(2)}, u32[]{:S(2)}) collective-permute-start(f32[192,128]{1,0:T(8,128)S(1)} %slice.39), channel_id=1, source_target_pairs={{0,4},{2,6},{4,0},{6,2},{1,5},{3,7},{5,1},{7,3},{8,12},{10,14},{12... | collective-permute-start | bytes 294920 | tf_op jit(solution)/shard_map/ppermute | solution.py:792
  132.6 10.3 %collective-permute-start.6 = (f32[192,128]{1,0:T(8,128)S(1)}, f32[192,128]{1,0:T(8,128)S(1)}, u32[]{:S(2)}, u32[]{:S(2)}) collective-permute-start(f32[192,128]{1,0:T(8,128)S(1)} %slice.39), channel_id=1, source_target_pairs={{0,2},{2,4},{4,6},{6,0},{1,3},{3,5},{5,7},{7,1},{8,10},{10,12},{12... | collective-permute-start | bytes 294920 | tf_op jit(solution)/shard_map/ppermute | solution.py:792
  143.0 2.0 %collective-permute-start.9 = (f32[768,128]{1,0:T(8,128)S(1)}, f32[768,128]{1,0:T(8,128)S(1)}, u32[]{:S(2)}, u32[]{:S(2)}) collective-permute-start(f32[768,128]{1,0:T(8,128)S(1)} %constant_dynamic-update-slice_fusion.own_ref), channel_id=1, source_target_pairs={{0,1},{1,0},{2,3},{3,2},{4,5},{5,4},{6,7},{7,6},{8,9},{9,8},{10,11... | collective-permute-start | bytes 1179656 | tf_op jit(solution)/shard_map/ppermute | solution.py:796

commit v5 on v4

--- a/solution.py
+++ b/solution.py
@@ -409,46 +409,41 @@
     return folded(nt(jnp.concatenate([high, low], axis=0), x))
 
 
-def right_own_kernel(halves_ref, own_ref, x_hbm, err_in_hbm, right_ref, token_ref, x_out, err_in_out, x_scr, err_in_scr, sem):
-    def near(j):
-        at = pl.ds(pl.multiple_of(halves_ref[0] * HALF + j * TILE, TILE), TILE)
-        return (
-            pltpu.make_async_copy(x_hbm.at[:, at], x_scr.at[j], sem.at[0, j]),
-            pltpu.make_async_copy(err_in_hbm.at[:, at], err_in_scr.at[j], sem.at[1, j]),
-        )
-
-    def far(j):
-        at = pl.ds(pl.multiple_of(halves_ref[1] * HALF + j * TILE, TILE), TILE)
+def near_copies(half, x_hbm, err_in_hbm, x_out, err_in_out, sem):
+    copies = []
+    for j in range(STEPS):
+        at = pl.ds(pl.multiple_of(half * HALF + j * TILE, TILE), TILE)
         to = slice(j * TILE, (j + 1) * TILE)
-        return (
-            pltpu.make_async_copy(x_hbm.at[:, at], x_out.at[:, to], sem.at[2, j]),
-            pltpu.make_async_copy(err_in_hbm.at[:, at], err_in_out.at[:, to], sem.at[3, j]),
-        )
-
-    copies = [near(j) for j in range(STEPS)] + [far(j) for j in range(STEPS)]
-    for pair in copies:
-        for copy in pair:
-            copy.start()
+        copies.append(pltpu.make_async_copy(x_hbm.at[:, at], x_out.at[:, to], sem.at[0, j]))
+        copies.append(pltpu.make_async_copy(err_in_hbm.at[:, at], err_in_out.at[:, to], sem.at[1, j]))
+    return copies
+
+
+def right_sums(left_ref, x_ref, err_in_ref, tokens, rights):
+    for j in range(STEPS):
+        mine = slice(j * TILE, (j + 1) * TILE)
+        rows = wide(left_ref[L_STEP * j : L_STEP * (j + 1), :], 3 * RANK)
+        tokens += right_tile(rows, x_ref[:, mine], err_in_ref.at[:, mine], rights)
+    return tokens
+
+
+def right_own_kernel(half_ref, own_ref, x_ref, err_in_ref, x_hbm, err_in_hbm, right_ref, token_ref, x_out, err_in_out, sem):
+    copies = near_copies(half_ref[0], x_hbm, err_in_hbm, x_out, err_in_out, sem)
+    for copy in copies:
+        copy.start()
     rights = [jnp.zeros((RANK, COLS), f32)] * 3
-    tokens = jnp.zeros((3 * RANK, TOK), f32)
-    for j in range(STEPS):
-        for copy in copies[j]:
-            copy.wait()
-        rows = wide(own_ref[L_STEP * j : L_STEP * (j + 1), :], 3 * RANK)
-        tokens += right_tile(rows, x_scr[j], err_in_scr.at[j], rights)
-    token_ref[...] = tokens
+    token_ref[...] = right_sums(own_ref, x_ref, err_in_ref, jnp.zeros((3 * RANK, TOK), f32), rights)
     for p in range(3):
         right_ref[p] = rights[p]
-    for pair in copies[STEPS:]:
-        for copy in pair:
-            copy.wait()
-
-
-def right_own(halves, own, inputs, err_in):
+    for copy in copies:
+        copy.wait()
+
+
+def right_own(other_half, own, near_inputs, near_err_in, inputs, err_in):
     whole = pl.BlockSpec(memory_space=pltpu.VMEM)
     return pl.pallas_call(
         right_own_kernel,
-        in_specs=[pl.BlockSpec(memory_space=pltpu.SMEM), whole, ANY, ANY],
+        in_specs=[pl.BlockSpec(memory_space=pltpu.SMEM), whole, whole, whole, ANY, ANY],
         out_specs=[whole, whole, ANY, ANY],
         out_shape=[
             jax.ShapeDtypeStruct((3, RANK, COLS), f32),
@@ -456,24 +451,16 @@
             pltpu.VMEM((TOK, HALF), bf16),
             pltpu.VMEM((3, HALF, COLS), bf16),
         ],
-        scratch_shapes=[
-            pltpu.VMEM((STEPS, TOK, TILE), bf16),
-            pltpu.VMEM((STEPS, 3, TILE, COLS), bf16),
-            pltpu.SemaphoreType.DMA((4, STEPS)),
-        ],
-        cost_estimate=cost(4),
+        scratch_shapes=[pltpu.SemaphoreType.DMA((2, STEPS))],
+        cost_estimate=cost(3),
         compiler_params=pltpu.CompilerParams(vmem_limit_bytes=VMEM),
         name="right_own",
-    )(halves, own, *streamed(inputs, err_in))
+    )(other_half, own, *held(near_inputs, near_err_in), *streamed(inputs, err_in))
 
 
 def right_other_kernel(other_ref, right_ref, token_ref, x_ref, err_in_ref, grads_ref, rows_ref):
     rights = [right_ref[p] for p in range(3)]
-    tokens = token_ref[...]
-    for j in range(STEPS):
-        mine = slice(j * TILE, (j + 1) * TILE)
-        rows = wide(other_ref[L_STEP * j : L_STEP * (j + 1), :], 3 * RANK)
-        tokens += right_tile(rows, x_ref[:, mine], err_in_ref.at[:, mine], rights)
+    tokens = right_sums(other_ref, x_ref, err_in_ref, token_ref[...], rights)
     for p in range(3):
         total = rights[p] + folded(nn(stacked(tokens[RANK * p : RANK * (p + 1)]), grads_ref[p]))
         for i, tile in enumerate(tiles_of(total)):
@@ -508,38 +495,60 @@
     )(*operands)
 
 
-def invert_kernel(own_ref, other_ref, left_out_ref, gram_out_ref, inverse_ref, ortho_out_ref):
+def gram_kernel(half_ref, own_ref, other_ref, x_hbm, err_in_hbm, gram_ref, x_out, err_in_out, sem):
+    copies = near_copies(half_ref[0], x_hbm, err_in_hbm, x_out, err_in_out, sem)
+    for copy in copies:
+        copy.start()
+    gram = jnp.zeros((3 * RANK, 3 * RANK), f32)
+    for ref in (own_ref, other_ref):
+        for i in range(STEPS):
+            rows = wide(ref[L_STEP * i : L_STEP * (i + 1), :], 3 * RANK)
+            gram += exact_nt(rows, rows)
+    gram_ref[...] = gram
+    for copy in copies:
+        copy.wait()
+
+
+def gram(half, own, other, inputs, err_in):
+    whole = pl.BlockSpec(memory_space=pltpu.VMEM)
+    return pl.pallas_call(
+        gram_kernel,
+        in_specs=[pl.BlockSpec(memory_space=pltpu.SMEM), whole, whole, ANY, ANY],
+        out_specs=[whole, ANY, ANY],
+        out_shape=[
+            jax.ShapeDtypeStruct((3 * RANK, 3 * RANK), f32),
+            pltpu.VMEM((TOK, HALF), bf16),
+            pltpu.VMEM((3, HALF, COLS), bf16),
+        ],
+        scratch_shapes=[pltpu.SemaphoreType.DMA((2, STEPS))],
+        cost_estimate=cost(3),
+        compiler_params=pltpu.CompilerParams(vmem_limit_bytes=VMEM),
+        name="gram",
+    )(half, own, other, *streamed(inputs, err_in))
+
+
+def invert_kernel(gram_in_ref, left_out_ref, gram_out_ref, inverse_ref, ortho_out_ref):
     eye = jnp.where(
         lax.broadcasted_iota(jnp.int32, (RANK, RANK), 0) == lax.broadcasted_iota(jnp.int32, (RANK, RANK), 1),
         1.0,
         0.0,
     )
-    gram = jnp.zeros((3 * RANK, 3 * RANK), f32)
-    for ref in (own_ref, other_ref):
-        for i in range(STEPS):
-            rows = wide(ref[L_STEP * i : L_STEP * (i + 1), :], 3 * RANK)
-            gram += exact_nt(rows, rows)
+    gram = gram_in_ref[...]
     for p in range(3):
         mine = slice(RANK * p, RANK * (p + 1))
         inverse_ref[p] = jnp.concatenate([gram[mine, mine], eye], axis=1)
     inverse_ref[3] = jnp.concatenate([gram_out_ref[:, :RANK], eye], axis=1)
     rows8 = lax.broadcasted_iota(jnp.int32, (1, 8, 1), 1)
     tiles = [inverse_ref[:, 8 * t : 8 * t + 8, :] for t in range(RANK // 8)]
-    for j in range(0, RANK, 2):
+    for j in range(RANK):
         top, at = divmod(j, 8)
-        first = tiles[top][:, at : at + 1, :]
-        second = tiles[top][:, at + 1 : at + 2, :]
-        first_scaled = first * (1.0 / first[:, :, j : j + 1])
-        ratio = first_scaled[:, :, j + 1 : j + 2]
-        second = second - second[:, :, j : j + 1] * first_scaled
-        second_scaled = second * (1.0 / second[:, :, j + 1 : j + 2])
+        pivot_row = tiles[top][:, at : at + 1, :]
+        scaled = pivot_row * (1.0 / pivot_row[:, :, j : j + 1])
         for t in range(top, RANK // 8):
             column = tiles[t][:, :, j : j + 1]
-            other = tiles[t][:, :, j + 1 : j + 2] - column * ratio
             if t == top:
                 column = jnp.where(rows8 > at, column, 0.0)
-                other = jnp.where(rows8 > at + 1, other, 0.0)
-            tiles[t] = tiles[t] - column * first_scaled - other * second_scaled
+            tiles[t] = tiles[t] - column * scaled
     work = jnp.concatenate(tiles, axis=1)
     lane = lax.broadcasted_iota(jnp.int32, (4, RANK, 128), 2)
     sub = lax.broadcasted_iota(jnp.int32, (4, RANK, 128), 1)
@@ -549,7 +558,7 @@
     ortho_out_ref[...] = exact_nn(inverse[3, :, RANK:], wide(left_out_ref[...], RANK))
 
 
-def invert(own, other, left_out_sum, gram_out):
+def invert(gram_in, left_out_sum, gram_out):
     return pl.pallas_call(
         invert_kernel,
         out_shape=[
@@ -559,7 +568,7 @@
         cost_estimate=cost(10),
         compiler_params=pltpu.CompilerParams(vmem_limit_bytes=VMEM),
         name="invert",
-    )(own, other, left_out_sum, gram_out)
+    )(gram_in, left_out_sum, gram_out)
 
 
 def turn_kernel(half_ref, own_ref, other_ref, inverse_ref, ortho_ref):
@@ -666,8 +675,10 @@
     )(summed, inverse, grads, *streamed(turned, ortho_in, err_in))
 
 
-def rest_out_kernel(place_ref, own_ref, other_ref, inverse_ref, ortho_out_ref, hid_ref, gy_hbm, err_out_hbm,
-                    rest_hbm, factor_hbm, gy_scr, err_out_scr, rest_scr, factor_scr, in_sem, out_sem):
+def rest_out_kernel(place_ref, *refs):
+    piece_refs, (inverse_ref, ortho_out_ref, hid_ref, gy_hbm, err_out_hbm) = refs[:4], refs[4:9]
+    rest_hbm, factor_hbm, gy_scr, err_out_scr, rest_scr, factor_scr, in_sem, out_sem = refs[9:]
+
     def column(j):
         at = lax.rem(place_ref[0] + j // 4, 2) * 4 + lax.rem(place_ref[1] + 4 - j % 4, 4)
         return pl.ds(pl.multiple_of(at * COLS, COLS), COLS)
@@ -694,8 +705,8 @@
     both = jnp.concatenate([hid_ref[...], stack], axis=0).astype(f32).T.astype(bf16)
     inverse = inverse_ref[3, :, RANK:]
     for j in range(0, 8, 2):
-        ref = own_ref if j < 4 else other_ref
-        right = jnp.concatenate([wide(ref[PIECE * (k % 4) : PIECE * (k % 4 + 1), :], RANK) for k in (j, j + 1)], axis=1)
+        mine = slice(PIECE * (j // 4), PIECE * (j // 4 + 1))
+        right = jnp.concatenate([wide(piece_refs[k % 4][mine, :], RANK) for k in (j, j + 1)], axis=1)
         factor = exact_nn(inverse, right * (1.0 / N_DP))
         high, low = split2(-factor)
         for k in (j, j + 1):
@@ -714,11 +725,11 @@
             copy.wait()
 
 
-def rest_out(place, own, other, inverse, ortho_out, hidden, grad_y, err_out):
+def rest_out(place, pieces, inverse, ortho_out, hidden, grad_y, err_out):
     whole = pl.BlockSpec(memory_space=pltpu.VMEM)
     return pl.pallas_call(
         rest_out_kernel,
-        in_specs=[pl.BlockSpec(memory_space=pltpu.SMEM)] + [whole] * 5 + [ANY] * 2,
+        in_specs=[pl.BlockSpec(memory_space=pltpu.SMEM)] + [whole] * 7 + [ANY] * 2,
         out_specs=[ANY, ANY],
         scratch_shapes=[
             pltpu.VMEM((8, TOK, COLS), bf16),
@@ -732,7 +743,7 @@
         cost_estimate=cost(6),
         compiler_params=pltpu.CompilerParams(vmem_limit_bytes=VMEM),
         name="rest_out",
-    )(place, own, other, inverse, ortho_out, hidden, *streamed(grad_y, err_out))
+    )(place, *pieces, inverse, ortho_out, hidden, *streamed(grad_y, err_out))
 
 
 CHIP = ("x", "y", "z")
@@ -771,16 +782,17 @@
 
     send, keep_out = right_out(place, left_out_sum, grad_y, hidden, err_out)
     arrived = lax.ppermute(send, "c", SWAP)
-    right_part = right_own(jnp.concatenate([mine, theirs]), own, inputs, err_in)
-    arrived, right_part = lax.optimization_barrier((arrived, right_part))
+    gram_in, near_inputs, near_err_in = gram(mine, own, other, inputs, err_in)
+    arrived, gram_in = lax.optimization_barrier((arrived, gram_in))
     gram_out = send[RO_ROWS:] + arrived[RO_ROWS:]
     quarters = (keep_out + arrived[:RO_ROWS]).reshape(4, PIECE, 128)
     pieces = [jnp.concatenate([quarters[shift], gram_out]) for shift in range(4)]
     pieces = [pieces[0]] + [lax.ppermute(pieces[shift], "z", ring(shift)) for shift in OTHERS]
+    right_part = right_own(theirs, own, near_inputs, near_err_in, inputs, err_in)
     rows, gram_out = join(right_other(other, *right_part, grads), *pieces)
 
     received = lax.all_to_all(rows.reshape(N_DP, EACH2, 128), ("x", "y"), 0, 0)
-    inverse, ortho_out = invert(own, other, left_out_sum, gram_out)
+    inverse, ortho_out = invert(gram_in, left_out_sum, gram_out)
     received, inverse, ortho_out = lax.optimization_barrier((received, inverse, ortho_out))
     everywhere = answer_right(received)
     everywhere, inverse = lax.optimization_barrier((everywhere, inverse))
@@ -788,13 +800,11 @@
     ortho_in = turn(mine, own, other, inverse)
     summed, ortho_in = lax.optimization_barrier((summed, ortho_in))
 
-    pieces = [summed[RI_ROWS:]]
+    piece = summed[RI_ROWS:]
+    pieces = [jnp.concatenate([piece, lax.ppermute(piece, "c", SWAP)])]
     pieces += [lax.ppermute(pieces[0], "z", ring(shift)) for shift in (1, 2, 3)]
     new_in, factor_in = rest_in(summed, inverse, inputs_turned, ortho_in, grads, err_in)
-    pieces, factor_in = lax.optimization_barrier((pieces, factor_in))
-    own_right = jnp.concatenate(pieces)
-    other_right = lax.ppermute(own_right, "c", SWAP)
-    new_out, factor_out = rest_out(place, own_right, other_right, inverse, ortho_out, hidden, grad_y, err_out)
+    new_out, factor_out = rest_out(place, pieces, inverse, ortho_out, hidden, grad_y, err_out)
     return new_in[None], new_out[None], factor_in, factor_out
 
 

time: 153 us -> 145 us (0.948)
  blocking collectives: 0 us -> 25 us
  waiting for transfers between devices: 49.2 us -> 29.7 us
  starting transfers between devices: 34.5 us -> 26 us
  Pallas kernels: 63.2 us -> 59.5 us
    all_to_all x0 -> x1, blocking collectives: none -> 25 us  [shards(): lax.all_to_all(answer_left(me[None], received), CHIP, 0, 0)]
    all_to_all x1 -> x0, waiting for transfers between devices: 20.3 us -> none  [shards(): lax.all_to_all(answer_left(me[None], received), CHIP, 0, 0)]
    pallas_call x1, Pallas kernels: 11.5 us -> 6.04 us  [invert(): pl.pallas_call(invert_kernel, out_shape=[jax.ShapeDtypeStruct((4, RANK, 1...]
    all_to_all x1 -> x0, starting transfers between devices: 4.84 us -> none  [shards(): lax.all_to_all(answer_left(me[None], received), CHIP, 0, 0)]
    pallas_call x0 -> x1, Pallas kernels: none -> 3.58 us  [gram(): pl.pallas_call(gram_kernel, in_specs=[pl.BlockSpec(memory_space=pltpu.SME...]
    ppermute x3, waiting for transfers between devices: 6.1 us -> 2.78 us  [shards(): lax.ppermute(pieces[shift], 'z', ring(shift))]
    all_to_all x1, waiting for transfers between devices: 0.01 us -> 3.25 us  [shards(): received = lax.all_to_all(rows.reshape(N_DP, EACH2, 128), ('x', 'y'), 0, 0)]
    all_to_all x1, starting transfers between devices: 7.15 us -> 3.93 us  [shards(): summed = lax.all_to_all(everywhere, ('x', 'y'), 0, 0).reshape(ROWS2, 128)]
  transfers between devices with their start and end apart: 14 -> 13, of which waited for: 8 -> 7; matrix products, arithmetic and copies ran while one was open for 0% -> 0% of each run, Pallas kernels for 28% -> 27%
where the time goes in v5:
time: 145 us; the launch traced here: 144 us
  Pallas kernels  59.5 us (41%)
  waiting for transfers between devices  29.7 us (20%)
  starting transfers between devices  26 us (18%)
  blocking collectives  25 us (17%)
  local copies, waits for them, and re-layouts  2.67 us (2%)
    all_to_all x1, blocking collectives, shards(): lax.all_to_all(answer_left(me[None], received), CHIP, 0, 0)  25 us
    all_to_all x1, waiting for transfers between devices, shards(): received = lax.all_to_all(rows.reshape(CHIPS, EACH1, 128), CHIP, 0, 0)  16.9 us
    all_to_all x1, starting transfers between devices, shards(): received = lax.all_to_all(rows.reshape(CHIPS, EACH1, 128), CHIP, 0, 0)  11.5 us
    pallas_call x1, Pallas kernels, rest_in(): pl.pallas_call(rest_in_kernel, grid=(D // TILE,), in_specs=[pl.BlockSpec(...  8.98 us
    pallas_call x1, Pallas kernels, recurrence(): pl.pallas_call(recurrence_kernel, in_specs=[ANY] * len(operands), out_spe...  8.59 us
    pallas_call x1, Pallas kernels, invert(): pl.pallas_call(invert_kernel, out_shape=[jax.ShapeDtypeStruct((4, RANK, 1...  6.04 us
    pallas_call x1, Pallas kernels, rest_out(): pl.pallas_call(rest_out_kernel, in_specs=[pl.BlockSpec(memory_space=pltpu...  5.83 us
    pallas_call x1, Pallas kernels, turned(): pl.pallas_call(turned_kernel, grid=(D // TILE,), in_specs=[pl.BlockSpec((...  4.85 us
  transfers between devices with their start and end apart: 13, of which 7 were waited for; matrix products, arithmetic and copies ran while one was open for 0% of the time, Pallas kernels for 27%

profile of v5, /device:TPU:0, one launch (start us, length us, event | category | flops | bytes accessed | tf_op | source)
XLA Modules:
  0.0 144.3 jit_solution(14708643891354064393)
XLA Ops:
  0.6 8.6 %recurrence.1 = (bf16[256,384]{1,0:T(8,128)(2,1)S(1)}, bf16[3,256,384]{2,1,0:T(8,128)(2,1)S(1)}, bf16[3,3072,384]{2,1,0:T(8,128)(2,1)S(1)}, bf16[384,3072]{1,0:T...) custom-call(bf16[256,384]{1,0:T(8,128)(2,1)} %q_hbm.1, bf16[256,384]{1,0:T(8,128)(2,1)} %f_hbm.1, ...), custom_call_target="tpu_custom_call" | custom-call | flops 8000000000 | bytes 24000000 | tf_op jit(solution)/shard_map/recurrence/pallas_call | solution.py:215
  9.3 1.6 %left_send.1 = f32[2304,128]{1,0:T(8,128)S(1)} custom-call(s32[1]{0:T(128)S(6)} %sub.3.half_ref, bf16[256,3072]{1,0:T(8,128)(2,1)S(1)} %get-tuple-element.40.x_ref, bf16[3,256,384]{2,1,0:T(8,128)(2,1)S(1)} %get-tuple-element.41.grads_ref, bf16[3,3072,384]{2,1,0:T(8,128)(2,1)S(1)} %get-tuple-element.42.err_in_ref, f32[3,64,384]{2,1,0:T(8,128)S(1)} %copy-done.2), custom_call_target="tpu_custom_call" | custom-call | flops 3000000000 | bytes 9000000 | tf_op jit(solution)/shard_map/left_send/pallas_call | solution.py:261
  11.0 1.9 %left_out.1.left_out_ref = f32[192,128]{1,0:T(8,128)S(1)} custom-call(bf16[256,3072]{1,0:T(8,128)(2,1)S(1)} %get-tuple-element.43.gy_ref, bf16[256,384]{1,0:T(8,128)(2,1)S(1)} %get-tuple-element.44.hid_ref.refs_6_, bf16[384,3072]{1,0:T(8,128)(2,1)S(1)} %get-tuple-element.45.err_out_ref, f32[64,3072]{1,0:T(8,128)S(1)} %copy-done.3), custom_call_target="tpu_custom_call" | custom-call | flops 4000000000 | bytes 12000000 | tf_op jit(solution)/shard_map/left_out/pallas_call | solution.py:280
  13.0 0.9 collective-permute-done.arrived_ref
  13.9 2.7 %left_keep.1 = f32[2560,128]{1,0:T(8,128)} custom-call(s32[1]{0:T(128)} %bitcast.1.half_ref, bf16[256,3072]{1,0:T(8,128)(2,1)S(1)} %get-tuple-element.40.x_ref, bf16[3,256,384]{2,1,0:T(8,128)(2,1)S(1)} %get-tuple-element.41.grads_ref, bf16[3,3072,384]{2,1,0:T(8,128)(2,1)S(1)} %get-tuple-element.42.err_in_ref, f32[3,64,384]{2,1,0:T(8,128)S(1)} %copy-done.2, ...), custom_call_target="tpu_custom_call" | custom-call | flops 3000000000 | bytes 9000000 | tf_op jit(solution)/shard_map/left_keep/pallas_call | solution.py:261
  16.6 11.5 %all-to-all-start = ((f32[64,40,128]{2,1,0:T(8,128)}), f32[64,40,128]{2,1,0:T(8,128)S(1)}, u32[]{:S(2)}, u32[]{:S(2)}) async-start(f32[64,40,128]{2,1,0:T(8,128)} %bitcast.4), calls=%async_computation | async-start | bytes 2621440 | tf_op jit(solution)/shard_map/all_to_all | solution.py:776
  28.1 4.8 %turned.1.turned_hbm = bf16[3072,256]{1,0:T(8,128)(2,1)} custom-call(bf16[256,3072]{1,0:T(8,128)(2,1)} %x_hbm.3), custom_call_target="tpu_custom_call" | custom-call | flops 3000000000 | bytes 9000000 | tf_op jit(solution)/shard_map/turned/pallas_call | solution.py:294
  33.0 16.9 %all-to-all-done.received_ref = f32[64,40,128]{2,1,0:T(8,128)S(1)} async-done(((f32[64,40,128]{2,1,0:T(8,128)}), f32[64,40,128]{2,1,0:T(8,128)S(1)}, u32[]{:S(2)}, u32[]{:S(2)}) %all-to-all-start) | async-done | bytes 1310752 | tf_op jit(solution)/shard_map/all_to_all | solution.py:776
  50.0 25.0 %all_to_all.20 = f32[64,40,128]{2,1,0:T(8,128)S(1)} all-to-all(f32[64,40,128]{2,1,0:T(8,128)S(1)} %answer_left.1), channel_id=1, replica_groups=mesh['x'=4,'y'=4,'z'=4,'c'=2] {'x','y','z'}, dimensions={0} | all-to-all | bytes 2621440 | tf_op jit(solution)/shard_map/all_to_all | solution.py:779
  75.2 4.0 %right_out.1 = (f32[832,128]{1,0:T(8,128)S(1)}, f32[768,128]{1,0:T(8,128)S(1)}) custom-call(s32[2]{0:T(128)S(1)} %pad_add_fusion.place_ref, f32[192,128]{1,0:T(8,128)S(1)} %slice.40.left_out_ref, bf16[256,384]{1,0:T(8,128)(2,1)S(1)} %get-tuple-element.44.hid_ref.refs_6_, bf16[256,3072]{1,0:T(8,128)(2,1)} %refs_7_.1, bf16[384,3072]{1,0:T(8,128)(2,1)} %bitcast.23), custom_call_target="tpu_custom_call" | custom-call | flops 3000000000 | bytes 9000000 | tf_op jit(solution)/shard_map/right_out/pallas_call | solution.py:386
  79.8 3.6 %gram.1 = (f32[192,192]{1,0:T(8,128)S(1)}, bf16[256,1536]{1,0:T(8,128)(2,1)S(1)}, bf16[3,1536,384]{2,1,0:T(8,128)(2,1)S(1)}) custom-call(s32[1]{0:T(128)} %bitcast.1.half_ref, f32[2560,128]{1,0:T(8,128)S(1)} %bitcast.13, f32[2560,128]{1,0:T(8,128)S(1)} %collective-permute-done.1.other_ref, bf16[256,3072]{1,0:T(8,128)(2,1)} %x_hbm.3, ...), custom_call_target="tpu_custom_call" | custom-call | flops 3000000000 | bytes 9000000 | tf_op jit(solution)/shard_map/gram/pallas_call | solution.py:514
  83.5 0.9 collective-permute-start.5
  84.4 1.8 %collective-permute-start.3 = (f32[256,128]{1,0:T(8,128)S(1)}, f32[256,128]{1,0:T(8,128)S(1)}, u32[]{:S(2)}, u32[]{:S(2)}) collective-permute-start(f32[256,128]{1,0:T(8,128)S(1)} %get-tuple-element.81), channel_id=1, source_target_pairs={{0,4},{2,6},{4,0},{6,2},{1,5},{3,7},{5,1},{7,3},{8,12},{10,14},{12... | collective-permute-start | bytes 393224 | tf_op jit(solution)/shard_map/ppermute | solution.py:790
  86.3 3.3 %right_own.1 = (f32[3,64,384]{2,1,0:T(8,128)S(1)}, f32[192,256]{1,0:T(8,128)S(1)}, bf16[256,1536]{1,0:T(8,128)(2,1)S(1)}, bf16[3,1536,384]{2,1,0:T(8,128)(2,1)S(1)}) custom-call(s32[1]{0:T(128)S(6)} %sub.3.half_ref, f32[2560,128]{1,0:T(8,128)S(1)} %bitcast.14, bf16[256,1536]{1,0:T(8,128)(2,1)S(1)} %get-tuple-element.49.x_ref, ...), custom_call_target="tpu_custom_call" | custom-call | flops 3000000000 | bytes 9000000 | tf_op jit(solution)/shard_map/right_own/pallas_call | solution.py:444
  89.6 1.5 %right_other.1.right_ref = f32[576,128]{1,0:T(8,128)S(1)} custom-call(f32[2560,128]{1,0:T(8,128)S(1)} %collective-permute-done.1.other_ref, f32[3,64,384]{2,1,0:T(8,128)S(1)} %get-tuple-element.51.right_ref, f32[192,256]{1,0:T(8,128)S(1)} %get-tuple-element.52.token_ref, bf16[256,1536]{1,0:T(8,128)(2,1)S(1)} %get-tuple-element.53.x_ref, ...), custom_call_target="tpu_custom_call" | custom-call | flops 4000000000 | bytes 12000000 | tf_op jit(solution)/shard_map/right_other/pallas_call | solution.py:472
  91.1 1.2 collective-permute-done.3.first_ref
  92.3 1.6 %collective-permute-done.4.second_ref = f32[256,128]{1,0:T(8,128)S(1)} collective-permute-done((f32[256,128]{1,0:T(8,128)S(1)}, f32[256,128]{1,0:T(8,128)S(1)}, u32[]{:S(2)}, u32[]{:S(2)}) %collective-permute-start.4) | collective-permute-done | bytes 131104 | tf_op jit(solution)/shard_map/ppermute | solution.py:790
  93.9 0.8 join.1
  94.7 3.6 %all-to-all-start.2 = ((f32[16,48,128]{2,1,0:T(8,128)}), f32[16,48,128]{2,1,0:T(8,128)S(1)}, u32[]{:S(2)}, u32[]{:S(2)}) async-start(f32[16,48,128]{2,1,0:T(8,128)} %bitcast.7), calls=%async_computation.2 | async-start | bytes 786432 | tf_op jit(solution)/shard_map/all_to_all | solution.py:794
  98.2 6.0 %invert.1 = (f32[4,64,128]{2,1,0:T(8,128)S(1)}, f32[64,384]{1,0:T(8,128)S(1)}) custom-call(f32[192,192]{1,0:T(8,128)S(1)} %get-tuple-element.60.gram_in_ref, f32[192,128]{1,0:T(8,128)S(1)} %slice.40.left_out_ref, f32[64,128]{1,0:T(8,128)S(1)} %get-tuple-element.61.gram_out_ref), custom_call_target="tpu_custom_call" | custom-call | flops 10000000000 | bytes 30000000 | tf_op jit(solution)/shard_map/invert/pallas_call | solution.py:562
  104.9 3.3 %all-to-all-done.2.received_ref = f32[16,48,128]{2,1,0:T(8,128)S(1)} async-done(((f32[16,48,128]{2,1,0:T(8,128)}), f32[16,48,128]{2,1,0:T(8,128)S(1)}, u32[]{:S(2)}, u32[]{:S(2)}) %all-to-all-start.2) | async-done | bytes 393248 | tf_op jit(solution)/shard_map/all_to_all | solution.py:794
  108.2 0.8 answer_right.1
  109.0 3.9 %all-to-all-start.3 = ((f32[16,48,128]{2,1,0:T(8,128)}), f32[16,48,128]{2,1,0:T(8,128)S(1)}, u32[]{:S(2)}, u32[]{:S(2)}) async-start(f32[16,48,128]{2,1,0:T(8,128)} %answer_right.1), calls=%async_computation.3 | async-start | bytes 786432 | tf_op jit(solution)/shard_map/all_to_all | solution.py:799
  112.9 4.8 %turn.1.ortho_hbm = bf16[3,3072,128]{2,1,0:T(8,128)(2,1)} custom-call(s32[1]{0:T(128)} %bitcast.1.half_ref, f32[2560,128]{1,0:T(8,128)S(1)} %bitcast.15, f32[2560,128]{1,0:T(8,128)S(1)} %collective-permute-done.1.other_ref, f32[4,64,128]{2,1,0:T(8,128)S(1)} %get-tuple-element.67.inverse_ref.refs_4_), custom_call_target="tpu_custom_call" | custom-call | flops 6000000000 | bytes 18000000 | tf_op jit(solution)/shard_map/turn/pallas_call | solution.py:597
  117.8 4.6 %all-to-all-done.3 = f32[16,48,128]{2,1,0:T(8,128)S(1)} async-done(((f32[16,48,128]{2,1,0:T(8,128)}), f32[16,48,128]{2,1,0:T(8,128)S(1)}, u32[]{:S(2)}, u32[]{:S(2)}) %all-to-all-start.3) | async-done | bytes 393248 | tf_op jit(solution)/shard_map/all_to_all | solution.py:799
  122.4 1.3 collective-permute-done.6
  124.1 1.8 %collective-permute-start.8 = (f32[384,128]{1,0:T(8,128)S(1)}, f32[384,128]{1,0:T(8,128)S(1)}, u32[]{:S(2)}, u32[]{:S(2)}) collective-permute-start(f32[384,128]{1,0:T(8,128)S(1)} %pad_maximum_fusion.4.refs_0_), channel_id=1, source_target_pairs={{0,4},{2,6},{4,0},{6,2},{1,5},{3,7},{5,1},{7,3},{8,12},{10,14},{12... | collective-permute-start | bytes 589832 | tf_op jit(solution)/shard_map/ppermute | solution.py:805
  125.9 1.3 collective-permute-start.7
  127.2 1.1 copy-done.1
  128.3 0.9 copy-done.7
  129.2 9.0 %rest_in.1 = (bf16[3,3072,384]{2,1,0:T(8,128)(2,1)}, f32[3,64,384]{2,1,0:T(8,128)}) custom-call(f32[768,128]{1,0:T(8,128)S(1)} %bitcast.17, f32[4,64,128]{2,1,0:T(8,128)S(1)} %copy-done.7, bf16[3,256,384]{2,1,0:T(8,128)(2,1)S(1)} %copy-done.1, bf16[3072,256]{1,0:T(8,128)(2,1)} %turned.1.turned_hbm, bf16[3,3072,128]{2,1,0:T(8,128)(2,1)} %turn.1.ortho_hbm, ...), custom_call_target="tpu_custom_call" | custom-call | flops 10000000000 | bytes 30000000 | tf_op jit(solution)/shard_map/rest_in/pallas_call | solution.py:646
  138.2 5.8 %rest_out.1 = (bf16[384,3072]{1,0:T(8,128)(2,1)}, f32[64,3072]{1,0:T(8,128)}) custom-call(s32[2]{0:T(128)S(1)} %pad_add_fusion.place_ref, f32[384,128]{1,0:T(8,128)S(1)} %pad_maximum_fusion.4.refs_0_, f32[384,128]{1,0:T(8,128)S(1)} %collective-permute-done.7.refs_1_, f32[384,128]{1,0:T(8,128)S(1)} %collective-permute-done.8.refs_2_, ...), custom_call_target="tpu_custom_call" | custom-call | flops 6000000000 | bytes 18000000 | tf_op jit(solution)/shard_map/rest_out/pallas_call | solution.py:730
  (39 shorter events, 2.3 us)
Async XLA Ops:
  0.6 8.6 %copy-start.2 = (f32[3,64,384]{2,1,0:T(8,128)S(1)}, f32[3,64,384]{2,1,0:T(8,128)}, u32[]{:S(2)}) copy-start(f32[3,64,384]{2,1,0:T(8,128)} %basis_in_ref.3) | copy-start | bytes 884740
  9.2 65.9 %copy-start.4 = (bf16[256,384]{1,0:T(8,128)(2,1)}, bf16[256,384]{1,0:T(8,128)(2,1)S(1)}, u32[]{:S(2)}) copy-start(bf16[256,384]{1,0:T(8,128)(2,1)S(1)} %get-tuple-element.44.hid_ref.refs_6_) | copy-start | bytes 589828
  9.3 80.4 %copy-start = (bf16[3,256,384]{2,1,0:T(8,128)(2,1)}, bf16[3,256,384]{2,1,0:T(8,128)(2,1)S(1)}, u32[]{:S(2)}) copy-start(bf16[3,256,384]{2,1,0:T(8,128)(2,1)S(1)} %get-tuple-element.41.grads_ref) | copy-start | bytes 1769476
  9.3 1.8 %copy-start.3 = (f32[64,3072]{1,0:T(8,128)S(1)}, f32[64,3072]{1,0:T(8,128)}, u32[]{:S(2)}) copy-start(f32[64,3072]{1,0:T(8,128)} %basis_out_ref.1) | copy-start | bytes 2359300
  10.9 2.9 %collective-permute-start = (f32[2304,128]{1,0:T(8,128)S(1)}, f32[2304,128]{1,0:T(8,128)S(1)}, u32[]{:S(2)}, u32[]{:S(2)}) collective-permute-start(f32[2304,128]{1,0:T(8,128)S(1)} %left_send.1), channel_id=1, source_target_pairs={{0,1},{1,0},{2,3},{3,2},{4,5},{5,4},{6,7},{7,6},{8,9},{9,8},{10,11... | collective-permute-start | bytes 3538952 | tf_op jit(solution)/shard_map/ppermute | solution.py:771
  16.6 33.3 %all-to-all-start = ((f32[64,40,128]{2,1,0:T(8,128)}), f32[64,40,128]{2,1,0:T(8,128)S(1)}, u32[]{:S(2)}, u32[]{:S(2)}) async-start(f32[64,40,128]{2,1,0:T(8,128)} %bitcast.4), calls=%async_computation | async-start | bytes 2621440 | tf_op jit(solution)/shard_map/all_to_all | solution.py:776
  75.1 4.7 %collective-permute-start.1 = (f32[2560,128]{1,0:T(8,128)S(1)}, f32[2560,128]{1,0:T(8,128)S(1)}, u32[]{:S(2)}, u32[]{:S(2)}) collective-permute-start(f32[2560,128]{1,0:T(8,128)S(1)} %bitcast.11), channel_id=1, source_target_pairs={{0,1},{1,0},{2,3},{3,2},{4,5},{5,4},{6,7},{7,6},{8,9},{9,8},{10,11... | collective-permute-start | bytes 3932168 | tf_op jit(solution)/shard_map/ppermute | solution.py:780
  79.2 4.2 %collective-permute-start.2 = (f32[832,128]{1,0:T(8,128)S(1)}, f32[832,128]{1,0:T(8,128)S(1)}, u32[]{:S(2)}, u32[]{:S(2)}) collective-permute-start(f32[832,128]{1,0:T(8,128)S(1)} %get-tuple-element.56), channel_id=1, source_target_pairs={{0,1},{1,0},{2,3},{3,2},{4,5},{5,4},{6,7},{7,6},{8,9},{9,8},{10,11... | collective-permute-start | bytes 1277960 | tf_op jit(solution)/shard_map/ppermute | solution.py:784
  83.5 7.6 %collective-permute-start.5 = (f32[256,128]{1,0:T(8,128)S(1)}, f32[256,128]{1,0:T(8,128)S(1)}, u32[]{:S(2)}, u32[]{:S(2)}) collective-permute-start(f32[256,128]{1,0:T(8,128)S(1)} %get-tuple-element.80), channel_id=1, source_target_pairs={{0,6},{2,0},{4,2},{6,4},{1,7},{3,1},{5,3},{7,5},{8,14},{10,8},{12,... | collective-permute-start | bytes 393224 | tf_op jit(solution)/shard_map/ppermute | solution.py:790
  84.4 7.9 %collective-permute-start.3 = (f32[256,128]{1,0:T(8,128)S(1)}, f32[256,128]{1,0:T(8,128)S(1)}, u32[]{:S(2)}, u32[]{:S(2)}) collective-permute-start(f32[256,128]{1,0:T(8,128)S(1)} %get-tuple-element.81), channel_id=1, source_target_pairs={{0,4},{2,6},{4,0},{6,2},{1,5},{3,7},{5,1},{7,3},{8,12},{10,14},{12... | collective-permute-start | bytes 393224 | tf_op jit(solution)/shard_map/ppermute | solution.py:790
  86.2 7.7 %collective-permute-start.4 = (f32[256,128]{1,0:T(8,128)S(1)}, f32[256,128]{1,0:T(8,128)S(1)}, u32[]{:S(2)}, u32[]{:S(2)}) collective-permute-start(f32[256,128]{1,0:T(8,128)S(1)} %get-tuple-element.82), channel_id=1, source_target_pairs={{0,2},{2,4},{4,6},{6,0},{1,3},{3,5},{5,7},{7,1},{8,10},{10,12},{12... | collective-permute-start | bytes 393224 | tf_op jit(solution)/shard_map/ppermute | solution.py:790
  94.7 13.5 %all-to-all-start.2 = ((f32[16,48,128]{2,1,0:T(8,128)}), f32[16,48,128]{2,1,0:T(8,128)S(1)}, u32[]{:S(2)}, u32[]{:S(2)}) async-start(f32[16,48,128]{2,1,0:T(8,128)} %bitcast.7), calls=%async_computation.2 | async-start | bytes 786432 | tf_op jit(solution)/shard_map/all_to_all | solution.py:794
  104.3 0.6 copy-start.8
  104.9 8.0 %copy-start.6 = (f32[4,64,128]{2,1,0:T(8,128)}, f32[4,64,128]{2,1,0:T(8,128)S(1)}, u32[]{:S(2)}) copy-start(f32[4,64,128]{2,1,0:T(8,128)S(1)} %get-tuple-element.67.inverse_ref.refs_4_) | copy-start | bytes 393220
  109.0 13.4 %all-to-all-start.3 = ((f32[16,48,128]{2,1,0:T(8,128)}), f32[16,48,128]{2,1,0:T(8,128)S(1)}, u32[]{:S(2)}, u32[]{:S(2)}) async-start(f32[16,48,128]{2,1,0:T(8,128)} %answer_right.1), calls=%async_computation.3 | async-start | bytes 786432 | tf_op jit(solution)/shard_map/all_to_all | solution.py:799
  122.3 1.4 collective-permute-start.6
  123.7 14.5 %copy-start.5 = (bf16[256,384]{1,0:T(8,128)(2,1)S(1)}, bf16[256,384]{1,0:T(8,128)(2,1)}, u32[]{:S(2)}) copy-start(bf16[256,384]{1,0:T(8,128)(2,1)} %copy-done.4) | copy-start | bytes 589828
  123.7 14.5 %copy-start.9 = (f32[64,384]{1,0:T(8,128)S(1)}, f32[64,384]{1,0:T(8,128)}, u32[]{:S(2)}) copy-start(f32[64,384]{1,0:T(8,128)} %copy-done.8) | copy-start | bytes 294916
  123.8 14.4 %collective-permute-start.9 = (f32[384,128]{1,0:T(8,128)S(1)}, f32[384,128]{1,0:T(8,128)S(1)}, u32[]{:S(2)}, u32[]{:S(2)}) collective-permute-start(f32[384,128]{1,0:T(8,128)S(1)} %pad_maximum_fusion.4.refs_0_), channel_id=1, source_target_pairs={{0,6},{2,0},{4,2},{6,4},{1,7},{3,1},{5,3},{7,5},{8,14},{10,8},{12,... | collective-permute-start | bytes 589832 | tf_op jit(solution)/shard_map/ppermute | solution.py:805
  124.1 14.1 %collective-permute-start.8 = (f32[384,128]{1,0:T(8,128)S(1)}, f32[384,128]{1,0:T(8,128)S(1)}, u32[]{:S(2)}, u32[]{:S(2)}) collective-permute-start(f32[384,128]{1,0:T(8,128)S(1)} %pad_maximum_fusion.4.refs_0_), channel_id=1, source_target_pairs={{0,4},{2,6},{4,0},{6,2},{1,5},{3,7},{5,1},{7,3},{8,12},{10,14},{12... | collective-permute-start | bytes 589832 | tf_op jit(solution)/shard_map/ppermute | solution.py:805
  125.9 12.3 %collective-permute-start.7 = (f32[384,128]{1,0:T(8,128)S(1)}, f32[384,128]{1,0:T(8,128)S(1)}, u32[]{:S(2)}, u32[]{:S(2)}) collective-permute-start(f32[384,128]{1,0:T(8,128)S(1)} %pad_maximum_fusion.4.refs_0_), channel_id=1, source_target_pairs={{0,2},{2,4},{4,6},{6,0},{1,3},{3,5},{5,7},{7,1},{8,10},{10,12},{12... | collective-permute-start | bytes 589832 | tf_op jit(solution)/shard_map/ppermute | solution.py:805
  127.2 1.1 copy-start.1
  128.3 0.9 copy-start.7

commit v6 on v5

--- a/solution.py
+++ b/solution.py
@@ -34,6 +34,7 @@
 bf16 = jnp.bfloat16
 EXACT = lax.Precision.HIGHEST
 VMEM = 24 * 1024 * 1024
+VMEM_LAST = 40 * 1024 * 1024
 
 
 def cost(us):
@@ -50,10 +51,6 @@
 
 def tn(a, b):
     return lax.dot_general(a, b, (((0,), (0,)), ((), ())), preferred_element_type=f32)
-
-
-def exact_nn(a, b):
-    return lax.dot_general(a, b, (((1,), (0,)), ((), ())), precision=EXACT, preferred_element_type=f32)
 
 
 def exact_nt(a, b):
@@ -63,6 +60,12 @@
 def split2(a):
     high = a.astype(bf16)
     return high, (a - high.astype(f32)).astype(bf16)
+
+
+def thrice(a, b):
+    a_high, a_low = split2(a)
+    b_high, b_low = split2(b)
+    return nn(jnp.concatenate([a_high, a_high, a_low], axis=1), jnp.concatenate([b_high, b_low, b_high], axis=0))
 
 
 def split3(a):
@@ -250,21 +253,34 @@
         left_ref[at : at + RANK, :] = tile
 
 
-def left_keep_kernel(half_ref, x_ref, grads_ref, err_in_ref, basis_in_ref, arrived_ref, left_out_ref, rows_ref):
-    rows_ref[L_ROWS : L_ROWS + LO_ROWS, :] = left_out_ref[...]
-    rows_ref[L_ROWS + LO_ROWS :, :] = jnp.zeros((ROWS1 - L_ROWS - LO_ROWS, 128), f32)
-    for at, tile in left_tiles(half_ref, x_ref, grads_ref, err_in_ref, basis_in_ref):
-        rows_ref[at : at + RANK, :] = tile + arrived_ref[at : at + RANK, :]
+def left_keep_kernel(half_ref, x_ref, grads_ref, err_in_ref, basis_in_ref, arrived_ref, left_out_ref, rows_hbm, rows_scr, sem):
+    parts = [slice(L_STEP * step, L_STEP * (step + 1)) for step in range(STEPS)] + [slice(L_ROWS, ROWS1)]
+    copies = [pltpu.make_async_copy(rows_scr.at[part], rows_hbm.at[part], sem.at[i]) for i, part in enumerate(parts)]
+    rows_scr[L_ROWS : L_ROWS + LO_ROWS, :] = left_out_ref[...]
+    rows_scr[L_ROWS + LO_ROWS :, :] = jnp.zeros((ROWS1 - L_ROWS - LO_ROWS, 128), f32)
+    copies[STEPS].start()
+    for i, (at, tile) in enumerate(left_tiles(half_ref, x_ref, grads_ref, err_in_ref, basis_in_ref)):
+        rows_scr[at : at + RANK, :] = tile + arrived_ref[at : at + RANK, :]
+        if (i + 1) % (3 * CT) == 0:
+            copies[i // (3 * CT)].start()
+    for copy in copies:
+        copy.wait()
 
 
 def left(half, inputs, grads, err_in, basis_in, *arrived):
+    keep = {}
+    if arrived:
+        keep = dict(
+            out_specs=ANY, scratch_shapes=[pltpu.VMEM((ROWS1, 128), f32), pltpu.SemaphoreType.DMA((STEPS + 1,))]
+        )
     return pl.pallas_call(
         left_keep_kernel if arrived else left_send_kernel,
         in_specs=[pl.BlockSpec(memory_space=pltpu.SMEM)] + [pl.BlockSpec(memory_space=pltpu.VMEM)] * (4 + len(arrived)),
-        out_shape=jax.ShapeDtypeStruct((ROWS1 if arrived else L_ROWS, 128), f32),
+        out_shape=pltpu.HBM((ROWS1, 128), f32) if arrived else jax.ShapeDtypeStruct((L_ROWS, 128), f32),
         cost_estimate=cost(3),
         compiler_params=pltpu.CompilerParams(vmem_limit_bytes=VMEM),
         name="left_keep" if arrived else "left_send",
+        **keep,
     )(half, *held(inputs), grads, *held(err_in), basis_in, *arrived)
 
 
@@ -286,21 +302,44 @@
     )(*held(grad_y), hidden, *held(err_out), basis_out)
 
 
-def turned_kernel(x_ref, turned_ref):
+def ahead_kernel(x_ref, grads_ref, err_in_ref, hid_ref, gy_ref, err_out_ref, x_later_ref, turned_ref, moment_in_ref,
+                 moment_out_ref):
     turned_ref[...] = x_ref[...].astype(f32).T.astype(bf16)
-
-
-def turned(inputs):
-    return pl.pallas_call(
-        turned_kernel,
-        grid=(D // TILE,),
-        in_specs=[pl.BlockSpec((TOK, TILE), lambda j: (0, j))],
-        out_specs=pl.BlockSpec((TILE, TOK), lambda j: (j, 0)),
-        out_shape=pltpu.HBM((D, TOK), bf16),
-        cost_estimate=cost(3),
-        compiler_params=pltpu.CompilerParams(vmem_limit_bytes=VMEM),
-        name="turned",
-    )(*streamed(inputs))
+    later = x_later_ref[...].astype(f32).T.astype(bf16)
+    moments = nn(later, jnp.concatenate([grads_ref[p] for p in range(3)], axis=1))
+    for p in range(3):
+        moment_in_ref[p] = moments[:, COLS * p : COLS * (p + 1)] + err_in_ref[p].astype(f32)
+    moment_out_ref[...] = tn(hid_ref[...], gy_ref[...]) + err_out_ref[...].astype(f32)
+
+
+def ahead(inputs, grads, err_in, hidden, grad_y, err_out):
+    wide_tile = D // STEPS
+    return pl.pallas_call(
+        ahead_kernel,
+        grid=(STEPS,),
+        in_specs=[
+            pl.BlockSpec((TOK, TILE), lambda j: (0, j)),
+            pl.BlockSpec((3, TOK, COLS), lambda j: (0, 0, 0)),
+            pl.BlockSpec((3, TILE, COLS), lambda j: (0, j + STEPS, 0)),
+            pl.BlockSpec((TOK, COLS), lambda j: (0, 0)),
+            pl.BlockSpec((TOK, wide_tile), lambda j: (0, j)),
+            pl.BlockSpec((COLS, wide_tile), lambda j: (0, j)),
+            pl.BlockSpec((TOK, TILE), lambda j: (0, j + STEPS)),
+        ],
+        out_specs=[
+            pl.BlockSpec((TILE, TOK), lambda j: (j, 0)),
+            pl.BlockSpec((3, TILE, COLS), lambda j: (0, j, 0)),
+            pl.BlockSpec((COLS, wide_tile), lambda j: (0, j)),
+        ],
+        out_shape=[
+            pltpu.HBM((HALF, TOK), bf16),
+            pltpu.HBM((3, HALF, COLS), f32),
+            pltpu.HBM((COLS, D), f32),
+        ],
+        cost_estimate=cost(9),
+        compiler_params=pltpu.CompilerParams(vmem_limit_bytes=VMEM),
+        name="ahead",
+    )(*streamed(inputs, grads, err_in, hidden, grad_y, err_out, inputs))
 
 
 def wide(block, rows):
@@ -371,10 +410,13 @@
     factor = stacked(left_out)
     both = jnp.concatenate([factor, stacked(folded(nt(factor, hid_ref[...])))], axis=1)
     send_ref[RO_ROWS:, :] = jnp.concatenate([exact_nt(left_out, left_out), jnp.zeros((RANK, RANK), f32)], axis=1)
-    for j in range(8):
-        for copy in copies[j]:
-            copy.wait()
-        part = folded(nn(both, jnp.concatenate([err_out_scr[j], gy_scr[j]], axis=0)))
+    for j in range(0, 8, 2):
+        for pair in copies[j : j + 2]:
+            for copy in pair:
+                copy.wait()
+        err_out = jnp.concatenate([err_out_scr[j], err_out_scr[j + 1]], axis=1)
+        gy = jnp.concatenate([gy_scr[j], gy_scr[j + 1]], axis=1)
+        part = folded(nn(both, jnp.concatenate([err_out, gy], axis=0)))
         ref = send_ref if j < 4 else keep_ref
         for i, tile in enumerate(tiles_of(part)):
             at = (j % 4) * PIECE + i * RANK
@@ -555,7 +597,7 @@
     diagonal = jnp.sum(jnp.where(lane == sub, work, 0.0), axis=2, keepdims=True)
     inverse = work * lax.rsqrt(diagonal)
     inverse_ref[...] = inverse
-    ortho_out_ref[...] = exact_nn(inverse[3, :, RANK:], wide(left_out_ref[...], RANK))
+    ortho_out_ref[...] = thrice(inverse[3, :, RANK:], wide(left_out_ref[...], RANK))
 
 
 def invert(gram_in, left_out_sum, gram_out):
@@ -577,7 +619,7 @@
     def turn(ref):
         rows = wide(ref[...], 3 * RANK)
         for p in range(3):
-            high, low = split2(exact_nn(inverse_ref[p, :, RANK:], rows[RANK * p : RANK * (p + 1)]))
+            high, low = split2(thrice(inverse_ref[p, :, RANK:], rows[RANK * p : RANK * (p + 1)]))
             both = jnp.concatenate([high.astype(f32), low.astype(f32)], axis=0)
             ortho_ref[p] = both.T.astype(bf16)
 
@@ -613,83 +655,95 @@
     )(half, own, other, inverse)
 
 
-def rest_in_kernel(summed_in_ref, inverse_ref, grads_ref, turned_hbm, ortho_hbm, err_in_hbm, rest_in_ref,
-                   factor_in_ref, in_scr, turned_scr, ortho_scr, err_in_scr, sem):
-    step = pl.program_id(0)
-    turned_ref, ortho_ref, err_in_ref = fetched(
-        step,
-        D // TILE,
-        lambda j: j,
-        TILE,
-        [(0, turned_hbm), (1, ortho_hbm), (1, err_in_hbm)],
-        [turned_scr, ortho_scr, err_in_scr],
-        sem,
-    )
-
-    @pl.when(step == 0)
-    def _():
+def rest_in_kernel(summed_in_ref, inverse_hbm, grads_hbm, turned_hbm, err_in_hbm, ortho_hbm, moment_hbm, rest_hbm,
+                   factor_in_ref, inverse_scr, grads_scr, turned_scr, err_in_scr, ortho_scr, moment_scr, rest_scr, in_sem,
+                   out_sem):
+    def rows(j):
+        return slice(TILE * j, TILE * (j + 1))
+
+    tiles = range(2 * STEPS)
+    first = [
+        pltpu.make_async_copy(inverse_hbm, inverse_scr, in_sem.at[0, len(tiles)]),
+        pltpu.make_async_copy(grads_hbm, grads_scr, in_sem.at[1, len(tiles)]),
+    ]
+    into = [[pltpu.make_async_copy(ortho_hbm.at[:, rows(j)], ortho_scr.at[j], in_sem.at[0, j])] for j in tiles]
+    for j in range(STEPS):
+        into[j].append(pltpu.make_async_copy(turned_hbm.at[rows(j)], turned_scr.at[j], in_sem.at[1, j]))
+        into[j].append(pltpu.make_async_copy(err_in_hbm.at[:, rows(j)], err_in_scr.at[j], in_sem.at[2, j]))
+        into[j + STEPS].append(
+            pltpu.make_async_copy(moment_hbm.at[:, rows(j)], moment_scr.at[j], in_sem.at[1, j + STEPS])
+        )
+    out = [pltpu.make_async_copy(rest_scr.at[j], rest_hbm.at[:, rows(j)], out_sem.at[j]) for j in tiles]
+    for copy in first:
+        copy.start()
+    for group in into:
+        for copy in group:
+            copy.start()
+    for copy in first:
+        copy.wait()
+    grads = jnp.concatenate([grads_scr[p] for p in range(3)], axis=1)
+    weights = []
+    for p in range(3):
+        right = wide(summed_in_ref[HEADS * RANK * p : HEADS * RANK * (p + 1), :], RANK) * (1.0 / N_DP)
+        factor = thrice(inverse_scr[p, :, RANK:], right)
+        factor_in_ref[p] = factor
+        high, low = split2(-factor)
+        weights.append(jnp.concatenate([high, high, low, jnp.zeros_like(low)], axis=0))
+    for j in tiles:
+        for copy in into[j]:
+            copy.wait()
+        moments = nn(turned_scr[j], grads) if j < STEPS else None
         for p in range(3):
-            right = wide(summed_in_ref[pl.ds(HEADS * RANK * p, HEADS * RANK), :], RANK) * (1.0 / N_DP)
-            factor = exact_nn(inverse_ref[p, :, RANK:], right)
-            factor_in_ref[p] = factor
-            high, low = split2(-factor)
-            in_scr[p] = jnp.concatenate([high, high, low, jnp.zeros_like(low)], axis=0)
-
-    moments = nn(turned_ref[...], jnp.concatenate([grads_ref[p] for p in range(3)], axis=1))
-    for p in range(3):
-        moment = moments[:, COLS * p : COLS * (p + 1)] + err_in_ref[p].astype(f32)
-        both = jnp.concatenate([ortho_ref[p], ortho_ref[p]], axis=1)
-        rest_in_ref[p] = (moment + nn(both, in_scr[p])).astype(bf16)
-
-
-def rest_in(summed, inverse, turned, ortho_in, grads, err_in):
+            if j < STEPS:
+                moment = moments[:, COLS * p : COLS * (p + 1)] + err_in_scr[j, p].astype(f32)
+            else:
+                moment = moment_scr[j - STEPS, p]
+            both = jnp.concatenate([ortho_scr[j, p], ortho_scr[j, p]], axis=1)
+            rest_scr[j, p] = (moment + nn(both, weights[p])).astype(bf16)
+        out[j].start()
+    for copy in out:
+        copy.wait()
+
+
+def rest_in(summed, inverse, grads, turned, err_in, ortho_in, moment_in):
+    whole = pl.BlockSpec(memory_space=pltpu.VMEM)
+    tiles = 2 * STEPS
     return pl.pallas_call(
         rest_in_kernel,
-        grid=(D // TILE,),
-        in_specs=[
-            pl.BlockSpec((RI_ROWS, 128), lambda j: (0, 0)),
-            pl.BlockSpec((4, RANK, 128), lambda j: (0, 0, 0)),
-            pl.BlockSpec((3, TOK, COLS), lambda j: (0, 0, 0)),
-            ANY,
-            ANY,
-            ANY,
-        ],
-        out_specs=[
-            pl.BlockSpec((3, TILE, COLS), lambda j: (0, j, 0)),
-            pl.BlockSpec((3, RANK, COLS), lambda j: (0, 0, 0)),
-        ],
+        in_specs=[whole] + [ANY] * 6,
+        out_specs=[ANY, whole],
         scratch_shapes=[
-            pltpu.VMEM((3, 4 * RANK, COLS), bf16),
-            pltpu.VMEM((D // TILE, TILE, TOK), bf16),
-            pltpu.VMEM((D // TILE, 3, TILE, 128), bf16),
-            pltpu.VMEM((D // TILE, 3, TILE, COLS), bf16),
-            pltpu.SemaphoreType.DMA((3, D // TILE)),
+            pltpu.VMEM((4, RANK, 128), f32),
+            pltpu.VMEM((3, TOK, COLS), bf16),
+            pltpu.VMEM((STEPS, TILE, TOK), bf16),
+            pltpu.VMEM((STEPS, 3, TILE, COLS), bf16),
+            pltpu.VMEM((tiles, 3, TILE, 128), bf16),
+            pltpu.VMEM((STEPS, 3, TILE, COLS), f32),
+            pltpu.VMEM((tiles, 3, TILE, COLS), bf16),
+            pltpu.SemaphoreType.DMA((3, tiles + 1)),
+            pltpu.SemaphoreType.DMA((tiles,)),
         ],
         out_shape=[
-            jax.ShapeDtypeStruct((3, D, COLS), bf16),
+            pltpu.HBM((3, D, COLS), bf16),
             jax.ShapeDtypeStruct((3, RANK, COLS), f32),
         ],
-        cost_estimate=cost(10),
-        compiler_params=pltpu.CompilerParams(vmem_limit_bytes=VMEM),
+        cost_estimate=cost(9),
+        compiler_params=pltpu.CompilerParams(vmem_limit_bytes=VMEM_LAST),
         name="rest_in",
-    )(summed, inverse, grads, *streamed(turned, ortho_in, err_in))
+    )(summed, *streamed(inverse, grads, turned, err_in, ortho_in, moment_in))
 
 
 def rest_out_kernel(place_ref, *refs):
-    piece_refs, (inverse_ref, ortho_out_ref, hid_ref, gy_hbm, err_out_hbm) = refs[:4], refs[4:9]
-    rest_hbm, factor_hbm, gy_scr, err_out_scr, rest_scr, factor_scr, in_sem, out_sem = refs[9:]
+    piece_refs, (inverse_hbm, ortho_out_hbm, moment_hbm) = refs[:4], refs[4:7]
+    rest_hbm, factor_hbm, inverse_scr, ortho_out_scr, moment_scr, rest_scr, factor_scr, first_sem, in_sem, out_sem = refs[7:]
+    small = zip((inverse_hbm.at[3], ortho_out_hbm), (inverse_scr, ortho_out_scr))
+    first = [pltpu.make_async_copy(a, b, first_sem.at[i]) for i, (a, b) in enumerate(small)]
 
     def column(j):
         at = lax.rem(place_ref[0] + j // 4, 2) * 4 + lax.rem(place_ref[1] + 4 - j % 4, 4)
         return pl.ds(pl.multiple_of(at * COLS, COLS), COLS)
 
-    into = [
-        (
-            pltpu.make_async_copy(gy_hbm.at[:, column(j)], gy_scr.at[j], in_sem.at[0, j]),
-            pltpu.make_async_copy(err_out_hbm.at[:, column(j)], err_out_scr.at[j], in_sem.at[1, j]),
-        )
-        for j in range(8)
-    ]
+    into = [pltpu.make_async_copy(moment_hbm.at[:, column(j)], moment_scr.at[j], in_sem.at[j]) for j in range(8)]
     out = [
         (
             pltpu.make_async_copy(rest_scr.at[j], rest_hbm.at[:, column(j)], out_sem.at[0, j]),
@@ -697,27 +751,28 @@
         )
         for j in range(8)
     ]
-    for pair in into:
-        for copy in pair:
-            copy.start()
-    high, low = split2(ortho_out_ref[...])
+    for copy in first:
+        copy.start()
+    for copy in into:
+        copy.start()
+    for copy in first:
+        copy.wait()
+    high, low = split2(ortho_out_scr[...])
     stack = jnp.concatenate([high, high, low, jnp.zeros_like(low)], axis=0)
-    both = jnp.concatenate([hid_ref[...], stack], axis=0).astype(f32).T.astype(bf16)
-    inverse = inverse_ref[3, :, RANK:]
+    both = stack.astype(f32).T.astype(bf16)
+    inverse = inverse_scr[:, RANK:]
     for j in range(0, 8, 2):
         mine = slice(PIECE * (j // 4), PIECE * (j // 4 + 1))
         right = jnp.concatenate([wide(piece_refs[k % 4][mine, :], RANK) for k in (j, j + 1)], axis=1)
-        factor = exact_nn(inverse, right * (1.0 / N_DP))
+        factor = thrice(inverse, right * (1.0 / N_DP))
         high, low = split2(-factor)
         for k in (j, j + 1):
-            for copy in into[k]:
-                copy.wait()
-        gy = jnp.concatenate([gy_scr[j], gy_scr[j + 1]], axis=1)
-        total = nn(both, jnp.concatenate([gy, high, low, high, jnp.zeros_like(low)], axis=0))
+            into[k].wait()
+        total = nn(both, jnp.concatenate([high, low, high, jnp.zeros_like(low)], axis=0))
         for i, k in enumerate((j, j + 1)):
             mine = slice(COLS * i, COLS * (i + 1))
             factor_scr[k] = factor[:, mine]
-            rest_scr[k] = (total[:, mine] + err_out_scr[k].astype(f32)).astype(bf16)
+            rest_scr[k] = (total[:, mine] + moment_scr[k]).astype(bf16)
             for copy in out[k]:
                 copy.start()
     for pair in out:
@@ -725,25 +780,27 @@
             copy.wait()
 
 
-def rest_out(place, pieces, inverse, ortho_out, hidden, grad_y, err_out):
+def rest_out(place, pieces, inverse, ortho_out, moment_out):
     whole = pl.BlockSpec(memory_space=pltpu.VMEM)
     return pl.pallas_call(
         rest_out_kernel,
-        in_specs=[pl.BlockSpec(memory_space=pltpu.SMEM)] + [whole] * 7 + [ANY] * 2,
+        in_specs=[pl.BlockSpec(memory_space=pltpu.SMEM)] + [whole] * 4 + [ANY] * 3,
         out_specs=[ANY, ANY],
         scratch_shapes=[
-            pltpu.VMEM((8, TOK, COLS), bf16),
-            pltpu.VMEM((8, COLS, COLS), bf16),
+            pltpu.VMEM((RANK, 128), f32),
+            pltpu.VMEM((RANK, COLS), f32),
+            pltpu.VMEM((8, COLS, COLS), f32),
             pltpu.VMEM((8, COLS, COLS), bf16),
             pltpu.VMEM((8, RANK, COLS), f32),
-            pltpu.SemaphoreType.DMA((2, 8)),
+            pltpu.SemaphoreType.DMA((2,)),
+            pltpu.SemaphoreType.DMA((8,)),
             pltpu.SemaphoreType.DMA((2, 8)),
         ],
         out_shape=[pltpu.HBM((COLS, D), bf16), pltpu.HBM((RANK, D), f32)],
         cost_estimate=cost(6),
         compiler_params=pltpu.CompilerParams(vmem_limit_bytes=VMEM),
         name="rest_out",
-    )(place, *pieces, inverse, ortho_out, hidden, *streamed(grad_y, err_out))
+    )(place, *pieces, *streamed(inverse, ortho_out, moment_out))
 
 
 CHIP = ("x", "y", "z")
@@ -772,9 +829,9 @@
     left_out_part = left_out(near_grad_y, hidden, near_err_out, basis_out)
     rows = left(mine, near_inputs, grads, near_err_in, basis_in, arrived, left_out_part)
 
-    rows, later_inputs = lax.optimization_barrier((rows, inputs))
+    rows, hidden_now = lax.optimization_barrier((rows, hidden))
     received = lax.all_to_all(rows.reshape(CHIPS, EACH1, 128), CHIP, 0, 0)
-    inputs_turned = turned(later_inputs)
+    inputs_turned, moment_in, moment_out = ahead(inputs, grads, err_in, hidden_now, grad_y, err_out)
     received, inputs_turned = lax.optimization_barrier((received, inputs_turned))
     own = lax.all_to_all(answer_left(me[None], received), CHIP, 0, 0).reshape(ROWS1, 128)
     other = lax.ppermute(own, "c", SWAP)
@@ -803,8 +860,8 @@
     piece = summed[RI_ROWS:]
     pieces = [jnp.concatenate([piece, lax.ppermute(piece, "c", SWAP)])]
     pieces += [lax.ppermute(pieces[0], "z", ring(shift)) for shift in (1, 2, 3)]
-    new_in, factor_in = rest_in(summed, inverse, inputs_turned, ortho_in, grads, err_in)
-    new_out, factor_out = rest_out(place, pieces, inverse, ortho_out, hidden, grad_y, err_out)
+    new_in, factor_in = rest_in(summed, inverse, grads, inputs_turned, err_in, ortho_in, moment_in)
+    new_out, factor_out = rest_out(place, pieces, inverse, ortho_out, moment_out)
     return new_in[None], new_out[None], factor_in, factor_out
 
 

time: 145 us -> 143 us (0.986)
  waiting for transfers between devices: 29.7 us -> 23.7 us
  Pallas kernels: 59.5 us -> 62.9 us
  starting transfers between devices: 26 us -> 28.4 us
  local copies, waits for them, and re-layouts: 2.67 us -> 0.71 us
    pallas_call x2, Pallas kernels: 13.8 us -> 19.3 us  [the longest x1 9.74 us: ahead(): pl.pallas_call(ahead_kernel, grid=(STEPS,), in_specs=[pl.BlockSpec((TOK,...]
    all_to_all x1, waiting for transfers between devices: 16.9 us -> 12 us  [shards(): received = lax.all_to_all(rows.reshape(CHIPS, EACH1, 128), CHIP, 0, 0)]
    ppermute x3, waiting for transfers between devices: 2.78 us -> 0.42 us  [shards(): lax.ppermute(pieces[shift], 'z', ring(shift))]
    unnamed x20 -> x16, local copies, waits for them, and re-layouts: 2.63 us -> 0.67 us
    ppermute x3, starting transfers between devices: 2.81 us -> 4.63 us  [shards(): lax.ppermute(pieces[shift], 'z', ring(shift))]
  transfers between devices with their start and end apart: 13 -> 13, of which waited for: 7 -> 6; matrix products, arithmetic and copies ran while one was open for 0% -> 0% of each run, Pallas kernels for 27% -> 30%
where the time goes in v6:
time: 143 us; the launch traced here: 142 us
  Pallas kernels  62.9 us (44%)
  starting transfers between devices  28.4 us (20%)
  blocking collectives  25.3 us (18%)
  waiting for transfers between devices  23.7 us (17%)
    all_to_all x1, blocking collectives, shards(): lax.all_to_all(answer_left(me[None], received), CHIP, 0, 0)  25.3 us
    all_to_all x1, waiting for transfers between devices, shards(): received = lax.all_to_all(rows.reshape(CHIPS, EACH1, 128), CHIP, 0, 0)  12 us
    all_to_all x1, starting transfers between devices, shards(): received = lax.all_to_all(rows.reshape(CHIPS, EACH1, 128), CHIP, 0, 0)  11.5 us
    pallas_call x1, Pallas kernels, ahead(): pl.pallas_call(ahead_kernel, grid=(STEPS,), in_specs=[pl.BlockSpec((TOK,...  9.74 us
    pallas_call x1, Pallas kernels, rest_in(): pl.pallas_call(rest_in_kernel, in_specs=[whole] + [ANY] * 6, out_specs=[A...  9.55 us
    pallas_call x1, Pallas kernels, recurrence(): pl.pallas_call(recurrence_kernel, in_specs=[ANY] * len(operands), out_spe...  8.59 us
    pallas_call x1, Pallas kernels, invert(): pl.pallas_call(invert_kernel, out_shape=[jax.ShapeDtypeStruct((4, RANK, 1...  5.87 us
    pallas_call x1, Pallas kernels, rest_out(): pl.pallas_call(rest_out_kernel, in_specs=[pl.BlockSpec(memory_space=pltpu...  5.49 us
  transfers between devices with their start and end apart: 13, of which 6 were waited for; matrix products, arithmetic and copies ran while one was open for 0% of the time, Pallas kernels for 30%

profile of v6, /device:TPU:0, one launch (start us, length us, event | category | flops | bytes accessed | tf_op | source)
XLA Modules:
  0.0 142.4 jit_solution(5889366205763450292)
XLA Ops:
  0.6 8.6 %recurrence.1 = (bf16[256,384]{1,0:T(8,128)(2,1)S(1)}, bf16[3,256,384]{2,1,0:T(8,128)(2,1)S(1)}, bf16[3,3072,384]{2,1,0:T(8,128)(2,1)S(1)}, bf16[384,3072]{1,0:T...) custom-call(bf16[256,384]{1,0:T(8,128)(2,1)} %q_hbm.1, bf16[256,384]{1,0:T(8,128)(2,1)} %f_hbm.1, ...), custom_call_target="tpu_custom_call" | custom-call | flops 8000000000 | bytes 24000000 | tf_op jit(solution)/shard_map/recurrence/pallas_call | solution.py:218
  9.3 1.7 %left_send.1 = f32[2304,128]{1,0:T(8,128)S(1)} custom-call(s32[1]{0:T(128)S(6)} %sub.3.half_ref, bf16[256,3072]{1,0:T(8,128)(2,1)S(1)} %get-tuple-element.43.x_ref, bf16[3,256,384]{2,1,0:T(8,128)(2,1)S(1)} %get-tuple-element.44.grads_ref.grads_hbm, bf16[3,3072,384]{2,1,0:T(8,128)(2,1)S(1)} %get-tuple-element.45.err_in_ref, f32[3,64,384]{2,1,0:T(8,128)S(1)} %copy-done.2), custom_call_target="tpu_custom_call" | custom-call | flops 3000000000 | bytes 9000000 | tf_op jit(solution)/shard_map/left_send/pallas_call | solution.py:276
  11.1 1.9 %left_out.1.left_out_ref = f32[192,128]{1,0:T(8,128)S(1)} custom-call(bf16[256,3072]{1,0:T(8,128)(2,1)S(1)} %get-tuple-element.46.gy_ref, bf16[256,384]{1,0:T(8,128)(2,1)S(1)} %get-tuple-element.50.hid_ref, bf16[384,3072]{1,0:T(8,128)(2,1)S(1)} %get-tuple-element.48.err_out_ref, f32[64,3072]{1,0:T(8,128)S(1)} %copy-done.3), custom_call_target="tpu_custom_call" | custom-call | flops 4000000000 | bytes 12000000 | tf_op jit(solution)/shard_map/left_out/pallas_call | solution.py:296
  13.0 0.9 collective-permute-done.arrived_ref
  13.9 2.5 %left_keep.1 = f32[2560,128]{1,0:T(8,128)} custom-call(s32[1]{0:T(128)} %bitcast.1.half_ref, bf16[256,3072]{1,0:T(8,128)(2,1)S(1)} %get-tuple-element.43.x_ref, bf16[3,256,384]{2,1,0:T(8,128)(2,1)S(1)} %get-tuple-element.44.grads_ref.grads_hbm, bf16[3,3072,384]{2,1,0:T(8,128)(2,1)S(1)} %get-tuple-element.45.err_in_ref, f32[3,64,384]{2,1,0:T(8,128)S(1)} %copy-done.2, ...), custom_call_target="tpu_custom_call" | custom-call | flops 3000000000 | bytes 9000000 | tf_op jit(solution)/shard_map/left_keep/pallas_call | solution.py:276
  16.3 11.5 %all-to-all-start = ((f32[64,40,128]{2,1,0:T(8,128)}), f32[64,40,128]{2,1,0:T(8,128)S(1)}, u32[]{:S(2)}, u32[]{:S(2)}) async-start(f32[64,40,128]{2,1,0:T(8,128)} %bitcast.23), calls=%async_computation | async-start | bytes 2621440 | tf_op jit(solution)/shard_map/all_to_all | solution.py:833
  27.9 9.7 %ahead.1 = (bf16[1536,256]{1,0:T(8,128)(2,1)}, f32[3,1536,384]{2,1,0:T(8,128)}, f32[384,3072]{1,0:T(8,128)}) custom-call(bf16[256,3072]{1,0:T(8,128)(2,1)} %x_hbm.3, bf16[3,256,384]{2,1,0:T(8,128)(2,1)} %copy-done, bf16[3,3072,384]{2,1,0:T(8,128)(2,1)} %bitcast.19, bf16[256,384]{1,0:T(8,128)(2,1)} %copy-done.4, bf16[256,3072]{1,0:T(8,128)(2,1)} %gy_hbm.3, ...), custom_call_target="tpu_custom_call" | custom-call | flops 8999999488 | bytes 27000000 | tf_op jit(solution)/shard_map/ahead/pallas_call | solution.py:317
  37.6 12.0 %all-to-all-done.received_ref = f32[64,40,128]{2,1,0:T(8,128)S(1)} async-done(((f32[64,40,128]{2,1,0:T(8,128)}), f32[64,40,128]{2,1,0:T(8,128)S(1)}, u32[]{:S(2)}, u32[]{:S(2)}) %all-to-all-start) | async-done | bytes 1310752 | tf_op jit(solution)/shard_map/all_to_all | solution.py:833
  49.8 25.3 %all_to_all.20 = f32[64,40,128]{2,1,0:T(8,128)S(1)} all-to-all(f32[64,40,128]{2,1,0:T(8,128)S(1)} %answer_left.1), channel_id=1, replica_groups=mesh['x'=4,'y'=4,'z'=4,'c'=2] {'x','y','z'}, dimensions={0} | all-to-all | bytes 2621440 | tf_op jit(solution)/shard_map/all_to_all | solution.py:836
  75.2 3.6 %right_out.1 = (f32[832,128]{1,0:T(8,128)S(1)}, f32[768,128]{1,0:T(8,128)S(1)}) custom-call(s32[2]{0:T(128)S(1)} %pad_add_fusion.place_ref, f32[192,128]{1,0:T(8,128)S(1)} %slice.40.left_out_ref, bf16[256,384]{1,0:T(8,128)(2,1)S(1)} %copy-done.5, bf16[256,3072]{1,0:T(8,128)(2,1)} %gy_hbm.3, bf16[384,3072]{1,0:T(8,128)(2,1)} %bitcast.26), custom_call_target="tpu_custom_call" | custom-call | flops 3000000000 | bytes 9000000 | tf_op jit(solution)/shard_map/right_out/pallas_call | solution.py:428
  78.8 0.6 collective-permute-start.2
  79.4 3.6 %gram.1 = (f32[192,192]{1,0:T(8,128)S(1)}, bf16[256,1536]{1,0:T(8,128)(2,1)S(1)}, bf16[3,1536,384]{2,1,0:T(8,128)(2,1)S(1)}) custom-call(s32[1]{0:T(128)} %bitcast.1.half_ref, f32[2560,128]{1,0:T(8,128)S(1)} %bitcast.13, f32[2560,128]{1,0:T(8,128)S(1)} %collective-permute-done.1.other_ref, bf16[256,3072]{1,0:T(8,128)(2,1)} %x_hbm.3, ...), custom_call_target="tpu_custom_call" | custom-call | flops 3000000000 | bytes 9000000 | tf_op jit(solution)/shard_map/gram/pallas_call | solution.py:556
  83.2 1.4 collective-permute-start.3
  85.0 2.8 %collective-permute-start.5 = (f32[256,128]{1,0:T(8,128)S(1)}, f32[256,128]{1,0:T(8,128)S(1)}, u32[]{:S(2)}, u32[]{:S(2)}) collective-permute-start(f32[256,128]{1,0:T(8,128)S(1)} %get-tuple-element.86), channel_id=1, source_target_pairs={{0,6},{2,0},{4,2},{6,4},{1,7},{3,1},{5,3},{7,5},{8,14},{10,8},{12,... | collective-permute-start | bytes 393224 | tf_op jit(solution)/shard_map/ppermute | solution.py:847
  87.8 3.3 %right_own.1 = (f32[3,64,384]{2,1,0:T(8,128)S(1)}, f32[192,256]{1,0:T(8,128)S(1)}, bf16[256,1536]{1,0:T(8,128)(2,1)S(1)}, bf16[3,1536,384]{2,1,0:T(8,128)(2,1)S(1)}) custom-call(s32[1]{0:T(128)S(6)} %sub.3.half_ref, f32[2560,128]{1,0:T(8,128)S(1)} %bitcast.14, bf16[256,1536]{1,0:T(8,128)(2,1)S(1)} %get-tuple-element.53.x_ref, ...), custom_call_target="tpu_custom_call" | custom-call | flops 3000000000 | bytes 9000000 | tf_op jit(solution)/shard_map/right_own/pallas_call | solution.py:486
  91.1 1.4 %right_other.1.right_ref = f32[576,128]{1,0:T(8,128)S(1)} custom-call(f32[2560,128]{1,0:T(8,128)S(1)} %collective-permute-done.1.other_ref, f32[3,64,384]{2,1,0:T(8,128)S(1)} %get-tuple-element.55.right_ref, f32[192,256]{1,0:T(8,128)S(1)} %get-tuple-element.56.token_ref, bf16[256,1536]{1,0:T(8,128)(2,1)S(1)} %get-tuple-element.57.x_ref, ...), custom_call_target="tpu_custom_call" | custom-call | flops 4000000000 | bytes 12000000 | tf_op jit(solution)/shard_map/right_other/pallas_call | solution.py:514
  92.6 0.4 collective-permute-done.4.second_ref
  93.0 0.8 join.1
  93.8 3.6 %all-to-all-start.2 = ((f32[16,48,128]{2,1,0:T(8,128)}), f32[16,48,128]{2,1,0:T(8,128)S(1)}, u32[]{:S(2)}, u32[]{:S(2)}) async-start(f32[16,48,128]{2,1,0:T(8,128)} %bitcast.7), calls=%async_computation.2 | async-start | bytes 786432 | tf_op jit(solution)/shard_map/all_to_all | solution.py:851
  97.3 5.9 %invert.1 = (f32[4,64,128]{2,1,0:T(8,128)S(1)}, f32[64,384]{1,0:T(8,128)S(1)}) custom-call(f32[192,192]{1,0:T(8,128)S(1)} %get-tuple-element.64.gram_in_ref, f32[192,128]{1,0:T(8,128)S(1)} %slice.40.left_out_ref, f32[64,128]{1,0:T(8,128)S(1)} %get-tuple-element.65.gram_out_ref), custom_call_target="tpu_custom_call" | custom-call | flops 10000000000 | bytes 30000000 | tf_op jit(solution)/shard_map/invert/pallas_call | solution.py:604
  103.2 0.6 copy-done.7
  103.9 3.7 %all-to-all-done.2.received_ref = f32[16,48,128]{2,1,0:T(8,128)S(1)} async-done(((f32[16,48,128]{2,1,0:T(8,128)}), f32[16,48,128]{2,1,0:T(8,128)S(1)}, u32[]{:S(2)}, u32[]{:S(2)}) %all-to-all-start.2) | async-done | bytes 393248 | tf_op jit(solution)/shard_map/all_to_all | solution.py:851
  107.6 0.8 answer_right.1
  108.4 3.7 %all-to-all-start.3 = ((f32[16,48,128]{2,1,0:T(8,128)}), f32[16,48,128]{2,1,0:T(8,128)S(1)}, u32[]{:S(2)}, u32[]{:S(2)}) async-start(f32[16,48,128]{2,1,0:T(8,128)} %answer_right.1), calls=%async_computation.3 | async-start | bytes 786432 | tf_op jit(solution)/shard_map/all_to_all | solution.py:856
  112.1 4.0 %turn.1.ortho_hbm = bf16[3,3072,128]{2,1,0:T(8,128)(2,1)} custom-call(s32[1]{0:T(128)} %bitcast.1.half_ref, f32[2560,128]{1,0:T(8,128)S(1)} %bitcast.15, f32[2560,128]{1,0:T(8,128)S(1)} %collective-permute-done.1.other_ref, f32[4,64,128]{2,1,0:T(8,128)S(1)} %get-tuple-element.71.inverse_ref.inverse_hbm.refs_4_), custom_call_target="tpu_custom_call" | custom-call | flops 6000000000 | bytes 18000000 | tf_op jit(solution)/shard_map/turn/pallas_call | solution.py:639
  116.2 5.4 %all-to-all-done.3 = f32[16,48,128]{2,1,0:T(8,128)S(1)} async-done(((f32[16,48,128]{2,1,0:T(8,128)}), f32[16,48,128]{2,1,0:T(8,128)S(1)}, u32[]{:S(2)}, u32[]{:S(2)}) %all-to-all-start.3) | async-done | bytes 393248 | tf_op jit(solution)/shard_map/all_to_all | solution.py:856
  121.9 1.3 collective-permute-done.6
  123.2 0.5 collective-permute-start.7
  123.7 1.8 %collective-permute-start.8 = (f32[384,128]{1,0:T(8,128)S(1)}, f32[384,128]{1,0:T(8,128)S(1)}, u32[]{:S(2)}, u32[]{:S(2)}) collective-permute-start(f32[384,128]{1,0:T(8,128)S(1)} %pad_maximum_fusion.4.refs_0_), channel_id=1, source_target_pairs={{0,4},{2,6},{4,0},{6,2},{1,5},{3,7},{5,1},{7,3},{8,12},{10,14},{12... | collective-permute-start | bytes 589832 | tf_op jit(solution)/shard_map/ppermute | solution.py:862
  125.4 1.7 %collective-permute-start.9 = (f32[384,128]{1,0:T(8,128)S(1)}, f32[384,128]{1,0:T(8,128)S(1)}, u32[]{:S(2)}, u32[]{:S(2)}) collective-permute-start(f32[384,128]{1,0:T(8,128)S(1)} %pad_maximum_fusion.4.refs_0_), channel_id=1, source_target_pairs={{0,6},{2,0},{4,2},{6,4},{1,7},{3,1},{5,3},{7,5},{8,14},{10,8},{12,... | collective-permute-start | bytes 589832 | tf_op jit(solution)/shard_map/ppermute | solution.py:862
  127.2 9.5 %rest_in.1 = (bf16[3,3072,384]{2,1,0:T(8,128)(2,1)}, f32[3,64,384]{2,1,0:T(8,128)}) custom-call(f32[768,128]{1,0:T(8,128)S(1)} %bitcast.17, f32[4,64,128]{2,1,0:T(8,128)} %copy-done.6, bf16[3,256,384]{2,1,0:T(8,128)(2,1)} %copy-done, bf16[1536,256]{1,0:T(8,128)(2,1)} %get-tuple-element.73.turned_hbm, bf16[3,3072,384]{2,1,0:T(8,128)(2,1)} %bitcast.22, ...), custom_call_target="tpu_custom_call" | custom-call | flops 8999999488 | bytes 27000000 | tf_op jit(solution)/shard_map/rest_in/pallas_call | solution.py:711
  136.8 5.5 %rest_out.1 = (bf16[384,3072]{1,0:T(8,128)(2,1)}, f32[64,3072]{1,0:T(8,128)}) custom-call(s32[2]{0:T(128)S(1)} %pad_add_fusion.place_ref, f32[384,128]{1,0:T(8,128)S(1)} %pad_maximum_fusion.4.refs_0_, f32[384,128]{1,0:T(8,128)S(1)} %collective-permute-done.7.refs_1_, f32[384,128]{1,0:T(8,128)S(1)} %collective-permute-done.8.refs_2_, ...), custom_call_target="tpu_custom_call" | custom-call | flops 6000000000 | bytes 18000000 | tf_op jit(solution)/shard_map/rest_out/pallas_call | solution.py:785
  (35 shorter events, 1.2 us)
Async XLA Ops:
  0.6 8.6 %copy-start.2 = (f32[3,64,384]{2,1,0:T(8,128)S(1)}, f32[3,64,384]{2,1,0:T(8,128)}, u32[]{:S(2)}) copy-start(f32[3,64,384]{2,1,0:T(8,128)} %basis_in_ref.3) | copy-start | bytes 884740
  9.2 1.8 %copy-start.4 = (bf16[256,384]{1,0:T(8,128)(2,1)}, bf16[256,384]{1,0:T(8,128)(2,1)S(1)}, u32[]{:S(2)}) copy-start(bf16[256,384]{1,0:T(8,128)(2,1)S(1)} %get-tuple-element.50.hid_ref) | copy-start | bytes 589828
  9.3 4.6 %copy-start = (bf16[3,256,384]{2,1,0:T(8,128)(2,1)}, bf16[3,256,384]{2,1,0:T(8,128)(2,1)S(1)}, u32[]{:S(2)}) copy-start(bf16[3,256,384]{2,1,0:T(8,128)(2,1)S(1)} %get-tuple-element.44.grads_ref.grads_hbm) | copy-start | bytes 1769476
  9.3 1.8 %copy-start.3 = (f32[64,3072]{1,0:T(8,128)S(1)}, f32[64,3072]{1,0:T(8,128)}, u32[]{:S(2)}) copy-start(f32[64,3072]{1,0:T(8,128)} %basis_out_ref.1) | copy-start | bytes 2359300
  11.0 2.9 %collective-permute-start = (f32[2304,128]{1,0:T(8,128)S(1)}, f32[2304,128]{1,0:T(8,128)S(1)}, u32[]{:S(2)}, u32[]{:S(2)}) collective-permute-start(f32[2304,128]{1,0:T(8,128)S(1)} %left_send.1), channel_id=1, source_target_pairs={{0,1},{1,0},{2,3},{3,2},{4,5},{5,4},{6,7},{7,6},{8,9},{9,8},{10,11... | collective-permute-start | bytes 3538952 | tf_op jit(solution)/shard_map/ppermute | solution.py:828
  16.3 33.3 %all-to-all-start = ((f32[64,40,128]{2,1,0:T(8,128)}), f32[64,40,128]{2,1,0:T(8,128)S(1)}, u32[]{:S(2)}, u32[]{:S(2)}) async-start(f32[64,40,128]{2,1,0:T(8,128)} %bitcast.23), calls=%async_computation | async-start | bytes 2621440 | tf_op jit(solution)/shard_map/all_to_all | solution.py:833
  49.8 25.4 %copy-start.5 = (bf16[256,384]{1,0:T(8,128)(2,1)S(1)}, bf16[256,384]{1,0:T(8,128)(2,1)}, u32[]{:S(2)}) copy-start(bf16[256,384]{1,0:T(8,128)(2,1)} %copy-done.4) | copy-start | bytes 589828
  75.1 4.2 %collective-permute-start.1 = (f32[2560,128]{1,0:T(8,128)S(1)}, f32[2560,128]{1,0:T(8,128)S(1)}, u32[]{:S(2)}, u32[]{:S(2)}) collective-permute-start(f32[2560,128]{1,0:T(8,128)S(1)} %bitcast.11), channel_id=1, source_target_pairs={{0,1},{1,0},{2,3},{3,2},{4,5},{5,4},{6,7},{7,6},{8,9},{9,8},{10,11... | collective-permute-start | bytes 3932168 | tf_op jit(solution)/shard_map/ppermute | solution.py:837
  78.8 4.2 %collective-permute-start.2 = (f32[832,128]{1,0:T(8,128)S(1)}, f32[832,128]{1,0:T(8,128)S(1)}, u32[]{:S(2)}, u32[]{:S(2)}) collective-permute-start(f32[832,128]{1,0:T(8,128)S(1)} %get-tuple-element.60), channel_id=1, source_target_pairs={{0,1},{1,0},{2,3},{3,2},{4,5},{5,4},{6,7},{7,6},{8,9},{9,8},{10,11... | collective-permute-start | bytes 1277960 | tf_op jit(solution)/shard_map/ppermute | solution.py:841
  83.2 9.4 %collective-permute-start.3 = (f32[256,128]{1,0:T(8,128)S(1)}, f32[256,128]{1,0:T(8,128)S(1)}, u32[]{:S(2)}, u32[]{:S(2)}) collective-permute-start(f32[256,128]{1,0:T(8,128)S(1)} %get-tuple-element.87), channel_id=1, source_target_pairs={{0,4},{2,6},{4,0},{6,2},{1,5},{3,7},{5,1},{7,3},{8,12},{10,14},{12... | collective-permute-start | bytes 393224 | tf_op jit(solution)/shard_map/ppermute | solution.py:847
  84.6 8.4 %collective-permute-start.4 = (f32[256,128]{1,0:T(8,128)S(1)}, f32[256,128]{1,0:T(8,128)S(1)}, u32[]{:S(2)}, u32[]{:S(2)}) collective-permute-start(f32[256,128]{1,0:T(8,128)S(1)} %get-tuple-element.88), channel_id=1, source_target_pairs={{0,2},{2,4},{4,6},{6,0},{1,3},{3,5},{5,7},{7,1},{8,10},{10,12},{12... | collective-permute-start | bytes 393224 | tf_op jit(solution)/shard_map/ppermute | solution.py:847
  85.0 8.0 %collective-permute-start.5 = (f32[256,128]{1,0:T(8,128)S(1)}, f32[256,128]{1,0:T(8,128)S(1)}, u32[]{:S(2)}, u32[]{:S(2)}) collective-permute-start(f32[256,128]{1,0:T(8,128)S(1)} %get-tuple-element.86), channel_id=1, source_target_pairs={{0,6},{2,0},{4,2},{6,4},{1,7},{3,1},{5,3},{7,5},{8,14},{10,8},{12,... | collective-permute-start | bytes 393224 | tf_op jit(solution)/shard_map/ppermute | solution.py:847
  87.8 3.3 %copy-start.1 = (bf16[3,256,384]{2,1,0:T(8,128)(2,1)S(1)}, bf16[3,256,384]{2,1,0:T(8,128)(2,1)}, u32[]{:S(2)}) copy-start(bf16[3,256,384]{2,1,0:T(8,128)(2,1)} %copy-done) | copy-start | bytes 1769476
  93.8 13.8 %all-to-all-start.2 = ((f32[16,48,128]{2,1,0:T(8,128)}), f32[16,48,128]{2,1,0:T(8,128)S(1)}, u32[]{:S(2)}, u32[]{:S(2)}) async-start(f32[16,48,128]{2,1,0:T(8,128)} %bitcast.7), calls=%async_computation.2 | async-start | bytes 786432 | tf_op jit(solution)/shard_map/all_to_all | solution.py:851
  103.2 0.6 copy-start.7
  103.9 12.3 %copy-start.6 = (f32[4,64,128]{2,1,0:T(8,128)}, f32[4,64,128]{2,1,0:T(8,128)S(1)}, u32[]{:S(2)}) copy-start(f32[4,64,128]{2,1,0:T(8,128)S(1)} %get-tuple-element.71.inverse_ref.inverse_hbm.refs_4_) | copy-start | bytes 393220
  108.4 13.2 %all-to-all-start.3 = ((f32[16,48,128]{2,1,0:T(8,128)}), f32[16,48,128]{2,1,0:T(8,128)S(1)}, u32[]{:S(2)}, u32[]{:S(2)}) async-start(f32[16,48,128]{2,1,0:T(8,128)} %answer_right.1), calls=%async_computation.3 | async-start | bytes 786432 | tf_op jit(solution)/shard_map/all_to_all | solution.py:856
  121.6 1.6 %collective-permute-start.6 = (f32[192,128]{1,0:T(8,128)S(1)}, f32[192,128]{1,0:T(8,128)S(1)}, u32[]{:S(2)}, u32[]{:S(2)}) collective-permute-start(f32[192,128]{1,0:T(8,128)S(1)} %slice.39), channel_id=1, source_target_pairs={{0,1},{1,0},{2,3},{3,2},{4,5},{5,4},{6,7},{7,6},{8,9},{9,8},{10,11... | collective-permute-start | bytes 294920 | tf_op jit(solution)/shard_map/ppermute | solution.py:861
  123.2 13.6 %collective-permute-start.7 = (f32[384,128]{1,0:T(8,128)S(1)}, f32[384,128]{1,0:T(8,128)S(1)}, u32[]{:S(2)}, u32[]{:S(2)}) collective-permute-start(f32[384,128]{1,0:T(8,128)S(1)} %pad_maximum_fusion.4.refs_0_), channel_id=1, source_target_pairs={{0,2},{2,4},{4,6},{6,0},{1,3},{3,5},{5,7},{7,1},{8,10},{10,12},{12... | collective-permute-start | bytes 589832 | tf_op jit(solution)/shard_map/ppermute | solution.py:862
  123.7 13.1 %collective-permute-start.8 = (f32[384,128]{1,0:T(8,128)S(1)}, f32[384,128]{1,0:T(8,128)S(1)}, u32[]{:S(2)}, u32[]{:S(2)}) collective-permute-start(f32[384,128]{1,0:T(8,128)S(1)} %pad_maximum_fusion.4.refs_0_), channel_id=1, source_target_pairs={{0,4},{2,6},{4,0},{6,2},{1,5},{3,7},{5,1},{7,3},{8,12},{10,14},{12... | collective-permute-start | bytes 589832 | tf_op jit(solution)/shard_map/ppermute | solution.py:862
  125.4 11.3 %collective-permute-start.9 = (f32[384,128]{1,0:T(8,128)S(1)}, f32[384,128]{1,0:T(8,128)S(1)}, u32[]{:S(2)}, u32[]{:S(2)}) collective-permute-start(f32[384,128]{1,0:T(8,128)S(1)} %pad_maximum_fusion.4.refs_0_), channel_id=1, source_target_pairs={{0,6},{2,0},{4,2},{6,4},{1,7},{3,1},{5,3},{7,5},{8,14},{10,8},{12,... | collective-permute-start | bytes 589832 | tf_op jit(solution)/shard_map/ppermute | solution.py:862

commit v7 on v6

--- a/solution.py
+++ b/solution.py
@@ -391,7 +391,8 @@
     )(received)
 
 
-def right_out_kernel(place_ref, left_out_ref, hid_ref, gy_hbm, err_out_hbm, send_ref, keep_ref, gy_scr, err_out_scr, sem):
+def right_out_kernel(place_ref, left_out_ref, hid_ref, gy_hbm, err_out_hbm, x_hbm, err_in_hbm, send_ref, keep_ref, x_out,
+                     err_in_out, gy_scr, err_out_scr, sem, near_sem):
     def column(j):
         at = lax.rem(place_ref[0] + 1 + j // 4, 2) * 4 + lax.rem(place_ref[1] + j % 4, 4)
         return pl.ds(pl.multiple_of(at * COLS, COLS), COLS)
@@ -403,7 +404,8 @@
         )
         for j in range(8)
     ]
-    for pair in copies:
+    near = near_copies(place_ref[0], x_hbm, err_in_hbm, x_out, err_in_out, near_sem)
+    for pair in copies + [near]:
         for copy in pair:
             copy.start()
     left_out = wide(left_out_ref[...], RANK)
@@ -421,26 +423,32 @@
         for i, tile in enumerate(tiles_of(part)):
             at = (j % 4) * PIECE + i * RANK
             ref[at : at + RANK, :] = tile
-
-
-def right_out(place, left_out_sum, grad_y, hidden, err_out):
+    for copy in near:
+        copy.wait()
+
+
+def right_out(place, left_out_sum, grad_y, hidden, err_out, inputs, err_in):
     whole = pl.BlockSpec(memory_space=pltpu.VMEM)
     return pl.pallas_call(
         right_out_kernel,
-        in_specs=[pl.BlockSpec(memory_space=pltpu.SMEM), whole, whole, ANY, ANY],
+        in_specs=[pl.BlockSpec(memory_space=pltpu.SMEM), whole, whole, ANY, ANY, ANY, ANY],
+        out_specs=[whole, whole, ANY, ANY],
         out_shape=[
             jax.ShapeDtypeStruct((RO_ROWS + RANK, 128), f32),
             jax.ShapeDtypeStruct((RO_ROWS, 128), f32),
+            pltpu.VMEM((TOK, HALF), bf16),
+            pltpu.VMEM((3, HALF, COLS), bf16),
         ],
         scratch_shapes=[
             pltpu.VMEM((8, TOK, COLS), bf16),
             pltpu.VMEM((8, COLS, COLS), bf16),
             pltpu.SemaphoreType.DMA((2, 8)),
+            pltpu.SemaphoreType.DMA((2, STEPS)),
         ],
         cost_estimate=cost(3),
         compiler_params=pltpu.CompilerParams(vmem_limit_bytes=VMEM),
         name="right_out",
-    )(place, left_out_sum, hidden, *streamed(grad_y, err_out))
+    )(place, left_out_sum, hidden, *streamed(grad_y, err_out, inputs, err_in))
 
 
 def right_tile(rows, x, err_in, rights):
@@ -537,36 +545,23 @@
     )(*operands)
 
 
-def gram_kernel(half_ref, own_ref, other_ref, x_hbm, err_in_hbm, gram_ref, x_out, err_in_out, sem):
-    copies = near_copies(half_ref[0], x_hbm, err_in_hbm, x_out, err_in_out, sem)
-    for copy in copies:
-        copy.start()
+def gram_kernel(own_ref, other_ref, gram_ref):
     gram = jnp.zeros((3 * RANK, 3 * RANK), f32)
     for ref in (own_ref, other_ref):
         for i in range(STEPS):
             rows = wide(ref[L_STEP * i : L_STEP * (i + 1), :], 3 * RANK)
             gram += exact_nt(rows, rows)
     gram_ref[...] = gram
-    for copy in copies:
-        copy.wait()
-
-
-def gram(half, own, other, inputs, err_in):
-    whole = pl.BlockSpec(memory_space=pltpu.VMEM)
+
+
+def gram(own, other):
     return pl.pallas_call(
         gram_kernel,
-        in_specs=[pl.BlockSpec(memory_space=pltpu.SMEM), whole, whole, ANY, ANY],
-        out_specs=[whole, ANY, ANY],
-        out_shape=[
-            jax.ShapeDtypeStruct((3 * RANK, 3 * RANK), f32),
-            pltpu.VMEM((TOK, HALF), bf16),
-            pltpu.VMEM((3, HALF, COLS), bf16),
-        ],
-        scratch_shapes=[pltpu.SemaphoreType.DMA((2, STEPS))],
-        cost_estimate=cost(3),
+        out_shape=jax.ShapeDtypeStruct((3 * RANK, 3 * RANK), f32),
+        cost_estimate=cost(2),
         compiler_params=pltpu.CompilerParams(vmem_limit_bytes=VMEM),
         name="gram",
-    )(half, own, other, *streamed(inputs, err_in))
+    )(own, other)
 
 
 def invert_kernel(gram_in_ref, left_out_ref, gram_out_ref, inverse_ref, ortho_out_ref):
@@ -676,8 +671,9 @@
     out = [pltpu.make_async_copy(rest_scr.at[j], rest_hbm.at[:, rows(j)], out_sem.at[j]) for j in tiles]
     for copy in first:
         copy.start()
-    for group in into:
-        for copy in group:
+    order = [j + half for j in range(STEPS) for half in (0, STEPS)]
+    for j in order:
+        for copy in into[j]:
             copy.start()
     for copy in first:
         copy.wait()
@@ -689,7 +685,7 @@
         factor_in_ref[p] = factor
         high, low = split2(-factor)
         weights.append(jnp.concatenate([high, high, low, jnp.zeros_like(low)], axis=0))
-    for j in tiles:
+    for j in order:
         for copy in into[j]:
             copy.wait()
         moments = nn(turned_scr[j], grads) if j < STEPS else None
@@ -820,6 +816,7 @@
     mine = core[None]
     theirs = 1 - mine
     place = jnp.stack([core, z])
+    q_pre, place, mine, theirs, me = lax.optimization_barrier((q_pre, place, mine, theirs, me[None]))
     hidden, grads, near_err_in, near_err_out, near_inputs, near_grad_y = recurrence(
         grad_y, w_out, q_pre, f_pre, v_pre, keep
     )
@@ -833,14 +830,16 @@
     received = lax.all_to_all(rows.reshape(CHIPS, EACH1, 128), CHIP, 0, 0)
     inputs_turned, moment_in, moment_out = ahead(inputs, grads, err_in, hidden_now, grad_y, err_out)
     received, inputs_turned = lax.optimization_barrier((received, inputs_turned))
-    own = lax.all_to_all(answer_left(me[None], received), CHIP, 0, 0).reshape(ROWS1, 128)
+    own = lax.all_to_all(answer_left(me, received), CHIP, 0, 0).reshape(ROWS1, 128)
     other = lax.ppermute(own, "c", SWAP)
     left_out_sum = own[L_ROWS : L_ROWS + LO_ROWS]
 
-    send, keep_out = right_out(place, left_out_sum, grad_y, hidden, err_out)
+    send, keep_out, near_inputs, near_err_in = right_out(
+        place, left_out_sum, grad_y, hidden, err_out, inputs, err_in
+    )
     arrived = lax.ppermute(send, "c", SWAP)
-    gram_in, near_inputs, near_err_in = gram(mine, own, other, inputs, err_in)
-    arrived, gram_in = lax.optimization_barrier((arrived, gram_in))
+    gram_in = gram(own, other)
+    arrived, gram_in, near_inputs = lax.optimization_barrier((arrived, gram_in, near_inputs))
     gram_out = send[RO_ROWS:] + arrived[RO_ROWS:]
     quarters = (keep_out + arrived[:RO_ROWS]).reshape(4, PIECE, 128)
     pieces = [jnp.concatenate([quarters[shift], gram_out]) for shift in range(4)]

time: 143 us -> 142 us (level)
  starting transfers between devices: 28.4 us -> 26.1 us
    ppermute x3, waiting for transfers between devices: 0.42 us -> 2.82 us  [shards(): lax.ppermute(pieces[shift], 'z', ring(shift))]
    ppermute x3, starting transfers between devices: 4.63 us -> 2.81 us  [shards(): lax.ppermute(pieces[shift], 'z', ring(shift))]
    all_to_all x1, waiting for transfers between devices: 5.39 us -> 3.83 us  [shards(): summed = lax.all_to_all(everywhere, ('x', 'y'), 0, 0).reshape(ROWS2, 128)]
    pallas_call x1, Pallas kernels: 3.61 us -> 2.14 us  [gram(): pl.pallas_call(gram_kernel, out_shape=jax.ShapeDtypeStruct((3 * RANK, 3 *...]
  transfers between devices with their start and end apart: 13 -> 13, of which waited for: 6 -> 7; matrix products, arithmetic and copies ran while one was open for 0% -> 0% of each run, Pallas kernels for 30% -> 30%
where the time goes in v7:
time: 142 us; the launch traced here: 141 us
  Pallas kernels  62 us (44%)
  starting transfers between devices  26.1 us (18%)
  blocking collectives  25.3 us (18%)
  waiting for transfers between devices  25 us (18%)
    all_to_all x1, blocking collectives, shards(): lax.all_to_all(answer_left(me, received), CHIP, 0, 0).reshape(ROWS1, 128)  25.3 us
    all_to_all x1, waiting for transfers between devices, shards(): received = lax.all_to_all(rows.reshape(CHIPS, EACH1, 128), CHIP, 0, 0)  12.1 us
    all_to_all x1, starting transfers between devices, shards(): received = lax.all_to_all(rows.reshape(CHIPS, EACH1, 128), CHIP, 0, 0)  11.5 us
    pallas_call x1, Pallas kernels, ahead(): pl.pallas_call(ahead_kernel, grid=(STEPS,), in_specs=[pl.BlockSpec((TOK,...  9.64 us
    pallas_call x1, Pallas kernels, rest_in(): pl.pallas_call(rest_in_kernel, in_specs=[whole] + [ANY] * 6, out_specs=[A...  9.47 us
    pallas_call x1, Pallas kernels, recurrence(): pl.pallas_call(recurrence_kernel, in_specs=[ANY] * len(operands), out_spe...  8.59 us
    pallas_call x1, Pallas kernels, invert(): pl.pallas_call(invert_kernel, out_shape=[jax.ShapeDtypeStruct((4, RANK, 1...  5.87 us
    pallas_call x1, Pallas kernels, rest_out(): pl.pallas_call(rest_out_kernel, in_specs=[pl.BlockSpec(memory_space=pltpu...  5.49 us
  transfers between devices with their start and end apart: 13, of which 7 were waited for; matrix products, arithmetic and copies ran while one was open for 0% of the time, Pallas kernels for 30%

profile of v7, /device:TPU:0, one launch (start us, length us, event | category | flops | bytes accessed | tf_op | source)
XLA Modules:
  0.0 141.1 jit_solution(16000306953457761074)
XLA Ops:
  0.7 8.6 %recurrence.1 = (bf16[256,384]{1,0:T(8,128)(2,1)S(1)}, bf16[3,256,384]{2,1,0:T(8,128)(2,1)S(1)}, bf16[3,3072,384]{2,1,0:T(8,128)(2,1)S(1)}, bf16[384,3072]{1,0:T...) custom-call(bf16[256,384]{1,0:T(8,128)(2,1)} %q_hbm, bf16[256,384]{1,0:T(8,128)(2,1)} %f_hbm.1, ...), custom_call_target="tpu_custom_call" | custom-call | flops 8000000000 | bytes 24000000 | tf_op jit(solution)/shard_map/recurrence/pallas_call | solution.py:218
  9.4 1.6 %left_send.1 = f32[2304,128]{1,0:T(8,128)S(1)} custom-call(s32[1]{0:T(128)S(6)} %sub.3.half_ref, bf16[256,3072]{1,0:T(8,128)(2,1)S(1)} %get-tuple-element.51.x_ref, bf16[3,256,384]{2,1,0:T(8,128)(2,1)S(1)} %get-tuple-element.52.grads_ref.grads_hbm, bf16[3,3072,384]{2,1,0:T(8,128)(2,1)S(1)} %get-tuple-element.53.err_in_ref, f32[3,64,384]{2,1,0:T(8,128)S(1)} %copy-done.2), custom_call_target="tpu_custom_call" | custom-call | flops 3000000000 | bytes 9000000 | tf_op jit(solution)/shard_map/left_send/pallas_call | solution.py:276
  11.1 1.9 %left_out.1.left_out_ref = f32[192,128]{1,0:T(8,128)S(1)} custom-call(bf16[256,3072]{1,0:T(8,128)(2,1)S(1)} %get-tuple-element.55.gy_ref, bf16[256,384]{1,0:T(8,128)(2,1)S(1)} %get-tuple-element.59.hid_ref, bf16[384,3072]{1,0:T(8,128)(2,1)S(1)} %get-tuple-element.57.err_out_ref, f32[64,3072]{1,0:T(8,128)S(1)} %copy-done.7), custom_call_target="tpu_custom_call" | custom-call | flops 4000000000 | bytes 12000000 | tf_op jit(solution)/shard_map/left_out/pallas_call | solution.py:296
  13.0 0.9 collective-permute-done.arrived_ref
  13.9 2.5 %left_keep.1 = f32[2560,128]{1,0:T(8,128)} custom-call(s32[1]{0:T(128)} %bitcast.half_ref, bf16[256,3072]{1,0:T(8,128)(2,1)S(1)} %get-tuple-element.51.x_ref, bf16[3,256,384]{2,1,0:T(8,128)(2,1)S(1)} %get-tuple-element.52.grads_ref.grads_hbm, bf16[3,3072,384]{2,1,0:T(8,128)(2,1)S(1)} %get-tuple-element.53.err_in_ref, f32[3,64,384]{2,1,0:T(8,128)S(1)} %copy-done.2, ...), custom_call_target="tpu_custom_call" | custom-call | flops 3000000000 | bytes 9000000 | tf_op jit(solution)/shard_map/left_keep/pallas_call | solution.py:276
  16.4 11.5 %all-to-all-start = ((f32[64,40,128]{2,1,0:T(8,128)}), f32[64,40,128]{2,1,0:T(8,128)S(1)}, u32[]{:S(2)}, u32[]{:S(2)}) async-start(f32[64,40,128]{2,1,0:T(8,128)} %bitcast.23), calls=%async_computation | async-start | bytes 2621440 | tf_op jit(solution)/shard_map/all_to_all | solution.py:830
  27.9 9.6 %ahead.1 = (bf16[1536,256]{1,0:T(8,128)(2,1)}, f32[3,1536,384]{2,1,0:T(8,128)}, f32[384,3072]{1,0:T(8,128)}) custom-call(bf16[256,3072]{1,0:T(8,128)(2,1)} %x_hbm.3, bf16[3,256,384]{2,1,0:T(8,128)(2,1)} %copy-done, bf16[3,3072,384]{2,1,0:T(8,128)(2,1)} %bitcast.19, bf16[256,384]{1,0:T(8,128)(2,1)} %copy-done.3, bf16[256,3072]{1,0:T(8,128)(2,1)} %gy_hbm.3, ...), custom_call_target="tpu_custom_call" | custom-call | flops 8999999488 | bytes 27000000 | tf_op jit(solution)/shard_map/ahead/pallas_call | solution.py:317
  37.6 12.1 %all-to-all-done.received_ref = f32[64,40,128]{2,1,0:T(8,128)S(1)} async-done(((f32[64,40,128]{2,1,0:T(8,128)}), f32[64,40,128]{2,1,0:T(8,128)S(1)}, u32[]{:S(2)}, u32[]{:S(2)}) %all-to-all-start) | async-done | bytes 1310752 | tf_op jit(solution)/shard_map/all_to_all | solution.py:830
  49.9 25.3 %all_to_all.20 = f32[64,40,128]{2,1,0:T(8,128)S(1)} all-to-all(f32[64,40,128]{2,1,0:T(8,128)S(1)} %answer_left.1), channel_id=1, replica_groups=mesh['x'=4,'y'=4,'z'=4,'c'=2] {'x','y','z'}, dimensions={0} | all-to-all | bytes 2621440 | tf_op jit(solution)/shard_map/all_to_all | solution.py:833
  75.2 4.4 %right_out.1 = (f32[832,128]{1,0:T(8,128)S(1)}, f32[768,128]{1,0:T(8,128)S(1)}, bf16[256,1536]{1,0:T(8,128)(2,1)S(1)}, bf16[3,1536,384]{2,1,0:T(8,128)(2,1)S(1)}) custom-call(s32[2]{0:T(128)S(1)} %pad_add_fusion.place_ref, f32[192,128]{1,0:T(8,128)S(1)} %slice.40.left_out_ref, bf16[256,384]{1,0:T(8,128)(2,1)S(1)} %copy-done.4, bf16[256,3072]{1,0:T(8,128)(2,1)} %gy_hbm.3, ...), custom_call_target="tpu_custom_call" | custom-call | flops 3000000000 | bytes 9000000 | tf_op jit(solution)/shard_map/right_out/pallas_call | solution.py:432
  79.6 0.6 collective-permute-start.2
  80.2 2.1 %gram.1.gram_in_ref = f32[192,192]{1,0:T(8,128)S(1)} custom-call(f32[2560,128]{1,0:T(8,128)S(1)} %bitcast.13, f32[2560,128]{1,0:T(8,128)S(1)} %collective-permute-done.1.other_ref), custom_call_target="tpu_custom_call" | custom-call | flops 2000000000 | bytes 6000000 | tf_op jit(solution)/shard_map/gram/pallas_call | solution.py:558
  82.5 0.9 collective-permute-start.5
  83.4 1.8 %collective-permute-start.3 = (f32[256,128]{1,0:T(8,128)S(1)}, f32[256,128]{1,0:T(8,128)S(1)}, u32[]{:S(2)}, u32[]{:S(2)}) collective-permute-start(f32[256,128]{1,0:T(8,128)S(1)} %get-tuple-element.97), channel_id=1, source_target_pairs={{0,4},{2,6},{4,0},{6,2},{1,5},{3,7},{5,1},{7,3},{8,12},{10,14},{12... | collective-permute-start | bytes 393224 | tf_op jit(solution)/shard_map/ppermute | solution.py:846
  85.3 3.3 %right_own.1 = (f32[3,64,384]{2,1,0:T(8,128)S(1)}, f32[192,256]{1,0:T(8,128)S(1)}, bf16[256,1536]{1,0:T(8,128)(2,1)S(1)}, bf16[3,1536,384]{2,1,0:T(8,128)(2,1)S(1)}) custom-call(s32[1]{0:T(128)S(6)} %sub.3.half_ref, f32[2560,128]{1,0:T(8,128)S(1)} %bitcast.14, bf16[256,1536]{1,0:T(8,128)(2,1)S(1)} %get-tuple-element.65.x_ref, ...), custom_call_target="tpu_custom_call" | custom-call | flops 3000000000 | bytes 9000000 | tf_op jit(solution)/shard_map/right_own/pallas_call | solution.py:494
  88.6 1.4 %right_other.1.right_ref = f32[576,128]{1,0:T(8,128)S(1)} custom-call(f32[2560,128]{1,0:T(8,128)S(1)} %collective-permute-done.1.other_ref, f32[3,64,384]{2,1,0:T(8,128)S(1)} %get-tuple-element.67.right_ref, f32[192,256]{1,0:T(8,128)S(1)} %get-tuple-element.68.token_ref, bf16[256,1536]{1,0:T(8,128)(2,1)S(1)} %get-tuple-element.69.x_ref, ...), custom_call_target="tpu_custom_call" | custom-call | flops 4000000000 | bytes 12000000 | tf_op jit(solution)/shard_map/right_other/pallas_call | solution.py:522
  90.1 1.3 collective-permute-done.3.first_ref
  91.3 1.6 %collective-permute-done.4.second_ref = f32[256,128]{1,0:T(8,128)S(1)} collective-permute-done((f32[256,128]{1,0:T(8,128)S(1)}, f32[256,128]{1,0:T(8,128)S(1)}, u32[]{:S(2)}, u32[]{:S(2)}) %collective-permute-start.4) | collective-permute-done | bytes 131104 | tf_op jit(solution)/shard_map/ppermute | solution.py:846
  92.9 0.8 join.1
  93.7 3.6 %all-to-all-start.2 = ((f32[16,48,128]{2,1,0:T(8,128)}), f32[16,48,128]{2,1,0:T(8,128)S(1)}, u32[]{:S(2)}, u32[]{:S(2)}) async-start(f32[16,48,128]{2,1,0:T(8,128)} %bitcast.7), calls=%async_computation.2 | async-start | bytes 786432 | tf_op jit(solution)/shard_map/all_to_all | solution.py:850
  97.2 5.9 %invert.1 = (f32[4,64,128]{2,1,0:T(8,128)S(1)}, f32[64,384]{1,0:T(8,128)S(1)}) custom-call(f32[192,192]{1,0:T(8,128)S(1)} %gram.1.gram_in_ref, f32[192,128]{1,0:T(8,128)S(1)} %slice.40.left_out_ref, f32[64,128]{1,0:T(8,128)S(1)} %get-tuple-element.75.gram_out_ref), custom_call_target="tpu_custom_call" | custom-call | flops 10000000000 | bytes 30000000 | tf_op jit(solution)/shard_map/invert/pallas_call | solution.py:599
  103.1 4.0 %all-to-all-done.2.received_ref = f32[16,48,128]{2,1,0:T(8,128)S(1)} async-done(((f32[16,48,128]{2,1,0:T(8,128)}), f32[16,48,128]{2,1,0:T(8,128)S(1)}, u32[]{:S(2)}, u32[]{:S(2)}) %all-to-all-start.2) | async-done | bytes 393248 | tf_op jit(solution)/shard_map/all_to_all | solution.py:850
  107.2 0.8 answer_right.1
  108.0 3.7 %all-to-all-start.3 = ((f32[16,48,128]{2,1,0:T(8,128)}), f32[16,48,128]{2,1,0:T(8,128)S(1)}, u32[]{:S(2)}, u32[]{:S(2)}) async-start(f32[16,48,128]{2,1,0:T(8,128)} %answer_right.1), calls=%async_computation.3 | async-start | bytes 786432 | tf_op jit(solution)/shard_map/all_to_all | solution.py:855
  111.7 1.3 copy-done.6
  113.0 4.0 %turn.1.ortho_hbm = bf16[3,3072,128]{2,1,0:T(8,128)(2,1)} custom-call(s32[1]{0:T(128)} %bitcast.half_ref, f32[2560,128]{1,0:T(8,128)S(1)} %bitcast.15, f32[2560,128]{1,0:T(8,128)S(1)} %copy-done.6, f32[4,64,128]{2,1,0:T(8,128)S(1)} %get-tuple-element.81.inverse_ref.inverse_hbm.refs_4_), custom_call_target="tpu_custom_call" | custom-call | flops 6000000000 | bytes 18000000 | tf_op jit(solution)/shard_map/turn/pallas_call | solution.py:634
  117.0 3.8 %all-to-all-done.3 = f32[16,48,128]{2,1,0:T(8,128)S(1)} async-done(((f32[16,48,128]{2,1,0:T(8,128)}), f32[16,48,128]{2,1,0:T(8,128)S(1)}, u32[]{:S(2)}, u32[]{:S(2)}) %all-to-all-start.3) | async-done | bytes 393248 | tf_op jit(solution)/shard_map/all_to_all | solution.py:855
  121.1 1.3 collective-permute-done.6
  122.6 2.1 %collective-permute-start.8 = (f32[384,128]{1,0:T(8,128)S(1)}, f32[384,128]{1,0:T(8,128)S(1)}, u32[]{:S(2)}, u32[]{:S(2)}) collective-permute-start(f32[384,128]{1,0:T(8,128)S(1)} %pad_maximum_fusion.4.refs_0_), channel_id=1, source_target_pairs={{0,4},{2,6},{4,0},{6,2},{1,5},{3,7},{5,1},{7,3},{8,12},{10,14},{12... | collective-permute-start | bytes 589832 | tf_op jit(solution)/shard_map/ppermute | solution.py:861
  124.6 1.3 collective-permute-start.7
  126.0 9.5 %rest_in.1 = (bf16[3,3072,384]{2,1,0:T(8,128)(2,1)}, f32[3,64,384]{2,1,0:T(8,128)}) custom-call(f32[768,128]{1,0:T(8,128)S(1)} %bitcast.17, f32[4,64,128]{2,1,0:T(8,128)} %copy-done.8, bf16[3,256,384]{2,1,0:T(8,128)(2,1)} %copy-done, bf16[1536,256]{1,0:T(8,128)(2,1)} %get-tuple-element.83.turned_hbm, bf16[3,3072,384]{2,1,0:T(8,128)(2,1)} %bitcast.22, ...), custom_call_target="tpu_custom_call" | custom-call | flops 8999999488 | bytes 27000000 | tf_op jit(solution)/shard_map/rest_in/pallas_call | solution.py:707
  135.5 5.5 %rest_out.1 = (bf16[384,3072]{1,0:T(8,128)(2,1)}, f32[64,3072]{1,0:T(8,128)}) custom-call(s32[2]{0:T(128)S(1)} %pad_add_fusion.place_ref, f32[384,128]{1,0:T(8,128)S(1)} %pad_maximum_fusion.4.refs_0_, f32[384,128]{1,0:T(8,128)S(1)} %collective-permute-done.7.refs_1_, f32[384,128]{1,0:T(8,128)S(1)} %collective-permute-done.8.refs_2_, ...), custom_call_target="tpu_custom_call" | custom-call | flops 6000000000 | bytes 18000000 | tf_op jit(solution)/shard_map/rest_out/pallas_call | solution.py:781
  (39 shorter events, 1.1 us)
Async XLA Ops:
  0.7 8.6 %copy-start.2 = (f32[3,64,384]{2,1,0:T(8,128)S(1)}, f32[3,64,384]{2,1,0:T(8,128)}, u32[]{:S(2)}) copy-start(f32[3,64,384]{2,1,0:T(8,128)} %basis_in_ref.3) | copy-start | bytes 884740
  9.3 1.8 %copy-start.3 = (bf16[256,384]{1,0:T(8,128)(2,1)}, bf16[256,384]{1,0:T(8,128)(2,1)S(1)}, u32[]{:S(2)}) copy-start(bf16[256,384]{1,0:T(8,128)(2,1)S(1)} %get-tuple-element.59.hid_ref) | copy-start | bytes 589828
  9.3 4.6 %copy-start = (bf16[3,256,384]{2,1,0:T(8,128)(2,1)}, bf16[3,256,384]{2,1,0:T(8,128)(2,1)S(1)}, u32[]{:S(2)}) copy-start(bf16[3,256,384]{2,1,0:T(8,128)(2,1)S(1)} %get-tuple-element.52.grads_ref.grads_hbm) | copy-start | bytes 1769476
  9.3 1.8 %copy-start.7 = (f32[64,3072]{1,0:T(8,128)S(1)}, f32[64,3072]{1,0:T(8,128)}, u32[]{:S(2)}) copy-start(f32[64,3072]{1,0:T(8,128)} %basis_out_ref.1) | copy-start | bytes 2359300
  11.0 2.9 %collective-permute-start = (f32[2304,128]{1,0:T(8,128)S(1)}, f32[2304,128]{1,0:T(8,128)S(1)}, u32[]{:S(2)}, u32[]{:S(2)}) collective-permute-start(f32[2304,128]{1,0:T(8,128)S(1)} %left_send.1), channel_id=1, source_target_pairs={{0,1},{1,0},{2,3},{3,2},{4,5},{5,4},{6,7},{7,6},{8,9},{9,8},{10,11... | collective-permute-start | bytes 3538952 | tf_op jit(solution)/shard_map/ppermute | solution.py:825
  16.4 33.3 %all-to-all-start = ((f32[64,40,128]{2,1,0:T(8,128)}), f32[64,40,128]{2,1,0:T(8,128)S(1)}, u32[]{:S(2)}, u32[]{:S(2)}) async-start(f32[64,40,128]{2,1,0:T(8,128)} %bitcast.23), calls=%async_computation | async-start | bytes 2621440 | tf_op jit(solution)/shard_map/all_to_all | solution.py:830
  49.8 25.4 %copy-start.4 = (bf16[256,384]{1,0:T(8,128)(2,1)S(1)}, bf16[256,384]{1,0:T(8,128)(2,1)}, u32[]{:S(2)}) copy-start(bf16[256,384]{1,0:T(8,128)(2,1)} %copy-done.3) | copy-start | bytes 589828
  75.2 5.0 %collective-permute-start.1 = (f32[2560,128]{1,0:T(8,128)S(1)}, f32[2560,128]{1,0:T(8,128)S(1)}, u32[]{:S(2)}, u32[]{:S(2)}) collective-permute-start(f32[2560,128]{1,0:T(8,128)S(1)} %bitcast.11), channel_id=1, source_target_pairs={{0,1},{1,0},{2,3},{3,2},{4,5},{5,4},{6,7},{7,6},{8,9},{9,8},{10,11... | collective-permute-start | bytes 3932168 | tf_op jit(solution)/shard_map/ppermute | solution.py:834
  79.6 2.7 %collective-permute-start.2 = (f32[832,128]{1,0:T(8,128)S(1)}, f32[832,128]{1,0:T(8,128)S(1)}, u32[]{:S(2)}, u32[]{:S(2)}) collective-permute-start(f32[832,128]{1,0:T(8,128)S(1)} %get-tuple-element.63), channel_id=1, source_target_pairs={{0,1},{1,0},{2,3},{3,2},{4,5},{5,4},{6,7},{7,6},{8,9},{9,8},{10,11... | collective-permute-start | bytes 1277960 | tf_op jit(solution)/shard_map/ppermute | solution.py:840
  80.2 8.4 %copy-start.5 = (f32[2560,128]{1,0:T(8,128)}, f32[2560,128]{1,0:T(8,128)S(1)}, u32[]{:S(2)}) copy-start(f32[2560,128]{1,0:T(8,128)S(1)} %collective-permute-done.1.other_ref) | copy-start | bytes 3932164
  82.5 7.6 %collective-permute-start.5 = (f32[256,128]{1,0:T(8,128)S(1)}, f32[256,128]{1,0:T(8,128)S(1)}, u32[]{:S(2)}, u32[]{:S(2)}) collective-permute-start(f32[256,128]{1,0:T(8,128)S(1)} %get-tuple-element.96), channel_id=1, source_target_pairs={{0,6},{2,0},{4,2},{6,4},{1,7},{3,1},{5,3},{7,5},{8,14},{10,8},{12,... | collective-permute-start | bytes 393224 | tf_op jit(solution)/shard_map/ppermute | solution.py:846
  83.4 7.9 %collective-permute-start.3 = (f32[256,128]{1,0:T(8,128)S(1)}, f32[256,128]{1,0:T(8,128)S(1)}, u32[]{:S(2)}, u32[]{:S(2)}) collective-permute-start(f32[256,128]{1,0:T(8,128)S(1)} %get-tuple-element.97), channel_id=1, source_target_pairs={{0,4},{2,6},{4,0},{6,2},{1,5},{3,7},{5,1},{7,3},{8,12},{10,14},{12... | collective-permute-start | bytes 393224 | tf_op jit(solution)/shard_map/ppermute | solution.py:846
  85.2 7.7 %collective-permute-start.4 = (f32[256,128]{1,0:T(8,128)S(1)}, f32[256,128]{1,0:T(8,128)S(1)}, u32[]{:S(2)}, u32[]{:S(2)}) collective-permute-start(f32[256,128]{1,0:T(8,128)S(1)} %get-tuple-element.98), channel_id=1, source_target_pairs={{0,2},{2,4},{4,6},{6,0},{1,3},{3,5},{5,7},{7,1},{8,10},{10,12},{12... | collective-permute-start | bytes 393224 | tf_op jit(solution)/shard_map/ppermute | solution.py:846
  85.3 3.3 %copy-start.1 = (bf16[3,256,384]{2,1,0:T(8,128)(2,1)S(1)}, bf16[3,256,384]{2,1,0:T(8,128)(2,1)}, u32[]{:S(2)}) copy-start(bf16[3,256,384]{2,1,0:T(8,128)(2,1)} %copy-done) | copy-start | bytes 1769476
  93.7 13.5 %all-to-all-start.2 = ((f32[16,48,128]{2,1,0:T(8,128)}), f32[16,48,128]{2,1,0:T(8,128)S(1)}, u32[]{:S(2)}, u32[]{:S(2)}) async-start(f32[16,48,128]{2,1,0:T(8,128)} %bitcast.7), calls=%async_computation.2 | async-start | bytes 786432 | tf_op jit(solution)/shard_map/all_to_all | solution.py:850
  103.1 13.9 %copy-start.8 = (f32[4,64,128]{2,1,0:T(8,128)}, f32[4,64,128]{2,1,0:T(8,128)S(1)}, u32[]{:S(2)}) copy-start(f32[4,64,128]{2,1,0:T(8,128)S(1)} %get-tuple-element.81.inverse_ref.inverse_hbm.refs_4_) | copy-start | bytes 393220
  103.1 13.9 %copy-start.9 = (f32[64,384]{1,0:T(8,128)}, f32[64,384]{1,0:T(8,128)S(1)}, u32[]{:S(2)}) copy-start(f32[64,384]{1,0:T(8,128)S(1)} %get-tuple-element.87.refs_5_) | copy-start | bytes 294916
  108.0 12.9 %all-to-all-start.3 = ((f32[16,48,128]{2,1,0:T(8,128)}), f32[16,48,128]{2,1,0:T(8,128)S(1)}, u32[]{:S(2)}, u32[]{:S(2)}) async-start(f32[16,48,128]{2,1,0:T(8,128)} %answer_right.1), calls=%async_computation.3 | async-start | bytes 786432 | tf_op jit(solution)/shard_map/all_to_all | solution.py:855
  111.7 1.3 copy-start.6
  120.8 1.6 %collective-permute-start.6 = (f32[192,128]{1,0:T(8,128)S(1)}, f32[192,128]{1,0:T(8,128)S(1)}, u32[]{:S(2)}, u32[]{:S(2)}) collective-permute-start(f32[192,128]{1,0:T(8,128)S(1)} %slice.39), channel_id=1, source_target_pairs={{0,1},{1,0},{2,3},{3,2},{4,5},{5,4},{6,7},{7,6},{8,9},{9,8},{10,11... | collective-permute-start | bytes 294920 | tf_op jit(solution)/shard_map/ppermute | solution.py:860
  122.4 13.0 %collective-permute-start.9 = (f32[384,128]{1,0:T(8,128)S(1)}, f32[384,128]{1,0:T(8,128)S(1)}, u32[]{:S(2)}, u32[]{:S(2)}) collective-permute-start(f32[384,128]{1,0:T(8,128)S(1)} %pad_maximum_fusion.4.refs_0_), channel_id=1, source_target_pairs={{0,6},{2,0},{4,2},{6,4},{1,7},{3,1},{5,3},{7,5},{8,14},{10,8},{12,... | collective-permute-start | bytes 589832 | tf_op jit(solution)/shard_map/ppermute | solution.py:861
  122.6 12.9 %collective-permute-start.8 = (f32[384,128]{1,0:T(8,128)S(1)}, f32[384,128]{1,0:T(8,128)S(1)}, u32[]{:S(2)}, u32[]{:S(2)}) collective-permute-start(f32[384,128]{1,0:T(8,128)S(1)} %pad_maximum_fusion.4.refs_0_), channel_id=1, source_target_pairs={{0,4},{2,6},{4,0},{6,2},{1,5},{3,7},{5,1},{7,3},{8,12},{10,14},{12... | collective-permute-start | bytes 589832 | tf_op jit(solution)/shard_map/ppermute | solution.py:861
  124.6 10.8 %collective-permute-start.7 = (f32[384,128]{1,0:T(8,128)S(1)}, f32[384,128]{1,0:T(8,128)S(1)}, u32[]{:S(2)}, u32[]{:S(2)}) collective-permute-start(f32[384,128]{1,0:T(8,128)S(1)} %pad_maximum_fusion.4.refs_0_), channel_id=1, source_target_pairs={{0,2},{2,4},{4,6},{6,0},{1,3},{3,5},{5,7},{7,1},{8,10},{10,12},{12... | collective-permute-start | bytes 589832 | tf_op jit(solution)/shard_map/ppermute | solution.py:861

commit v8 on v7

--- a/solution.py
+++ b/solution.py
@@ -29,6 +29,7 @@
 ROWS2 = 768
 EACH2 = 48
 PIECE = HEADS * RANK
+GRAM_ROWS = RANK // 2
 
 f32 = jnp.float32
 bf16 = jnp.bfloat16
@@ -411,7 +412,8 @@
     left_out = wide(left_out_ref[...], RANK)
     factor = stacked(left_out)
     both = jnp.concatenate([factor, stacked(folded(nt(factor, hid_ref[...])))], axis=1)
-    send_ref[RO_ROWS:, :] = jnp.concatenate([exact_nt(left_out, left_out), jnp.zeros((RANK, RANK), f32)], axis=1)
+    gram = exact_nt(left_out, left_out)
+    send_ref[RO_ROWS:, :] = jnp.concatenate([gram[:GRAM_ROWS], gram[GRAM_ROWS:]], axis=1)
     for j in range(0, 8, 2):
         for pair in copies[j : j + 2]:
             for copy in pair:
@@ -434,7 +436,7 @@
         in_specs=[pl.BlockSpec(memory_space=pltpu.SMEM), whole, whole, ANY, ANY, ANY, ANY],
         out_specs=[whole, whole, ANY, ANY],
         out_shape=[
-            jax.ShapeDtypeStruct((RO_ROWS + RANK, 128), f32),
+            jax.ShapeDtypeStruct((RO_ROWS + GRAM_ROWS, 128), f32),
             jax.ShapeDtypeStruct((RO_ROWS, 128), f32),
             pltpu.VMEM((TOK, HALF), bf16),
             pltpu.VMEM((3, HALF, COLS), bf16),
@@ -538,7 +540,7 @@
 def join(*operands):
     return pl.pallas_call(
         join_kernel,
-        out_shape=[jax.ShapeDtypeStruct((ROWS2, 128), f32), jax.ShapeDtypeStruct((RANK, 128), f32)],
+        out_shape=[jax.ShapeDtypeStruct((ROWS2, 128), f32), jax.ShapeDtypeStruct((GRAM_ROWS, 128), f32)],
         cost_estimate=cost(1),
         compiler_params=pltpu.CompilerParams(vmem_limit_bytes=VMEM),
         name="join",
@@ -574,7 +576,8 @@
     for p in range(3):
         mine = slice(RANK * p, RANK * (p + 1))
         inverse_ref[p] = jnp.concatenate([gram[mine, mine], eye], axis=1)
-    inverse_ref[3] = jnp.concatenate([gram_out_ref[:, :RANK], eye], axis=1)
+    gram_out = jnp.concatenate([gram_out_ref[:, :RANK], gram_out_ref[:, RANK:]], axis=0)
+    inverse_ref[3] = jnp.concatenate([gram_out, eye], axis=1)
     rows8 = lax.broadcasted_iota(jnp.int32, (1, 8, 1), 1)
     tiles = [inverse_ref[:, 8 * t : 8 * t + 8, :] for t in range(RANK // 8)]
     for j in range(RANK):

time: 142 us -> 142 us (level)
  no operation moved by 1% of the time
where the time goes in v8:
time: 142 us; the launch traced here: 140 us
  Pallas kernels  62 us (44%)
  starting transfers between devices  26.1 us (18%)
  blocking collectives  25.3 us (18%)
  waiting for transfers between devices  24.3 us (17%)
    all_to_all x1, blocking collectives, shards(): lax.all_to_all(answer_left(me, received), CHIP, 0, 0).reshape(ROWS1, 128)  25.3 us
    all_to_all x1, waiting for transfers between devices, shards(): received = lax.all_to_all(rows.reshape(CHIPS, EACH1, 128), CHIP, 0, 0)  12.1 us
    all_to_all x1, starting transfers between devices, shards(): received = lax.all_to_all(rows.reshape(CHIPS, EACH1, 128), CHIP, 0, 0)  11.5 us
    pallas_call x1, Pallas kernels, ahead(): pl.pallas_call(ahead_kernel, grid=(STEPS,), in_specs=[pl.BlockSpec((TOK,...  9.64 us
    pallas_call x1, Pallas kernels, rest_in(): pl.pallas_call(rest_in_kernel, in_specs=[whole] + [ANY] * 6, out_specs=[A...  9.47 us
    pallas_call x1, Pallas kernels, recurrence(): pl.pallas_call(recurrence_kernel, in_specs=[ANY] * len(operands), out_spe...  8.59 us
    pallas_call x1, Pallas kernels, invert(): pl.pallas_call(invert_kernel, out_shape=[jax.ShapeDtypeStruct((4, RANK, 1...  5.87 us
    pallas_call x1, Pallas kernels, rest_out(): pl.pallas_call(rest_out_kernel, in_specs=[pl.BlockSpec(memory_space=pltpu...  5.49 us
  transfers between devices with their start and end apart: 13, of which 7 were waited for; matrix products, arithmetic and copies ran while one was open for 0% of the time, Pallas kernels for 30%

profile of v8, /device:TPU:0, one launch (start us, length us, event | category | flops | bytes accessed | tf_op | source)
XLA Modules:
  0.0 140.5 jit_solution(8531358305725988250)
XLA Ops:
  0.7 8.6 %recurrence.1 = (bf16[256,384]{1,0:T(8,128)(2,1)S(1)}, bf16[3,256,384]{2,1,0:T(8,128)(2,1)S(1)}, bf16[3,3072,384]{2,1,0:T(8,128)(2,1)S(1)}, bf16[384,3072]{1,0:T...) custom-call(bf16[256,384]{1,0:T(8,128)(2,1)} %q_hbm, bf16[256,384]{1,0:T(8,128)(2,1)} %f_hbm.1, ...), custom_call_target="tpu_custom_call" | custom-call | flops 8000000000 | bytes 24000000 | tf_op jit(solution)/shard_map/recurrence/pallas_call | solution.py:219
  9.4 1.6 %left_send.1 = f32[2304,128]{1,0:T(8,128)S(1)} custom-call(s32[1]{0:T(128)S(6)} %sub.3.half_ref, bf16[256,3072]{1,0:T(8,128)(2,1)S(1)} %get-tuple-element.51.x_ref, bf16[3,256,384]{2,1,0:T(8,128)(2,1)S(1)} %get-tuple-element.52.grads_ref.grads_hbm, bf16[3,3072,384]{2,1,0:T(8,128)(2,1)S(1)} %get-tuple-element.53.err_in_ref, f32[3,64,384]{2,1,0:T(8,128)S(1)} %copy-done.2), custom_call_target="tpu_custom_call" | custom-call | flops 3000000000 | bytes 9000000 | tf_op jit(solution)/shard_map/left_send/pallas_call | solution.py:277
  11.1 1.9 %left_out.1.left_out_ref = f32[192,128]{1,0:T(8,128)S(1)} custom-call(bf16[256,3072]{1,0:T(8,128)(2,1)S(1)} %get-tuple-element.55.gy_ref, bf16[256,384]{1,0:T(8,128)(2,1)S(1)} %get-tuple-element.59.hid_ref, bf16[384,3072]{1,0:T(8,128)(2,1)S(1)} %get-tuple-element.57.err_out_ref, f32[64,3072]{1,0:T(8,128)S(1)} %copy-done.7), custom_call_target="tpu_custom_call" | custom-call | flops 4000000000 | bytes 12000000 | tf_op jit(solution)/shard_map/left_out/pallas_call | solution.py:297
  13.0 0.9 collective-permute-done.arrived_ref
  13.9 2.5 %left_keep.1 = f32[2560,128]{1,0:T(8,128)} custom-call(s32[1]{0:T(128)} %bitcast.half_ref, bf16[256,3072]{1,0:T(8,128)(2,1)S(1)} %get-tuple-element.51.x_ref, bf16[3,256,384]{2,1,0:T(8,128)(2,1)S(1)} %get-tuple-element.52.grads_ref.grads_hbm, bf16[3,3072,384]{2,1,0:T(8,128)(2,1)S(1)} %get-tuple-element.53.err_in_ref, f32[3,64,384]{2,1,0:T(8,128)S(1)} %copy-done.2, ...), custom_call_target="tpu_custom_call" | custom-call | flops 3000000000 | bytes 9000000 | tf_op jit(solution)/shard_map/left_keep/pallas_call | solution.py:277
  16.4 11.5 %all-to-all-start = ((f32[64,40,128]{2,1,0:T(8,128)}), f32[64,40,128]{2,1,0:T(8,128)S(1)}, u32[]{:S(2)}, u32[]{:S(2)}) async-start(f32[64,40,128]{2,1,0:T(8,128)} %bitcast.23), calls=%async_computation | async-start | bytes 2621440 | tf_op jit(solution)/shard_map/all_to_all | solution.py:833
  27.9 9.6 %ahead.1 = (bf16[1536,256]{1,0:T(8,128)(2,1)}, f32[3,1536,384]{2,1,0:T(8,128)}, f32[384,3072]{1,0:T(8,128)}) custom-call(bf16[256,3072]{1,0:T(8,128)(2,1)} %x_hbm.3, bf16[3,256,384]{2,1,0:T(8,128)(2,1)} %copy-done, bf16[3,3072,384]{2,1,0:T(8,128)(2,1)} %bitcast.19, bf16[256,384]{1,0:T(8,128)(2,1)} %copy-done.3, bf16[256,3072]{1,0:T(8,128)(2,1)} %gy_hbm.3, ...), custom_call_target="tpu_custom_call" | custom-call | flops 8999999488 | bytes 27000000 | tf_op jit(solution)/shard_map/ahead/pallas_call | solution.py:318
  37.6 12.1 %all-to-all-done.received_ref = f32[64,40,128]{2,1,0:T(8,128)S(1)} async-done(((f32[64,40,128]{2,1,0:T(8,128)}), f32[64,40,128]{2,1,0:T(8,128)S(1)}, u32[]{:S(2)}, u32[]{:S(2)}) %all-to-all-start) | async-done | bytes 1310752 | tf_op jit(solution)/shard_map/all_to_all | solution.py:833
  49.9 25.3 %all_to_all.20 = f32[64,40,128]{2,1,0:T(8,128)S(1)} all-to-all(f32[64,40,128]{2,1,0:T(8,128)S(1)} %answer_left.1), channel_id=1, replica_groups=mesh['x'=4,'y'=4,'z'=4,'c'=2] {'x','y','z'}, dimensions={0} | all-to-all | bytes 2621440 | tf_op jit(solution)/shard_map/all_to_all | solution.py:836
  75.2 4.4 %right_out.1 = (f32[800,128]{1,0:T(8,128)S(1)}, f32[768,128]{1,0:T(8,128)S(1)}, bf16[256,1536]{1,0:T(8,128)(2,1)S(1)}, bf16[3,1536,384]{2,1,0:T(8,128)(2,1)S(1)}) custom-call(s32[2]{0:T(128)S(1)} %pad_add_fusion.place_ref, f32[192,128]{1,0:T(8,128)S(1)} %slice.40.left_out_ref, bf16[256,384]{1,0:T(8,128)(2,1)S(1)} %copy-done.4, bf16[256,3072]{1,0:T(8,128)(2,1)} %gy_hbm.3, ...), custom_call_target="tpu_custom_call" | custom-call | flops 3000000000 | bytes 9000000 | tf_op jit(solution)/shard_map/right_out/pallas_call | solution.py:434
  80.2 2.1 %gram.1.gram_in_ref = f32[192,192]{1,0:T(8,128)S(1)} custom-call(f32[2560,128]{1,0:T(8,128)S(1)} %bitcast.13, f32[2560,128]{1,0:T(8,128)S(1)} %collective-permute-done.1.other_ref), custom_call_target="tpu_custom_call" | custom-call | flops 2000000000 | bytes 6000000 | tf_op jit(solution)/shard_map/gram/pallas_call | solution.py:560
  82.5 0.9 collective-permute-start.5
  83.5 1.8 %collective-permute-start.3 = (f32[224,128]{1,0:T(8,128)S(1)}, f32[224,128]{1,0:T(8,128)S(1)}, u32[]{:S(2)}, u32[]{:S(2)}) collective-permute-start(f32[224,128]{1,0:T(8,128)S(1)} %get-tuple-element.97), channel_id=1, source_target_pairs={{0,4},{2,6},{4,0},{6,2},{1,5},{3,7},{5,1},{7,3},{8,12},{10,14},{12... | collective-permute-start | bytes 344072 | tf_op jit(solution)/shard_map/ppermute | solution.py:849
  85.3 3.3 %right_own.1 = (f32[3,64,384]{2,1,0:T(8,128)S(1)}, f32[192,256]{1,0:T(8,128)S(1)}, bf16[256,1536]{1,0:T(8,128)(2,1)S(1)}, bf16[3,1536,384]{2,1,0:T(8,128)(2,1)S(1)}) custom-call(s32[1]{0:T(128)S(6)} %sub.3.half_ref, f32[2560,128]{1,0:T(8,128)S(1)} %bitcast.14, bf16[256,1536]{1,0:T(8,128)(2,1)S(1)} %get-tuple-element.65.x_ref, ...), custom_call_target="tpu_custom_call" | custom-call | flops 3000000000 | bytes 9000000 | tf_op jit(solution)/shard_map/right_own/pallas_call | solution.py:496
  88.7 1.4 %right_other.1.right_ref = f32[576,128]{1,0:T(8,128)S(1)} custom-call(f32[2560,128]{1,0:T(8,128)S(1)} %collective-permute-done.1.other_ref, f32[3,64,384]{2,1,0:T(8,128)S(1)} %get-tuple-element.67.right_ref, f32[192,256]{1,0:T(8,128)S(1)} %get-tuple-element.68.token_ref, bf16[256,1536]{1,0:T(8,128)(2,1)S(1)} %get-tuple-element.69.x_ref, ...), custom_call_target="tpu_custom_call" | custom-call | flops 4000000000 | bytes 12000000 | tf_op jit(solution)/shard_map/right_other/pallas_call | solution.py:524
  90.1 0.6 collective-permute-done.3.first_ref
  90.7 1.5 %collective-permute-done.4.second_ref = f32[224,128]{1,0:T(8,128)S(1)} collective-permute-done((f32[224,128]{1,0:T(8,128)S(1)}, f32[224,128]{1,0:T(8,128)S(1)}, u32[]{:S(2)}, u32[]{:S(2)}) %collective-permute-start.4) | collective-permute-done | bytes 114720 | tf_op jit(solution)/shard_map/ppermute | solution.py:849
  92.2 0.8 join.1
  93.0 3.6 %all-to-all-start.2 = ((f32[16,48,128]{2,1,0:T(8,128)}), f32[16,48,128]{2,1,0:T(8,128)S(1)}, u32[]{:S(2)}, u32[]{:S(2)}) async-start(f32[16,48,128]{2,1,0:T(8,128)} %bitcast.7), calls=%async_computation.2 | async-start | bytes 786432 | tf_op jit(solution)/shard_map/all_to_all | solution.py:853
  96.6 5.9 %invert.1 = (f32[4,64,128]{2,1,0:T(8,128)S(1)}, f32[64,384]{1,0:T(8,128)S(1)}) custom-call(f32[192,192]{1,0:T(8,128)S(1)} %gram.1.gram_in_ref, f32[192,128]{1,0:T(8,128)S(1)} %slice.40.left_out_ref, f32[32,128]{1,0:T(8,128)S(1)} %get-tuple-element.75.gram_out_ref), custom_call_target="tpu_custom_call" | custom-call | flops 10000000000 | bytes 30000000 | tf_op jit(solution)/shard_map/invert/pallas_call | solution.py:602
  102.5 4.0 %all-to-all-done.2.received_ref = f32[16,48,128]{2,1,0:T(8,128)S(1)} async-done(((f32[16,48,128]{2,1,0:T(8,128)}), f32[16,48,128]{2,1,0:T(8,128)S(1)}, u32[]{:S(2)}, u32[]{:S(2)}) %all-to-all-start.2) | async-done | bytes 393248 | tf_op jit(solution)/shard_map/all_to_all | solution.py:853
  106.5 0.8 answer_right.1
  107.3 3.7 %all-to-all-start.3 = ((f32[16,48,128]{2,1,0:T(8,128)}), f32[16,48,128]{2,1,0:T(8,128)S(1)}, u32[]{:S(2)}, u32[]{:S(2)}) async-start(f32[16,48,128]{2,1,0:T(8,128)} %answer_right.1), calls=%async_computation.3 | async-start | bytes 786432 | tf_op jit(solution)/shard_map/all_to_all | solution.py:858
  111.0 1.3 copy-done.6
  112.3 4.0 %turn.1.ortho_hbm = bf16[3,3072,128]{2,1,0:T(8,128)(2,1)} custom-call(s32[1]{0:T(128)} %bitcast.half_ref, f32[2560,128]{1,0:T(8,128)S(1)} %bitcast.15, f32[2560,128]{1,0:T(8,128)S(1)} %copy-done.6, f32[4,64,128]{2,1,0:T(8,128)S(1)} %get-tuple-element.81.inverse_ref.inverse_hbm.refs_4_), custom_call_target="tpu_custom_call" | custom-call | flops 6000000000 | bytes 18000000 | tf_op jit(solution)/shard_map/turn/pallas_call | solution.py:637
  116.3 3.8 %all-to-all-done.3 = f32[16,48,128]{2,1,0:T(8,128)S(1)} async-done(((f32[16,48,128]{2,1,0:T(8,128)}), f32[16,48,128]{2,1,0:T(8,128)S(1)}, u32[]{:S(2)}, u32[]{:S(2)}) %all-to-all-start.3) | async-done | bytes 393248 | tf_op jit(solution)/shard_map/all_to_all | solution.py:858
  120.4 1.3 collective-permute-done.6
  121.7 0.6 collective-permute-start.9
  122.4 1.6 %collective-permute-start.8 = (f32[384,128]{1,0:T(8,128)S(1)}, f32[384,128]{1,0:T(8,128)S(1)}, u32[]{:S(2)}, u32[]{:S(2)}) collective-permute-start(f32[384,128]{1,0:T(8,128)S(1)} %pad_maximum_fusion.4.refs_0_), channel_id=1, source_target_pairs={{0,4},{2,6},{4,0},{6,2},{1,5},{3,7},{5,1},{7,3},{8,12},{10,14},{12... | collective-permute-start | bytes 589832 | tf_op jit(solution)/shard_map/ppermute | solution.py:864
  123.9 1.3 collective-permute-start.7
  125.3 9.5 %rest_in.1 = (bf16[3,3072,384]{2,1,0:T(8,128)(2,1)}, f32[3,64,384]{2,1,0:T(8,128)}) custom-call(f32[768,128]{1,0:T(8,128)S(1)} %bitcast.17, f32[4,64,128]{2,1,0:T(8,128)} %copy-done.8, bf16[3,256,384]{2,1,0:T(8,128)(2,1)} %copy-done, bf16[1536,256]{1,0:T(8,128)(2,1)} %get-tuple-element.83.turned_hbm, bf16[3,3072,384]{2,1,0:T(8,128)(2,1)} %bitcast.22, ...), custom_call_target="tpu_custom_call" | custom-call | flops 8999999488 | bytes 27000000 | tf_op jit(solution)/shard_map/rest_in/pallas_call | solution.py:710
  134.8 5.5 %rest_out.1 = (bf16[384,3072]{1,0:T(8,128)(2,1)}, f32[64,3072]{1,0:T(8,128)}) custom-call(s32[2]{0:T(128)S(1)} %pad_add_fusion.place_ref, f32[384,128]{1,0:T(8,128)S(1)} %pad_maximum_fusion.4.refs_0_, f32[384,128]{1,0:T(8,128)S(1)} %collective-permute-done.7.refs_1_, f32[384,128]{1,0:T(8,128)S(1)} %collective-permute-done.8.refs_2_, ...), custom_call_target="tpu_custom_call" | custom-call | flops 6000000000 | bytes 18000000 | tf_op jit(solution)/shard_map/rest_out/pallas_call | solution.py:784
  (39 shorter events, 1.5 us)
Async XLA Ops:
  0.7 8.6 %copy-start.2 = (f32[3,64,384]{2,1,0:T(8,128)S(1)}, f32[3,64,384]{2,1,0:T(8,128)}, u32[]{:S(2)}) copy-start(f32[3,64,384]{2,1,0:T(8,128)} %basis_in_ref.3) | copy-start | bytes 884740
  9.3 1.8 %copy-start.3 = (bf16[256,384]{1,0:T(8,128)(2,1)}, bf16[256,384]{1,0:T(8,128)(2,1)S(1)}, u32[]{:S(2)}) copy-start(bf16[256,384]{1,0:T(8,128)(2,1)S(1)} %get-tuple-element.59.hid_ref) | copy-start | bytes 589828
  9.3 4.6 %copy-start = (bf16[3,256,384]{2,1,0:T(8,128)(2,1)}, bf16[3,256,384]{2,1,0:T(8,128)(2,1)S(1)}, u32[]{:S(2)}) copy-start(bf16[3,256,384]{2,1,0:T(8,128)(2,1)S(1)} %get-tuple-element.52.grads_ref.grads_hbm) | copy-start | bytes 1769476
  9.3 1.8 %copy-start.7 = (f32[64,3072]{1,0:T(8,128)S(1)}, f32[64,3072]{1,0:T(8,128)}, u32[]{:S(2)}) copy-start(f32[64,3072]{1,0:T(8,128)} %basis_out_ref.1) | copy-start | bytes 2359300
  11.0 2.9 %collective-permute-start = (f32[2304,128]{1,0:T(8,128)S(1)}, f32[2304,128]{1,0:T(8,128)S(1)}, u32[]{:S(2)}, u32[]{:S(2)}) collective-permute-start(f32[2304,128]{1,0:T(8,128)S(1)} %left_send.1), channel_id=1, source_target_pairs={{0,1},{1,0},{2,3},{3,2},{4,5},{5,4},{6,7},{7,6},{8,9},{9,8},{10,11... | collective-permute-start | bytes 3538952 | tf_op jit(solution)/shard_map/ppermute | solution.py:828
  16.4 33.3 %all-to-all-start = ((f32[64,40,128]{2,1,0:T(8,128)}), f32[64,40,128]{2,1,0:T(8,128)S(1)}, u32[]{:S(2)}, u32[]{:S(2)}) async-start(f32[64,40,128]{2,1,0:T(8,128)} %bitcast.23), calls=%async_computation | async-start | bytes 2621440 | tf_op jit(solution)/shard_map/all_to_all | solution.py:833
  49.8 25.4 %copy-start.4 = (bf16[256,384]{1,0:T(8,128)(2,1)S(1)}, bf16[256,384]{1,0:T(8,128)(2,1)}, u32[]{:S(2)}) copy-start(bf16[256,384]{1,0:T(8,128)(2,1)} %copy-done.3) | copy-start | bytes 589828
  75.2 5.0 %collective-permute-start.1 = (f32[2560,128]{1,0:T(8,128)S(1)}, f32[2560,128]{1,0:T(8,128)S(1)}, u32[]{:S(2)}, u32[]{:S(2)}) collective-permute-start(f32[2560,128]{1,0:T(8,128)S(1)} %bitcast.11), channel_id=1, source_target_pairs={{0,1},{1,0},{2,3},{3,2},{4,5},{5,4},{6,7},{7,6},{8,9},{9,8},{10,11... | collective-permute-start | bytes 3932168 | tf_op jit(solution)/shard_map/ppermute | solution.py:837
  79.6 2.7 %collective-permute-start.2 = (f32[800,128]{1,0:T(8,128)S(1)}, f32[800,128]{1,0:T(8,128)S(1)}, u32[]{:S(2)}, u32[]{:S(2)}) collective-permute-start(f32[800,128]{1,0:T(8,128)S(1)} %get-tuple-element.63), channel_id=1, source_target_pairs={{0,1},{1,0},{2,3},{3,2},{4,5},{5,4},{6,7},{7,6},{8,9},{9,8},{10,11... | collective-permute-start | bytes 1228808 | tf_op jit(solution)/shard_map/ppermute | solution.py:843
  80.2 8.4 %copy-start.5 = (f32[2560,128]{1,0:T(8,128)}, f32[2560,128]{1,0:T(8,128)S(1)}, u32[]{:S(2)}) copy-start(f32[2560,128]{1,0:T(8,128)S(1)} %collective-permute-done.1.other_ref) | copy-start | bytes 3932164
  82.5 7.6 %collective-permute-start.5 = (f32[224,128]{1,0:T(8,128)S(1)}, f32[224,128]{1,0:T(8,128)S(1)}, u32[]{:S(2)}, u32[]{:S(2)}) collective-permute-start(f32[224,128]{1,0:T(8,128)S(1)} %get-tuple-element.96), channel_id=1, source_target_pairs={{0,6},{2,0},{4,2},{6,4},{1,7},{3,1},{5,3},{7,5},{8,14},{10,8},{12,... | collective-permute-start | bytes 344072 | tf_op jit(solution)/shard_map/ppermute | solution.py:849
  83.5 7.3 %collective-permute-start.3 = (f32[224,128]{1,0:T(8,128)S(1)}, f32[224,128]{1,0:T(8,128)S(1)}, u32[]{:S(2)}, u32[]{:S(2)}) collective-permute-start(f32[224,128]{1,0:T(8,128)S(1)} %get-tuple-element.97), channel_id=1, source_target_pairs={{0,4},{2,6},{4,0},{6,2},{1,5},{3,7},{5,1},{7,3},{8,12},{10,14},{12... | collective-permute-start | bytes 344072 | tf_op jit(solution)/shard_map/ppermute | solution.py:849
  85.2 7.0 %collective-permute-start.4 = (f32[224,128]{1,0:T(8,128)S(1)}, f32[224,128]{1,0:T(8,128)S(1)}, u32[]{:S(2)}, u32[]{:S(2)}) collective-permute-start(f32[224,128]{1,0:T(8,128)S(1)} %get-tuple-element.98), channel_id=1, source_target_pairs={{0,2},{2,4},{4,6},{6,0},{1,3},{3,5},{5,7},{7,1},{8,10},{10,12},{12... | collective-permute-start | bytes 344072 | tf_op jit(solution)/shard_map/ppermute | solution.py:849
  85.3 3.3 %copy-start.1 = (bf16[3,256,384]{2,1,0:T(8,128)(2,1)S(1)}, bf16[3,256,384]{2,1,0:T(8,128)(2,1)}, u32[]{:S(2)}) copy-start(bf16[3,256,384]{2,1,0:T(8,128)(2,1)} %copy-done) | copy-start | bytes 1769476
  93.0 13.5 %all-to-all-start.2 = ((f32[16,48,128]{2,1,0:T(8,128)}), f32[16,48,128]{2,1,0:T(8,128)S(1)}, u32[]{:S(2)}, u32[]{:S(2)}) async-start(f32[16,48,128]{2,1,0:T(8,128)} %bitcast.7), calls=%async_computation.2 | async-start | bytes 786432 | tf_op jit(solution)/shard_map/all_to_all | solution.py:853
  102.4 13.8 %copy-start.8 = (f32[4,64,128]{2,1,0:T(8,128)}, f32[4,64,128]{2,1,0:T(8,128)S(1)}, u32[]{:S(2)}) copy-start(f32[4,64,128]{2,1,0:T(8,128)S(1)} %get-tuple-element.81.inverse_ref.inverse_hbm.refs_4_) | copy-start | bytes 393220
  102.5 13.8 %copy-start.9 = (f32[64,384]{1,0:T(8,128)}, f32[64,384]{1,0:T(8,128)S(1)}, u32[]{:S(2)}) copy-start(f32[64,384]{1,0:T(8,128)S(1)} %get-tuple-element.87.refs_5_) | copy-start | bytes 294916
  107.3 12.9 %all-to-all-start.3 = ((f32[16,48,128]{2,1,0:T(8,128)}), f32[16,48,128]{2,1,0:T(8,128)S(1)}, u32[]{:S(2)}, u32[]{:S(2)}) async-start(f32[16,48,128]{2,1,0:T(8,128)} %answer_right.1), calls=%async_computation.3 | async-start | bytes 786432 | tf_op jit(solution)/shard_map/all_to_all | solution.py:858
  111.0 1.3 copy-start.6
  120.1 1.6 %collective-permute-start.6 = (f32[192,128]{1,0:T(8,128)S(1)}, f32[192,128]{1,0:T(8,128)S(1)}, u32[]{:S(2)}, u32[]{:S(2)}) collective-permute-start(f32[192,128]{1,0:T(8,128)S(1)} %slice.39), channel_id=1, source_target_pairs={{0,1},{1,0},{2,3},{3,2},{4,5},{5,4},{6,7},{7,6},{8,9},{9,8},{10,11... | collective-permute-start | bytes 294920 | tf_op jit(solution)/shard_map/ppermute | solution.py:863
  121.7 13.0 %collective-permute-start.9 = (f32[384,128]{1,0:T(8,128)S(1)}, f32[384,128]{1,0:T(8,128)S(1)}, u32[]{:S(2)}, u32[]{:S(2)}) collective-permute-start(f32[384,128]{1,0:T(8,128)S(1)} %pad_maximum_fusion.4.refs_0_), channel_id=1, source_target_pairs={{0,6},{2,0},{4,2},{6,4},{1,7},{3,1},{5,3},{7,5},{8,14},{10,8},{12,... | collective-permute-start | bytes 589832 | tf_op jit(solution)/shard_map/ppermute | solution.py:864
  122.4 12.4 %collective-permute-start.8 = (f32[384,128]{1,0:T(8,128)S(1)}, f32[384,128]{1,0:T(8,128)S(1)}, u32[]{:S(2)}, u32[]{:S(2)}) collective-permute-start(f32[384,128]{1,0:T(8,128)S(1)} %pad_maximum_fusion.4.refs_0_), channel_id=1, source_target_pairs={{0,4},{2,6},{4,0},{6,2},{1,5},{3,7},{5,1},{7,3},{8,12},{10,14},{12... | collective-permute-start | bytes 589832 | tf_op jit(solution)/shard_map/ppermute | solution.py:864
  123.9 10.8 %collective-permute-start.7 = (f32[384,128]{1,0:T(8,128)S(1)}, f32[384,128]{1,0:T(8,128)S(1)}, u32[]{:S(2)}, u32[]{:S(2)}) collective-permute-start(f32[384,128]{1,0:T(8,128)S(1)} %pad_maximum_fusion.4.refs_0_), channel_id=1, source_target_pairs={{0,2},{2,4},{4,6},{6,0},{1,3},{3,5},{5,7},{7,1},{8,10},{10,12},{12... | collective-permute-start | bytes 589832 | tf_op jit(solution)/shard_map/ppermute | solution.py:864

commit v9 on v8

--- a/solution.py
+++ b/solution.py
@@ -841,14 +841,16 @@
         place, left_out_sum, grad_y, hidden, err_out, inputs, err_in
     )
     arrived = lax.ppermute(send, "c", SWAP)
-    gram_in = gram(own, other)
-    arrived, gram_in, near_inputs = lax.optimization_barrier((arrived, gram_in, near_inputs))
+    arrived, near_inputs = lax.optimization_barrier((arrived, near_inputs))
     gram_out = send[RO_ROWS:] + arrived[RO_ROWS:]
     quarters = (keep_out + arrived[:RO_ROWS]).reshape(4, PIECE, 128)
     pieces = [jnp.concatenate([quarters[shift], gram_out]) for shift in range(4)]
     pieces = [pieces[0]] + [lax.ppermute(pieces[shift], "z", ring(shift)) for shift in OTHERS]
     right_part = right_own(theirs, own, near_inputs, near_err_in, inputs, err_in)
+    right_part, own = lax.optimization_barrier((right_part, own))
+    gram_in = gram(own, other)
     rows, gram_out = join(right_other(other, *right_part, grads), *pieces)
+    rows, gram_in = lax.optimization_barrier((rows, gram_in))
 
     received = lax.all_to_all(rows.reshape(N_DP, EACH2, 128), ("x", "y"), 0, 0)
     inverse, ortho_out = invert(gram_in, left_out_sum, gram_out)

time: 142 us -> 144 us (1.014)
  starting transfers between devices: 26.1 us -> 28.5 us
    ppermute x3, starting transfers between devices: 2.81 us -> 4.63 us  [shards(): lax.ppermute(pieces[shift], 'z', ring(shift))]
  transfers between devices with their start and end apart: 13 -> 13, of which waited for: 7 -> 7; matrix products, arithmetic and copies ran while one was open for 0% -> 0% of each run, Pallas kernels for 30% -> 26%
where the time goes in v9:
time: 144 us; the launch traced here: 143 us
  Pallas kernels  62 us (43%)
  starting transfers between devices  28.5 us (20%)
  blocking collectives  25.4 us (18%)
  waiting for transfers between devices  24.7 us (17%)
    all_to_all x1, blocking collectives, shards(): lax.all_to_all(answer_left(me, received), CHIP, 0, 0).reshape(ROWS1, 128)  25.4 us
    all_to_all x1, waiting for transfers between devices, shards(): received = lax.all_to_all(rows.reshape(CHIPS, EACH1, 128), CHIP, 0, 0)  12.1 us
    all_to_all x1, starting transfers between devices, shards(): received = lax.all_to_all(rows.reshape(CHIPS, EACH1, 128), CHIP, 0, 0)  11.5 us
    pallas_call x1, Pallas kernels, ahead(): pl.pallas_call(ahead_kernel, grid=(STEPS,), in_specs=[pl.BlockSpec((TOK,...  9.63 us
    pallas_call x1, Pallas kernels, rest_in(): pl.pallas_call(rest_in_kernel, in_specs=[whole] + [ANY] * 6, out_specs=[A...  9.47 us
    pallas_call x1, Pallas kernels, recurrence(): pl.pallas_call(recurrence_kernel, in_specs=[ANY] * len(operands), out_spe...  8.59 us
    pallas_call x1, Pallas kernels, invert(): pl.pallas_call(invert_kernel, out_shape=[jax.ShapeDtypeStruct((4, RANK, 1...  5.87 us
    pallas_call x1, Pallas kernels, rest_out(): pl.pallas_call(rest_out_kernel, in_specs=[pl.BlockSpec(memory_space=pltpu...  5.49 us
  transfers between devices with their start and end apart: 13, of which 7 were waited for; matrix products, arithmetic and copies ran while one was open for 0% of the time, Pallas kernels for 26%

profile of v9, /device:TPU:0, one launch (start us, length us, event | category | flops | bytes accessed | tf_op | source)
XLA Modules:
  0.0 143.2 jit_solution(4446031365825441409)
XLA Ops:
  0.7 8.6 %recurrence.1 = (bf16[256,384]{1,0:T(8,128)(2,1)S(1)}, bf16[3,256,384]{2,1,0:T(8,128)(2,1)S(1)}, bf16[3,3072,384]{2,1,0:T(8,128)(2,1)S(1)}, bf16[384,3072]{1,0:T...) custom-call(bf16[256,384]{1,0:T(8,128)(2,1)} %q_hbm, bf16[256,384]{1,0:T(8,128)(2,1)} %f_hbm.1, ...), custom_call_target="tpu_custom_call" | custom-call | flops 8000000000 | bytes 24000000 | tf_op jit(solution)/shard_map/recurrence/pallas_call | solution.py:219
  9.4 1.6 %left_send.1 = f32[2304,128]{1,0:T(8,128)S(1)} custom-call(s32[1]{0:T(128)S(6)} %sub.3.half_ref, bf16[256,3072]{1,0:T(8,128)(2,1)S(1)} %get-tuple-element.57.x_ref, bf16[3,256,384]{2,1,0:T(8,128)(2,1)S(1)} %get-tuple-element.58.grads_ref.grads_hbm, bf16[3,3072,384]{2,1,0:T(8,128)(2,1)S(1)} %get-tuple-element.59.err_in_ref, f32[3,64,384]{2,1,0:T(8,128)S(1)} %copy-done.2), custom_call_target="tpu_custom_call" | custom-call | flops 3000000000 | bytes 9000000 | tf_op jit(solution)/shard_map/left_send/pallas_call | solution.py:277
  11.1 1.9 %left_out.1.left_out_ref = f32[192,128]{1,0:T(8,128)S(1)} custom-call(bf16[256,3072]{1,0:T(8,128)(2,1)S(1)} %get-tuple-element.61.gy_ref, bf16[256,384]{1,0:T(8,128)(2,1)S(1)} %get-tuple-element.65.hid_ref, bf16[384,3072]{1,0:T(8,128)(2,1)S(1)} %get-tuple-element.63.err_out_ref, f32[64,3072]{1,0:T(8,128)S(1)} %copy-done.7), custom_call_target="tpu_custom_call" | custom-call | flops 4000000000 | bytes 12000000 | tf_op jit(solution)/shard_map/left_out/pallas_call | solution.py:297
  13.0 0.9 collective-permute-done.arrived_ref
  13.9 2.4 %left_keep.1 = f32[2560,128]{1,0:T(8,128)} custom-call(s32[1]{0:T(128)} %bitcast.half_ref, bf16[256,3072]{1,0:T(8,128)(2,1)S(1)} %get-tuple-element.57.x_ref, bf16[3,256,384]{2,1,0:T(8,128)(2,1)S(1)} %get-tuple-element.58.grads_ref.grads_hbm, bf16[3,3072,384]{2,1,0:T(8,128)(2,1)S(1)} %get-tuple-element.59.err_in_ref, f32[3,64,384]{2,1,0:T(8,128)S(1)} %copy-done.2, ...), custom_call_target="tpu_custom_call" | custom-call | flops 3000000000 | bytes 9000000 | tf_op jit(solution)/shard_map/left_keep/pallas_call | solution.py:277
  16.4 11.5 %all-to-all-start = ((f32[64,40,128]{2,1,0:T(8,128)}), f32[64,40,128]{2,1,0:T(8,128)S(1)}, u32[]{:S(2)}, u32[]{:S(2)}) async-start(f32[64,40,128]{2,1,0:T(8,128)} %bitcast.23), calls=%async_computation | async-start | bytes 2621440 | tf_op jit(solution)/shard_map/all_to_all | solution.py:833
  27.9 9.6 %ahead.1 = (bf16[1536,256]{1,0:T(8,128)(2,1)}, f32[3,1536,384]{2,1,0:T(8,128)}, f32[384,3072]{1,0:T(8,128)}) custom-call(bf16[256,3072]{1,0:T(8,128)(2,1)} %x_hbm.3, bf16[3,256,384]{2,1,0:T(8,128)(2,1)} %copy-done, bf16[3,3072,384]{2,1,0:T(8,128)(2,1)} %bitcast.19, bf16[256,384]{1,0:T(8,128)(2,1)} %copy-done.3, bf16[256,3072]{1,0:T(8,128)(2,1)} %gy_hbm.3, ...), custom_call_target="tpu_custom_call" | custom-call | flops 8999999488 | bytes 27000000 | tf_op jit(solution)/shard_map/ahead/pallas_call | solution.py:318
  37.5 12.1 %all-to-all-done.received_ref = f32[64,40,128]{2,1,0:T(8,128)S(1)} async-done(((f32[64,40,128]{2,1,0:T(8,128)}), f32[64,40,128]{2,1,0:T(8,128)S(1)}, u32[]{:S(2)}, u32[]{:S(2)}) %all-to-all-start) | async-done | bytes 1310752 | tf_op jit(solution)/shard_map/all_to_all | solution.py:833
  49.8 25.4 %all_to_all.20 = f32[64,40,128]{2,1,0:T(8,128)S(1)} all-to-all(f32[64,40,128]{2,1,0:T(8,128)S(1)} %answer_left.1), channel_id=1, replica_groups=mesh['x'=4,'y'=4,'z'=4,'c'=2] {'x','y','z'}, dimensions={0} | all-to-all | bytes 2621440 | tf_op jit(solution)/shard_map/all_to_all | solution.py:836
  75.2 4.4 %right_out.1 = (f32[800,128]{1,0:T(8,128)S(1)}, f32[768,128]{1,0:T(8,128)S(1)}, bf16[256,1536]{1,0:T(8,128)(2,1)S(1)}, bf16[3,1536,384]{2,1,0:T(8,128)(2,1)S(1)}) custom-call(s32[2]{0:T(128)S(1)} %pad_add_fusion.place_ref, f32[192,128]{1,0:T(8,128)S(1)} %slice.40.left_out_ref, bf16[256,384]{1,0:T(8,128)(2,1)S(1)} %copy-done.4, bf16[256,3072]{1,0:T(8,128)(2,1)} %gy_hbm.3, ...), custom_call_target="tpu_custom_call" | custom-call | flops 3000000000 | bytes 9000000 | tf_op jit(solution)/shard_map/right_out/pallas_call | solution.py:434
  79.7 0.5 collective-permute-start.1
  80.2 1.2 collective-permute-done.2
  81.5 3.3 %right_own.1 = (f32[3,64,384]{2,1,0:T(8,128)S(1)}, f32[192,256]{1,0:T(8,128)S(1)}, bf16[256,1536]{1,0:T(8,128)(2,1)S(1)}, bf16[3,1536,384]{2,1,0:T(8,128)(2,1)S(1)}) custom-call(s32[1]{0:T(128)S(6)} %sub.3.half_ref, f32[2560,128]{1,0:T(8,128)S(1)} %bitcast.13, bf16[256,1536]{1,0:T(8,128)(2,1)S(1)} %get-tuple-element.71.x_ref, ...), custom_call_target="tpu_custom_call" | custom-call | flops 3000000000 | bytes 9000000 | tf_op jit(solution)/shard_map/right_own/pallas_call | solution.py:496
  84.9 1.4 collective-permute-start.3
  86.7 2.8 %collective-permute-start.5 = (f32[224,128]{1,0:T(8,128)S(1)}, f32[224,128]{1,0:T(8,128)S(1)}, u32[]{:S(2)}, u32[]{:S(2)}) collective-permute-start(f32[224,128]{1,0:T(8,128)S(1)} %get-tuple-element.108), channel_id=1, source_target_pairs={{0,6},{2,0},{4,2},{6,4},{1,7},{3,1},{5,3},{7,5},{8,14},{10,8},{12,... | collective-permute-start | bytes 344072 | tf_op jit(solution)/shard_map/ppermute | solution.py:848
  89.5 1.4 right_other.1.right_ref
  91.0 2.1 %gram.1.gram_in_ref = f32[192,192]{1,0:T(8,128)S(1)} custom-call(f32[2560,128]{1,0:T(8,128)S(1)} %bitcast.14, f32[2560,128]{1,0:T(8,128)S(1)} %collective-permute-done.1.other_ref), custom_call_target="tpu_custom_call" | custom-call | flops 2000000000 | bytes 6000000 | tf_op jit(solution)/shard_map/gram/pallas_call | solution.py:560
  93.1 1.0 collective-permute-done.4.second_ref
  94.1 0.8 join.1
  94.9 3.6 %all-to-all-start.2 = ((f32[16,48,128]{2,1,0:T(8,128)}), f32[16,48,128]{2,1,0:T(8,128)S(1)}, u32[]{:S(2)}, u32[]{:S(2)}) async-start(f32[16,48,128]{2,1,0:T(8,128)} %bitcast.7), calls=%async_computation.2 | async-start | bytes 786432 | tf_op jit(solution)/shard_map/all_to_all | solution.py:855
  98.5 5.9 %invert.1 = (f32[4,64,128]{2,1,0:T(8,128)S(1)}, f32[64,384]{1,0:T(8,128)S(1)}) custom-call(f32[192,192]{1,0:T(8,128)S(1)} %gram.1.gram_in_ref, f32[192,128]{1,0:T(8,128)S(1)} %slice.40.left_out_ref, f32[32,128]{1,0:T(8,128)S(1)} %get-tuple-element.87.gram_out_ref), custom_call_target="tpu_custom_call" | custom-call | flops 10000000000 | bytes 30000000 | tf_op jit(solution)/shard_map/invert/pallas_call | solution.py:602
  104.4 4.3 %all-to-all-done.2.received_ref = f32[16,48,128]{2,1,0:T(8,128)S(1)} async-done(((f32[16,48,128]{2,1,0:T(8,128)}), f32[16,48,128]{2,1,0:T(8,128)S(1)}, u32[]{:S(2)}, u32[]{:S(2)}) %all-to-all-start.2) | async-done | bytes 393248 | tf_op jit(solution)/shard_map/all_to_all | solution.py:855
  108.7 0.8 answer_right.1
  109.5 3.7 %all-to-all-start.3 = ((f32[16,48,128]{2,1,0:T(8,128)}), f32[16,48,128]{2,1,0:T(8,128)S(1)}, u32[]{:S(2)}, u32[]{:S(2)}) async-start(f32[16,48,128]{2,1,0:T(8,128)} %answer_right.1), calls=%async_computation.3 | async-start | bytes 786432 | tf_op jit(solution)/shard_map/all_to_all | solution.py:860
  113.2 1.3 copy-done.6
  114.6 4.0 %turn.1.ortho_hbm = bf16[3,3072,128]{2,1,0:T(8,128)(2,1)} custom-call(s32[1]{0:T(128)} %bitcast.half_ref, f32[2560,128]{1,0:T(8,128)S(1)} %bitcast.15, f32[2560,128]{1,0:T(8,128)S(1)} %copy-done.6, f32[4,64,128]{2,1,0:T(8,128)S(1)} %get-tuple-element.93.inverse_ref.inverse_hbm.refs_4_), custom_call_target="tpu_custom_call" | custom-call | flops 6000000000 | bytes 18000000 | tf_op jit(solution)/shard_map/turn/pallas_call | solution.py:637
  118.5 3.8 %all-to-all-done.3 = f32[16,48,128]{2,1,0:T(8,128)S(1)} async-done(((f32[16,48,128]{2,1,0:T(8,128)}), f32[16,48,128]{2,1,0:T(8,128)S(1)}, u32[]{:S(2)}, u32[]{:S(2)}) %all-to-all-start.3) | async-done | bytes 393248 | tf_op jit(solution)/shard_map/all_to_all | solution.py:860
  122.7 1.3 collective-permute-done.6
  124.4 1.6 %collective-permute-start.8 = (f32[384,128]{1,0:T(8,128)S(1)}, f32[384,128]{1,0:T(8,128)S(1)}, u32[]{:S(2)}, u32[]{:S(2)}) collective-permute-start(f32[384,128]{1,0:T(8,128)S(1)} %pad_maximum_fusion.4.refs_0_), channel_id=1, source_target_pairs={{0,4},{2,6},{4,0},{6,2},{1,5},{3,7},{5,1},{7,3},{8,12},{10,14},{12... | collective-permute-start | bytes 589832 | tf_op jit(solution)/shard_map/ppermute | solution.py:866
  126.1 2.0 %collective-permute-start.9 = (f32[384,128]{1,0:T(8,128)S(1)}, f32[384,128]{1,0:T(8,128)S(1)}, u32[]{:S(2)}, u32[]{:S(2)}) collective-permute-start(f32[384,128]{1,0:T(8,128)S(1)} %pad_maximum_fusion.4.refs_0_), channel_id=1, source_target_pairs={{0,6},{2,0},{4,2},{6,4},{1,7},{3,1},{5,3},{7,5},{8,14},{10,8},{12,... | collective-permute-start | bytes 589832 | tf_op jit(solution)/shard_map/ppermute | solution.py:866
  128.0 9.5 %rest_in.1 = (bf16[3,3072,384]{2,1,0:T(8,128)(2,1)}, f32[3,64,384]{2,1,0:T(8,128)}) custom-call(f32[768,128]{1,0:T(8,128)S(1)} %bitcast.17, f32[4,64,128]{2,1,0:T(8,128)} %copy-done.8, bf16[3,256,384]{2,1,0:T(8,128)(2,1)} %copy-done, bf16[1536,256]{1,0:T(8,128)(2,1)} %get-tuple-element.95.turned_hbm, bf16[3,3072,384]{2,1,0:T(8,128)(2,1)} %bitcast.22, ...), custom_call_target="tpu_custom_call" | custom-call | flops 8999999488 | bytes 27000000 | tf_op jit(solution)/shard_map/rest_in/pallas_call | solution.py:710
  137.6 5.5 %rest_out.1 = (bf16[384,3072]{1,0:T(8,128)(2,1)}, f32[64,3072]{1,0:T(8,128)}) custom-call(s32[2]{0:T(128)S(1)} %pad_add_fusion.place_ref, f32[384,128]{1,0:T(8,128)S(1)} %pad_maximum_fusion.4.refs_0_, f32[384,128]{1,0:T(8,128)S(1)} %collective-permute-done.7.refs_1_, f32[384,128]{1,0:T(8,128)S(1)} %collective-permute-done.8.refs_2_, ...), custom_call_target="tpu_custom_call" | custom-call | flops 6000000000 | bytes 18000000 | tf_op jit(solution)/shard_map/rest_out/pallas_call | solution.py:784
  (39 shorter events, 1.7 us)
Async XLA Ops:
  0.7 8.6 %copy-start.2 = (f32[3,64,384]{2,1,0:T(8,128)S(1)}, f32[3,64,384]{2,1,0:T(8,128)}, u32[]{:S(2)}) copy-start(f32[3,64,384]{2,1,0:T(8,128)} %basis_in_ref.3) | copy-start | bytes 884740
  9.3 1.8 %copy-start.3 = (bf16[256,384]{1,0:T(8,128)(2,1)}, bf16[256,384]{1,0:T(8,128)(2,1)S(1)}, u32[]{:S(2)}) copy-start(bf16[256,384]{1,0:T(8,128)(2,1)S(1)} %get-tuple-element.65.hid_ref) | copy-start | bytes 589828
  9.3 4.6 %copy-start = (bf16[3,256,384]{2,1,0:T(8,128)(2,1)}, bf16[3,256,384]{2,1,0:T(8,128)(2,1)S(1)}, u32[]{:S(2)}) copy-start(bf16[3,256,384]{2,1,0:T(8,128)(2,1)S(1)} %get-tuple-element.58.grads_ref.grads_hbm) | copy-start | bytes 1769476
  9.3 1.8 %copy-start.7 = (f32[64,3072]{1,0:T(8,128)S(1)}, f32[64,3072]{1,0:T(8,128)}, u32[]{:S(2)}) copy-start(f32[64,3072]{1,0:T(8,128)} %basis_out_ref.1) | copy-start | bytes 2359300
  11.0 2.9 %collective-permute-start = (f32[2304,128]{1,0:T(8,128)S(1)}, f32[2304,128]{1,0:T(8,128)S(1)}, u32[]{:S(2)}, u32[]{:S(2)}) collective-permute-start(f32[2304,128]{1,0:T(8,128)S(1)} %left_send.1), channel_id=1, source_target_pairs={{0,1},{1,0},{2,3},{3,2},{4,5},{5,4},{6,7},{7,6},{8,9},{9,8},{10,11... | collective-permute-start | bytes 3538952 | tf_op jit(solution)/shard_map/ppermute | solution.py:828
  16.4 33.3 %all-to-all-start = ((f32[64,40,128]{2,1,0:T(8,128)}), f32[64,40,128]{2,1,0:T(8,128)S(1)}, u32[]{:S(2)}, u32[]{:S(2)}) async-start(f32[64,40,128]{2,1,0:T(8,128)} %bitcast.23), calls=%async_computation | async-start | bytes 2621440 | tf_op jit(solution)/shard_map/all_to_all | solution.py:833
  49.8 25.4 %copy-start.4 = (bf16[256,384]{1,0:T(8,128)(2,1)S(1)}, bf16[256,384]{1,0:T(8,128)(2,1)}, u32[]{:S(2)}) copy-start(bf16[256,384]{1,0:T(8,128)(2,1)} %copy-done.3) | copy-start | bytes 589828
  79.6 1.8 %collective-permute-start.2 = (f32[800,128]{1,0:T(8,128)S(1)}, f32[800,128]{1,0:T(8,128)S(1)}, u32[]{:S(2)}, u32[]{:S(2)}) collective-permute-start(f32[800,128]{1,0:T(8,128)S(1)} %get-tuple-element.69), channel_id=1, source_target_pairs={{0,1},{1,0},{2,3},{3,2},{4,5},{5,4},{6,7},{7,6},{8,9},{9,8},{10,11... | collective-permute-start | bytes 1228808 | tf_op jit(solution)/shard_map/ppermute | solution.py:843
  79.7 9.8 %collective-permute-start.1 = (f32[2560,128]{1,0:T(8,128)S(1)}, f32[2560,128]{1,0:T(8,128)S(1)}, u32[]{:S(2)}, u32[]{:S(2)}) collective-permute-start(f32[2560,128]{1,0:T(8,128)S(1)} %bitcast.12), channel_id=1, source_target_pairs={{0,1},{1,0},{2,3},{3,2},{4,5},{5,4},{6,7},{7,6},{8,9},{9,8},{10,11... | collective-permute-start | bytes 3932168 | tf_op jit(solution)/shard_map/ppermute | solution.py:837
  84.8 4.8 %copy-start.1 = (bf16[3,256,384]{2,1,0:T(8,128)(2,1)S(1)}, bf16[3,256,384]{2,1,0:T(8,128)(2,1)}, u32[]{:S(2)}) copy-start(bf16[3,256,384]{2,1,0:T(8,128)(2,1)} %copy-done) | copy-start | bytes 1769476
  84.9 8.2 %collective-permute-start.3 = (f32[224,128]{1,0:T(8,128)S(1)}, f32[224,128]{1,0:T(8,128)S(1)}, u32[]{:S(2)}, u32[]{:S(2)}) collective-permute-start(f32[224,128]{1,0:T(8,128)S(1)} %get-tuple-element.109), channel_id=1, source_target_pairs={{0,4},{2,6},{4,0},{6,2},{1,5},{3,7},{5,1},{7,3},{8,12},{10,14},{12... | collective-permute-start | bytes 344072 | tf_op jit(solution)/shard_map/ppermute | solution.py:848
  86.3 7.8 %collective-permute-start.4 = (f32[224,128]{1,0:T(8,128)S(1)}, f32[224,128]{1,0:T(8,128)S(1)}, u32[]{:S(2)}, u32[]{:S(2)}) collective-permute-start(f32[224,128]{1,0:T(8,128)S(1)} %get-tuple-element.110), channel_id=1, source_target_pairs={{0,2},{2,4},{4,6},{6,0},{1,3},{3,5},{5,7},{7,1},{8,10},{10,12},{12... | collective-permute-start | bytes 344072 | tf_op jit(solution)/shard_map/ppermute | solution.py:848
  86.7 7.4 %collective-permute-start.5 = (f32[224,128]{1,0:T(8,128)S(1)}, f32[224,128]{1,0:T(8,128)S(1)}, u32[]{:S(2)}, u32[]{:S(2)}) collective-permute-start(f32[224,128]{1,0:T(8,128)S(1)} %get-tuple-element.108), channel_id=1, source_target_pairs={{0,6},{2,0},{4,2},{6,4},{1,7},{3,1},{5,3},{7,5},{8,14},{10,8},{12,... | collective-permute-start | bytes 344072 | tf_op jit(solution)/shard_map/ppermute | solution.py:848
  89.5 1.4 %copy-start.5 = (f32[2560,128]{1,0:T(8,128)}, f32[2560,128]{1,0:T(8,128)S(1)}, u32[]{:S(2)}) copy-start(f32[2560,128]{1,0:T(8,128)S(1)} %collective-permute-done.1.other_ref) | copy-start | bytes 3932164
  94.9 13.8 %all-to-all-start.2 = ((f32[16,48,128]{2,1,0:T(8,128)}), f32[16,48,128]{2,1,0:T(8,128)S(1)}, u32[]{:S(2)}, u32[]{:S(2)}) async-start(f32[16,48,128]{2,1,0:T(8,128)} %bitcast.7), calls=%async_computation.2 | async-start | bytes 786432 | tf_op jit(solution)/shard_map/all_to_all | solution.py:855
  104.4 14.2 %copy-start.8 = (f32[4,64,128]{2,1,0:T(8,128)}, f32[4,64,128]{2,1,0:T(8,128)S(1)}, u32[]{:S(2)}) copy-start(f32[4,64,128]{2,1,0:T(8,128)S(1)} %get-tuple-element.93.inverse_ref.inverse_hbm.refs_4_) | copy-start | bytes 393220
  104.4 14.2 %copy-start.9 = (f32[64,384]{1,0:T(8,128)}, f32[64,384]{1,0:T(8,128)S(1)}, u32[]{:S(2)}) copy-start(f32[64,384]{1,0:T(8,128)S(1)} %get-tuple-element.99.refs_5_) | copy-start | bytes 294916
  109.5 12.9 %all-to-all-start.3 = ((f32[16,48,128]{2,1,0:T(8,128)}), f32[16,48,128]{2,1,0:T(8,128)S(1)}, u32[]{:S(2)}, u32[]{:S(2)}) async-start(f32[16,48,128]{2,1,0:T(8,128)} %answer_right.1), calls=%async_computation.3 | async-start | bytes 786432 | tf_op jit(solution)/shard_map/all_to_all | solution.py:860
  113.2 1.3 copy-start.6
  122.4 1.6 %collective-permute-start.6 = (f32[192,128]{1,0:T(8,128)S(1)}, f32[192,128]{1,0:T(8,128)S(1)}, u32[]{:S(2)}, u32[]{:S(2)}) collective-permute-start(f32[192,128]{1,0:T(8,128)S(1)} %slice.39), channel_id=1, source_target_pairs={{0,1},{1,0},{2,3},{3,2},{4,5},{5,4},{6,7},{7,6},{8,9},{9,8},{10,11... | collective-permute-start | bytes 294920 | tf_op jit(solution)/shard_map/ppermute | solution.py:865
  124.0 13.5 %collective-permute-start.7 = (f32[384,128]{1,0:T(8,128)S(1)}, f32[384,128]{1,0:T(8,128)S(1)}, u32[]{:S(2)}, u32[]{:S(2)}) collective-permute-start(f32[384,128]{1,0:T(8,128)S(1)} %pad_maximum_fusion.4.refs_0_), channel_id=1, source_target_pairs={{0,2},{2,4},{4,6},{6,0},{1,3},{3,5},{5,7},{7,1},{8,10},{10,12},{12... | collective-permute-start | bytes 589832 | tf_op jit(solution)/shard_map/ppermute | solution.py:866
  124.4 13.1 %collective-permute-start.8 = (f32[384,128]{1,0:T(8,128)S(1)}, f32[384,128]{1,0:T(8,128)S(1)}, u32[]{:S(2)}, u32[]{:S(2)}) collective-permute-start(f32[384,128]{1,0:T(8,128)S(1)} %pad_maximum_fusion.4.refs_0_), channel_id=1, source_target_pairs={{0,4},{2,6},{4,0},{6,2},{1,5},{3,7},{5,1},{7,3},{8,12},{10,14},{12... | collective-permute-start | bytes 589832 | tf_op jit(solution)/shard_map/ppermute | solution.py:866
  126.1 11.5 %collective-permute-start.9 = (f32[384,128]{1,0:T(8,128)S(1)}, f32[384,128]{1,0:T(8,128)S(1)}, u32[]{:S(2)}, u32[]{:S(2)}) collective-permute-start(f32[384,128]{1,0:T(8,128)S(1)} %pad_maximum_fusion.4.refs_0_), channel_id=1, source_target_pairs={{0,6},{2,0},{4,2},{6,4},{1,7},{3,1},{5,3},{7,5},{8,14},{10,8},{12,... | collective-permute-start | bytes 589832 | tf_op jit(solution)/shard_map/ppermute | solution.py:866
